TPU v7x, 32 devices: a whole 2x2x4 slice. The times are simulated.
32 devices in a mesh: emb: 16 (over z, y, x), bal: 2 (over core).
Axes of the slice: x: 2, y: 2, z: 4, core: 2. Of those that a mesh axis runs over, the one named last changes fastest.
Arguments:
- item_ids: int32 [2, 4096, 4], P('bal'), may hold values from 0 to 1023
- seq_lengths: int32 [2, 16, 2], P(None, 'emb'), may hold values from 1 to 128, as said below
- surplus_slot: int32 [2, 16], P(None, 'emb'), may hold values from 0 to 1
- helper_map: int32 [2, 16], P(None, 'emb'), may hold values from 0 to 1, as said below
- embed_tables: bfloat16 [16, 1024, 128], P('emb'), may hold values from -3 to 3
- weight_in: bfloat16 [512, 2048], P('bal'), may hold values from -0.25 to 0.25
- weight_out: bfloat16 [512, 512], P('bal'), may hold values from -0.25 to 0.25
- cotangent: bfloat16 [2, 4096, 512], P('bal', 'emb'), may hold values from -6 to 6
Outputs:
- layer_out: bfloat16 [2, 4096, 512], P('bal', 'emb')
- table_grad: float32 [16, 1024, 128], P('emb', 'bal')
- grad_in: float32 [512, 2048], P('bal')
- grad_out: float32 [512, 512], P('bal')
Inputs may be any that keep to these rules, and one draw needn't show every extreme that they name: `seq_lengths`: some slot has 128 live events. Each column helper_map[:, e] is a permutation of the bal indices.
All inputs are finite; a program needn't handle non-finite values.
Results may differ from a plain program's by a relative error of at most 0.014.
Values may be sent and summed in bfloat16 or wider, within the bound.
No kernel may reach another device: no remote copies, remote signals or barrier semaphores. Data moves between devices by JAX's collectives and lax.ppermute only.
A program may use at most 64 MiB of HBM per device.

v0:
```python
import jax
import jax.numpy as jnp
from jax import lax
from jax.sharding import PartitionSpec as P

D = 512
HEADS = 8
COLS = 128
DISTINCT = 1024
SLOT = 128
NSEQ = 2


EPS = 1e-05


def silu_grad(argument):
    logistic = jax.nn.sigmoid(argument)
    return logistic * (1.0 + argument * (1.0 - logistic))


def seq_mask(lengths, row_count, slot_rows):
    position = jnp.arange(row_count, dtype=jnp.int32)
    slot_of = position // slot_rows
    within = position - slot_of * slot_rows
    slot_ids = jnp.arange(lengths.shape[0], dtype=jnp.int32)
    row_length = jnp.sum(
        jnp.where(slot_of[:, None] == slot_ids[None, :], lengths[None, :], 0), axis=1
    )
    same_slot = slot_of[:, None] == slot_of[None, :]
    causal = position[None, :] <= position[:, None]
    live = within[:, None] < row_length[:, None]
    return jnp.where(same_slot & causal & live, 1.0, 0.0).astype(jnp.float32)


def normalize(values):
    average = jnp.mean(values, axis=1, keepdims=True)
    centred = values - average
    inverse = lax.rsqrt(jnp.mean(centred * centred, axis=1, keepdims=True) + EPS)
    return (centred * inverse, inverse)


def norm_back(incoming, normed, inverse):
    first = jnp.mean(incoming, axis=1, keepdims=True)
    second = jnp.mean(incoming * normed, axis=1, keepdims=True)
    return inverse * (incoming - first - normed * second)


def head_slices(heads_input, head_index, head_width, model_width):
    head_values = lax.dynamic_slice_in_dim(heads_input, head_index * head_width, head_width, 1)
    head_query = lax.dynamic_slice_in_dim(
        heads_input, model_width + head_index * head_width, head_width, 1
    )
    head_keys = lax.dynamic_slice_in_dim(
        heads_input, 2 * model_width + head_index * head_width, head_width, 1
    )
    return (head_values, head_query, head_keys)


def head_forward(heads_input, allowed, head_index, head_width, model_width, seq_bound):
    head_values, head_query, head_keys = head_slices(
        heads_input, head_index, head_width, model_width
    )
    scores = jnp.dot(head_query, head_keys.T, preferred_element_type=jnp.float32) * head_width ** (
        -0.5
    )
    silu_weights = (jax.nn.silu(scores) * allowed / seq_bound).astype(jnp.bfloat16)
    return jnp.dot(silu_weights, head_values, preferred_element_type=jnp.float32)


def head_backward(
    heads_input, allowed, grad_attended, head_index, head_width, model_width, seq_bound
):
    head_values, head_query, head_keys = head_slices(
        heads_input, head_index, head_width, model_width
    )
    score_scale = head_width ** (-0.5)
    scores = jnp.dot(head_query, head_keys.T, preferred_element_type=jnp.float32) * score_scale
    silu_weights = (jax.nn.silu(scores) * allowed / seq_bound).astype(jnp.bfloat16)
    grad_head = lax.dynamic_slice_in_dim(grad_attended, head_index * head_width, head_width, 1)
    grad_weights = jnp.dot(grad_head, head_values.T, preferred_element_type=jnp.float32)
    grad_values = jnp.dot(silu_weights.T, grad_head, preferred_element_type=jnp.float32)
    grad_scores = (grad_weights * allowed / seq_bound * silu_grad(scores)).astype(jnp.bfloat16)
    grad_query = jnp.dot(grad_scores, head_keys, preferred_element_type=jnp.float32) * score_scale
    grad_keys = jnp.dot(grad_scores.T, head_query, preferred_element_type=jnp.float32) * score_scale
    return (grad_values, grad_query, grad_keys)


def join_heads(stacked):
    head_count, row_count, head_width = stacked.shape
    return jnp.transpose(stacked, (1, 0, 2)).reshape(row_count, head_count * head_width)


def layer_forward(inputs, lengths, weight_in, weight_out, head_count, slot_rows):
    row_count, model_width = inputs.shape
    head_width = model_width // head_count
    allowed = seq_mask(lengths, row_count, slot_rows)
    normed_in, in_inverse = normalize(inputs.astype(jnp.float32))
    normed_half = normed_in.astype(jnp.bfloat16)
    projected = jnp.dot(normed_half, weight_in, preferred_element_type=jnp.float32)
    activated = jax.nn.silu(projected)
    gate_rows = activated[:, :model_width]
    heads_input = activated[:, model_width:].astype(jnp.bfloat16)
    head_ids = jnp.arange(head_count, dtype=jnp.int32)
    attended = lax.map(
        lambda head_index: head_forward(
            heads_input, allowed, head_index, head_width, model_width, slot_rows
        ),
        head_ids,
    )
    normed_out, out_inverse = normalize(join_heads(attended))
    mixed_rows = (normed_out * gate_rows).astype(jnp.bfloat16)
    forward_out = (
        inputs.astype(jnp.float32)
        + jnp.dot(mixed_rows, weight_out, preferred_element_type=jnp.float32)
    ).astype(jnp.bfloat16)
    stored = (
        allowed,
        normed_in,
        in_inverse,
        normed_half,
        projected,
        gate_rows,
        heads_input,
        normed_out,
        out_inverse,
        mixed_rows,
    )
    return (forward_out, stored)


def layer_backward(stored, cotangent, weight_in, weight_out, head_count, slot_rows):
    (
        allowed,
        normed_in,
        in_inverse,
        normed_half,
        projected,
        gate_rows,
        heads_input,
        normed_out,
        out_inverse,
        mixed_rows,
    ) = stored
    row_count, model_width = normed_in.shape
    head_width = model_width // head_count
    partial_out = jnp.dot(mixed_rows.T, cotangent, preferred_element_type=jnp.float32)
    grad_mixed = jnp.dot(cotangent, weight_out.T, preferred_element_type=jnp.float32)
    grad_gate = grad_mixed * normed_out
    grad_attended = norm_back(grad_mixed * gate_rows, normed_out, out_inverse).astype(jnp.bfloat16)
    head_ids = jnp.arange(head_count, dtype=jnp.int32)
    head_grads = lax.map(
        lambda head_index: head_backward(
            heads_input, allowed, grad_attended, head_index, head_width, model_width, slot_rows
        ),
        head_ids,
    )
    grad_heads = jnp.concatenate(
        [join_heads(head_grads[0]), join_heads(head_grads[1]), join_heads(head_grads[2])], axis=1
    )
    grad_projected = (
        jnp.concatenate([grad_gate, grad_heads], axis=1) * silu_grad(projected)
    ).astype(jnp.bfloat16)
    partial_in = jnp.dot(normed_half.T, grad_projected, preferred_element_type=jnp.float32)
    grad_normed = jnp.dot(grad_projected, weight_in.T, preferred_element_type=jnp.float32)
    grad_rows = (
        cotangent.astype(jnp.float32) + norm_back(grad_normed, normed_in, in_inverse)
    ).astype(jnp.bfloat16)
    return (grad_rows, partial_in, partial_out)


def on_device(
    item_ids, seq_lengths, surplus_slot, helper_map, embed_tables, weight_in, weight_out, cotangent
):
    bal_index = lax.axis_index("bal")
    emb_index = lax.axis_index("emb")
    bal_count = lax.axis_size("bal")
    emb_count = lax.axis_size("emb")
    table_count = item_ids.shape[2]
    group_count = D // COLS
    table_pick = emb_index // group_count
    table_ids = lax.dynamic_index_in_dim(item_ids[0], table_pick, 1, keepdims=False)
    looked = embed_tables[0][table_ids]
    pieces = lax.all_to_all(looked, "emb", split_axis=0, concat_axis=1, tiled=True)
    row_count = pieces.shape[0]
    embedded = jnp.sum(pieces.reshape(row_count, table_count, D), axis=1, dtype=jnp.float32).astype(
        jnp.bfloat16
    )
    own_slots = embedded.reshape(NSEQ, SLOT, D)
    surplus_col = surplus_slot[:, 0]
    helper_col = helper_map[:, 0]
    length_col = seq_lengths[:, 0, :]
    bal_ids = jnp.arange(bal_count, dtype=jnp.int32)
    slot_ids = jnp.arange(NSEQ, dtype=jnp.int32)
    my_slot = lax.dynamic_index_in_dim(surplus_col, bal_index, 0, keepdims=False)
    leaving = lax.dynamic_index_in_dim(own_slots, my_slot, 0, keepdims=True)
    arrived_all = lax.all_gather(leaving, "bal", axis=0, tiled=True)
    source = jnp.sum(jnp.where(helper_col == bal_index, bal_ids, 0))
    arrived = lax.dynamic_index_in_dim(arrived_all, source, 0, keepdims=True)
    replaced = slot_ids == my_slot
    proc_rows = jnp.where(replaced[:, None, None], arrived, own_slots).reshape(row_count, D)
    own_lengths = lax.dynamic_index_in_dim(length_col, bal_index, 0, keepdims=False)
    source_lengths = lax.dynamic_index_in_dim(length_col, source, 0, keepdims=False)
    source_slot = lax.dynamic_index_in_dim(surplus_col, source, 0, keepdims=False)
    moved_length = jnp.sum(jnp.where(slot_ids == source_slot, source_lengths, 0))
    proc_lengths = jnp.where(replaced, moved_length, own_lengths)
    full_in, full_out = (
        lax.all_gather(weight_in, "bal", axis=0, tiled=True),
        lax.all_gather(weight_out, "bal", axis=0, tiled=True),
    )
    forward_out, stored = layer_forward(proc_rows, proc_lengths, full_in, full_out, HEADS, SLOT)
    retained = lax.optimization_barrier((weight_in, weight_out, forward_out))
    back_in, back_out = (
        lax.all_gather(retained[0], "bal", axis=0, tiled=True),
        lax.all_gather(retained[1], "bal", axis=0, tiled=True),
    )
    grad_rows, partial_in, partial_out = layer_backward(
        stored, cotangent[0], back_in, back_out, HEADS, SLOT
    )
    grad_slots = grad_rows.reshape(NSEQ, SLOT, D)
    outgoing = lax.dynamic_index_in_dim(grad_slots, my_slot, 0, keepdims=True)
    returned_all = lax.all_gather(outgoing, "bal", axis=0, tiled=True)
    helper = lax.dynamic_index_in_dim(helper_col, bal_index, 0, keepdims=False)
    came_back = lax.dynamic_index_in_dim(returned_all, helper, 0, keepdims=True)
    anchor_grads = jnp.where(replaced[:, None, None], came_back, grad_slots).reshape(row_count, D)
    copies = jnp.tile(anchor_grads, (1, table_count))
    table_rows = lax.all_to_all(copies, "emb", split_axis=1, concat_axis=0, tiled=True)
    table_part = (
        jnp.zeros((DISTINCT, COLS), jnp.float32).at[table_ids].add(table_rows.astype(jnp.float32))
    )
    table_sum = lax.psum_scatter(
        table_part.astype(jnp.bfloat16), "bal", scatter_dimension=0, tiled=True
    ).astype(jnp.float32)
    table_scale = (DISTINCT / (bal_count * item_ids.shape[1])) ** 0.5
    owned_in, owned_out = (
        lax.psum_scatter(
            partial_in.astype(jnp.bfloat16), "bal", scatter_dimension=0, tiled=True
        ).astype(jnp.float32),
        lax.psum_scatter(
            partial_out.astype(jnp.bfloat16), "bal", scatter_dimension=0, tiled=True
        ).astype(jnp.float32),
    )
    total_in, total_out = lax.psum((owned_in, owned_out), "emb")
    events = row_count * emb_count * bal_count
    grad_scale = events ** (-0.5)
    return (
        forward_out[None],
        (table_sum * table_scale)[None],
        total_in * grad_scale,
        total_out * grad_scale,
    )


def solution(mesh):
    placed = (
        P("bal", None, None),
        P(None, "emb", None),
        P(None, "emb"),
        P(None, "emb"),
        P("emb", None, None),
        P("bal", None),
        P("bal", None),
        P("bal", "emb", None),
    )
    return jax.shard_map(
        on_device,
        mesh=mesh,
        in_specs=placed,
        out_specs=(P("bal", "emb", None), P("emb", "bal", None), P("bal", None), P("bal", None)),
        check_vma=False,
    )
```

profile of v0, /device:TPU:0, one launch (start us, length us, event | category | flops | bytes accessed | tf_op | source)
XLA Modules:
  0.0 314.5 jit_solution(6480352963317922703)
XLA Ops:
  8.2 12.1 %gather_fusion = bf16[4096,128]{1,0:T(8,128)(2,1)S(1)} fusion(bf16[1024,128]{1,0:T(8,128)(2,1)S(1)} %bitcast.114, s32[4096]{0:T(1024)S(1)} %broadcast_clamp_fusion), kind=kCustom, calls=%fused_computation | custom fusion | bytes 2113536 | tf_op jit(solution)/shard_map/gather | solution.py:183
  21.6 8.5 %all-to-all-start = ((bf16[16,256,128]{1,2,0:T(8,128)(2,1)}), bf16[16,256,128]{1,2,0:T(8,128)(2,1)S(1)}, u32[]{:S(2)}, u32[]{:S(2)}) async-start(bf16[16,256,128]{1,2,0:T(8,128)(2,1)} %copy.42), calls=%async_computation | async-start | bytes 2097152 | tf_op jit(solution)/shard_map/all_to_all | solution.py:184
  39.3 2.2 all_gather.20
  41.6 12.9 %all-to-all-done = bf16[16,256,128]{1,2,0:T(8,128)(2,1)S(1)} async-done(((bf16[16,256,128]{1,2,0:T(8,128)(2,1)}), bf16[16,256,128]{1,2,0:T(8,128)(2,1)S(1)}, u32[]{:S(2)}, u32[]{:S(2)}) %all-to-all-start) | async-done | bytes 1048608 | tf_op jit(solution)/shard_map/all_to_all | solution.py:184
  55.0 2.0 all_gather.18
  57.5 4.4 %fusion.64 = (f32[256,2048]{1,0:T(8,128)}, f32[256,2048]{1,0:T(8,128)}) fusion(bf16[512,2048]{1,0:T(8,128)(2,1)} %all-gather.3.cloned.1.call-done, bf16[256,512]{1,0:T(8,128)(2,1)S(1)} %get-tuple-element.257, f32[256]{0:T(256)S(1)} %add_rsqrt_fusion.1, f32[256]{0:T(256)S(1)} %broadcast_multiply_fusion.7), kind=kOutput, calls=%fused_computation.75 | convolution fusion | flops 539492352 | bytes 6555648 | tf_op jit(solution)/shard_map/dot_general | solution.py:100
  61.8 1.5 slice.22
  63.4 13.9 %while.30 = (s32[]{:T(128)}, f32[8,256,64]{1,2,0:T(8,128)S(1)}, s32[8]{0:T(128)S(1)}, bf16[256,1536]{1,0:T(8,128)(2,1)S(1)}, s32[256]{0:T(256)S(1)}, /*index=5*/...) while((s32[]{:T(128)}, f32[8,256,64]{1,2,0:T(8,128)S(1)}, ...), condition=%wide.region_7.8_spmd.clone, body=%wide.region_6.7_spmd.clone.sunk | while | flops 17629196 | bytes 265003 | solution.py:105
  80.1 2.2 all_gather.21
  82.2 1.5 fusion.93
  85.0 2.0 fusion.79
  87.9 26.8 %while.31 = (s32[]{:T(128)}, f32[8,256,64]{1,2,0:T(8,128)S(1)}, f32[8,256,64]{1,2,0:T(8,128)S(1)}, f32[8,256,64]{1,2,0:T(8,128)}, s32[8]{0:T(128)S(1)}, /*index=...) while((s32[]{:T(128)}, f32[8,256,64]{1,2,0:T(8,128)S(1)}, ...), condition=%wide.region_13.14_spmd.clone, body=%wide.region_12.13_spmd.clone.sunk | while | flops 43876364 | bytes 1840996 | solution.py:152
  116.8 2.0 copy.49
  118.9 2.7 fusion.63
  121.5 2.2 convolution_convert_fusion
  125.6 2.4 fusion.94
  128.3 2.2 all_gather.23
  131.8 5.8 %all-to-all-start.1 = ((bf16[256,16,128]{0,2,1:T(8,128)(2,1)}), bf16[256,16,128]{0,2,1:T(8,128)(2,1)S(1)}, u32[]{:S(2)}, u32[]{:S(2)}) async-start(bf16[256,16,128]{0,2,1:T(8,128)(2,1)} %bitcast.30), calls=%async_computation.1 | async-start | bytes 2097152 | tf_op jit(solution)/shard_map/all_to_all | solution.py:227
  137.9 24.4 %all-to-all-done.1 = bf16[256,16,128]{0,2,1:T(8,128)(2,1)S(1)} async-done(((bf16[256,16,128]{0,2,1:T(8,128)(2,1)}), bf16[256,16,128]{0,2,1:T(8,128)(2,1)S(1)}, u32[]{:S(2)}, u32[]{:S(2)}) %all-to-all-start.1) | async-done | bytes 1048608 | tf_op jit(solution)/shard_map/all_to_all | solution.py:227
  162.5 1.8 copy.51
  164.3 22.8 %scatter_custom_fusion = f32[1024,128]{1,0:T(8,128)S(1)} fusion(s32[4096]{0:T(1024)S(1)} %bitcast.126, f32[4096,128]{1,0:T(8,128)} %bitcast.118, f32[]{:T(128)} %constant.231.clone.1), kind=kCustom, calls=%fused_computation.110 | custom fusion | flops 524288 | bytes 524800 | tf_op jit(solution)/shard_map/scatter-add | solution.py:229
  187.9 116.1 %all-reduce.2 = (f32[256,2048]{1,0:T(8,128)S(1)}, f32[256,512]{1,0:T(8,128)S(1)}) all-reduce(bf16[256,2048]{1,0:T(8,128)(2,1)} %reduce-scatter.6.cloned.1.call-done, bf16[256,512]{1,0:T(8,128)(2,1)S(1)} %copy-done.4), channel_id=1, replica_groups=mesh['emb'=16,'bal'=2] {'emb'}, use_global_device_ids=true, to_apply=%region_19.20 | all-reduce | flops 655360 | bytes 3932160 | tf_op jit(solution)/shard_map/psum | solution.py:243
  304.8 1.5 broadcast_multiply_fusion
  306.3 1.6 multiply_bitcast_fusion
  (144 shorter events, 48.6 us)
Async XLA Ops:
  7.2 1.0 copy-start
  21.6 9.3 %copy-start.7 = (s32[2,1]{0,1:T(1,128)S(1)}, s32[2,1]{0,1:T(1,128)}, u32[]{:S(2)}) copy-start(s32[2,1]{0,1:T(1,128)} %param.15) | copy-start | bytes 28
  21.6 11.8 %copy-start.5 = (s32[2,1]{0,1:T(1,128)S(1)}, s32[2,1]{0,1:T(1,128)}, u32[]{:S(2)}) copy-start(s32[2,1]{0,1:T(1,128)} %param.14) | copy-start | bytes 28
  21.6 14.4 %copy-start.6 = (s32[2,1,2]{2,1,0:T(1,128)S(1)}, s32[2,1,2]{2,1,0:T(1,128)}, u32[]{:S(2)}) copy-start(s32[2,1,2]{2,1,0:T(1,128)} %param.13) | copy-start | bytes 52
  21.6 17.7 %copy-start.3 = (bf16[256,512]{1,0:T(8,128)(2,1)S(1)}, bf16[256,512]{1,0:T(8,128)(2,1)}, u32[]{:S(2)}) copy-start(bf16[256,512]{1,0:T(8,128)(2,1)} %param.18) | copy-start | bytes 786436
  21.6 32.9 %all-to-all-start = ((bf16[16,256,128]{1,2,0:T(8,128)(2,1)}), bf16[16,256,128]{1,2,0:T(8,128)(2,1)S(1)}, u32[]{:S(2)}, u32[]{:S(2)}) async-start(bf16[16,256,128]{1,2,0:T(8,128)(2,1)} %copy.42), calls=%async_computation | async-start | bytes 2097152 | tf_op jit(solution)/shard_map/all_to_all | solution.py:184
  30.1 27.4 %all-gather.3.cloned.1.call-start = ((), (), s32[]{:S(2)}) async-start(), calls=%async_computation.5 | async-start | bytes 3145728 | tf_op jit(solution)/shard_map/all_gather | solution.py:208
  30.8 94.8 %all-gather.5.cloned.1.call-start = ((), (), s32[]{:S(2)}) async-start(), calls=%async_computation.6 | async-start | bytes 3145728 | tf_op jit(solution)/shard_map/all_gather | solution.py:214
  77.7 4.5 %copy-start.1 = (bf16[1,256,512]{2,1,0:T(8,128)(2,1)S(1)}, bf16[1,256,512]{2,1,0:T(8,128)(2,1)}, u32[]{:S(2)}) copy-start(bf16[1,256,512]{2,1,0:T(8,128)(2,1)} %param.19) | copy-start | bytes 786436
  80.0 57.9 %reduce-scatter.8.cloned.1.call-start = ((), (), s32[]{:S(2)}) async-start(), calls=%async_computation.9 | async-start | bytes 786432 | tf_op jit(solution)/shard_map/reduce_scatter | solution.py:239
  84.9 103.0 %reduce-scatter.6.cloned.1.call-start = ((), (), s32[]{:S(2)}) async-start(), calls=%async_computation.8 | async-start | bytes 3145728 | tf_op jit(solution)/shard_map/reduce_scatter | solution.py:236
  114.8 0.8 copy-start.2
  131.8 30.5 %all-to-all-start.1 = ((bf16[256,16,128]{0,2,1:T(8,128)(2,1)}), bf16[256,16,128]{0,2,1:T(8,128)(2,1)S(1)}, u32[]{:S(2)}, u32[]{:S(2)}) async-start(bf16[256,16,128]{0,2,1:T(8,128)(2,1)} %bitcast.30), calls=%async_computation.1 | async-start | bytes 2097152 | tf_op jit(solution)/shard_map/all_to_all | solution.py:227
  137.7 168.7 %reduce-scatter.4.cloned.1.call-start = ((), (), s32[]{:S(2)}) async-start(), calls=%async_computation.7 | async-start | bytes 393216 | tf_op jit(solution)/shard_map/reduce_scatter | solution.py:231
  162.5 25.4 %copy-start.4 = (bf16[256,512]{1,0:T(8,128)(2,1)S(1)}, bf16[256,512]{1,0:T(8,128)(2,1)}, u32[]{:S(2)}) copy-start(bf16[256,512]{1,0:T(8,128)(2,1)} %reduce-scatter.8.cloned.1.call-done) | copy-start | bytes 786436
Sparse Core Ops, SparseCore 0:
  32.5 11.8 all-gather.2
  80.1 10.9 all-gather.4
  93.3 8.9 reduce-scatter.7
  123.8 9.9 reduce-scatter.5
  188.0 8.1 reduce-scatter.3
where the time goes:
time: 316 us; the launch traced here: 314 us
  blocking collectives  125 us (40%)
  other arithmetic  39.8 us (13%)
  waiting for transfers between devices  38.1 us (12%)
  local copies, waits for them, and re-layouts  33.4 us (11%)
  matrix products  32.7 us (10%)
  between operations  19.9 us (6%)
  starting transfers between devices  14.7 us (5%)
  loops' own time  11.2 us (4%)
    psum x1, blocking collectives, on_device(): total_in, total_out = lax.psum((owned_in, owned_out), 'emb')  116 us
    all_to_all x1, waiting for transfers between devices, on_device(): lax.all_to_all(copies, 'emb', split_axis=1, concat_axis=0, tiled=True)  24.4 us
    scatter-add x1, other arithmetic, on_device(): jnp.zeros((DISTINCT, COLS), jnp.float32).at[table_ids]  22.8 us
    all_to_all x1, waiting for transfers between devices, on_device(): lax.all_to_all(looked, 'emb', split_axis=0, concat_axis=1, tiled=True)  12.9 us
    gather x1, local copies, waits for them, and re-layouts, on_device(): looked = embed_tables[0][table_ids]  12.1 us
    dynamic_slice x16, local copies, waits for them, and re-layouts, layer_forward(): lax.map(lambda head_index: head_forward(heads_input, allowed, head_index,...  9.4 us
    all_to_all x1, starting transfers between devices, on_device(): lax.all_to_all(looked, 'emb', split_axis=0, concat_axis=1, tiled=True)  8.46 us
    dot_general x8, matrix products, head_backward(): jnp.dot(grad_scores.T, head_query, preferred_element_type=jnp.float32)  7.27 us
  transfers between devices with their start and end apart: 7, of which 2 were waited for; matrix products, arithmetic and copies ran while one was open for 23% of the time, Pallas kernels for 0%

commit v1 on v0

v1 whole, which is shorter than its diff:
```python
import functools

import jax
import jax.numpy as jnp
from jax import lax
from jax.experimental import pallas as pl
from jax.experimental.pallas import tpu as pltpu
from jax.sharding import PartitionSpec as P

HEADS = 8
EPS = 1e-05
LANES = 128
TILE_ROWS = 16
ROOM = 48 * 1024 * 1024

VMEM = pl.BlockSpec(memory_space=pltpu.VMEM)
SMEM = pl.BlockSpec(memory_space=pltpu.SMEM)
f32 = jnp.float32
bf16 = jnp.bfloat16


def matmul(left, right):
    return lax.dot_general(left, right, (((1,), (0,)), ((), ())), preferred_element_type=f32)


def matmul_nt(left, right):
    return lax.dot_general(left, right, (((1,), (1,)), ((), ())), preferred_element_type=f32)


def matmul_tn(left, right):
    return lax.dot_general(left, right, (((0,), (0,)), ((), ())), preferred_element_type=f32)


def sigmoid(value):
    return 0.5 * jnp.tanh(0.5 * value) + 0.5


def bal_swap(value, step, count):
    return lax.ppermute(value, "bal", [(i, i ^ step) for i in range(count)])


def emb_swap(value, step, count):
    return lax.ppermute(value, "emb", [(i, i ^ step) for i in range(count)])


def lookup_kernel(tables, groups, bals, pos_ref, *refs):
    ids_refs = refs[:groups]
    piece_refs = refs[groups : groups + 1 + (tables - 1) * bals]
    out_refs = refs[groups + 1 + (tables - 1) * bals :]
    bal = pos_ref[0]
    table_here = pos_ref[1]
    own_ref = piece_refs[0]
    distinct = own_ref.shape[0]
    part = distinct // bals
    rows = ids_refs[0].shape[2]
    lane = lax.broadcasted_iota(jnp.int32, (LANES, LANES), 1)
    for group in range(groups):
        for first in range(0, rows, LANES):
            total = jnp.zeros((LANES, own_ref.shape[1]), f32)
            for step in range(tables):
                row = ids_refs[group][table_here ^ step, :, first : first + LANES]
                column = jnp.transpose(jnp.broadcast_to(row, (LANES, LANES)))
                if step == 0:
                    pieces = [(own_ref, 0, distinct)]
                else:
                    base = 1 + (step - 1) * bals
                    pieces = [
                        (piece_refs[base + turn], (bal ^ turn) * part, part)
                        for turn in range(bals)
                    ]
                for ref, start, height in pieces:
                    shifted = column - start
                    hot = jnp.concatenate(
                        [
                            jnp.where(shifted == lane + at, 1.0, 0.0).astype(bf16)
                            for at in range(0, height, LANES)
                        ],
                        axis=1,
                    )
                    total = total + matmul(hot, ref[...])
            out_refs[group][first : first + LANES, :] = total.astype(bf16)


def scatter_kernel(tables, groups, bals, pos_ref, *refs):
    ids_refs = refs[:groups]
    grad_refs = refs[groups : 2 * groups]
    out_refs = refs[2 * groups :]
    bal = pos_ref[0]
    table_here = pos_ref[1]
    part = out_refs[0].shape[1]
    rows = ids_refs[0].shape[2]
    height = min(part, 256)
    iota = lax.broadcasted_iota(jnp.int32, (height, rows), 0)
    grads = jnp.concatenate([ref[...] for ref in grad_refs], axis=0)
    for step in range(tables):
        id_rows = [ref[table_here ^ step] for ref in ids_refs]
        for turn in range(bals):
            for at in range(0, part, height):
                start = (bal ^ turn) * part + at
                hot = jnp.concatenate(
                    [jnp.where(iota == row - start, 1.0, 0.0).astype(bf16) for row in id_rows],
                    axis=1,
                )
                out_refs[turn][step, at : at + height, :] = matmul(hot, grads).astype(bf16)


def norm(values):
    average = jnp.mean(values, axis=1, keepdims=True)
    centred = values - average
    inverse = lax.rsqrt(jnp.mean(centred * centred, axis=1, keepdims=True) + EPS)
    return centred * inverse, inverse


def norm_back(incoming, normed, inverse):
    first = jnp.mean(incoming, axis=1, keepdims=True)
    second = jnp.mean(incoming * normed, axis=1, keepdims=True)
    return inverse * (incoming - first - normed * second)


def layer_kernel(groups, bals, chunked, pos_ref, seq_ref, surplus_ref, helper_ref, *refs):
    refs = list(refs)
    take = lambda count: [refs.pop(0) for _ in range(count)]
    piece_refs = take(groups)
    in_refs = take(bals)
    out_refs = take(bals)
    (cot_ref,) = take(1)
    (layer_ref,) = take(1)
    grad_refs = take(groups)
    part_in_refs = take(bals)
    part_out_refs = take(bals)
    (x_ref, w_in, w_out, nt_ref, mt_ref, weights_ref, slope_ref, gate_ref, heads_ref, dsilu_ref, grads_ref) = refs

    bal = pos_ref[0]
    table_here = pos_ref[1]
    group_here = pos_ref[2]
    rows, width = cot_ref.shape
    slots = seq_ref.shape[1]
    slot_rows = rows // slots
    head_width = width // HEADS
    score_scale = head_width**-0.5
    piece = piece_refs[0].shape[1]

    for step in range(groups):
        x_ref[group_here ^ step] = piece_refs[step][...]
    part = in_refs[0].shape[0]
    for turn in range(bals):
        at = pl.ds(pl.multiple_of((bal ^ turn) * part, part), part)
        w_in[at, :] = in_refs[turn][...]
        w_out[at, :] = out_refs[turn][...]

    source = jnp.int32(0)
    for index in range(bals):
        source = source + jnp.where(helper_ref[index, 0] == bal, index, 0)
    my_slot = surplus_ref[bal, 0]
    moved = seq_ref[source, surplus_ref[source, 0]]
    lengths = [jnp.where(my_slot == slot, moved, seq_ref[bal, slot]) for slot in range(slots)]

    x = jnp.concatenate([x_ref[group] for group in range(groups)], axis=1).astype(f32)
    normed_in, in_inverse = norm(x)
    nt_ref[...] = jnp.transpose(normed_in).astype(bf16)
    projected = matmul(normed_in.astype(bf16), w_in[...])
    logistic = sigmoid(projected)
    active = projected * logistic
    dsilu_ref[...] = logistic + active * (1.0 - logistic)
    gate_ref[...] = active[:, :width]
    heads_ref[...] = active[:, width:].astype(bf16)

    pair_width = 2 * head_width
    low = lax.broadcasted_iota(jnp.int32, (slot_rows, pair_width), 1) < head_width
    row_at = lax.broadcasted_iota(jnp.int32, (slot_rows, slot_rows), 0)
    col_at = lax.broadcasted_iota(jnp.int32, (slot_rows, slot_rows), 1)

    def split(value):
        zero = jnp.zeros_like(value)
        return jnp.concatenate([jnp.where(low, value, zero), jnp.where(low, zero, value)], axis=0)

    def side_by_side(value):
        return jnp.concatenate([value[:slot_rows], value[slot_rows:]], axis=1)

    def part_of(slot, pair, which):
        first = which * width + pair * pair_width
        return heads_ref[slot * slot_rows : (slot + 1) * slot_rows, first : first + pair_width]

    pairs = HEADS // 2
    attended = []
    for slot in range(slots):
        live = (col_at <= row_at) & (row_at < lengths[slot])
        allowed = jnp.where(live, 1.0 / slot_rows, 0.0)
        allowed = jnp.concatenate([allowed, allowed], axis=0)
        across = []
        for pair in range(pairs):
            value, query, key = (part_of(slot, pair, which) for which in range(3))
            scores = matmul_nt(split(query), key) * score_scale
            q = sigmoid(scores)
            sq = scores * q
            weights = (sq * allowed).astype(bf16)
            weights_ref[slot * pairs + pair] = weights
            slope_ref[slot * pairs + pair] = allowed * (q + sq * (1.0 - q))
            across.append(matmul(side_by_side(weights), split(value)))
        attended.append(jnp.concatenate(across, axis=1))
    normed_out, out_inverse = norm(jnp.concatenate(attended, axis=0))
    gate = gate_ref[...]
    mixed = normed_out * gate
    mt_ref[...] = jnp.transpose(mixed).astype(bf16)
    layer_ref[...] = (x + matmul(mixed.astype(bf16), w_out[...])).astype(bf16)

    cot = cot_ref[...]
    grad_mixed = matmul_nt(cot, w_out[...])
    grad_attended = norm_back(grad_mixed * gate, normed_out, out_inverse).astype(bf16)
    grads_ref[:, :width] = (grad_mixed * normed_out * dsilu_ref[:, :width]).astype(bf16)

    chunk = TILE_ROWS if chunked else part

    def emit(ref, value, me):
        for index in range(part // chunk):
            at = (index ^ me) * chunk if chunked else index * chunk
            ref[pl.ds(pl.multiple_of(at, chunk), chunk), :] = value[index * chunk : (index + 1) * chunk]

    tables = part // chunk // groups if chunked else 1
    plane_first = group_here * tables + table_here
    table_first = table_here * groups + group_here
    for turn in range(bals):
        at = pl.ds(pl.multiple_of((bal ^ turn) * part, part), part)
        emit(part_out_refs[turn], matmul(mt_ref[at, :], cot).astype(bf16), table_first)

    for slot in range(slots):
        here = slice(slot * slot_rows, (slot + 1) * slot_rows)
        for pair in range(pairs):
            value, query, key = (part_of(slot, pair, which) for which in range(3))
            lanes = slice(pair * pair_width, (pair + 1) * pair_width)
            upper = split(grad_attended[here, lanes])
            grad_weights = matmul_nt(upper, value)
            grad_scores = (grad_weights * slope_ref[slot * pairs + pair]).astype(bf16)
            grad_value = matmul_tn(weights_ref[slot * pairs + pair], upper)
            grad_query = matmul(side_by_side(grad_scores), split(key)) * score_scale
            grad_key = matmul_tn(grad_scores, split(query)) * score_scale
            for which, found in enumerate((grad_value, grad_query, grad_key)):
                first = (1 + which) * width + pair * pair_width
                at = slice(first, first + pair_width)
                grads_ref[here, at] = (found * dsilu_ref[here, at]).astype(bf16)

    grad_projected = grads_ref[...]
    for turn in range(bals):
        at = pl.ds(pl.multiple_of((bal ^ turn) * part, part), part)
        emit(part_in_refs[turn], matmul(nt_ref[at, :], grad_projected).astype(bf16), plane_first)

    grad_normed = matmul_nt(grad_projected, w_in[...])
    grad_rows = (cot.astype(f32) + norm_back(grad_normed, normed_in, in_inverse)).astype(bf16)
    for group in range(groups):
        x_ref[group] = grad_rows[:, group * piece : (group + 1) * piece]
    for step in range(groups):
        grad_refs[step][...] = x_ref[group_here ^ step]


def place_kernel(scale, inner, pos_ref, me_ref, *refs):
    out_ref = refs[-1]
    me = me_ref[0]
    for outer, ref in enumerate(refs[:-1]):
        for index in range(inner):
            at = pl.multiple_of(((outer * inner + index) ^ me) * TILE_ROWS, TILE_ROWS)
            value = ref[index * TILE_ROWS : (index + 1) * TILE_ROWS, :]
            out_ref[pl.ds(at, TILE_ROWS), :] = value.astype(f32) * scale


def sum_rounded(terms):
    total = terms[0].astype(f32)
    for term in terms[1:]:
        total = total + term.astype(f32)
    return total.astype(bf16)


def reduce_scatter(value, count, stride, emb_count):
    pieces = value.reshape(count, value.shape[0] // count, value.shape[1])
    terms = [pieces[0]] + [
        emb_swap(pieces[step], step * stride, emb_count) for step in range(1, count)
    ]
    return sum_rounded(terms)


def gather(value, count, stride, emb_count):
    return [value] + [emb_swap(value, step * stride, emb_count) for step in range(1, count)]


def reduce_weights(terms, order, me, scale, emb_count, chunked, pos):
    own = sum_rounded(terms)
    rows, columns = own.shape
    if not chunked:
        return lax.psum(own.astype(f32), "emb") * scale
    (first, first_stride), (second, second_stride) = order
    own = reduce_scatter(own, first, first_stride, emb_count)
    own = reduce_scatter(own, second, second_stride, emb_count)
    inner = jnp.concatenate(gather(own, second, second_stride, emb_count), axis=0)
    outer = gather(inner, first, first_stride, emb_count)
    return pl.pallas_call(
        functools.partial(place_kernel, scale, second),
        out_shape=jax.ShapeDtypeStruct((rows, columns), f32),
        in_specs=[SMEM, SMEM] + [VMEM] * first,
        out_specs=VMEM,
        compiler_params=pltpu.CompilerParams(vmem_limit_bytes=ROOM),
    )(pos, me, *outer)


def on_device(
    item_ids, seq_lengths, surplus_slot, helper_map, embed_tables, weight_in, weight_out, cotangent
):
    bal = lax.axis_index("bal")
    emb = lax.axis_index("emb")
    bals = lax.axis_size("bal")
    embs = lax.axis_size("emb")
    tables = item_ids.shape[2]
    groups = embs // tables
    _, rows, width = cotangent.shape
    slots = seq_lengths.shape[2]
    slot_rows = rows // slots
    distinct, columns = embed_tables.shape[1:]
    features = weight_in.shape[1]
    part = distinct // bals
    weight_part = weight_in.shape[0]
    chunked = weight_part == embs * TILE_ROWS
    table_here = emb // groups
    group_here = emb % groups
    pos = jnp.stack([bal, table_here, group_here]).astype(jnp.int32)
    params = pltpu.CompilerParams(vmem_limit_bytes=ROOM)

    own_table = embed_tables[0]
    share = lax.dynamic_slice_in_dim(own_table, bal * part, part, 0)
    pieces = [own_table]
    for step in range(1, tables):
        fetched = emb_swap(share, step * groups, embs)
        pieces += [fetched] + [bal_swap(fetched, turn, bals) for turn in range(1, bals)]

    ids = lax.dynamic_slice_in_dim(jnp.transpose(item_ids[0]), emb * rows, rows, 1)
    ids = ids.reshape(tables, slots, slot_rows)
    my_slot = lax.dynamic_index_in_dim(surplus_slot[:, 0], bal, 0, keepdims=False)
    leaving = lax.dynamic_index_in_dim(ids, my_slot, 1, keepdims=False)
    bal_ids = jnp.arange(bals, dtype=jnp.int32)
    source = jnp.sum(jnp.where(helper_map[:, 0] == bal, bal_ids, 0))
    arrived = leaving
    for turn in range(1, bals):
        arrived = jnp.where(source == bal ^ turn, bal_swap(leaving, turn, bals), arrived)
    replaced = jnp.arange(slots, dtype=jnp.int32) == my_slot
    proc_ids = jnp.where(replaced[None, :, None], arrived[:, None, :], ids).reshape(tables, 1, rows)
    plane_ids = gather(proc_ids, groups, 1, embs)

    all_in = [weight_in] + [bal_swap(weight_in, turn, bals) for turn in range(1, bals)]
    all_out = [weight_out] + [bal_swap(weight_out, turn, bals) for turn in range(1, bals)]

    found = pl.pallas_call(
        functools.partial(lookup_kernel, tables, groups, bals),
        out_shape=[jax.ShapeDtypeStruct((rows, columns), bf16)] * groups,
        in_specs=[SMEM] + [VMEM] * (groups + len(pieces)),
        out_specs=[VMEM] * groups,
        compiler_params=params,
    )(pos, *plane_ids, *pieces)
    block = [found[0]] + [emb_swap(found[step], step, embs) for step in range(1, groups)]

    pairs = slots * HEADS // 2
    results = pl.pallas_call(
        functools.partial(layer_kernel, groups, bals, chunked),
        out_shape=[jax.ShapeDtypeStruct((rows, width), bf16)]
        + [jax.ShapeDtypeStruct((rows, columns), bf16)] * groups
        + [jax.ShapeDtypeStruct((weight_part, features), bf16)] * bals
        + [jax.ShapeDtypeStruct((weight_part, width), bf16)] * bals,
        in_specs=[SMEM] * 4 + [VMEM] * (groups + 2 * bals + 1),
        out_specs=[VMEM] * (1 + groups + 2 * bals),
        scratch_shapes=[
            pltpu.VMEM((groups, rows, columns), bf16),
            pltpu.VMEM((width, features), bf16),
            pltpu.VMEM((width, width), bf16),
            pltpu.VMEM((width, rows), bf16),
            pltpu.VMEM((width, rows), bf16),
            pltpu.VMEM((pairs, 2 * slot_rows, slot_rows), bf16),
            pltpu.VMEM((pairs, 2 * slot_rows, slot_rows), f32),
            pltpu.VMEM((rows, width), f32),
            pltpu.VMEM((rows, features - width), bf16),
            pltpu.VMEM((rows, features), f32),
            pltpu.VMEM((rows, features), bf16),
        ],
        compiler_params=params,
    )(
        pos,
        seq_lengths[:, 0, :],
        surplus_slot,
        helper_map,
        *block,
        *all_in,
        *all_out,
        cotangent[0],
    )
    layer_out, results = results[0], results[1:]
    grads, results = results[:groups], results[groups:]
    parts_in, parts_out = results[:bals], results[bals:]

    plane_grads = [grads[0]] + [emb_swap(grads[step], step, embs) for step in range(1, groups)]
    sums = pl.pallas_call(
        functools.partial(scatter_kernel, tables, groups, bals),
        out_shape=[jax.ShapeDtypeStruct((tables, part, columns), bf16)] * bals,
        in_specs=[SMEM] + [VMEM] * (2 * groups),
        out_specs=[VMEM] * bals,
        compiler_params=params,
    )(pos, *plane_ids, *plane_grads)
    own_sums = sum_rounded([sums[0]] + [bal_swap(sums[turn], turn, bals) for turn in range(1, bals)])
    table_sum = own_sums[0].astype(f32)
    for step in range(1, tables):
        table_sum = table_sum + emb_swap(own_sums[step], step * groups, embs).astype(f32)
    table_scale = (distinct / (bals * item_ids.shape[1])) ** 0.5

    grad_scale = (rows * embs * bals) ** -0.5
    plane, depth = (groups, 1), (tables, groups)
    plane_first = (group_here * tables + table_here).reshape(1).astype(jnp.int32)
    table_first = (table_here * groups + group_here).reshape(1).astype(jnp.int32)
    terms_in = [parts_in[0]] + [bal_swap(parts_in[turn], turn, bals) for turn in range(1, bals)]
    terms_out = [parts_out[0]] + [bal_swap(parts_out[turn], turn, bals) for turn in range(1, bals)]
    total_out = reduce_weights(terms_out, (depth, plane), table_first, grad_scale, embs, chunked, pos)
    total_in = reduce_weights(terms_in, (plane, depth), plane_first, grad_scale, embs, chunked, pos)
    return layer_out[None], (table_sum * table_scale)[None], total_in, total_out


def solution(mesh):
    placed = (
        P("bal", None, None),
        P(None, "emb", None),
        P(None, "emb"),
        P(None, "emb"),
        P("emb", None, None),
        P("bal", None),
        P("bal", None),
        P("bal", "emb", None),
    )
    return jax.shard_map(
        on_device,
        mesh=mesh,
        in_specs=placed,
        out_specs=(P("bal", "emb", None), P("emb", "bal", None), P("bal", None), P("bal", None)),
        check_vma=False,
    )
```

time: 316 us -> 129 us (0.41)
  blocking collectives: 125 us -> 0 us
  starting transfers between devices: 14.7 us -> 50.3 us
  other arithmetic: 39.8 us -> 4.33 us
  matrix products: 32.7 us -> 0 us
  local copies, waits for them, and re-layouts: 33.4 us -> 8.18 us
  between operations: 19.9 us -> 3.52 us
  Pallas kernels: 0 us -> 16.3 us
  loops' own time: 11.2 us -> 0 us
  waiting for transfers between devices: 38.1 us -> 46.1 us
    psum x1 -> x0, blocking collectives: 116 us -> none  [on_device(): total_in, total_out = lax.psum((owned_in, owned_out), 'emb')]
    ppermute x0 -> x48, starting transfers between devices: none -> 50.3 us  [the longest x39 48.2 us: emb_swap(): return lax.ppermute(value, 'emb', [(i, i ^ step) for i in range(count)])]
    ppermute x0 -> x48, waiting for transfers between devices: none -> 46.1 us  [the longest x39 44.1 us: emb_swap(): return lax.ppermute(value, 'emb', [(i, i ^ step) for i in range(count)])]
    all_to_all x2 -> x0, waiting for transfers between devices: 37.3 us -> none  [the longest x1 24.4 us: on_device(): lax.all_to_all(copies, 'emb', split_axis=1, concat_axis=0, tiled=True)]
    dot_general x54 -> x0, matrix products: 32.7 us -> none  [the longest x8 7.27 us: head_backward(): jnp.dot(grad_scores.T, head_query, preferred_element_type=jnp.float32)]
    scatter-add x1 -> x0, other arithmetic: 22.8 us -> none  [on_device(): jnp.zeros((DISTINCT, COLS), jnp.float32).at[table_ids]]
    pallas_call x0 -> x5, Pallas kernels: none -> 16.3 us  [the longest x1 6.53 us: on_device(): pl.pallas_call(functools.partial(layer_kernel, groups, bals, chunked), ou...]
    all_to_all x2 -> x0, starting transfers between devices: 14.3 us -> none  [the longest x1 8.46 us: on_device(): lax.all_to_all(looked, 'emb', split_axis=0, concat_axis=1, tiled=True)]
  transfers between devices with their start and end apart: 7 -> 48, of which waited for: 2 -> 20; matrix products, arithmetic and copies ran while one was open for 23% -> 6% of each run, Pallas kernels for 0% -> 6%
where the time goes in v1:
time: 129 us
  starting transfers between devices  50.3 us (39%)
  waiting for transfers between devices  46.1 us (36%)
  Pallas kernels  16.3 us (13%)
  local copies, waits for them, and re-layouts  8.18 us (6%)
  other arithmetic  4.33 us (3%)
  between operations  3.52 us (3%)
    ppermute x39, starting transfers between devices, emb_swap(): return lax.ppermute(value, 'emb', [(i, i ^ step) for i in range(count)])  48.2 us
    ppermute x39, waiting for transfers between devices, emb_swap(): return lax.ppermute(value, 'emb', [(i, i ^ step) for i in range(count)])  44.1 us
    pallas_call x1, Pallas kernels, on_device(): pl.pallas_call(functools.partial(layer_kernel, groups, bals, chunked), ou...  6.53 us
    unnamed x13, local copies, waits for them, and re-layouts  5.02 us
    pallas_call x2, Pallas kernels, reduce_weights(): pl.pallas_call(functools.partial(place_kernel, scale, second), out_shape=...  3.4 us
    pallas_call x1, Pallas kernels, on_device(): pl.pallas_call(functools.partial(lookup_kernel, tables, groups, bals), ou...  3.25 us
    pallas_call x1, Pallas kernels, on_device(): pl.pallas_call(functools.partial(scatter_kernel, tables, groups, bals), o...  3.08 us
  transfers between devices with their start and end apart: 48, of which 20 were waited for; matrix products, arithmetic and copies ran while one was open for 6% of the time, Pallas kernels for 6%

profile of v1, /device:TPU:0, one launch (start us, length us, event | category | flops | bytes accessed | tf_op | source)
XLA Modules:
  0.0 128.7 jit_solution(9044799776817831946)
XLA Ops:
  1.7 5.1 %collective-permute-start.8 = (bf16[512,128]{1,0:T(8,128)(2,1)S(1)}, bf16[512,128]{1,0:T(8,128)(2,1)S(1)}, u32[]{:S(2)}, u32[]{:S(2)}) collective-permute-start(bf16[512,128]{1,0:T(8,128)(2,1)S(1)} %dynamic-slice_bitcast_fusion), channel_id=1, source_target_pairs={{0,24},{2,26},{4,28},{6,30},{8,16},{10,18},{12,20},{14,22},{16,8},... | collective-permute-start | bytes 393224 | tf_op jit(solution)/shard_map/ppermute | solution.py:43
  15.3 2.6 %collective-permute-start.3 = (s32[4,1,256]{2,1,0:T(1,128)S(1)}, s32[4,1,256]{2,1,0:T(1,128)S(1)}, u32[]{:S(2)}, u32[]{:S(2)}) collective-permute-start(s32[4,1,256]{2,1,0:T(1,128)S(1)} %select_n.54.refs_0_), channel_id=1, source_target_pairs={{0,6},{2,4},{4,2},{6,0},{8,14},{10,12},{12,10},{14,8},{16,22},{18,... | collective-permute-start | bytes 12296 | tf_op jit(solution)/shard_map/ppermute | solution.py:43
  18.0 1.9 %collective-permute-done.3.refs_3_ = s32[4,1,256]{2,1,0:T(1,128)S(1)} collective-permute-done((s32[4,1,256]{2,1,0:T(1,128)S(1)}, s32[4,1,256]{2,1,0:T(1,128)S(1)}, u32[]{:S(2)}, u32[]{:S(2)}) %collective-permute-start.3) | collective-permute-done | bytes 4128 | tf_op jit(solution)/shard_map/ppermute | solution.py:43
  21.5 1.9 %collective-permute-done.2.refs_2_ = s32[4,1,256]{2,1,0:T(1,128)S(1)} collective-permute-done((s32[4,1,256]{2,1,0:T(1,128)S(1)}, s32[4,1,256]{2,1,0:T(1,128)S(1)}, u32[]{:S(2)}, u32[]{:S(2)}) %collective-permute-start.2) | collective-permute-done | bytes 4128 | tf_op jit(solution)/shard_map/ppermute | solution.py:43
  25.1 2.0 %collective-permute-done.1.refs_1_ = s32[4,1,256]{2,1,0:T(1,128)S(1)} collective-permute-done((s32[4,1,256]{2,1,0:T(1,128)S(1)}, s32[4,1,256]{2,1,0:T(1,128)S(1)}, u32[]{:S(2)}, u32[]{:S(2)}) %collective-permute-start.1) | collective-permute-done | bytes 4128 | tf_op jit(solution)/shard_map/ppermute | solution.py:43
  30.1 3.2 %shard_map.111 = (bf16[256,128]{1,0:T(8,128)(2,1)S(1)}, bf16[256,128]{1,0:T(8,128)(2,1)S(1)}, bf16[256,128]{1,0:T(8,128)(2,1)S(1)}, bf16[256,128]{1,0:T(8,128)(2,1)S(1)}) custom-call(s32[3]{0:T(128)S(1)} %pad_add_fusion.pos_ref, s32[4,1,256]{2,1,0:T(1,128)S(1)} %select_n.54.refs_0_, s32[4,1,256]{2,1,0:T(1,128)S(1)} %collective-permute-done.1.refs_1_, ...), custom_call_target="tpu_custom_call" | custom-call | tf_op jit(solution)/shard_map/pallas_call | solution.py:348
  39.4 2.4 %collective-permute-done.12.refs_3_ = bf16[256,128]{1,0:T(8,128)(2,1)S(1)} collective-permute-done((bf16[256,128]{1,0:T(8,128)(2,1)S(1)}, bf16[256,128]{1,0:T(8,128)(2,1)S(1)}, u32[]{:S(2)}, u32[]{:S(2)}) %collective-permute-start.12) | collective-permute-done | bytes 65568 | tf_op jit(solution)/shard_map/ppermute | solution.py:43
  44.4 6.5 %shard_map.112 = (bf16[256,512]{1,0:T(8,128)(2,1)}, bf16[256,128]{1,0:T(8,128)(2,1)S(1)}, bf16[256,128]{1,0:T(8,128)(2,1)S(1)}, bf16[256,128]{1,0:T(8,128)(2,1)S...) custom-call(s32[3]{0:T(128)S(1)} %pad_add_fusion.pos_ref, ...), custom_call_target="tpu_custom_call" | custom-call | tf_op jit(solution)/shard_map/pallas_call | solution.py:358
  53.8 2.4 %collective-permute-start.38 = (bf16[64,512]{1,0:T(8,128)(2,1)S(1)}, bf16[64,512]{1,0:T(8,128)(2,1)S(1)}, u32[]{:S(2)}, u32[]{:S(2)}) collective-permute-start(bf16[64,512]{1,0:T(8,128)(2,1)S(1)} %get-tuple-element.41), channel_id=1, source_target_pairs={{0,24},{2,26},{4,28},{6,30},{8,16},{10,18},{12,20},{14,22},{16,8},... | collective-permute-start | bytes 196616 | tf_op jit(solution)/shard_map/ppermute | solution.py:43
  57.8 2.5 %collective-permute-done.38 = bf16[64,512]{1,0:T(8,128)(2,1)S(1)} collective-permute-done((bf16[64,512]{1,0:T(8,128)(2,1)S(1)}, bf16[64,512]{1,0:T(8,128)(2,1)S(1)}, u32[]{:S(2)}, u32[]{:S(2)}) %collective-permute-start.38) | collective-permute-done | bytes 65568 | tf_op jit(solution)/shard_map/ppermute | solution.py:43
  60.3 2.8 %collective-permute-done.37 = bf16[64,512]{1,0:T(8,128)(2,1)S(1)} collective-permute-done((bf16[64,512]{1,0:T(8,128)(2,1)S(1)}, bf16[64,512]{1,0:T(8,128)(2,1)S(1)}, u32[]{:S(2)}, u32[]{:S(2)}) %collective-permute-start.37) | collective-permute-done | bytes 65568 | tf_op jit(solution)/shard_map/ppermute | solution.py:43
  71.4 2.4 %collective-permute-start.44 = (bf16[16,512]{1,0:T(8,128)(2,1)S(1)}, bf16[16,512]{1,0:T(8,128)(2,1)S(1)}, u32[]{:S(2)}, u32[]{:S(2)}) collective-permute-start(bf16[16,512]{1,0:T(8,128)(2,1)S(1)} %add_convert_fusion.6), channel_id=1, source_target_pairs={{0,6},{2,4},{4,2},{6,0},{8,14},{10,12},{12,10},{14,8},{16,22},{18,... | collective-permute-start | bytes 49160 | tf_op jit(solution)/shard_map/ppermute | solution.py:43
  74.3 8.6 %collective-permute-done.44 = bf16[16,512]{1,0:T(8,128)(2,1)S(1)} collective-permute-done((bf16[16,512]{1,0:T(8,128)(2,1)S(1)}, bf16[16,512]{1,0:T(8,128)(2,1)S(1)}, u32[]{:S(2)}, u32[]{:S(2)}) %collective-permute-start.44) | collective-permute-done | bytes 16416 | tf_op jit(solution)/shard_map/ppermute | solution.py:43
  84.0 3.1 %shard_map.113 = (bf16[4,512,128]{2,1,0:T(8,128)(2,1)S(1)}, bf16[4,512,128]{2,1,0:T(8,128)(2,1)S(1)}) custom-call(s32[3]{0:T(128)S(1)} %pad_add_fusion.pos_ref, s32[4,1,256]{2,1,0:T(1,128)S(1)} %select_n.54.refs_0_, s32[4,1,256]{2,1,0:T(1,128)S(1)} %collective-permute-done.1.refs_1_, s32[4,1,256]{2,1,0:T(1,128)S(1)} %collective-permute-done.2.refs_2_, ...), custom_call_target="tpu_custom_call" | custom-call | tf_op jit(solution)/shard_map/pallas_call | solution.py:395
  87.2 1.8 %collective-permute-start.47 = (bf16[64,512]{1,0:T(8,128)(2,1)S(1)}, bf16[64,512]{1,0:T(8,128)(2,1)S(1)}, u32[]{:S(2)}, u32[]{:S(2)}) collective-permute-start(bf16[64,512]{1,0:T(8,128)(2,1)S(1)} %pad_maximum_fusion.1.refs_0_), channel_id=1, source_target_pairs={{0,24},{2,26},{4,28},{6,30},{8,16},{10,18},{12,20},{14,22},{16,8},... | collective-permute-start | bytes 196616 | tf_op jit(solution)/shard_map/ppermute | solution.py:43
  89.1 2.7 %collective-permute-start.26 = (bf16[16,2048]{1,0:T(8,128)(2,1)S(1)}, bf16[16,2048]{1,0:T(8,128)(2,1)S(1)}, u32[]{:S(2)}, u32[]{:S(2)}) collective-permute-start(bf16[16,2048]{1,0:T(8,128)(2,1)S(1)} %get-tuple-element.43), channel_id=1, source_target_pairs={{0,8},{2,10},{4,12},{6,14},{8,0},{10,2},{12,4},{14,6},{16,24},{18,... | collective-permute-start | bytes 196616 | tf_op jit(solution)/shard_map/ppermute | solution.py:43
  95.4 3.2 %collective-permute-done.28 = bf16[16,2048]{1,0:T(8,128)(2,1)S(1)} collective-permute-done((bf16[16,2048]{1,0:T(8,128)(2,1)S(1)}, bf16[16,2048]{1,0:T(8,128)(2,1)S(1)}, u32[]{:S(2)}, u32[]{:S(2)}) %collective-permute-start.28) | collective-permute-done | bytes 65568 | tf_op jit(solution)/shard_map/ppermute | solution.py:43
  98.6 3.4 %collective-permute-done.27 = bf16[16,2048]{1,0:T(8,128)(2,1)S(1)} collective-permute-done((bf16[16,2048]{1,0:T(8,128)(2,1)S(1)}, bf16[16,2048]{1,0:T(8,128)(2,1)S(1)}, u32[]{:S(2)}, u32[]{:S(2)}) %collective-permute-start.27) | collective-permute-done | bytes 65568 | tf_op jit(solution)/shard_map/ppermute | solution.py:43
  103.8 2.7 %collective-permute-start.29 = (bf16[16,2048]{1,0:T(8,128)(2,1)S(1)}, bf16[16,2048]{1,0:T(8,128)(2,1)S(1)}, u32[]{:S(2)}, u32[]{:S(2)}) collective-permute-start(bf16[16,2048]{1,0:T(8,128)(2,1)S(1)} %add_convert_fusion.5), channel_id=1, source_target_pairs={{0,8},{2,10},{4,12},{6,14},{8,0},{10,2},{12,4},{14,6},{16,24},{18,... | collective-permute-start | bytes 196616 | tf_op jit(solution)/shard_map/ppermute | solution.py:43
  106.6 2.3 %collective-permute-done.31 = bf16[16,2048]{1,0:T(8,128)(2,1)S(1)} collective-permute-done((bf16[16,2048]{1,0:T(8,128)(2,1)S(1)}, bf16[16,2048]{1,0:T(8,128)(2,1)S(1)}, u32[]{:S(2)}, u32[]{:S(2)}) %collective-permute-start.31) | collective-permute-done | bytes 65568 | tf_op jit(solution)/shard_map/ppermute | solution.py:43
  108.9 1.9 %collective-permute-done.30 = bf16[16,2048]{1,0:T(8,128)(2,1)S(1)} collective-permute-done((bf16[16,2048]{1,0:T(8,128)(2,1)S(1)}, bf16[16,2048]{1,0:T(8,128)(2,1)S(1)}, u32[]{:S(2)}, u32[]{:S(2)}) %collective-permute-start.30) | collective-permute-done | bytes 65568 | tf_op jit(solution)/shard_map/ppermute | solution.py:43
  119.0 4.7 %collective-permute-done.20 = bf16[512,128]{1,0:T(8,128)(2,1)S(1)} collective-permute-done((bf16[512,128]{1,0:T(8,128)(2,1)S(1)}, bf16[512,128]{1,0:T(8,128)(2,1)S(1)}, u32[]{:S(2)}, u32[]{:S(2)}) %collective-permute-start.20) | collective-permute-done | bytes 131104 | tf_op jit(solution)/shard_map/ppermute | solution.py:43
  124.5 2.2 %collective-permute-done.33.refs_2_ = bf16[64,2048]{1,0:T(8,128)(2,1)S(1)} collective-permute-done((bf16[64,2048]{1,0:T(8,128)(2,1)S(1)}, bf16[64,2048]{1,0:T(8,128)(2,1)S(1)}, u32[]{:S(2)}, u32[]{:S(2)}) %collective-permute-start.33) | collective-permute-done | bytes 262176 | tf_op jit(solution)/shard_map/ppermute | solution.py:43
  126.7 2.0 %shard_map.114 = f32[256,2048]{1,0:T(8,128)} custom-call(s32[3]{0:T(128)S(1)} %pad_add_fusion.pos_ref, s32[1]{0:T(128)} %bitcast.19.me_ref, bf16[64,2048]{1,0:T(8,128)(2,1)S(1)} %pad_maximum_fusion.refs_0_, bf16[64,2048]{1,0:T(8,128)(2,1)S(1)} %collective-permute-done.32.refs_1_, bf16[64,2048]{1,0:T(8,128)(2,1)S(1)} %collective-permute-done.33.refs_2_, ...), custom_call_target="tpu_custom_call" | custom-call | tf_op jit(solution)/shard_map/pallas_call | solution.py:294
  (117 shorter events, 50.7 us)
Async XLA Ops:
  1.7 25.5 %collective-permute-start.8 = (bf16[512,128]{1,0:T(8,128)(2,1)S(1)}, bf16[512,128]{1,0:T(8,128)(2,1)S(1)}, u32[]{:S(2)}, u32[]{:S(2)}) collective-permute-start(bf16[512,128]{1,0:T(8,128)(2,1)S(1)} %dynamic-slice_bitcast_fusion), channel_id=1, source_target_pairs={{0,24},{2,26},{4,28},{6,30},{8,16},{10,18},{12,20},{14,22},{16,8},... | collective-permute-start | bytes 393224 | tf_op jit(solution)/shard_map/ppermute | solution.py:43
  6.8 20.8 %collective-permute-start.6 = (bf16[512,128]{1,0:T(8,128)(2,1)S(1)}, bf16[512,128]{1,0:T(8,128)(2,1)S(1)}, u32[]{:S(2)}, u32[]{:S(2)}) collective-permute-start(bf16[512,128]{1,0:T(8,128)(2,1)S(1)} %dynamic-slice_bitcast_fusion), channel_id=1, source_target_pairs={{0,16},{2,18},{4,20},{6,22},{8,24},{10,26},{12,28},{14,30},{16,0},... | collective-permute-start | bytes 393224 | tf_op jit(solution)/shard_map/ppermute | solution.py:43
  6.8 20.9 %collective-permute-start.4 = (bf16[512,128]{1,0:T(8,128)(2,1)S(1)}, bf16[512,128]{1,0:T(8,128)(2,1)S(1)}, u32[]{:S(2)}, u32[]{:S(2)}) collective-permute-start(bf16[512,128]{1,0:T(8,128)(2,1)S(1)} %dynamic-slice_bitcast_fusion), channel_id=1, source_target_pairs={{0,8},{2,10},{4,12},{6,14},{8,0},{10,2},{12,4},{14,6},{16,24},{18,... | collective-permute-start | bytes 393224 | tf_op jit(solution)/shard_map/ppermute | solution.py:43
  11.4 30.4 %collective-permute-start.13 = (bf16[256,2048]{1,0:T(8,128)(2,1)}, bf16[256,2048]{1,0:T(8,128)(2,1)S(1)}, u32[]{:S(2)}, u32[]{:S(2)}) collective-permute-start(bf16[256,2048]{1,0:T(8,128)(2,1)} %refs_4_.1), channel_id=1, source_target_pairs={{0,1},{1,0},{2,3},{3,2},{4,5},{5,4},{6,7},{7,6},{8,9},{9,8},{10,11... | collective-permute-start | bytes 3145736 | tf_op jit(solution)/shard_map/ppermute | solution.py:39
  27.1 11.3 %collective-permute-start.14 = (bf16[256,512]{1,0:T(8,128)(2,1)}, bf16[256,512]{1,0:T(8,128)(2,1)S(1)}, u32[]{:S(2)}, u32[]{:S(2)}) collective-permute-start(bf16[256,512]{1,0:T(8,128)(2,1)} %refs_6_.1), channel_id=1, source_target_pairs={{0,1},{1,0},{2,3},{3,2},{4,5},{5,4},{6,7},{7,6},{8,9},{9,8},{10,11... | collective-permute-start | bytes 786440 | tf_op jit(solution)/shard_map/ppermute | solution.py:39
  50.9 14.3 %collective-permute-start.22 = (bf16[256,2048]{1,0:T(8,128)(2,1)S(1)}, bf16[256,2048]{1,0:T(8,128)(2,1)S(1)}, u32[]{:S(2)}, u32[]{:S(2)}) collective-permute-start(bf16[256,2048]{1,0:T(8,128)(2,1)S(1)} %get-tuple-element.31), channel_id=1, source_target_pairs={{0,1},{1,0},{2,3},{3,2},{4,5},{5,4},{6,7},{7,6},{8,9},{9,8},{10,11... | collective-permute-start | bytes 3145736 | tf_op jit(solution)/shard_map/ppermute | solution.py:39
  56.7 10.4 %collective-permute-start.15 = (bf16[256,128]{1,0:T(8,128)(2,1)S(1)}, bf16[256,128]{1,0:T(8,128)(2,1)S(1)}, u32[]{:S(2)}, u32[]{:S(2)}) collective-permute-start(bf16[256,128]{1,0:T(8,128)(2,1)S(1)} %get-tuple-element.25), channel_id=1, source_target_pairs={{0,2},{2,0},{4,6},{6,4},{8,10},{10,8},{12,14},{14,12},{16,18},{18,... | collective-permute-start | bytes 196616 | tf_op jit(solution)/shard_map/ppermute | solution.py:43
  57.3 14.1 %collective-permute-start.16 = (bf16[256,128]{1,0:T(8,128)(2,1)S(1)}, bf16[256,128]{1,0:T(8,128)(2,1)S(1)}, u32[]{:S(2)}, u32[]{:S(2)}) collective-permute-start(bf16[256,128]{1,0:T(8,128)(2,1)S(1)} %get-tuple-element.26), channel_id=1, source_target_pairs={{0,4},{2,6},{4,0},{6,2},{8,12},{10,14},{12,8},{14,10},{16,20},{18,... | collective-permute-start | bytes 196616 | tf_op jit(solution)/shard_map/ppermute | solution.py:43
  67.8 21.2 %collective-permute-start.23 = (bf16[64,2048]{1,0:T(8,128)(2,1)S(1)}, bf16[64,2048]{1,0:T(8,128)(2,1)S(1)}, u32[]{:S(2)}, u32[]{:S(2)}) collective-permute-start(bf16[64,2048]{1,0:T(8,128)(2,1)S(1)} %get-tuple-element.34), channel_id=1, source_target_pairs={{0,2},{2,0},{4,6},{6,4},{8,10},{10,8},{12,14},{14,12},{16,18},{18,... | collective-permute-start | bytes 786440 | tf_op jit(solution)/shard_map/ppermute | solution.py:43
  69.3 19.7 %collective-permute-start.25 = (bf16[64,2048]{1,0:T(8,128)(2,1)S(1)}, bf16[64,2048]{1,0:T(8,128)(2,1)S(1)}, u32[]{:S(2)}, u32[]{:S(2)}) collective-permute-start(bf16[64,2048]{1,0:T(8,128)(2,1)S(1)} %get-tuple-element.35), channel_id=1, source_target_pairs={{0,6},{2,4},{4,2},{6,0},{8,14},{10,12},{12,10},{14,8},{16,22},{18,... | collective-permute-start | bytes 786440 | tf_op jit(solution)/shard_map/ppermute | solution.py:43
  70.8 18.2 %collective-permute-start.24 = (bf16[64,2048]{1,0:T(8,128)(2,1)S(1)}, bf16[64,2048]{1,0:T(8,128)(2,1)S(1)}, u32[]{:S(2)}, u32[]{:S(2)}) collective-permute-start(bf16[64,2048]{1,0:T(8,128)(2,1)S(1)} %get-tuple-element.36), channel_id=1, source_target_pairs={{0,4},{2,6},{4,0},{6,2},{8,12},{10,14},{12,8},{14,10},{16,20},{18,... | collective-permute-start | bytes 786440 | tf_op jit(solution)/shard_map/ppermute | solution.py:43
  71.4 11.6 %collective-permute-start.44 = (bf16[16,512]{1,0:T(8,128)(2,1)S(1)}, bf16[16,512]{1,0:T(8,128)(2,1)S(1)}, u32[]{:S(2)}, u32[]{:S(2)}) collective-permute-start(bf16[16,512]{1,0:T(8,128)(2,1)S(1)} %add_convert_fusion.6), channel_id=1, source_target_pairs={{0,6},{2,4},{4,2},{6,0},{8,14},{10,12},{12,10},{14,8},{16,22},{18,... | collective-permute-start | bytes 49160 | tf_op jit(solution)/shard_map/ppermute | solution.py:43
  73.8 13.3 %collective-permute-start.43 = (bf16[16,512]{1,0:T(8,128)(2,1)S(1)}, bf16[16,512]{1,0:T(8,128)(2,1)S(1)}, u32[]{:S(2)}, u32[]{:S(2)}) collective-permute-start(bf16[16,512]{1,0:T(8,128)(2,1)S(1)} %add_convert_fusion.6), channel_id=1, source_target_pairs={{0,4},{2,6},{4,0},{6,2},{8,12},{10,14},{12,8},{14,10},{16,20},{18,... | collective-permute-start | bytes 49160 | tf_op jit(solution)/shard_map/ppermute | solution.py:43
  87.2 19.3 %collective-permute-start.47 = (bf16[64,512]{1,0:T(8,128)(2,1)S(1)}, bf16[64,512]{1,0:T(8,128)(2,1)S(1)}, u32[]{:S(2)}, u32[]{:S(2)}) collective-permute-start(bf16[64,512]{1,0:T(8,128)(2,1)S(1)} %pad_maximum_fusion.1.refs_0_), channel_id=1, source_target_pairs={{0,24},{2,26},{4,28},{6,30},{8,16},{10,18},{12,20},{14,22},{16,8},... | collective-permute-start | bytes 196616 | tf_op jit(solution)/shard_map/ppermute | solution.py:43
  89.0 23.5 %collective-permute-start.46 = (bf16[64,512]{1,0:T(8,128)(2,1)S(1)}, bf16[64,512]{1,0:T(8,128)(2,1)S(1)}, u32[]{:S(2)}, u32[]{:S(2)}) collective-permute-start(bf16[64,512]{1,0:T(8,128)(2,1)S(1)} %pad_maximum_fusion.1.refs_0_), channel_id=1, source_target_pairs={{0,16},{2,18},{4,20},{6,22},{8,24},{10,26},{12,28},{14,30},{16,0},... | collective-permute-start | bytes 196616 | tf_op jit(solution)/shard_map/ppermute | solution.py:43
  93.6 8.4 %collective-permute-start.27 = (bf16[16,2048]{1,0:T(8,128)(2,1)S(1)}, bf16[16,2048]{1,0:T(8,128)(2,1)S(1)}, u32[]{:S(2)}, u32[]{:S(2)}) collective-permute-start(bf16[16,2048]{1,0:T(8,128)(2,1)S(1)} %get-tuple-element.45), channel_id=1, source_target_pairs={{0,16},{2,18},{4,20},{6,22},{8,24},{10,26},{12,28},{14,30},{16,0},... | collective-permute-start | bytes 196616 | tf_op jit(solution)/shard_map/ppermute | solution.py:43
  103.8 7.0 %collective-permute-start.30 = (bf16[16,2048]{1,0:T(8,128)(2,1)S(1)}, bf16[16,2048]{1,0:T(8,128)(2,1)S(1)}, u32[]{:S(2)}, u32[]{:S(2)}) collective-permute-start(bf16[16,2048]{1,0:T(8,128)(2,1)S(1)} %add_convert_fusion.5), channel_id=1, source_target_pairs={{0,16},{2,18},{4,20},{6,22},{8,24},{10,26},{12,28},{14,30},{16,0},... | collective-permute-start | bytes 196616 | tf_op jit(solution)/shard_map/ppermute | solution.py:43
  103.8 8.7 %collective-permute-start.29 = (bf16[16,2048]{1,0:T(8,128)(2,1)S(1)}, bf16[16,2048]{1,0:T(8,128)(2,1)S(1)}, u32[]{:S(2)}, u32[]{:S(2)}) collective-permute-start(bf16[16,2048]{1,0:T(8,128)(2,1)S(1)} %add_convert_fusion.5), channel_id=1, source_target_pairs={{0,8},{2,10},{4,12},{6,14},{8,0},{10,2},{12,4},{14,6},{16,24},{18,... | collective-permute-start | bytes 196616 | tf_op jit(solution)/shard_map/ppermute | solution.py:43
  106.5 7.0 %collective-permute-start.45 = (bf16[64,512]{1,0:T(8,128)(2,1)S(1)}, bf16[64,512]{1,0:T(8,128)(2,1)S(1)}, u32[]{:S(2)}, u32[]{:S(2)}) collective-permute-start(bf16[64,512]{1,0:T(8,128)(2,1)S(1)} %pad_maximum_fusion.1.refs_0_), channel_id=1, source_target_pairs={{0,8},{2,10},{4,12},{6,14},{8,0},{10,2},{12,4},{14,6},{16,24},{18,... | collective-permute-start | bytes 196616 | tf_op jit(solution)/shard_map/ppermute | solution.py:43
  110.8 8.2 %collective-permute-start.21 = (bf16[512,128]{1,0:T(8,128)(2,1)S(1)}, bf16[512,128]{1,0:T(8,128)(2,1)S(1)}, u32[]{:S(2)}, u32[]{:S(2)}) collective-permute-start(bf16[512,128]{1,0:T(8,128)(2,1)S(1)} %get-tuple-element.38), channel_id=1, source_target_pairs={{0,24},{2,26},{4,28},{6,30},{8,16},{10,18},{12,20},{14,22},{16,8},... | collective-permute-start | bytes 393224 | tf_op jit(solution)/shard_map/ppermute | solution.py:43
  112.5 11.2 %collective-permute-start.20 = (bf16[512,128]{1,0:T(8,128)(2,1)S(1)}, bf16[512,128]{1,0:T(8,128)(2,1)S(1)}, u32[]{:S(2)}, u32[]{:S(2)}) collective-permute-start(bf16[512,128]{1,0:T(8,128)(2,1)S(1)} %get-tuple-element.39), channel_id=1, source_target_pairs={{0,16},{2,18},{4,20},{6,22},{8,24},{10,26},{12,28},{14,30},{16,0},... | collective-permute-start | bytes 393224 | tf_op jit(solution)/shard_map/ppermute | solution.py:43
  112.5 12.0 %collective-permute-start.34 = (bf16[64,2048]{1,0:T(8,128)(2,1)S(1)}, bf16[64,2048]{1,0:T(8,128)(2,1)S(1)}, u32[]{:S(2)}, u32[]{:S(2)}) collective-permute-start(bf16[64,2048]{1,0:T(8,128)(2,1)S(1)} %pad_maximum_fusion.refs_0_), channel_id=1, source_target_pairs={{0,6},{2,4},{4,2},{6,0},{8,14},{10,12},{12,10},{14,8},{16,22},{18,... | collective-permute-start | bytes 786440 | tf_op jit(solution)/shard_map/ppermute | solution.py:43
  113.5 13.2 %collective-permute-start.33 = (bf16[64,2048]{1,0:T(8,128)(2,1)S(1)}, bf16[64,2048]{1,0:T(8,128)(2,1)S(1)}, u32[]{:S(2)}, u32[]{:S(2)}) collective-permute-start(bf16[64,2048]{1,0:T(8,128)(2,1)S(1)} %pad_maximum_fusion.refs_0_), channel_id=1, source_target_pairs={{0,4},{2,6},{4,0},{6,2},{8,12},{10,14},{12,8},{14,10},{16,20},{18,... | collective-permute-start | bytes 786440 | tf_op jit(solution)/shard_map/ppermute | solution.py:43
  115.0 11.7 %collective-permute-start.32 = (bf16[64,2048]{1,0:T(8,128)(2,1)S(1)}, bf16[64,2048]{1,0:T(8,128)(2,1)S(1)}, u32[]{:S(2)}, u32[]{:S(2)}) collective-permute-start(bf16[64,2048]{1,0:T(8,128)(2,1)S(1)} %pad_maximum_fusion.refs_0_), channel_id=1, source_target_pairs={{0,2},{2,0},{4,6},{6,4},{8,10},{10,8},{12,14},{14,12},{16,18},{18,... | collective-permute-start | bytes 786440 | tf_op jit(solution)/shard_map/ppermute | solution.py:43
  (29 other events, 157.2 us)

commit v2 on v1

v2 whole, which is shorter than its diff:
```python
import functools

import jax
import jax.numpy as jnp
from jax import lax
from jax.experimental import pallas as pl
from jax.experimental.pallas import tpu as pltpu
from jax.sharding import PartitionSpec as P

HEADS = 8
EPS = 1e-05
LANES = 128
ROOM = 48 * 1024 * 1024

VMEM = pl.BlockSpec(memory_space=pltpu.VMEM)
SMEM = pl.BlockSpec(memory_space=pltpu.SMEM)
ANY = pl.BlockSpec(memory_space=pl.ANY)
f32 = jnp.float32
bf16 = jnp.bfloat16


def matmul(left, right):
    return lax.dot_general(left, right, (((1,), (0,)), ((), ())), preferred_element_type=f32)


def matmul_nt(left, right):
    return lax.dot_general(left, right, (((1,), (1,)), ((), ())), preferred_element_type=f32)


def matmul_tn(left, right):
    return lax.dot_general(left, right, (((0,), (0,)), ((), ())), preferred_element_type=f32)


def sigmoid(value):
    return 0.5 * jnp.tanh(0.5 * value) + 0.5


def bal_swap(value, step, count):
    return lax.ppermute(value, "bal", [(i, i ^ step) for i in range(count)])


def with_swapped(value, count):
    return [value] + [bal_swap(value, turn, count) for turn in range(1, count)]


def exchange(value, members):
    return lax.all_to_all(value, "emb", 0, 0, axis_index_groups=members, tiled=True)


def gather(value, members):
    count = len(members[0])
    copies = jnp.broadcast_to(value[None], (count,) + value.shape)
    return exchange(copies.reshape((count * value.shape[0],) + value.shape[1:]), members)


def pick_ids(pos_ref, moves_ref, ids_refs, groups, slots, tables):
    bal = pos_ref[0]
    bals = len(ids_refs)
    found = []
    for group in range(groups):
        source = jnp.int32(0)
        for index in range(bals):
            source = source + jnp.where(moves_ref[group, bals + index] == bal, index, 0)
        my_slot = moves_ref[group, bal]
        from_slot = moves_ref[group, source]
        turn_of = source ^ bal
        by_slot = [[] for _ in range(slots)]
        for table in range(tables):
            arrived = ids_refs[0][table, group * slots + from_slot]
            for turn in range(1, bals):
                other = ids_refs[turn][table, group * slots + from_slot]
                arrived = jnp.where(turn_of == turn, other, arrived)
            for slot in range(slots):
                own = ids_refs[0][table, group * slots + slot]
                by_slot[slot].append(jnp.where(my_slot == slot, arrived, own))
        found.append(by_slot)
    return found


def lookup_kernel(groups, slots, pos_ref, moves_ref, *refs):
    bals = (len(refs) - 1) // 2
    ids_refs, piece_refs, out_ref = refs[:bals], refs[bals : 2 * bals], refs[-1]
    bal = pos_ref[0]
    tables, part, columns = piece_refs[0].shape
    slot_rows = ids_refs[0].shape[3]
    lane = lax.broadcasted_iota(jnp.int32, (LANES, LANES), 1)
    ids = pick_ids(pos_ref, moves_ref, ids_refs, groups, slots, tables)
    for group in range(groups):
        for slot in range(slots):
            for first in range(0, slot_rows, LANES):
                total = jnp.zeros((LANES, columns), f32)
                for table in range(tables):
                    row = ids[group][slot][table][:, first : first + LANES]
                    column = jnp.transpose(jnp.broadcast_to(row, (LANES, LANES)))
                    for turn in range(bals):
                        shifted = column - (bal ^ turn) * part
                        hot = jnp.concatenate(
                            [
                                jnp.where(shifted == lane + at, 1.0, 0.0).astype(bf16)
                                for at in range(0, part, LANES)
                            ],
                            axis=1,
                        )
                        total = total + matmul(hot, piece_refs[turn][table])
                at = (group * slots + slot) * slot_rows + first
                out_ref[at : at + LANES, :] = total.astype(bf16)


def scatter_kernel(groups, slots, pos_ref, moves_ref, *refs):
    bals = (len(refs) - 1) // 2
    ids_refs, grad_ref, out_refs = refs[:bals], refs[bals], refs[bals + 1 :]
    bal = pos_ref[0]
    tables, part, _ = out_refs[0].shape
    slot_rows = ids_refs[0].shape[3]
    height = min(part, 256)
    iota = lax.broadcasted_iota(jnp.int32, (height, slot_rows), 0)
    ids = pick_ids(pos_ref, moves_ref, ids_refs, groups, slots, tables)
    grads = grad_ref[...]
    for table in range(tables):
        for turn in range(bals):
            for at in range(0, part, height):
                start = (bal ^ turn) * part + at
                hot = jnp.concatenate(
                    [
                        jnp.where(iota == ids[group][slot][table] - start, 1.0, 0.0).astype(bf16)
                        for group in range(groups)
                        for slot in range(slots)
                    ],
                    axis=1,
                )
                out_refs[turn][table, at : at + height, :] = matmul(hot, grads).astype(bf16)


def norm(values):
    average = jnp.mean(values, axis=1, keepdims=True)
    centred = values - average
    inverse = lax.rsqrt(jnp.mean(centred * centred, axis=1, keepdims=True) + EPS)
    return centred * inverse, inverse


def norm_back(incoming, normed, inverse):
    first = jnp.mean(incoming, axis=1, keepdims=True)
    second = jnp.mean(incoming * normed, axis=1, keepdims=True)
    return inverse * (incoming - first - normed * second)


def layer_kernel(groups, bals, pos_ref, seq_ref, surplus_ref, helper_ref, *refs):
    refs = list(refs)
    take = lambda count: [refs.pop(0) for _ in range(count)]
    (block_ref,) = take(1)
    in_refs = take(bals)
    out_refs = take(bals)
    (cot_ref,) = take(1)
    (layer_ref,) = take(1)
    (grad_ref,) = take(1)
    early_refs = take(bals)
    late_refs = take(bals)
    (w_in, w_out, cot_here, nt_ref, mt_ref, weights_ref, slope_ref, gate_ref, heads_ref, dsilu_ref, grads_ref, sems) = refs

    bal = pos_ref[0]
    rows, width = cot_here.shape
    slots = seq_ref.shape[1]
    slot_rows = rows // slots
    head_width = width // HEADS
    score_scale = head_width**-0.5
    piece = block_ref.shape[1]
    part = in_refs[0].shape[0]

    in_copies, out_copies = [], []
    for turn in range(bals):
        at = pl.ds(pl.multiple_of((bal ^ turn) * part, part), part)
        in_copies.append(pltpu.make_async_copy(in_refs[turn], w_in.at[at, :], sems.at[2 * turn]))
        out_copies.append(pltpu.make_async_copy(out_refs[turn], w_out.at[at, :], sems.at[2 * turn + 1]))
    cot_copy = pltpu.make_async_copy(cot_ref, cot_here, sems.at[2 * bals])
    for copy in in_copies + out_copies + [cot_copy]:
        copy.start()

    source = jnp.int32(0)
    for index in range(bals):
        source = source + jnp.where(helper_ref[index, 0] == bal, index, 0)
    my_slot = surplus_ref[bal, 0]
    moved = seq_ref[source, surplus_ref[source, 0]]
    lengths = [jnp.where(my_slot == slot, moved, seq_ref[bal, slot]) for slot in range(slots)]

    x = jnp.concatenate(
        [block_ref[group * rows : (group + 1) * rows, :] for group in range(groups)], axis=1
    ).astype(f32)
    normed_in, in_inverse = norm(x)
    nt_ref[...] = jnp.transpose(normed_in).astype(bf16)
    for copy in in_copies:
        copy.wait()
    projected = matmul(normed_in.astype(bf16), w_in[...])
    logistic = sigmoid(projected)
    active = projected * logistic
    dsilu_ref[...] = logistic + active * (1.0 - logistic)
    gate_ref[...] = active[:, :width]
    heads_ref[...] = active[:, width:].astype(bf16)

    pair_width = 2 * head_width
    low = lax.broadcasted_iota(jnp.int32, (slot_rows, pair_width), 1) < head_width
    row_at = lax.broadcasted_iota(jnp.int32, (slot_rows, slot_rows), 0)
    col_at = lax.broadcasted_iota(jnp.int32, (slot_rows, slot_rows), 1)

    def split(value):
        zero = jnp.zeros_like(value)
        return jnp.concatenate([jnp.where(low, value, zero), jnp.where(low, zero, value)], axis=0)

    def side_by_side(value):
        return jnp.concatenate([value[:slot_rows], value[slot_rows:]], axis=1)

    def part_of(slot, pair, which):
        first = which * width + pair * pair_width
        return heads_ref[slot * slot_rows : (slot + 1) * slot_rows, first : first + pair_width]

    pairs = HEADS // 2
    attended = []
    for slot in range(slots):
        live = (col_at <= row_at) & (row_at < lengths[slot])
        allowed = jnp.where(live, 1.0 / slot_rows, 0.0)
        allowed = jnp.concatenate([allowed, allowed], axis=0)
        across = []
        for pair in range(pairs):
            value, query, key = (part_of(slot, pair, which) for which in range(3))
            scores = matmul_nt(split(query), key) * score_scale
            q = sigmoid(scores)
            sq = scores * q
            weights = (sq * allowed).astype(bf16)
            weights_ref[slot * pairs + pair] = weights
            slope_ref[slot * pairs + pair] = allowed * (q + sq * (1.0 - q))
            across.append(matmul(side_by_side(weights), split(value)))
        attended.append(jnp.concatenate(across, axis=1))
    normed_out, out_inverse = norm(jnp.concatenate(attended, axis=0))
    gate = gate_ref[...]
    mixed = normed_out * gate
    mt_ref[...] = jnp.transpose(mixed).astype(bf16)
    for copy in out_copies + [cot_copy]:
        copy.wait()
    layer_ref[...] = (x + matmul(mixed.astype(bf16), w_out[...])).astype(bf16)

    cot = cot_here[...]
    grad_mixed = matmul_nt(cot, w_out[...])
    grad_attended = norm_back(grad_mixed * gate, normed_out, out_inverse).astype(bf16)
    grads_ref[:, :width] = (grad_mixed * normed_out * dsilu_ref[:, :width]).astype(bf16)

    for turn in range(bals):
        at = pl.ds(pl.multiple_of((bal ^ turn) * part, part), part)
        early_refs[turn][:, :width] = matmul(mt_ref[at, :], cot).astype(bf16)
        early_refs[turn][:, width:] = matmul(nt_ref[at, :], grads_ref[:, :width]).astype(bf16)

    for slot in range(slots):
        here = slice(slot * slot_rows, (slot + 1) * slot_rows)
        for pair in range(pairs):
            value, query, key = (part_of(slot, pair, which) for which in range(3))
            lanes = slice(pair * pair_width, (pair + 1) * pair_width)
            upper = split(grad_attended[here, lanes])
            grad_weights = matmul_nt(upper, value)
            grad_scores = (grad_weights * slope_ref[slot * pairs + pair]).astype(bf16)
            grad_value = matmul_tn(weights_ref[slot * pairs + pair], upper)
            grad_query = matmul(side_by_side(grad_scores), split(key)) * score_scale
            grad_key = matmul_tn(grad_scores, split(query)) * score_scale
            for which, found in enumerate((grad_value, grad_query, grad_key)):
                first = (1 + which) * width + pair * pair_width
                at = slice(first, first + pair_width)
                grads_ref[here, at] = (found * dsilu_ref[here, at]).astype(bf16)

    for turn in range(bals):
        at = pl.ds(pl.multiple_of((bal ^ turn) * part, part), part)
        late_refs[turn][...] = matmul(nt_ref[at, :], grads_ref[:, width:]).astype(bf16)

    grad_normed = matmul_nt(grads_ref[...], w_in[...])
    grad_rows = (cot.astype(f32) + norm_back(grad_normed, normed_in, in_inverse)).astype(bf16)
    for group in range(groups):
        grad_ref[group * rows : (group + 1) * rows, :] = grad_rows[:, group * piece : (group + 1) * piece]


def sum_rounded(terms):
    total = terms[0].astype(f32)
    for term in terms[1:]:
        total = total + term.astype(f32)
    return total.astype(bf16)


def sum_exchanged(value, members):
    count = len(members[0])
    came = exchange(value, members)
    came = came.reshape((count, came.shape[0] // count) + came.shape[1:])
    return sum_rounded([came[index] for index in range(count)])


def on_device(
    item_ids, seq_lengths, surplus_slot, helper_map, embed_tables, weight_in, weight_out, cotangent
):
    bal = lax.axis_index("bal")
    emb = lax.axis_index("emb")
    bals = lax.axis_size("bal")
    embs = lax.axis_size("emb")
    tables = item_ids.shape[2]
    groups = embs // tables
    _, rows, width = cotangent.shape
    slots = seq_lengths.shape[2]
    slot_rows = rows // slots
    distinct, columns = embed_tables.shape[1:]
    features = weight_in.shape[1]
    part = distinct // bals
    weight_part = weight_in.shape[0]
    table_here = emb // groups
    pos = bal.reshape(1).astype(jnp.int32)
    params = pltpu.CompilerParams(vmem_limit_bytes=ROOM)

    plane = [[table * groups + group for group in range(groups)] for table in range(tables)]
    depth = [[table * groups + group for table in range(tables)] for group in range(groups)]

    share = lax.dynamic_slice_in_dim(embed_tables[0], bal * part, part, 0)
    fetched = gather(share, depth).reshape(tables, part, columns)
    pieces = with_swapped(fetched, bals)

    ids = lax.dynamic_slice_in_dim(
        jnp.transpose(item_ids[0]), table_here * groups * rows, groups * rows, 1
    )
    plane_ids = with_swapped(ids.reshape(tables, groups * slots, 1, slot_rows), bals)
    moves = jnp.concatenate([surplus_slot[:, 0], helper_map[:, 0]])
    moves = gather(jnp.pad(moves, (0, LANES - 2 * bals))[None], plane)

    all_in = with_swapped(weight_in, bals)
    all_out = with_swapped(weight_out, bals)

    found = pl.pallas_call(
        functools.partial(lookup_kernel, groups, slots),
        out_shape=jax.ShapeDtypeStruct((groups * rows, columns), bf16),
        in_specs=[SMEM] * 2 + [VMEM] * (2 * bals),
        out_specs=VMEM,
        compiler_params=params,
    )(pos, moves, *plane_ids, *pieces)
    block = exchange(found, plane)

    pairs = slots * HEADS // 2
    early, late = 2 * width, features - width
    results = pl.pallas_call(
        functools.partial(layer_kernel, groups, bals),
        out_shape=[jax.ShapeDtypeStruct((rows, width), bf16)]
        + [jax.ShapeDtypeStruct((groups * rows, columns), bf16)]
        + [jax.ShapeDtypeStruct((weight_part, early), bf16)] * bals
        + [jax.ShapeDtypeStruct((weight_part, late), bf16)] * bals,
        in_specs=[SMEM] * 4 + [VMEM] + [ANY] * (2 * bals + 1),
        out_specs=[VMEM] * (2 + 2 * bals),
        scratch_shapes=[
            pltpu.VMEM((width, features), bf16),
            pltpu.VMEM((width, width), bf16),
            pltpu.VMEM((rows, width), bf16),
            pltpu.VMEM((width, rows), bf16),
            pltpu.VMEM((width, rows), bf16),
            pltpu.VMEM((pairs, 2 * slot_rows, slot_rows), bf16),
            pltpu.VMEM((pairs, 2 * slot_rows, slot_rows), f32),
            pltpu.VMEM((rows, width), f32),
            pltpu.VMEM((rows, features - width), bf16),
            pltpu.VMEM((rows, features), f32),
            pltpu.VMEM((rows, features), bf16),
            pltpu.SemaphoreType.DMA((2 * bals + 1,)),
        ],
        compiler_params=params,
    )(
        pos,
        seq_lengths[:, 0, :],
        surplus_slot,
        helper_map,
        block,
        *all_in,
        *all_out,
        cotangent[0],
    )
    layer_out, grads = results[:2]
    early_parts, late_parts = results[2 : 2 + bals], results[2 + bals :]

    def over_cores(parts):
        return sum_rounded([parts[0]] + [bal_swap(parts[turn], turn, bals) for turn in range(1, bals)])

    plane_grads = exchange(grads, plane)
    early_sum = sum_exchanged(over_cores(early_parts), plane)
    sums = pl.pallas_call(
        functools.partial(scatter_kernel, groups, slots),
        out_shape=[jax.ShapeDtypeStruct((tables, part, columns), bf16)] * bals,
        in_specs=[SMEM] * 2 + [VMEM] * (bals + 1),
        out_specs=[VMEM] * bals,
        compiler_params=params,
    )(pos, moves, *plane_ids, plane_grads)
    late_sum = sum_exchanged(over_cores(late_parts), plane)
    table_rows = exchange(over_cores(sums), depth)
    table_sum = jnp.sum(table_rows.astype(f32), axis=0)
    table_scale = (distinct / (bals * item_ids.shape[1])) ** 0.5

    grad_scale = (rows * embs * bals) ** -0.5
    early_all = gather(gather(sum_exchanged(early_sum, depth), depth), plane)
    late_all = gather(gather(sum_exchanged(late_sum, depth), depth), plane)
    total_out = early_all[:, :width].astype(f32) * grad_scale
    total_in = jnp.concatenate([early_all[:, width:], late_all], axis=1).astype(f32) * grad_scale
    return layer_out[None], (table_sum * table_scale)[None], total_in, total_out


def solution(mesh):
    placed = (
        P("bal", None, None),
        P(None, "emb", None),
        P(None, "emb"),
        P(None, "emb"),
        P("emb", None, None),
        P("bal", None),
        P("bal", None),
        P("bal", "emb", None),
    )
    return jax.shard_map(
        on_device,
        mesh=mesh,
        in_specs=placed,
        out_specs=(P("bal", "emb", None), P("emb", "bal", None), P("bal", None), P("bal", None)),
        check_vma=False,
    )
```

time: 129 us -> 173 us (1.34)
  waiting for transfers between devices: 46.1 us -> 74.9 us
  blocking collectives: 0 us -> 26.6 us
  starting transfers between devices: 50.3 us -> 38.3 us
  other arithmetic: 4.33 us -> 8.89 us
  between operations: 3.52 us -> 0.87 us
  Pallas kernels: 16.3 us -> 14.3 us
    all_to_all x0 -> x10, waiting for transfers between devices: none -> 73 us  [exchange(): lax.all_to_all(value, 'emb', 0, 0, axis_index_groups=members, tiled=True)]
    ppermute x39 -> x0, starting transfers between devices: 48.2 us -> none  [emb_swap(): return lax.ppermute(value, 'emb', [(i, i ^ step) for i in range(count)])]
    ppermute x39 -> x0, waiting for transfers between devices: 44.1 us -> none  [emb_swap(): return lax.ppermute(value, 'emb', [(i, i ^ step) for i in range(count)])]
    all_to_all x0 -> x10, starting transfers between devices: none -> 37.4 us  [exchange(): lax.all_to_all(value, 'emb', 0, 0, axis_index_groups=members, tiled=True)]
    all_to_all x0 -> x3, blocking collectives: none -> 26.6 us  [exchange(): lax.all_to_all(value, 'emb', 0, 0, axis_index_groups=members, tiled=True)]
    broadcast_in_dim x1 -> x6, local copies, waits for them, and re-layouts: 0.07 us -> 3.34 us  [gather(): copies = jnp.broadcast_to(value[None], (count,) + value.shape)]
    convert_element_type x7 -> x3, other arithmetic: 0.81 us -> 4.03 us  [sum_rounded(): return total.astype(bf16)]
    mul x0 -> x3, other arithmetic: none -> 3.17 us  [the longest x1 1.58 us: on_device(): jnp.concatenate([early_all[:, width:], late_all], axis=1).astype(f32)]
  transfers between devices with their start and end apart: 48 -> 17, of which waited for: 20 -> 11; matrix products, arithmetic and copies ran while one was open for 6% -> 5% of each run, Pallas kernels for 6% -> 4%
where the time goes in v2:
time: 173 us; the launch traced here: 172 us
  waiting for transfers between devices  74.9 us (43%)
  starting transfers between devices  38.3 us (22%)
  blocking collectives  26.6 us (15%)
  Pallas kernels  14.3 us (8%)
  other arithmetic  8.89 us (5%)
  local copies, waits for them, and re-layouts  8.01 us (5%)
    all_to_all x10, waiting for transfers between devices, exchange(): lax.all_to_all(value, 'emb', 0, 0, axis_index_groups=members, tiled=True)  73 us
    all_to_all x10, starting transfers between devices, exchange(): lax.all_to_all(value, 'emb', 0, 0, axis_index_groups=members, tiled=True)  37.4 us
    all_to_all x3, blocking collectives, exchange(): lax.all_to_all(value, 'emb', 0, 0, axis_index_groups=members, tiled=True)  26.6 us
    pallas_call x1, Pallas kernels, on_device(): pl.pallas_call(functools.partial(layer_kernel, groups, bals), out_shape=[...  7.19 us
    pallas_call x1, Pallas kernels, on_device(): pl.pallas_call(functools.partial(lookup_kernel, groups, slots), out_shape...  4.16 us
    convert_element_type x3, other arithmetic, sum_rounded(): return total.astype(bf16)  4.03 us
    unnamed x22, local copies, waits for them, and re-layouts  3.89 us
  transfers between devices with their start and end apart: 17, of which 11 were waited for; matrix products, arithmetic and copies ran while one was open for 5% of the time, Pallas kernels for 4%

profile of v2, /device:TPU:0, one launch (start us, length us, event | category | flops | bytes accessed | tf_op | source)
XLA Modules:
  0.0 171.9 jit_solution(2767951741069057292)
XLA Ops:
  2.5 6.3 %all-to-all-start.1 = ((bf16[4,512,128]{2,1,0:T(8,128)(2,1)}), bf16[4,512,128]{2,1,0:T(8,128)(2,1)S(1)}, u32[]{:S(2)}, u32[]{:S(2)}) async-start(bf16[4,512,128]{2,1,0:T(8,128)(2,1)} %broadcast_in_dim.23), calls=%async_computation.1 | async-start | bytes 1048576 | tf_op jit(solution)/shard_map/all_to_all | solution.py:47
  8.8 14.5 %all-to-all-done.1.refs_2_ = bf16[4,512,128]{2,1,0:T(8,128)(2,1)S(1)} async-done(((bf16[4,512,128]{2,1,0:T(8,128)(2,1)}), bf16[4,512,128]{2,1,0:T(8,128)(2,1)S(1)}, u32[]{:S(2)}, u32[]{:S(2)}) %all-to-all-start.1) | async-done | bytes 524320 | tf_op jit(solution)/shard_map/all_to_all | solution.py:47
  25.4 8.2 %all_to_all.101 = s32[4,1,128]{2,1,0:T(1,128)S(1)} all-to-all(s32[4,1,128]{2,1,0:T(1,128)S(1)} %reshape.178), channel_id=1, replica_groups={{0,2,4,6},{8,10,12,14},{16,18,20,22},{24,26,28,30},{1,3,5,7},{9,11,13,1..., dimensions={0} | all-to-all | bytes 4096 | tf_op jit(solution)/shard_map/all_to_all | solution.py:47
  33.6 4.2 %shard_map.111 = bf16[1024,128]{1,0:T(8,128)(2,1)} custom-call(s32[1]{0:T(128)} %bitcast.pos_ref, s32[4,128]{1,0:T(4,128)S(1)} %bitcast.34, s32[4,8,1,128]{3,2,1,0:T(1,128)S(1)} %reshape.180.refs_0_, s32[4,8,1,128]{3,2,1,0:T(1,128)S(1)} %collective-permute-done.refs_1_, bf16[4,512,128]{2,1,0:T(8,128)(2,1)S(1)} %all-to-all-done.1.refs_2_, ...), custom_call_target="tpu_custom_call" | custom-call | tf_op jit(solution)/shard_map/pallas_call | solution.py:327
  37.8 3.4 %all-to-all-start.2 = ((bf16[4,256,128]{2,1,0:T(8,128)(2,1)}), bf16[4,256,128]{2,1,0:T(8,128)(2,1)S(1)}, u32[]{:S(2)}, u32[]{:S(2)}) async-start(bf16[4,256,128]{2,1,0:T(8,128)(2,1)} %bitcast.8), calls=%async_computation.2 | async-start | bytes 524288 | tf_op jit(solution)/shard_map/all_to_all | solution.py:47
  41.4 5.1 %all-to-all-done.2 = bf16[4,256,128]{2,1,0:T(8,128)(2,1)S(1)} async-done(((bf16[4,256,128]{2,1,0:T(8,128)(2,1)}), bf16[4,256,128]{2,1,0:T(8,128)(2,1)S(1)}, u32[]{:S(2)}, u32[]{:S(2)}) %all-to-all-start.2) | async-done | bytes 262176 | tf_op jit(solution)/shard_map/all_to_all | solution.py:47
  48.4 7.2 %shard_map.112 = (bf16[256,512]{1,0:T(8,128)(2,1)}, bf16[1024,128]{1,0:T(8,128)(2,1)}, bf16[256,1024]{1,0:T(8,128)(2,1)S(1)}, bf16[256,1024]{1,0:T(8,128)(2,1)S(...) custom-call(s32[1]{0:T(128)} %bitcast.pos_ref, s32[2,2]{1,0:T(2,128)S(1)} %bitcast.36, ...), custom_call_target="tpu_custom_call" | custom-call | tf_op jit(solution)/shard_map/pallas_call | solution.py:338
  59.4 3.5 %all-to-all-start.5 = ((bf16[4,64,1024]{2,1,0:T(8,128)(2,1)}), bf16[4,64,1024]{2,1,0:T(8,128)(2,1)S(1)}, u32[]{:S(2)}, u32[]{:S(2)}) async-start(bf16[4,64,1024]{2,1,0:T(8,128)(2,1)} %bitcast.15), calls=%async_computation.5 | async-start | bytes 1048576 | tf_op jit(solution)/shard_map/all_to_all | solution.py:47
  63.1 8.4 %all-to-all-done.5 = bf16[4,64,1024]{2,1,0:T(8,128)(2,1)S(1)} async-done(((bf16[4,64,1024]{2,1,0:T(8,128)(2,1)}), bf16[4,64,1024]{2,1,0:T(8,128)(2,1)S(1)}, u32[]{:S(2)}, u32[]{:S(2)}) %all-to-all-start.5) | async-done | bytes 524320 | tf_op jit(solution)/shard_map/all_to_all | solution.py:47
  71.5 3.4 %all-to-all-start.3 = ((bf16[4,256,128]{2,1,0:T(8,128)(2,1)}), bf16[4,256,128]{2,1,0:T(8,128)(2,1)S(1)}, u32[]{:S(2)}, u32[]{:S(2)}) async-start(bf16[4,256,128]{2,1,0:T(8,128)(2,1)} %bitcast.12), calls=%async_computation.3 | async-start | bytes 524288 | tf_op jit(solution)/shard_map/all_to_all | solution.py:47
  75.6 4.6 %all-to-all-done.3 = bf16[4,256,128]{2,1,0:T(8,128)(2,1)S(1)} async-done(((bf16[4,256,128]{2,1,0:T(8,128)(2,1)}), bf16[4,256,128]{2,1,0:T(8,128)(2,1)S(1)}, u32[]{:S(2)}, u32[]{:S(2)}) %all-to-all-start.3) | async-done | bytes 262176 | tf_op jit(solution)/shard_map/all_to_all | solution.py:47
  80.2 3.5 %all-to-all-start.6 = ((bf16[4,16,1024]{2,1,0:T(8,128)(2,1)}), bf16[4,16,1024]{2,1,0:T(8,128)(2,1)S(1)}, u32[]{:S(2)}, u32[]{:S(2)}) async-start(bf16[4,16,1024]{2,1,0:T(8,128)(2,1)} %bitcast.16), calls=%async_computation.6 | async-start | bytes 262144 | tf_op jit(solution)/shard_map/all_to_all | solution.py:47
  90.1 3.3 %all-to-all-start.7 = ((bf16[4,16,1024]{2,1,0:T(8,128)(2,1)}), bf16[4,16,1024]{2,1,0:T(8,128)(2,1)S(1)}, u32[]{:S(2)}, u32[]{:S(2)}) async-start(bf16[4,16,1024]{2,1,0:T(8,128)(2,1)} %broadcast_in_dim.51), calls=%async_computation.7 | async-start | bytes 262144 | tf_op jit(solution)/shard_map/all_to_all | solution.py:47
  94.5 4.8 %all-to-all-done.7 = bf16[4,16,1024]{2,1,0:T(8,128)(2,1)S(1)} async-done(((bf16[4,16,1024]{2,1,0:T(8,128)(2,1)}), bf16[4,16,1024]{2,1,0:T(8,128)(2,1)S(1)}, u32[]{:S(2)}, u32[]{:S(2)}) %all-to-all-start.7) | async-done | bytes 131104 | tf_op jit(solution)/shard_map/all_to_all | solution.py:47
  99.3 3.5 %all-to-all-start.9 = ((bf16[4,64,1536]{2,1,0:T(8,128)(2,1)}), bf16[4,64,1536]{2,1,0:T(8,128)(2,1)S(1)}, u32[]{:S(2)}, u32[]{:S(2)}) async-start(bf16[4,64,1536]{2,1,0:T(8,128)(2,1)} %bitcast.20), calls=%async_computation.9 | async-start | bytes 1572864 | tf_op jit(solution)/shard_map/all_to_all | solution.py:47
  104.8 7.2 %all-to-all-done.9 = bf16[4,64,1536]{2,1,0:T(8,128)(2,1)S(1)} async-done(((bf16[4,64,1536]{2,1,0:T(8,128)(2,1)}), bf16[4,64,1536]{2,1,0:T(8,128)(2,1)S(1)}, u32[]{:S(2)}, u32[]{:S(2)}) %all-to-all-start.9) | async-done | bytes 786464 | tf_op jit(solution)/shard_map/all_to_all | solution.py:47
  112.0 3.5 %all-to-all-start.4 = ((bf16[4,512,128]{2,1,0:T(8,128)(2,1)}), bf16[4,512,128]{2,1,0:T(8,128)(2,1)S(1)}, u32[]{:S(2)}, u32[]{:S(2)}) async-start(bf16[4,512,128]{2,1,0:T(8,128)(2,1)} %add_convert_fusion.2), calls=%async_computation.4 | async-start | bytes 1048576 | tf_op jit(solution)/shard_map/all_to_all | solution.py:47
  115.6 12.9 %all-to-all-done.4 = bf16[4,512,128]{2,1,0:T(8,128)(2,1)S(1)} async-done(((bf16[4,512,128]{2,1,0:T(8,128)(2,1)}), bf16[4,512,128]{2,1,0:T(8,128)(2,1)S(1)}, u32[]{:S(2)}, u32[]{:S(2)}) %all-to-all-start.4) | async-done | bytes 524320 | tf_op jit(solution)/shard_map/all_to_all | solution.py:47
  128.5 9.3 %all_to_all.102 = bf16[4,16,1536]{2,1,0:T(8,128)(2,1)S(1)} all-to-all(bf16[4,16,1536]{2,1,0:T(8,128)(2,1)S(1)} %bitcast.40), channel_id=1, replica_groups={{0,8,16,24},{2,10,18,26},{4,12,20,28},{6,14,22,30},{1,9,17,25},{3,11,19..., dimensions={0} | all-to-all | bytes 393216 | tf_op jit(solution)/shard_map/all_to_all | solution.py:47
  138.7 3.5 %all-to-all-start.8 = ((bf16[4,64,1024]{2,1,0:T(8,128)(2,1)}), bf16[4,64,1024]{2,1,0:T(8,128)(2,1)S(1)}, u32[]{:S(2)}, u32[]{:S(2)}) async-start(bf16[4,64,1024]{2,1,0:T(8,128)(2,1)} %broadcast_in_dim.53), calls=%async_computation.8 | async-start | bytes 1048576 | tf_op jit(solution)/shard_map/all_to_all | solution.py:47
  142.2 6.5 %all-to-all-done.8 = bf16[4,64,1024]{2,1,0:T(8,128)(2,1)S(1)} async-done(((bf16[4,64,1024]{2,1,0:T(8,128)(2,1)}), bf16[4,64,1024]{2,1,0:T(8,128)(2,1)S(1)}, u32[]{:S(2)}, u32[]{:S(2)}) %all-to-all-start.8) | async-done | bytes 524320 | tf_op jit(solution)/shard_map/all_to_all | solution.py:47
  148.7 9.2 %all_to_all.103 = bf16[4,16,1536]{2,1,0:T(8,128)(2,1)S(1)} all-to-all(bf16[4,16,1536]{2,1,0:T(8,128)(2,1)S(1)} %broadcast_in_dim.55), channel_id=1, replica_groups={{0,8,16,24},{2,10,18,26},{4,12,20,28},{6,14,22,30},{1,9,17,25},{3,11,19..., dimensions={0} | all-to-all | bytes 393216 | tf_op jit(solution)/shard_map/all_to_all | solution.py:47
  158.8 3.5 %all-to-all-start.12 = ((bf16[4,64,1536]{2,1,0:T(8,128)(2,1)}), bf16[4,64,1536]{2,1,0:T(8,128)(2,1)S(1)}, u32[]{:S(2)}, u32[]{:S(2)}) async-start(bf16[4,64,1536]{2,1,0:T(8,128)(2,1)} %broadcast_in_dim.57), calls=%async_computation.12 | async-start | bytes 1572864 | tf_op jit(solution)/shard_map/all_to_all | solution.py:47
  164.0 6.3 %all-to-all-done.12 = bf16[4,64,1536]{2,1,0:T(8,128)(2,1)S(1)} async-done(((bf16[4,64,1536]{2,1,0:T(8,128)(2,1)}), bf16[4,64,1536]{2,1,0:T(8,128)(2,1)S(1)}, u32[]{:S(2)}, u32[]{:S(2)}) %all-to-all-start.12) | async-done | bytes 786464 | tf_op jit(solution)/shard_map/all_to_all | solution.py:47
  (61 shorter events, 25.4 us)
Async XLA Ops:
  0.6 1.0 copy-start
  0.6 45.9 %copy-start.1 = (bf16[256,2048]{1,0:T(8,128)(2,1)S(1)}, bf16[256,2048]{1,0:T(8,128)(2,1)}, u32[]{:S(2)}) copy-start(bf16[256,2048]{1,0:T(8,128)(2,1)} %refs_1_.1) | copy-start | bytes 3145732
  0.7 40.5 %copy-start.8 = (s32[2,1]{0,1:T(1,128)S(1)}, s32[2,1]{0,1:T(1,128)}, u32[]{:S(2)}) copy-start(s32[2,1]{0,1:T(1,128)} %param.10) | copy-start | bytes 28
  0.7 40.6 %copy-start.9 = (s32[2,1]{0,1:T(1,128)S(1)}, s32[2,1]{0,1:T(1,128)}, u32[]{:S(2)}) copy-start(s32[2,1]{0,1:T(1,128)} %param.11) | copy-start | bytes 28
  0.7 45.8 %copy-start.6 = (s32[2,1,2]{2,1,0:T(1,128)S(1)}, s32[2,1,2]{2,1,0:T(1,128)}, u32[]{:S(2)}) copy-start(s32[2,1,2]{2,1,0:T(1,128)} %param.9) | copy-start | bytes 52
  2.5 20.8 %all-to-all-start.1 = ((bf16[4,512,128]{2,1,0:T(8,128)(2,1)}), bf16[4,512,128]{2,1,0:T(8,128)(2,1)S(1)}, u32[]{:S(2)}, u32[]{:S(2)}) async-start(bf16[4,512,128]{2,1,0:T(8,128)(2,1)} %broadcast_in_dim.23), calls=%async_computation.1 | async-start | bytes 1048576 | tf_op jit(solution)/shard_map/all_to_all | solution.py:47
  8.8 32.6 %collective-permute-start.2 = (bf16[256,2048]{1,0:T(8,128)(2,1)}, bf16[256,2048]{1,0:T(8,128)(2,1)S(1)}, u32[]{:S(2)}, u32[]{:S(2)}) collective-permute-start(bf16[256,2048]{1,0:T(8,128)(2,1)} %refs_1_.1), channel_id=1, source_target_pairs={{0,1},{1,0},{2,3},{3,2},{4,5},{5,4},{6,7},{7,6},{8,9},{9,8},{10,11... | collective-permute-start | bytes 3145736 | tf_op jit(solution)/shard_map/ppermute | solution.py:39
  23.3 10.3 %collective-permute-start.1 = (bf16[4,512,128]{2,1,0:T(8,128)(2,1)S(1)}, bf16[4,512,128]{2,1,0:T(8,128)(2,1)S(1)}, u32[]{:S(2)}, u32[]{:S(2)}) collective-permute-start(bf16[4,512,128]{2,1,0:T(8,128)(2,1)S(1)} %all-to-all-done.1.refs_2_), channel_id=1, source_target_pairs={{0,1},{1,0},{2,3},{3,2},{4,5},{5,4},{6,7},{7,6},{8,9},{9,8},{10,11... | collective-permute-start | bytes 1572872 | tf_op jit(solution)/shard_map/ppermute | solution.py:39
  24.0 9.6 %collective-permute-start = (s32[4,8,1,128]{3,2,1,0:T(1,128)S(1)}, s32[4,8,1,128]{3,2,1,0:T(1,128)S(1)}, u32[]{:S(2)}, u32[]{:S(2)}) collective-permute-start(s32[4,8,1,128]{3,2,1,0:T(1,128)S(1)} %reshape.180.refs_0_), channel_id=1, source_target_pairs={{0,1},{1,0},{2,3},{3,2},{4,5},{5,4},{6,7},{7,6},{8,9},{9,8},{10,11... | collective-permute-start | bytes 49160 | tf_op jit(solution)/shard_map/ppermute | solution.py:39
  24.6 16.8 %collective-permute-start.3 = (bf16[256,512]{1,0:T(8,128)(2,1)}, bf16[256,512]{1,0:T(8,128)(2,1)}, u32[]{:S(2)}, u32[]{:S(2)}) collective-permute-start(bf16[256,512]{1,0:T(8,128)(2,1)} %refs_3_.1), channel_id=1, source_target_pairs={{0,1},{1,0},{2,3},{3,2},{4,5},{5,4},{6,7},{7,6},{8,9},{9,8},{10,11... | collective-permute-start | bytes 786440 | tf_op jit(solution)/shard_map/ppermute | solution.py:39
  37.8 8.8 %all-to-all-start.2 = ((bf16[4,256,128]{2,1,0:T(8,128)(2,1)}), bf16[4,256,128]{2,1,0:T(8,128)(2,1)S(1)}, u32[]{:S(2)}, u32[]{:S(2)}) async-start(bf16[4,256,128]{2,1,0:T(8,128)(2,1)} %bitcast.8), calls=%async_computation.2 | async-start | bytes 524288 | tf_op jit(solution)/shard_map/all_to_all | solution.py:47
  56.5 2.9 %copy-start.7 = (bf16[256,1536]{1,0:T(8,128)(2,1)}, bf16[256,1536]{1,0:T(8,128)(2,1)S(1)}, u32[]{:S(2)}) copy-start(bf16[256,1536]{1,0:T(8,128)(2,1)S(1)} %get-tuple-element.19) | copy-start | bytes 2359300
  56.5 1.9 %collective-permute-start.5 = (bf16[256,1024]{1,0:T(8,128)(2,1)S(1)}, bf16[256,1024]{1,0:T(8,128)(2,1)S(1)}, u32[]{:S(2)}, u32[]{:S(2)}) collective-permute-start(bf16[256,1024]{1,0:T(8,128)(2,1)S(1)} %get-tuple-element.17), channel_id=1, source_target_pairs={{0,1},{1,0},{2,3},{3,2},{4,5},{5,4},{6,7},{7,6},{8,9},{9,8},{10,11... | collective-permute-start | bytes 1572872 | tf_op jit(solution)/shard_map/ppermute | solution.py:39
  58.4 35.0 %copy-start.3 = (bf16[256,1536]{1,0:T(8,128)(2,1)S(1)}, bf16[256,1536]{1,0:T(8,128)(2,1)}, u32[]{:S(2)}) copy-start(bf16[256,1536]{1,0:T(8,128)(2,1)} %copy-done.2) | copy-start | bytes 2359300
  59.4 12.0 %all-to-all-start.5 = ((bf16[4,64,1024]{2,1,0:T(8,128)(2,1)}), bf16[4,64,1024]{2,1,0:T(8,128)(2,1)S(1)}, u32[]{:S(2)}, u32[]{:S(2)}) async-start(bf16[4,64,1024]{2,1,0:T(8,128)(2,1)} %bitcast.15), calls=%async_computation.5 | async-start | bytes 1048576 | tf_op jit(solution)/shard_map/all_to_all | solution.py:47
  62.9 30.6 %collective-permute-start.6 = (bf16[256,1536]{1,0:T(8,128)(2,1)}, bf16[256,1536]{1,0:T(8,128)(2,1)S(1)}, u32[]{:S(2)}, u32[]{:S(2)}) collective-permute-start(bf16[256,1536]{1,0:T(8,128)(2,1)} %copy-done.7), channel_id=1, source_target_pairs={{0,1},{1,0},{2,3},{3,2},{4,5},{5,4},{6,7},{7,6},{8,9},{9,8},{10,11... | collective-permute-start | bytes 2359304 | tf_op jit(solution)/shard_map/ppermute | solution.py:39
  71.5 8.8 %all-to-all-start.3 = ((bf16[4,256,128]{2,1,0:T(8,128)(2,1)}), bf16[4,256,128]{2,1,0:T(8,128)(2,1)S(1)}, u32[]{:S(2)}, u32[]{:S(2)}) async-start(bf16[4,256,128]{2,1,0:T(8,128)(2,1)} %bitcast.12), calls=%async_computation.3 | async-start | bytes 524288 | tf_op jit(solution)/shard_map/all_to_all | solution.py:47
  80.2 9.2 %all-to-all-start.6 = ((bf16[4,16,1024]{2,1,0:T(8,128)(2,1)}), bf16[4,16,1024]{2,1,0:T(8,128)(2,1)S(1)}, u32[]{:S(2)}, u32[]{:S(2)}) async-start(bf16[4,16,1024]{2,1,0:T(8,128)(2,1)} %bitcast.16), calls=%async_computation.6 | async-start | bytes 262144 | tf_op jit(solution)/shard_map/all_to_all | solution.py:47
  86.6 16.2 %collective-permute-start.4 = (bf16[4,512,128]{2,1,0:T(8,128)(2,1)S(1)}, bf16[4,512,128]{2,1,0:T(8,128)(2,1)}, u32[]{:S(2)}, u32[]{:S(2)}) collective-permute-start(bf16[4,512,128]{2,1,0:T(8,128)(2,1)S(1)} %get-tuple-element.15), channel_id=1, source_target_pairs={{0,1},{1,0},{2,3},{3,2},{4,5},{5,4},{6,7},{7,6},{8,9},{9,8},{10,11... | collective-permute-start | bytes 1572872 | tf_op jit(solution)/shard_map/ppermute | solution.py:39
  90.1 9.2 %all-to-all-start.7 = ((bf16[4,16,1024]{2,1,0:T(8,128)(2,1)}), bf16[4,16,1024]{2,1,0:T(8,128)(2,1)S(1)}, u32[]{:S(2)}, u32[]{:S(2)}) async-start(bf16[4,16,1024]{2,1,0:T(8,128)(2,1)} %broadcast_in_dim.51), calls=%async_computation.7 | async-start | bytes 262144 | tf_op jit(solution)/shard_map/all_to_all | solution.py:47
  99.3 12.7 %all-to-all-start.9 = ((bf16[4,64,1536]{2,1,0:T(8,128)(2,1)}), bf16[4,64,1536]{2,1,0:T(8,128)(2,1)S(1)}, u32[]{:S(2)}, u32[]{:S(2)}) async-start(bf16[4,64,1536]{2,1,0:T(8,128)(2,1)} %bitcast.20), calls=%async_computation.9 | async-start | bytes 1572864 | tf_op jit(solution)/shard_map/all_to_all | solution.py:47
  112.0 16.5 %all-to-all-start.4 = ((bf16[4,512,128]{2,1,0:T(8,128)(2,1)}), bf16[4,512,128]{2,1,0:T(8,128)(2,1)S(1)}, u32[]{:S(2)}, u32[]{:S(2)}) async-start(bf16[4,512,128]{2,1,0:T(8,128)(2,1)} %add_convert_fusion.2), calls=%async_computation.4 | async-start | bytes 1048576 | tf_op jit(solution)/shard_map/all_to_all | solution.py:47
  138.7 10.0 %all-to-all-start.8 = ((bf16[4,64,1024]{2,1,0:T(8,128)(2,1)}), bf16[4,64,1024]{2,1,0:T(8,128)(2,1)S(1)}, u32[]{:S(2)}, u32[]{:S(2)}) async-start(bf16[4,64,1024]{2,1,0:T(8,128)(2,1)} %broadcast_in_dim.53), calls=%async_computation.8 | async-start | bytes 1048576 | tf_op jit(solution)/shard_map/all_to_all | solution.py:47
  158.8 11.5 %all-to-all-start.12 = ((bf16[4,64,1536]{2,1,0:T(8,128)(2,1)}), bf16[4,64,1536]{2,1,0:T(8,128)(2,1)S(1)}, u32[]{:S(2)}, u32[]{:S(2)}) async-start(bf16[4,64,1536]{2,1,0:T(8,128)(2,1)} %broadcast_in_dim.57), calls=%async_computation.12 | async-start | bytes 1572864 | tf_op jit(solution)/shard_map/all_to_all | solution.py:47
  (3 other events, 2.8 us)

commit v3 on v2

--- a/solution.py
+++ b/solution.py
@@ -14,7 +14,7 @@
 
 VMEM = pl.BlockSpec(memory_space=pltpu.VMEM)
 SMEM = pl.BlockSpec(memory_space=pltpu.SMEM)
-ANY = pl.BlockSpec(memory_space=pl.ANY)
+HBM = pl.BlockSpec(memory_space=pltpu.HBM)
 f32 = jnp.float32
 bf16 = jnp.bfloat16
 
@@ -43,29 +43,24 @@
     return [value] + [bal_swap(value, turn, count) for turn in range(1, count)]
 
 
-def exchange(value, members):
-    return lax.all_to_all(value, "emb", 0, 0, axis_index_groups=members, tiled=True)
-
-
-def gather(value, members):
-    count = len(members[0])
-    copies = jnp.broadcast_to(value[None], (count,) + value.shape)
-    return exchange(copies.reshape((count * value.shape[0],) + value.shape[1:]), members)
-
-
-def pick_ids(pos_ref, moves_ref, ids_refs, groups, slots, tables):
+def emb_swap(value, step, count):
+    return lax.ppermute(value, "emb", [(i, i ^ step) for i in range(count)])
+
+
+def pick_ids(pos_ref, moves_refs, ids_refs, slots, tables):
     bal = pos_ref[0]
     bals = len(ids_refs)
     found = []
-    for group in range(groups):
+    for step, moves_ref in enumerate(moves_refs):
+        group = pos_ref[1] ^ step
         source = jnp.int32(0)
         for index in range(bals):
-            source = source + jnp.where(moves_ref[group, bals + index] == bal, index, 0)
-        my_slot = moves_ref[group, bal]
-        from_slot = moves_ref[group, source]
+            source = source + jnp.where(moves_ref[0, bals + index] == bal, index, 0)
+        my_slot = moves_ref[0, bal]
+        from_slot = moves_ref[0, source]
         turn_of = source ^ bal
         by_slot = [[] for _ in range(slots)]
-        for table in range(tables):
+        for table in tables:
             arrived = ids_refs[0][table, group * slots + from_slot]
             for turn in range(1, bals):
                 other = ids_refs[turn][table, group * slots + from_slot]
@@ -77,14 +72,24 @@
     return found
 
 
-def lookup_kernel(groups, slots, pos_ref, moves_ref, *refs):
-    bals = (len(refs) - 1) // 2
-    ids_refs, piece_refs, out_ref = refs[:bals], refs[bals : 2 * bals], refs[-1]
+def table_order(table_here, tables):
+    return [table_here ^ step for step in range(tables)]
+
+
+def lookup_kernel(groups, slots, tables, bals, pos_ref, *refs):
+    refs = list(refs)
+    take = lambda count: [refs.pop(0) for _ in range(count)]
+    moves_refs, ids_refs = take(groups), take(bals)
+    (own_ref,) = take(1)
+    others = [take(bals) for _ in range(1, tables)]
+    out_refs = refs
     bal = pos_ref[0]
-    tables, part, columns = piece_refs[0].shape
+    table_here = pos_ref[2]
+    distinct, columns = own_ref.shape
+    part = distinct // bals
     slot_rows = ids_refs[0].shape[3]
     lane = lax.broadcasted_iota(jnp.int32, (LANES, LANES), 1)
-    ids = pick_ids(pos_ref, moves_ref, ids_refs, groups, slots, tables)
+    ids = pick_ids(pos_ref, moves_refs, ids_refs, slots, table_order(table_here, tables))
     for group in range(groups):
         for slot in range(slots):
             for first in range(0, slot_rows, LANES):
@@ -92,30 +97,39 @@
                 for table in range(tables):
                     row = ids[group][slot][table][:, first : first + LANES]
                     column = jnp.transpose(jnp.broadcast_to(row, (LANES, LANES)))
-                    for turn in range(bals):
-                        shifted = column - (bal ^ turn) * part
+                    if table == 0:
+                        pieces = [(own_ref, 0, distinct)]
+                    else:
+                        pieces = [
+                            (ref, (bal ^ turn) * part, part)
+                            for turn, ref in enumerate(others[table - 1])
+                        ]
+                    for ref, start, height in pieces:
+                        shifted = column - start
                         hot = jnp.concatenate(
                             [
                                 jnp.where(shifted == lane + at, 1.0, 0.0).astype(bf16)
-                                for at in range(0, part, LANES)
+                                for at in range(0, height, LANES)
                             ],
                             axis=1,
                         )
-                        total = total + matmul(hot, piece_refs[turn][table])
-                at = (group * slots + slot) * slot_rows + first
-                out_ref[at : at + LANES, :] = total.astype(bf16)
-
-
-def scatter_kernel(groups, slots, pos_ref, moves_ref, *refs):
-    bals = (len(refs) - 1) // 2
-    ids_refs, grad_ref, out_refs = refs[:bals], refs[bals], refs[bals + 1 :]
+                        total = total + matmul(hot, ref[...])
+                at = slot * slot_rows + first
+                out_refs[group][at : at + LANES, :] = total.astype(bf16)
+
+
+def scatter_kernel(groups, slots, bals, pos_ref, *refs):
+    refs = list(refs)
+    take = lambda count: [refs.pop(0) for _ in range(count)]
+    moves_refs, ids_refs, grad_refs, out_refs = take(groups), take(bals), take(groups), refs
     bal = pos_ref[0]
+    table_here = pos_ref[2]
     tables, part, _ = out_refs[0].shape
     slot_rows = ids_refs[0].shape[3]
     height = min(part, 256)
     iota = lax.broadcasted_iota(jnp.int32, (height, slot_rows), 0)
-    ids = pick_ids(pos_ref, moves_ref, ids_refs, groups, slots, tables)
-    grads = grad_ref[...]
+    ids = pick_ids(pos_ref, moves_refs, ids_refs, slots, table_order(table_here, tables))
+    grads = jnp.concatenate([ref[...] for ref in grad_refs], axis=0)
     for table in range(tables):
         for turn in range(bals):
             for at in range(0, part, height):
@@ -147,15 +161,15 @@
 def layer_kernel(groups, bals, pos_ref, seq_ref, surplus_ref, helper_ref, *refs):
     refs = list(refs)
     take = lambda count: [refs.pop(0) for _ in range(count)]
-    (block_ref,) = take(1)
+    block_refs = take(groups)
     in_refs = take(bals)
     out_refs = take(bals)
     (cot_ref,) = take(1)
     (layer_ref,) = take(1)
-    (grad_ref,) = take(1)
+    grad_refs = take(groups)
     early_refs = take(bals)
     late_refs = take(bals)
-    (w_in, w_out, cot_here, nt_ref, mt_ref, weights_ref, slope_ref, gate_ref, heads_ref, dsilu_ref, grads_ref, sems) = refs
+    (x_ref, w_in, w_out, cot_here, nt_ref, mt_ref, weights_ref, slope_ref, gate_ref, heads_ref, dsilu_ref, grads_ref, sems) = refs
 
     bal = pos_ref[0]
     rows, width = cot_here.shape
@@ -163,7 +177,8 @@
     slot_rows = rows // slots
     head_width = width // HEADS
     score_scale = head_width**-0.5
-    piece = block_ref.shape[1]
+    piece = block_refs[0].shape[1]
+    group_here = pos_ref[1]
     part = in_refs[0].shape[0]
 
     in_copies, out_copies = [], []
@@ -182,9 +197,9 @@
     moved = seq_ref[source, surplus_ref[source, 0]]
     lengths = [jnp.where(my_slot == slot, moved, seq_ref[bal, slot]) for slot in range(slots)]
 
-    x = jnp.concatenate(
-        [block_ref[group * rows : (group + 1) * rows, :] for group in range(groups)], axis=1
-    ).astype(f32)
+    for step in range(groups):
+        x_ref[group_here ^ step] = block_refs[step][...]
+    x = jnp.concatenate([x_ref[group] for group in range(groups)], axis=1).astype(f32)
     normed_in, in_inverse = norm(x)
     nt_ref[...] = jnp.transpose(normed_in).astype(bf16)
     for copy in in_copies:
@@ -270,7 +285,9 @@
     grad_normed = matmul_nt(grads_ref[...], w_in[...])
     grad_rows = (cot.astype(f32) + norm_back(grad_normed, normed_in, in_inverse)).astype(bf16)
     for group in range(groups):
-        grad_ref[group * rows : (group + 1) * rows, :] = grad_rows[:, group * piece : (group + 1) * piece]
+        x_ref[group] = grad_rows[:, group * piece : (group + 1) * piece]
+    for step in range(groups):
+        grad_refs[step][...] = x_ref[group_here ^ step]
 
 
 def sum_rounded(terms):
@@ -278,13 +295,6 @@
     for term in terms[1:]:
         total = total + term.astype(f32)
     return total.astype(bf16)
-
-
-def sum_exchanged(value, members):
-    count = len(members[0])
-    came = exchange(value, members)
-    came = came.reshape((count, came.shape[0] // count) + came.shape[1:])
-    return sum_rounded([came[index] for index in range(count)])
 
 
 def on_device(
@@ -304,46 +314,47 @@
     part = distinct // bals
     weight_part = weight_in.shape[0]
     table_here = emb // groups
-    pos = bal.reshape(1).astype(jnp.int32)
+    group_here = emb % groups
+    pos = jnp.stack([bal, group_here, table_here]).astype(jnp.int32)
     params = pltpu.CompilerParams(vmem_limit_bytes=ROOM)
 
-    plane = [[table * groups + group for group in range(groups)] for table in range(tables)]
-    depth = [[table * groups + group for table in range(tables)] for group in range(groups)]
 
     share = lax.dynamic_slice_in_dim(embed_tables[0], bal * part, part, 0)
-    fetched = gather(share, depth).reshape(tables, part, columns)
-    pieces = with_swapped(fetched, bals)
+    fetched = [emb_swap(share, step * groups, embs) for step in range(1, tables)]
+    pieces = [embed_tables[0]] + [piece for one in fetched for piece in with_swapped(one, bals)]
 
     ids = lax.dynamic_slice_in_dim(
         jnp.transpose(item_ids[0]), table_here * groups * rows, groups * rows, 1
     )
     plane_ids = with_swapped(ids.reshape(tables, groups * slots, 1, slot_rows), bals)
     moves = jnp.concatenate([surplus_slot[:, 0], helper_map[:, 0]])
-    moves = gather(jnp.pad(moves, (0, LANES - 2 * bals))[None], plane)
+    moves = jnp.pad(moves, (0, LANES - 2 * bals))[None]
+    plane_moves = [moves] + [emb_swap(moves, step, embs) for step in range(1, groups)]
 
     all_in = with_swapped(weight_in, bals)
     all_out = with_swapped(weight_out, bals)
 
     found = pl.pallas_call(
-        functools.partial(lookup_kernel, groups, slots),
-        out_shape=jax.ShapeDtypeStruct((groups * rows, columns), bf16),
-        in_specs=[SMEM] * 2 + [VMEM] * (2 * bals),
-        out_specs=VMEM,
+        functools.partial(lookup_kernel, groups, slots, tables, bals),
+        out_shape=[jax.ShapeDtypeStruct((rows, columns), bf16)] * groups,
+        in_specs=[SMEM] * (1 + groups) + [VMEM] * (bals + len(pieces)),
+        out_specs=[VMEM] * groups,
         compiler_params=params,
-    )(pos, moves, *plane_ids, *pieces)
-    block = exchange(found, plane)
+    )(pos, *plane_moves, *plane_ids, *pieces)
+    block = [found[0]] + [emb_swap(found[step], step, embs) for step in range(1, groups)]
 
     pairs = slots * HEADS // 2
     early, late = 2 * width, features - width
     results = pl.pallas_call(
         functools.partial(layer_kernel, groups, bals),
         out_shape=[jax.ShapeDtypeStruct((rows, width), bf16)]
-        + [jax.ShapeDtypeStruct((groups * rows, columns), bf16)]
+        + [jax.ShapeDtypeStruct((rows, columns), bf16)] * groups
         + [jax.ShapeDtypeStruct((weight_part, early), bf16)] * bals
         + [jax.ShapeDtypeStruct((weight_part, late), bf16)] * bals,
-        in_specs=[SMEM] * 4 + [VMEM] + [ANY] * (2 * bals + 1),
-        out_specs=[VMEM] * (2 + 2 * bals),
+        in_specs=[SMEM] * 4 + [VMEM] * groups + [HBM] * (2 * bals + 1),
+        out_specs=[VMEM] * (1 + groups + 2 * bals),
         scratch_shapes=[
+            pltpu.VMEM((groups, rows, columns), bf16),
             pltpu.VMEM((width, features), bf16),
             pltpu.VMEM((width, width), bf16),
             pltpu.VMEM((rows, width), bf16),
@@ -363,36 +374,38 @@
         seq_lengths[:, 0, :],
         surplus_slot,
         helper_map,
-        block,
+        *block,
         *all_in,
         *all_out,
         cotangent[0],
     )
-    layer_out, grads = results[:2]
-    early_parts, late_parts = results[2 : 2 + bals], results[2 + bals :]
+    layer_out, results = results[0], results[1:]
+    grads, results = results[:groups], results[groups:]
+    early_parts, late_parts = results[:bals], results[bals:]
 
     def over_cores(parts):
         return sum_rounded([parts[0]] + [bal_swap(parts[turn], turn, bals) for turn in range(1, bals)])
 
-    plane_grads = exchange(grads, plane)
-    early_sum = sum_exchanged(over_cores(early_parts), plane)
+    plane_grads = [grads[0]] + [emb_swap(grads[step], step, embs) for step in range(1, groups)]
+    weight_sum = jnp.concatenate([over_cores(early_parts), over_cores(late_parts)], axis=1)
+    owned = lax.psum_scatter(weight_sum, "emb", scatter_dimension=0, tiled=True)
+    total = lax.all_gather(owned, "emb", axis=0, tiled=True)
     sums = pl.pallas_call(
-        functools.partial(scatter_kernel, groups, slots),
+        functools.partial(scatter_kernel, groups, slots, bals),
         out_shape=[jax.ShapeDtypeStruct((tables, part, columns), bf16)] * bals,
-        in_specs=[SMEM] * 2 + [VMEM] * (bals + 1),
+        in_specs=[SMEM] * (1 + groups) + [VMEM] * (bals + groups),
         out_specs=[VMEM] * bals,
         compiler_params=params,
-    )(pos, moves, *plane_ids, plane_grads)
-    late_sum = sum_exchanged(over_cores(late_parts), plane)
-    table_rows = exchange(over_cores(sums), depth)
-    table_sum = jnp.sum(table_rows.astype(f32), axis=0)
+    )(pos, *plane_moves, *plane_ids, *plane_grads)
+    own_sums = over_cores(sums)
+    table_sum = own_sums[0].astype(f32)
+    for step in range(1, tables):
+        table_sum = table_sum + emb_swap(own_sums[step], step * groups, embs).astype(f32)
     table_scale = (distinct / (bals * item_ids.shape[1])) ** 0.5
 
     grad_scale = (rows * embs * bals) ** -0.5
-    early_all = gather(gather(sum_exchanged(early_sum, depth), depth), plane)
-    late_all = gather(gather(sum_exchanged(late_sum, depth), depth), plane)
-    total_out = early_all[:, :width].astype(f32) * grad_scale
-    total_in = jnp.concatenate([early_all[:, width:], late_all], axis=1).astype(f32) * grad_scale
+    total_out = total[:, :width].astype(f32) * grad_scale
+    total_in = total[:, width:].astype(f32) * grad_scale
     return layer_out[None], (table_sum * table_scale)[None], total_in, total_out
 
 

time: 173 us -> 207 us (1.20)
  waiting for transfers between devices: 74.9 us -> 144 us
  blocking collectives: 26.6 us -> 0 us
  starting transfers between devices: 38.3 us -> 21.7 us
  between operations: 0.87 us -> 14.2 us
    reduce_scatter x0 -> x1, waiting for transfers between devices: none -> 76.7 us  [on_device(): owned = lax.psum_scatter(weight_sum, 'emb', scatter_dimension=0, tiled=True)]
    all_to_all x10 -> x0, waiting for transfers between devices: 73 us -> none  [exchange(): lax.all_to_all(value, 'emb', 0, 0, axis_index_groups=members, tiled=True)]
    all_to_all x10 -> x0, starting transfers between devices: 37.4 us -> none  [exchange(): lax.all_to_all(value, 'emb', 0, 0, axis_index_groups=members, tiled=True)]
    all_gather x0 -> x1, waiting for transfers between devices: none -> 33.8 us  [on_device(): total = lax.all_gather(owned, 'emb', axis=0, tiled=True)]
    ppermute x0 -> x15, waiting for transfers between devices: none -> 26.8 us  [emb_swap(): return lax.ppermute(value, 'emb', [(i, i ^ step) for i in range(count)])]
    all_to_all x3 -> x0, blocking collectives: 26.6 us -> none  [exchange(): lax.all_to_all(value, 'emb', 0, 0, axis_index_groups=members, tiled=True)]
    ppermute x0 -> x15, starting transfers between devices: none -> 19.6 us  [emb_swap(): return lax.ppermute(value, 'emb', [(i, i ^ step) for i in range(count)])]
    ppermute x7 -> x9, waiting for transfers between devices: 1.92 us -> 6.34 us  [bal_swap(): return lax.ppermute(value, 'bal', [(i, i ^ step) for i in range(count)])]
  transfers between devices with their start and end apart: 17 -> 26, of which waited for: 11 -> 18; matrix products, arithmetic and copies ran while one was open for 5% -> 2% of each run, Pallas kernels for 4% -> 3%
where the time goes in v3:
time: 207 us; the launch traced here: 206 us
  waiting for transfers between devices  144 us (70%)
  starting transfers between devices  21.7 us (10%)
  between operations  14.2 us (7%)
  Pallas kernels  12.9 us (6%)
  other arithmetic  7.86 us (4%)
  local copies, waits for them, and re-layouts  6 us (3%)
    reduce_scatter x1, waiting for transfers between devices, on_device(): owned = lax.psum_scatter(weight_sum, 'emb', scatter_dimension=0, tiled=True)  76.7 us
    all_gather x1, waiting for transfers between devices, on_device(): total = lax.all_gather(owned, 'emb', axis=0, tiled=True)  33.8 us
    ppermute x15, waiting for transfers between devices, emb_swap(): return lax.ppermute(value, 'emb', [(i, i ^ step) for i in range(count)])  26.8 us
    ppermute x15, starting transfers between devices, emb_swap(): return lax.ppermute(value, 'emb', [(i, i ^ step) for i in range(count)])  19.6 us
    pallas_call x1, Pallas kernels, on_device(): pl.pallas_call(functools.partial(layer_kernel, groups, bals), out_shape=[...  6.56 us
    ppermute x9, waiting for transfers between devices, bal_swap(): return lax.ppermute(value, 'bal', [(i, i ^ step) for i in range(count)])  6.34 us
    unnamed x14, local copies, waits for them, and re-layouts  5.02 us
  transfers between devices with their start and end apart: 26, of which 18 were waited for; matrix products, arithmetic and copies ran while one was open for 2% of the time, Pallas kernels for 3%

profile of v3, /device:TPU:0, one launch (start us, length us, event | category | flops | bytes accessed | tf_op | source)
XLA Modules:
  0.0 206.3 jit_solution(10719471632553711556)
XLA Ops:
  8.5 3.5 %collective-permute-start.2 = (s32[1,128]{1,0:T(1,128)S(1)}, s32[1,128]{1,0:T(1,128)S(1)}, u32[]{:S(2)}, u32[]{:S(2)}) collective-permute-start(s32[1,128]{1,0:T(1,128)S(1)} %pad_bitcast_fusion.refs_0_), channel_id=1, source_target_pairs={{0,6},{2,4},{4,2},{6,0},{8,14},{10,12},{12,10},{14,8},{16,22},{18,... | collective-permute-start | bytes 1544 | tf_op jit(solution)/shard_map/ppermute | solution.py:47
  13.6 4.1 %collective-permute-start.8 = (bf16[512,128]{1,0:T(8,128)(2,1)S(1)}, bf16[512,128]{1,0:T(8,128)(2,1)S(1)}, u32[]{:S(2)}, u32[]{:S(2)}) collective-permute-start(bf16[512,128]{1,0:T(8,128)(2,1)S(1)} %dynamic-slice_bitcast_fusion), channel_id=1, source_target_pairs={{0,24},{2,26},{4,28},{6,30},{8,16},{10,18},{12,20},{14,22},{16,8},... | collective-permute-start | bytes 393224 | tf_op jit(solution)/shard_map/ppermute | solution.py:47
  18.5 1.2 collective-permute-done.3.refs_5_
  19.8 2.3 %collective-permute-done.8.refs_11_ = bf16[512,128]{1,0:T(8,128)(2,1)S(1)} collective-permute-done((bf16[512,128]{1,0:T(8,128)(2,1)S(1)}, bf16[512,128]{1,0:T(8,128)(2,1)S(1)}, u32[]{:S(2)}, u32[]{:S(2)}) %collective-permute-start.8) | collective-permute-done | bytes 131104 | tf_op jit(solution)/shard_map/ppermute | solution.py:47
  22.1 6.4 %collective-permute-done.6.refs_9_ = bf16[512,128]{1,0:T(8,128)(2,1)S(1)} collective-permute-done((bf16[512,128]{1,0:T(8,128)(2,1)S(1)}, bf16[512,128]{1,0:T(8,128)(2,1)S(1)}, u32[]{:S(2)}, u32[]{:S(2)}) %collective-permute-start.6) | collective-permute-done | bytes 131104 | tf_op jit(solution)/shard_map/ppermute | solution.py:47
  31.0 3.4 %shard_map.111 = (bf16[256,128]{1,0:T(8,128)(2,1)S(1)}, bf16[256,128]{1,0:T(8,128)(2,1)S(1)}, bf16[256,128]{1,0:T(8,128)(2,1)S(1)}, bf16[256,128]{1,0:T(8,128)(2,1)S(1)}) custom-call(s32[3]{0:T(128)S(1)} %pad_add_fusion.pos_ref, s32[1,128]{1,0:T(1,128)S(1)} %pad_bitcast_fusion.refs_0_, s32[1,128]{1,0:T(1,128)S(1)} %collective-permute-done.refs_1_, ...), custom_call_target="tpu_custom_call" | custom-call | tf_op jit(solution)/shard_map/pallas_call | solution.py:337
  34.4 1.6 collective-permute-start.10
  35.9 1.5 collective-permute-start.11
  40.2 2.4 %collective-permute-done.12.refs_3_ = bf16[256,128]{1,0:T(8,128)(2,1)S(1)} collective-permute-done((bf16[256,128]{1,0:T(8,128)(2,1)S(1)}, bf16[256,128]{1,0:T(8,128)(2,1)S(1)}, u32[]{:S(2)}, u32[]{:S(2)}) %collective-permute-start.12) | collective-permute-done | bytes 65568 | tf_op jit(solution)/shard_map/ppermute | solution.py:47
  45.2 6.6 %shard_map.112 = (bf16[256,512]{1,0:T(8,128)(2,1)}, bf16[256,128]{1,0:T(8,128)(2,1)S(1)}, bf16[256,128]{1,0:T(8,128)(2,1)S(1)}, bf16[256,128]{1,0:T(8,128)(2,1)S...) custom-call(s32[3]{0:T(128)S(1)} %pad_add_fusion.pos_ref, ...), custom_call_target="tpu_custom_call" | custom-call | tf_op jit(solution)/shard_map/pallas_call | solution.py:348
  52.4 1.4 collective-permute-done.22
  55.1 1.1 pad_maximum_fusion
  56.5 76.7 %reduce-scatter.2.cloned.1.call-done = bf16[16,2560]{1,0:T(8,128)(2,1)} async-done(((bf16[256,2560]{1,0:T(8,128)(2,1)}), bf16[16,2560]{1,0:T(8,128)(2,1)}) %reduce-scatter.2.cloned.1.call-update) | async-done | bytes 81936 | tf_op jit(solution)/shard_map/reduce_scatter | solution.py:391
  133.3 3.4 %collective-permute-start.17 = (bf16[256,128]{1,0:T(8,128)(2,1)S(1)}, bf16[256,128]{1,0:T(8,128)(2,1)S(1)}, u32[]{:S(2)}, u32[]{:S(2)}) collective-permute-start(bf16[256,128]{1,0:T(8,128)(2,1)S(1)} %get-tuple-element.27), channel_id=1, source_target_pairs={{0,6},{2,4},{4,2},{6,0},{8,14},{10,12},{12,10},{14,8},{16,22},{18,... | collective-permute-start | bytes 196616 | tf_op jit(solution)/shard_map/ppermute | solution.py:47
  137.6 1.4 collective-permute-done.17.refs_9_
  138.9 2.9 %shard_map.113 = (bf16[4,512,128]{2,1,0:T(8,128)(2,1)S(1)}, bf16[4,512,128]{2,1,0:T(8,128)(2,1)S(1)}) custom-call(s32[3]{0:T(128)S(1)} %pad_add_fusion.pos_ref, s32[1,128]{1,0:T(1,128)S(1)} %pad_bitcast_fusion.refs_0_, s32[1,128]{1,0:T(1,128)S(1)} %collective-permute-done.refs_1_, s32[1,128]{1,0:T(1,128)S(1)} %collective-permute-done.1.refs_2_, ...), custom_call_target="tpu_custom_call" | custom-call | tf_op jit(solution)/shard_map/pallas_call | solution.py:393
  141.9 1.9 collective-permute-done.18
  144.1 1.4 collective-permute-start.21
  145.5 2.1 %collective-permute-start.20 = (bf16[512,128]{1,0:T(8,128)(2,1)S(1)}, bf16[512,128]{1,0:T(8,128)(2,1)S(1)}, u32[]{:S(2)}, u32[]{:S(2)}) collective-permute-start(bf16[512,128]{1,0:T(8,128)(2,1)S(1)} %get-tuple-element.36), channel_id=1, source_target_pairs={{0,16},{2,18},{4,20},{6,22},{8,24},{10,26},{12,28},{14,30},{16,0},... | collective-permute-start | bytes 393224 | tf_op jit(solution)/shard_map/ppermute | solution.py:47
  147.6 5.7 %collective-permute-done.19 = bf16[512,128]{1,0:T(8,128)(2,1)S(1)} collective-permute-done((bf16[512,128]{1,0:T(8,128)(2,1)S(1)}, bf16[512,128]{1,0:T(8,128)(2,1)S(1)}, u32[]{:S(2)}, u32[]{:S(2)}) %collective-permute-start.19) | collective-permute-done | bytes 131104 | tf_op jit(solution)/shard_map/ppermute | solution.py:47
  153.6 6.6 %collective-permute-done.20 = bf16[512,128]{1,0:T(8,128)(2,1)S(1)} collective-permute-done((bf16[512,128]{1,0:T(8,128)(2,1)S(1)}, bf16[512,128]{1,0:T(8,128)(2,1)S(1)}, u32[]{:S(2)}, u32[]{:S(2)}) %collective-permute-start.20) | collective-permute-done | bytes 131104 | tf_op jit(solution)/shard_map/ppermute | solution.py:47
  161.0 33.8 %all-gather.2.cloned.1.call-done = bf16[256,2560]{1,0:T(8,128)(2,1)} async-done(((bf16[16,2560]{1,0:T(8,128)(2,1)}), bf16[256,2560]{1,0:T(8,128)(2,1)}) %all-gather.2.cloned.1.call-update) | async-done | bytes 1310736 | tf_op jit(solution)/shard_map/all_gather | solution.py:392
  194.8 1.8 convert_multiply_fusion.1
  196.6 2.8 %convert_multiply_fusion = f32[256,2048]{1,0:T(8,128)} fusion(bf16[256,2560]{1,0:T(8,128)(2,1)} %all-gather.2.cloned.1.call-done), kind=kLoop, calls=%fused_computation | loop fusion | flops 1048576 | bytes 3145728 | tf_op jit(solution)/shard_map/mul | solution.py:408
  (61 shorter events, 16.2 us)
Async XLA Ops:
  7.2 125.9 %reduce-scatter.2.cloned.1.call-start = ((), (), s32[]{:S(2)}) async-start(), calls=%async_computation.1 | async-start | bytes 1392640 | tf_op jit(solution)/shard_map/reduce_scatter | solution.py:391
  7.2 35.4 %collective-permute-start.13 = (bf16[256,2048]{1,0:T(8,128)(2,1)}, bf16[256,2048]{1,0:T(8,128)(2,1)S(1)}, u32[]{:S(2)}, u32[]{:S(2)}) collective-permute-start(bf16[256,2048]{1,0:T(8,128)(2,1)} %refs_4_.1), channel_id=1, source_target_pairs={{0,1},{1,0},{2,3},{3,2},{4,5},{5,4},{6,7},{7,6},{8,9},{9,8},{10,11... | collective-permute-start | bytes 3145736 | tf_op jit(solution)/shard_map/ppermute | solution.py:39
  8.5 9.2 %collective-permute-start.2 = (s32[1,128]{1,0:T(1,128)S(1)}, s32[1,128]{1,0:T(1,128)S(1)}, u32[]{:S(2)}, u32[]{:S(2)}) collective-permute-start(s32[1,128]{1,0:T(1,128)S(1)} %pad_bitcast_fusion.refs_0_), channel_id=1, source_target_pairs={{0,6},{2,4},{4,2},{6,0},{8,14},{10,12},{12,10},{14,8},{16,22},{18,... | collective-permute-start | bytes 1544 | tf_op jit(solution)/shard_map/ppermute | solution.py:47
  12.1 5.6 %collective-permute-start.1 = (s32[1,128]{1,0:T(1,128)S(1)}, s32[1,128]{1,0:T(1,128)S(1)}, u32[]{:S(2)}, u32[]{:S(2)}) collective-permute-start(s32[1,128]{1,0:T(1,128)S(1)} %pad_bitcast_fusion.refs_0_), channel_id=1, source_target_pairs={{0,4},{2,6},{4,0},{6,2},{8,12},{10,14},{12,8},{14,10},{16,20},{18,... | collective-permute-start | bytes 1544 | tf_op jit(solution)/shard_map/ppermute | solution.py:47
  12.6 5.8 %collective-permute-start = (s32[1,128]{1,0:T(1,128)S(1)}, s32[1,128]{1,0:T(1,128)S(1)}, u32[]{:S(2)}, u32[]{:S(2)}) collective-permute-start(s32[1,128]{1,0:T(1,128)S(1)} %pad_bitcast_fusion.refs_0_), channel_id=1, source_target_pairs={{0,2},{2,0},{4,6},{6,4},{8,10},{10,8},{12,14},{14,12},{16,18},{18,... | collective-permute-start | bytes 1544 | tf_op jit(solution)/shard_map/ppermute | solution.py:47
  13.6 8.5 %collective-permute-start.8 = (bf16[512,128]{1,0:T(8,128)(2,1)S(1)}, bf16[512,128]{1,0:T(8,128)(2,1)S(1)}, u32[]{:S(2)}, u32[]{:S(2)}) collective-permute-start(bf16[512,128]{1,0:T(8,128)(2,1)S(1)} %dynamic-slice_bitcast_fusion), channel_id=1, source_target_pairs={{0,24},{2,26},{4,28},{6,30},{8,16},{10,18},{12,20},{14,22},{16,8},... | collective-permute-start | bytes 393224 | tf_op jit(solution)/shard_map/ppermute | solution.py:47
  17.7 10.8 %collective-permute-start.6 = (bf16[512,128]{1,0:T(8,128)(2,1)S(1)}, bf16[512,128]{1,0:T(8,128)(2,1)S(1)}, u32[]{:S(2)}, u32[]{:S(2)}) collective-permute-start(bf16[512,128]{1,0:T(8,128)(2,1)S(1)} %dynamic-slice_bitcast_fusion), channel_id=1, source_target_pairs={{0,16},{2,18},{4,20},{6,22},{8,24},{10,26},{12,28},{14,30},{16,0},... | collective-permute-start | bytes 393224 | tf_op jit(solution)/shard_map/ppermute | solution.py:47
  17.7 10.8 %collective-permute-start.4 = (bf16[512,128]{1,0:T(8,128)(2,1)S(1)}, bf16[512,128]{1,0:T(8,128)(2,1)S(1)}, u32[]{:S(2)}, u32[]{:S(2)}) collective-permute-start(bf16[512,128]{1,0:T(8,128)(2,1)S(1)} %dynamic-slice_bitcast_fusion), channel_id=1, source_target_pairs={{0,8},{2,10},{4,12},{6,14},{8,0},{10,2},{12,4},{14,6},{16,24},{18,... | collective-permute-start | bytes 393224 | tf_op jit(solution)/shard_map/ppermute | solution.py:47
  19.7 19.8 %collective-permute-start.14 = (bf16[256,512]{1,0:T(8,128)(2,1)}, bf16[256,512]{1,0:T(8,128)(2,1)S(1)}, u32[]{:S(2)}, u32[]{:S(2)}) collective-permute-start(bf16[256,512]{1,0:T(8,128)(2,1)} %refs_6_.1), channel_id=1, source_target_pairs={{0,1},{1,0},{2,3},{3,2},{4,5},{5,4},{6,7},{7,6},{8,9},{9,8},{10,11... | collective-permute-start | bytes 786440 | tf_op jit(solution)/shard_map/ppermute | solution.py:39
  22.1 7.0 %collective-permute-start.9 = (bf16[512,128]{1,0:T(8,128)(2,1)S(1)}, bf16[512,128]{1,0:T(8,128)(2,1)S(1)}, u32[]{:S(2)}, u32[]{:S(2)}) collective-permute-start(bf16[512,128]{1,0:T(8,128)(2,1)S(1)} %collective-permute-done.8.refs_11_), channel_id=1, source_target_pairs={{0,1},{1,0},{2,3},{3,2},{4,5},{5,4},{6,7},{7,6},{8,9},{9,8},{10,11... | collective-permute-start | bytes 393224 | tf_op jit(solution)/shard_map/ppermute | solution.py:39
  28.5 1.5 collective-permute-start.5
  34.4 5.0 %collective-permute-start.10 = (bf16[256,128]{1,0:T(8,128)(2,1)S(1)}, bf16[256,128]{1,0:T(8,128)(2,1)S(1)}, u32[]{:S(2)}, u32[]{:S(2)}) collective-permute-start(bf16[256,128]{1,0:T(8,128)(2,1)S(1)} %get-tuple-element.20), channel_id=1, source_target_pairs={{0,2},{2,0},{4,6},{6,4},{8,10},{10,8},{12,14},{14,12},{16,18},{18,... | collective-permute-start | bytes 196616 | tf_op jit(solution)/shard_map/ppermute | solution.py:47
  35.9 4.3 %collective-permute-start.11 = (bf16[256,128]{1,0:T(8,128)(2,1)S(1)}, bf16[256,128]{1,0:T(8,128)(2,1)S(1)}, u32[]{:S(2)}, u32[]{:S(2)}) collective-permute-start(bf16[256,128]{1,0:T(8,128)(2,1)S(1)} %get-tuple-element.21), channel_id=1, source_target_pairs={{0,4},{2,6},{4,0},{6,2},{8,12},{10,14},{12,8},{14,10},{16,20},{18,... | collective-permute-start | bytes 196616 | tf_op jit(solution)/shard_map/ppermute | solution.py:47
  37.5 5.2 %collective-permute-start.12 = (bf16[256,128]{1,0:T(8,128)(2,1)S(1)}, bf16[256,128]{1,0:T(8,128)(2,1)S(1)}, u32[]{:S(2)}, u32[]{:S(2)}) collective-permute-start(bf16[256,128]{1,0:T(8,128)(2,1)S(1)} %get-tuple-element.22), channel_id=1, source_target_pairs={{0,6},{2,4},{4,2},{6,0},{8,14},{10,12},{12,10},{14,8},{16,22},{18,... | collective-permute-start | bytes 196616 | tf_op jit(solution)/shard_map/ppermute | solution.py:47
  51.8 2.0 collective-permute-start.22
  51.9 3.0 %collective-permute-start.23 = (bf16[256,1536]{1,0:T(8,128)(2,1)S(1)}, bf16[256,1536]{1,0:T(8,128)(2,1)S(1)}, u32[]{:S(2)}, u32[]{:S(2)}) collective-permute-start(bf16[256,1536]{1,0:T(8,128)(2,1)S(1)} %get-tuple-element.33), channel_id=1, source_target_pairs={{0,1},{1,0},{2,3},{3,2},{4,5},{5,4},{6,7},{7,6},{8,9},{9,8},{10,11... | collective-permute-start | bytes 2359304 | tf_op jit(solution)/shard_map/ppermute | solution.py:39
  56.2 138.6 %all-gather.2.cloned.1.call-start = ((), (), s32[]{:S(2)}) async-start(), calls=%async_computation.2 | async-start | bytes 1392640 | tf_op jit(solution)/shard_map/all_gather | solution.py:392
  133.2 4.3 %collective-permute-start.15 = (bf16[256,128]{1,0:T(8,128)(2,1)S(1)}, bf16[256,128]{1,0:T(8,128)(2,1)S(1)}, u32[]{:S(2)}, u32[]{:S(2)}) collective-permute-start(bf16[256,128]{1,0:T(8,128)(2,1)S(1)} %get-tuple-element.25), channel_id=1, source_target_pairs={{0,2},{2,0},{4,6},{6,4},{8,10},{10,8},{12,14},{14,12},{16,18},{18,... | collective-permute-start | bytes 196616 | tf_op jit(solution)/shard_map/ppermute | solution.py:47
  133.2 4.3 %collective-permute-start.16 = (bf16[256,128]{1,0:T(8,128)(2,1)S(1)}, bf16[256,128]{1,0:T(8,128)(2,1)S(1)}, u32[]{:S(2)}, u32[]{:S(2)}) collective-permute-start(bf16[256,128]{1,0:T(8,128)(2,1)S(1)} %get-tuple-element.26), channel_id=1, source_target_pairs={{0,4},{2,6},{4,0},{6,2},{8,12},{10,14},{12,8},{14,10},{16,20},{18,... | collective-permute-start | bytes 196616 | tf_op jit(solution)/shard_map/ppermute | solution.py:47
  133.3 5.6 %collective-permute-start.17 = (bf16[256,128]{1,0:T(8,128)(2,1)S(1)}, bf16[256,128]{1,0:T(8,128)(2,1)S(1)}, u32[]{:S(2)}, u32[]{:S(2)}) collective-permute-start(bf16[256,128]{1,0:T(8,128)(2,1)S(1)} %get-tuple-element.27), channel_id=1, source_target_pairs={{0,6},{2,4},{4,2},{6,0},{8,14},{10,12},{12,10},{14,8},{16,22},{18,... | collective-permute-start | bytes 196616 | tf_op jit(solution)/shard_map/ppermute | solution.py:47
  141.9 2.0 collective-permute-start.18
  144.0 9.2 %collective-permute-start.19 = (bf16[512,128]{1,0:T(8,128)(2,1)S(1)}, bf16[512,128]{1,0:T(8,128)(2,1)S(1)}, u32[]{:S(2)}, u32[]{:S(2)}) collective-permute-start(bf16[512,128]{1,0:T(8,128)(2,1)S(1)} %get-tuple-element.34), channel_id=1, source_target_pairs={{0,8},{2,10},{4,12},{6,14},{8,0},{10,2},{12,4},{14,6},{16,24},{18,... | collective-permute-start | bytes 393224 | tf_op jit(solution)/shard_map/ppermute | solution.py:47
  144.1 9.5 %collective-permute-start.21 = (bf16[512,128]{1,0:T(8,128)(2,1)S(1)}, bf16[512,128]{1,0:T(8,128)(2,1)S(1)}, u32[]{:S(2)}, u32[]{:S(2)}) collective-permute-start(bf16[512,128]{1,0:T(8,128)(2,1)S(1)} %get-tuple-element.35), channel_id=1, source_target_pairs={{0,24},{2,26},{4,28},{6,30},{8,16},{10,18},{12,20},{14,22},{16,8},... | collective-permute-start | bytes 393224 | tf_op jit(solution)/shard_map/ppermute | solution.py:47
  145.5 14.8 %collective-permute-start.20 = (bf16[512,128]{1,0:T(8,128)(2,1)S(1)}, bf16[512,128]{1,0:T(8,128)(2,1)S(1)}, u32[]{:S(2)}, u32[]{:S(2)}) collective-permute-start(bf16[512,128]{1,0:T(8,128)(2,1)S(1)} %get-tuple-element.36), channel_id=1, source_target_pairs={{0,16},{2,18},{4,20},{6,22},{8,24},{10,26},{12,28},{14,30},{16,0},... | collective-permute-start | bytes 393224 | tf_op jit(solution)/shard_map/ppermute | solution.py:47
  (8 other events, 52.8 us)
Sparse Core Ops, SparseCore 0:
  56.4 76.7 reduce-scatter.1
  135.9 58.8 all-gather.1

commit v4 on v3

--- a/solution.py
+++ b/solution.py
@@ -47,24 +47,41 @@
     return lax.ppermute(value, "emb", [(i, i ^ step) for i in range(count)])
 
 
-def pick_ids(pos_ref, moves_refs, ids_refs, slots, tables):
-    bal = pos_ref[0]
-    bals = len(ids_refs)
+class Scalars:
+    def __init__(self, ref, bals, slots):
+        self.ref, self.bals, self.slots = ref, bals, slots
+
+    def surplus(self, bal):
+        return self.ref[0, bal]
+
+    def source(self, bal):
+        found = jnp.int32(0)
+        for index in range(self.bals):
+            found = found + jnp.where(self.ref[0, self.bals + index] == bal, index, 0)
+        return found
+
+    def length(self, bal, slot):
+        return self.ref[0, 2 * self.bals + bal * self.slots + slot]
+
+    def place(self):
+        first = self.bals * (2 + self.slots)
+        return self.ref[0, first], self.ref[0, first + 1], self.ref[0, first + 2]
+
+
+def pick_ids(scalars, ids_refs, slots, tables):
+    bal, group_here, _ = scalars[0].place()
     found = []
-    for step, moves_ref in enumerate(moves_refs):
-        group = pos_ref[1] ^ step
-        source = jnp.int32(0)
-        for index in range(bals):
-            source = source + jnp.where(moves_ref[0, bals + index] == bal, index, 0)
-        my_slot = moves_ref[0, bal]
-        from_slot = moves_ref[0, source]
-        turn_of = source ^ bal
+    for step, there in enumerate(scalars):
+        group = group_here ^ step
+        my_slot = there.surplus(bal)
+        source = there.source(bal)
+        from_slot = there.surplus(source)
         by_slot = [[] for _ in range(slots)]
         for table in tables:
             arrived = ids_refs[0][table, group * slots + from_slot]
-            for turn in range(1, bals):
+            for turn in range(1, len(ids_refs)):
                 other = ids_refs[turn][table, group * slots + from_slot]
-                arrived = jnp.where(turn_of == turn, other, arrived)
+                arrived = jnp.where(source ^ bal == turn, other, arrived)
             for slot in range(slots):
                 own = ids_refs[0][table, group * slots + slot]
                 by_slot[slot].append(jnp.where(my_slot == slot, arrived, own))
@@ -76,20 +93,32 @@
     return [table_here ^ step for step in range(tables)]
 
 
-def lookup_kernel(groups, slots, tables, bals, pos_ref, *refs):
+def stage_kernel(*refs):
+    count = len(refs) // 2
+    copies = [
+        pltpu.make_async_copy(refs[index], refs[count + index], refs[-1].at[index])
+        for index in range(count)
+    ]
+    for copy in copies:
+        copy.start()
+    for copy in copies:
+        copy.wait()
+
+
+def lookup_kernel(groups, slots, tables, bals, *refs):
     refs = list(refs)
     take = lambda count: [refs.pop(0) for _ in range(count)]
-    moves_refs, ids_refs = take(groups), take(bals)
+    scalars = [Scalars(ref, bals, slots) for ref in take(groups)]
+    ids_refs = take(bals)
     (own_ref,) = take(1)
     others = [take(bals) for _ in range(1, tables)]
     out_refs = refs
-    bal = pos_ref[0]
-    table_here = pos_ref[2]
+    bal, _, table_here = scalars[0].place()
     distinct, columns = own_ref.shape
     part = distinct // bals
     slot_rows = ids_refs[0].shape[3]
     lane = lax.broadcasted_iota(jnp.int32, (LANES, LANES), 1)
-    ids = pick_ids(pos_ref, moves_refs, ids_refs, slots, table_order(table_here, tables))
+    ids = pick_ids(scalars, ids_refs, slots, table_order(table_here, tables))
     for group in range(groups):
         for slot in range(slots):
             for first in range(0, slot_rows, LANES):
@@ -118,17 +147,17 @@
                 out_refs[group][at : at + LANES, :] = total.astype(bf16)
 
 
-def scatter_kernel(groups, slots, bals, pos_ref, *refs):
+def scatter_kernel(groups, slots, bals, *refs):
     refs = list(refs)
     take = lambda count: [refs.pop(0) for _ in range(count)]
-    moves_refs, ids_refs, grad_refs, out_refs = take(groups), take(bals), take(groups), refs
-    bal = pos_ref[0]
-    table_here = pos_ref[2]
+    scalars = [Scalars(ref, bals, slots) for ref in take(groups)]
+    ids_refs, grad_refs, out_refs = take(bals), take(groups), refs
+    bal, _, table_here = scalars[0].place()
     tables, part, _ = out_refs[0].shape
     slot_rows = ids_refs[0].shape[3]
     height = min(part, 256)
     iota = lax.broadcasted_iota(jnp.int32, (height, slot_rows), 0)
-    ids = pick_ids(pos_ref, moves_refs, ids_refs, slots, table_order(table_here, tables))
+    ids = pick_ids(scalars, ids_refs, slots, table_order(table_here, tables))
     grads = jnp.concatenate([ref[...] for ref in grad_refs], axis=0)
     for table in range(tables):
         for turn in range(bals):
@@ -158,7 +187,7 @@
     return inverse * (incoming - first - normed * second)
 
 
-def layer_kernel(groups, bals, pos_ref, seq_ref, surplus_ref, helper_ref, *refs):
+def layer_kernel(groups, slots, tables, bals, unit, scalar_ref, *refs):
     refs = list(refs)
     take = lambda count: [refs.pop(0) for _ in range(count)]
     block_refs = take(groups)
@@ -167,19 +196,18 @@
     (cot_ref,) = take(1)
     (layer_ref,) = take(1)
     grad_refs = take(groups)
-    early_refs = take(bals)
-    late_refs = take(bals)
+    far_refs = take(bals)
+    near_refs = take(bals)
     (x_ref, w_in, w_out, cot_here, nt_ref, mt_ref, weights_ref, slope_ref, gate_ref, heads_ref, dsilu_ref, grads_ref, sems) = refs
 
-    bal = pos_ref[0]
+    scalars = Scalars(scalar_ref, bals, slots)
+    bal, group_here, table_here = scalars.place()
     rows, width = cot_here.shape
-    slots = seq_ref.shape[1]
     slot_rows = rows // slots
     head_width = width // HEADS
     score_scale = head_width**-0.5
     piece = block_refs[0].shape[1]
-    group_here = pos_ref[1]
-    part = in_refs[0].shape[0]
+    part, features = in_refs[0].shape
 
     in_copies, out_copies = [], []
     for turn in range(bals):
@@ -190,12 +218,10 @@
     for copy in in_copies + out_copies + [cot_copy]:
         copy.start()
 
-    source = jnp.int32(0)
-    for index in range(bals):
-        source = source + jnp.where(helper_ref[index, 0] == bal, index, 0)
-    my_slot = surplus_ref[bal, 0]
-    moved = seq_ref[source, surplus_ref[source, 0]]
-    lengths = [jnp.where(my_slot == slot, moved, seq_ref[bal, slot]) for slot in range(slots)]
+    my_slot = scalars.surplus(bal)
+    source = scalars.source(bal)
+    moved = scalars.length(source, scalars.surplus(source))
+    lengths = [jnp.where(my_slot == slot, moved, scalars.length(bal, slot)) for slot in range(slots)]
 
     for step in range(groups):
         x_ref[group_here ^ step] = block_refs[step][...]
@@ -257,10 +283,24 @@
     grad_attended = norm_back(grad_mixed * gate, normed_out, out_inverse).astype(bf16)
     grads_ref[:, :width] = (grad_mixed * normed_out * dsilu_ref[:, :width]).astype(bf16)
 
+    def owner_order(ref, turn, far):
+        start = (bal ^ turn) * part
+        if part != groups * tables * unit:
+            half = part // 2
+            at = pl.multiple_of(start + (0 if far else half), half)
+            return ref[pl.ds(at, half), :]
+        steps = range(tables // 2, tables) if far else range(tables // 2)
+        found = []
+        for group_step in range(groups):
+            for table_step in steps:
+                owner = (group_here ^ group_step) * tables + (table_here ^ table_step)
+                at = pl.multiple_of(start + owner * unit, unit)
+                found.append(ref[pl.ds(at, unit), :])
+        return jnp.concatenate(found, axis=0)
+
     for turn in range(bals):
-        at = pl.ds(pl.multiple_of((bal ^ turn) * part, part), part)
-        early_refs[turn][:, :width] = matmul(mt_ref[at, :], cot).astype(bf16)
-        early_refs[turn][:, width:] = matmul(nt_ref[at, :], grads_ref[:, :width]).astype(bf16)
+        for far, out in ((True, far_refs[turn]), (False, near_refs[turn])):
+            out[:, features:] = matmul(owner_order(mt_ref, turn, far), cot).astype(bf16)
 
     for slot in range(slots):
         here = slice(slot * slot_rows, (slot + 1) * slot_rows)
@@ -279,8 +319,8 @@
                 grads_ref[here, at] = (found * dsilu_ref[here, at]).astype(bf16)
 
     for turn in range(bals):
-        at = pl.ds(pl.multiple_of((bal ^ turn) * part, part), part)
-        late_refs[turn][...] = matmul(nt_ref[at, :], grads_ref[:, width:]).astype(bf16)
+        for far, out in ((True, far_refs[turn]), (False, near_refs[turn])):
+            out[:, :features] = matmul(owner_order(nt_ref, turn, far), grads_ref[...]).astype(bf16)
 
     grad_normed = matmul_nt(grads_ref[...], w_in[...])
     grad_rows = (cot.astype(f32) + norm_back(grad_normed, normed_in, in_inverse)).astype(bf16)
@@ -290,11 +330,46 @@
         grad_refs[step][...] = x_ref[group_here ^ step]
 
 
+def place_kernel(scale, groups, slots, tables, bals, unit, scalar_ref, *refs):
+    pieces = refs[: 2 * groups]
+    in_ref, out_ref, scaled_ref, sems = refs[2 * groups :]
+    _, group_here, table_here = Scalars(scalar_ref, bals, slots).place()
+    features = in_ref.shape[1]
+    half = tables // 2
+    copies = []
+    for index, piece in enumerate(pieces):
+        far, group_step = divmod(index, groups)
+        for inner in range(half):
+            table_step = far * half + inner
+            at = (index * half + inner) * unit
+            scaled_ref[at : at + unit, :] = piece[inner * unit : (inner + 1) * unit, :].astype(f32) * scale
+            owner = (group_here ^ group_step) * tables + (table_here ^ table_step)
+            to = pl.ds(pl.multiple_of(owner * unit, unit), unit)
+            rows = scaled_ref.at[pl.ds(at, unit), :]
+            sem = sems.at[index * half + inner]
+            copies.append(
+                pltpu.make_async_copy(rows.at[:, pl.ds(0, features)], in_ref.at[to, :], sem.at[0])
+            )
+            copies.append(
+                pltpu.make_async_copy(
+                    rows.at[:, pl.ds(features, out_ref.shape[1])], out_ref.at[to, :], sem.at[1]
+                )
+            )
+            copies[-2].start()
+            copies[-1].start()
+    for copy in copies:
+        copy.wait()
+
+
 def sum_rounded(terms):
     total = terms[0].astype(f32)
     for term in terms[1:]:
         total = total + term.astype(f32)
     return total.astype(bf16)
+
+
+def after(value, *others):
+    return lax.optimization_barrier((value,) + others)[0]
 
 
 def on_device(
@@ -310,48 +385,62 @@
     slots = seq_lengths.shape[2]
     slot_rows = rows // slots
     distinct, columns = embed_tables.shape[1:]
-    features = weight_in.shape[1]
     part = distinct // bals
     weight_part = weight_in.shape[0]
     table_here = emb // groups
     group_here = emb % groups
-    pos = jnp.stack([bal, group_here, table_here]).astype(jnp.int32)
+    width, features = weight_out.shape[1], weight_in.shape[1]
+    unit = weight_part // embs
+    owned = unit % 16 == 0 and tables % 2 == 0
+    unit = unit if owned else 0
     params = pltpu.CompilerParams(vmem_limit_bytes=ROOM)
-
+    place = jnp.stack([bal, group_here, table_here]).astype(jnp.int32)
+    scalars = jnp.concatenate(
+        [surplus_slot[:, 0], helper_map[:, 0], seq_lengths[:, 0, :].reshape(-1), place]
+    )
+    scalars = jnp.pad(scalars, (0, LANES - scalars.shape[0]))[None]
 
     share = lax.dynamic_slice_in_dim(embed_tables[0], bal * part, part, 0)
     fetched = [emb_swap(share, step * groups, embs) for step in range(1, tables)]
-    pieces = [embed_tables[0]] + [piece for one in fetched for piece in with_swapped(one, bals)]
 
     ids = lax.dynamic_slice_in_dim(
-        jnp.transpose(item_ids[0]), table_here * groups * rows, groups * rows, 1
+        jnp.transpose(after(item_ids[0], share)), table_here * groups * rows, groups * rows, 1
     )
     plane_ids = with_swapped(ids.reshape(tables, groups * slots, 1, slot_rows), bals)
-    moves = jnp.concatenate([surplus_slot[:, 0], helper_map[:, 0]])
-    moves = jnp.pad(moves, (0, LANES - 2 * bals))[None]
-    plane_moves = [moves] + [emb_swap(moves, step, embs) for step in range(1, groups)]
+    sent = after(scalars, fetched[0])
+    plane_scalars = [scalars] + [emb_swap(sent, step, embs) for step in range(1, groups)]
 
     all_in = with_swapped(weight_in, bals)
     all_out = with_swapped(weight_out, bals)
+    to_stage = [embed_tables[0], weight_in, weight_out, cotangent[0]]
+    own_table, own_in, own_out, cot = pl.pallas_call(
+        stage_kernel,
+        out_shape=[jax.ShapeDtypeStruct(value.shape, value.dtype) for value in to_stage],
+        in_specs=[HBM] * len(to_stage),
+        out_specs=[VMEM] * len(to_stage),
+        scratch_shapes=[pltpu.SemaphoreType.DMA((len(to_stage),))],
+        compiler_params=params,
+    )(*to_stage)
+    fetched[-1] = after(fetched[-1], own_table)
+    pieces = [own_table] + [piece for one in fetched for piece in with_swapped(one, bals)]
 
     found = pl.pallas_call(
         functools.partial(lookup_kernel, groups, slots, tables, bals),
         out_shape=[jax.ShapeDtypeStruct((rows, columns), bf16)] * groups,
-        in_specs=[SMEM] * (1 + groups) + [VMEM] * (bals + len(pieces)),
+        in_specs=[SMEM] * groups + [VMEM] * (bals + len(pieces)),
         out_specs=[VMEM] * groups,
         compiler_params=params,
-    )(pos, *plane_moves, *plane_ids, *pieces)
+    )(*plane_scalars, *plane_ids, *pieces)
     block = [found[0]] + [emb_swap(found[step], step, embs) for step in range(1, groups)]
 
     pairs = slots * HEADS // 2
-    early, late = 2 * width, features - width
+    terms = jax.ShapeDtypeStruct((weight_part // 2, features + width), bf16)
     results = pl.pallas_call(
-        functools.partial(layer_kernel, groups, bals),
+        functools.partial(layer_kernel, groups, slots, tables, bals, unit),
         out_shape=[jax.ShapeDtypeStruct((rows, width), bf16)]
         + [jax.ShapeDtypeStruct((rows, columns), bf16)] * groups
-        + [jax.ShapeDtypeStruct((weight_part, early), bf16)] * bals
-        + [jax.ShapeDtypeStruct((weight_part, late), bf16)] * bals,
-        in_specs=[SMEM] * 4 + [VMEM] * groups + [HBM] * (2 * bals + 1),
+        + [terms] * (2 * bals),
+        in_specs=[SMEM] + [VMEM] * groups + [HBM] * (2 * bals + 1),
         out_specs=[VMEM] * (1 + groups + 2 * bals),
         scratch_shapes=[
             pltpu.VMEM((groups, rows, columns), bf16),
@@ -369,43 +458,71 @@
             pltpu.SemaphoreType.DMA((2 * bals + 1,)),
         ],
         compiler_params=params,
-    )(
-        pos,
-        seq_lengths[:, 0, :],
-        surplus_slot,
-        helper_map,
-        *block,
-        *all_in,
-        *all_out,
-        cotangent[0],
-    )
+    )(scalars, *block, own_in, *all_in[1:], own_out, *all_out[1:], cot)
     layer_out, results = results[0], results[1:]
     grads, results = results[:groups], results[groups:]
-    early_parts, late_parts = results[:bals], results[bals:]
+    far_terms, near_terms = results[:bals], results[bals:]
 
     def over_cores(parts):
-        return sum_rounded([parts[0]] + [bal_swap(parts[turn], turn, bals) for turn in range(1, bals)])
+        return [parts[0]] + [bal_swap(parts[turn], turn, bals) for turn in range(1, bals)]
+
+    def over_plane(value, *others):
+        pieces = value.reshape(groups, value.shape[0] // groups, value.shape[1])
+        came = [emb_swap(pieces[step], step, embs) for step in range(1, groups)]
+        return sum_rounded([pieces[0]] + [after(piece, *others) for piece in came])
+
+    def to_plane(value):
+        return [value] + [emb_swap(value, step, embs) for step in range(1, groups)]
+
+    far_terms = over_cores(far_terms)
+    near_terms = over_cores([near_terms[0]] + [after(term, far_terms[-1]) for term in near_terms[1:]])
+    far, near = sum_rounded(far_terms), sum_rounded(near_terms)
+    grad_scale = (rows * embs * bals) ** -0.5
+    if owned:
+        half = tables // 2
+        far, near = over_plane(far, near), over_plane(near)
+        grads = [grads[0]] + [after(grad, far) for grad in grads[1:]]
+        rel = [near[at * unit : (at + 1) * unit] for at in range(half)]
+        rel += [far[at * unit : (at + 1) * unit] for at in range(half)]
+        final = sum_rounded(
+            [rel[0]] + [emb_swap(rel[step], step * groups, embs) for step in range(1, tables)]
+        )
+        gathered = [final] + [emb_swap(final, step * groups, embs) for step in range(1, tables)]
+        ready = gathered[half - 1]
+        back = to_plane(jnp.concatenate(gathered[:half], axis=0))
+        back += to_plane(jnp.concatenate(gathered[half:], axis=0))
+        total_in, total_out = pl.pallas_call(
+            functools.partial(place_kernel, grad_scale, groups, slots, tables, bals, unit),
+            out_shape=[
+                jax.ShapeDtypeStruct((weight_part, features), f32),
+                jax.ShapeDtypeStruct((weight_part, width), f32),
+            ],
+            in_specs=[SMEM] + [VMEM] * (2 * groups),
+            out_specs=[HBM] * 2,
+            scratch_shapes=[
+                pltpu.VMEM((weight_part, features + width), f32),
+                pltpu.SemaphoreType.DMA((groups * tables, 2)),
+            ],
+            compiler_params=params,
+        )(scalars, *back)
+    else:
+        total = lax.psum(jnp.concatenate([far, near], axis=0).astype(f32), "emb") * grad_scale
+        total_in, total_out = total[:, :features], total[:, features:]
+        ready = far
 
     plane_grads = [grads[0]] + [emb_swap(grads[step], step, embs) for step in range(1, groups)]
-    weight_sum = jnp.concatenate([over_cores(early_parts), over_cores(late_parts)], axis=1)
-    owned = lax.psum_scatter(weight_sum, "emb", scatter_dimension=0, tiled=True)
-    total = lax.all_gather(owned, "emb", axis=0, tiled=True)
     sums = pl.pallas_call(
         functools.partial(scatter_kernel, groups, slots, bals),
         out_shape=[jax.ShapeDtypeStruct((tables, part, columns), bf16)] * bals,
-        in_specs=[SMEM] * (1 + groups) + [VMEM] * (bals + groups),
+        in_specs=[SMEM] * groups + [VMEM] * (bals + groups),
         out_specs=[VMEM] * bals,
         compiler_params=params,
-    )(pos, *plane_moves, *plane_ids, *plane_grads)
-    own_sums = over_cores(sums)
+    )(*plane_scalars, *plane_ids, *plane_grads)
+    own_sums = after(sum_rounded(over_cores(sums)), ready)
     table_sum = own_sums[0].astype(f32)
     for step in range(1, tables):
         table_sum = table_sum + emb_swap(own_sums[step], step * groups, embs).astype(f32)
     table_scale = (distinct / (bals * item_ids.shape[1])) ** 0.5
-
-    grad_scale = (rows * embs * bals) ** -0.5
-    total_out = total[:, :width].astype(f32) * grad_scale
-    total_in = total[:, width:].astype(f32) * grad_scale
     return layer_out[None], (table_sum * table_scale)[None], total_in, total_out
 
 

time: 207 us -> 117 us (0.57)
  waiting for transfers between devices: 144 us -> 47.3 us
  starting transfers between devices: 21.7 us -> 43.4 us
  between operations: 14.2 us -> 0.89 us
  other arithmetic: 7.86 us -> 2.79 us
  Pallas kernels: 12.9 us -> 15.3 us
    reduce_scatter x1 -> x0, waiting for transfers between devices: 76.7 us -> none  [on_device(): owned = lax.psum_scatter(weight_sum, 'emb', scatter_dimension=0, tiled=True)]
    all_gather x1 -> x0, waiting for transfers between devices: 33.8 us -> none  [on_device(): total = lax.all_gather(owned, 'emb', axis=0, tiled=True)]
    ppermute x15 -> x33, starting transfers between devices: 19.6 us -> 41.3 us  [emb_swap(): return lax.ppermute(value, 'emb', [(i, i ^ step) for i in range(count)])]
    ppermute x15 -> x33, waiting for transfers between devices: 26.8 us -> 44 us  [emb_swap(): return lax.ppermute(value, 'emb', [(i, i ^ step) for i in range(count)])]
    mul x2 -> x0, other arithmetic: 4.61 us -> none  [the longest x1 2.8 us: on_device(): total_in = total[:, width:].astype(f32) * grad_scale]
    ppermute x9, waiting for transfers between devices: 6.34 us -> 3.36 us  [bal_swap(): return lax.ppermute(value, 'bal', [(i, i ^ step) for i in range(count)])]
    pallas_call x1 -> x3, Pallas kernels: 6.56 us -> 9.14 us  [the longest x1 6.68 us: on_device(): pl.pallas_call(functools.partial(layer_kernel, groups, slots, tables, bal...]
    unnamed x14 -> x12, local copies, waits for them, and re-layouts: 5.02 us -> 4.6 us
  transfers between devices with their start and end apart: 26 -> 42, of which waited for: 18 -> 25; matrix products, arithmetic and copies ran while one was open for 2% -> 4% of each run, Pallas kernels for 3% -> 7%
where the time goes in v4:
time: 117 us; the launch traced here: 116 us
  waiting for transfers between devices  47.3 us (40%)
  starting transfers between devices  43.4 us (37%)
  Pallas kernels  15.3 us (13%)
  local copies, waits for them, and re-layouts  6.51 us (6%)
  other arithmetic  2.79 us (2%)
    ppermute x33, waiting for transfers between devices, emb_swap(): return lax.ppermute(value, 'emb', [(i, i ^ step) for i in range(count)])  44 us
    ppermute x33, starting transfers between devices, emb_swap(): return lax.ppermute(value, 'emb', [(i, i ^ step) for i in range(count)])  41.3 us
    pallas_call x1, Pallas kernels, on_device(): pl.pallas_call(functools.partial(layer_kernel, groups, slots, tables, bal...  6.68 us
    unnamed x12, local copies, waits for them, and re-layouts  4.6 us
    ppermute x9, waiting for transfers between devices, bal_swap(): return lax.ppermute(value, 'bal', [(i, i ^ step) for i in range(count)])  3.36 us
    pallas_call x1, Pallas kernels, on_device(): pl.pallas_call(functools.partial(lookup_kernel, groups, slots, tables, ba...  3.3 us
    pallas_call x1, Pallas kernels, on_device(): pl.pallas_call(functools.partial(scatter_kernel, groups, slots, bals), ou...  2.89 us
  transfers between devices with their start and end apart: 42, of which 25 were waited for; matrix products, arithmetic and copies ran while one was open for 4% of the time, Pallas kernels for 7%

profile of v4, /device:TPU:0, one launch (start us, length us, event | category | flops | bytes accessed | tf_op | source)
XLA Modules:
  0.0 116.2 jit_solution(15070449078688352449)
XLA Ops:
  2.1 2.7 %collective-permute-start = (bf16[512,128]{1,0:T(8,128)(2,1)S(1)}, bf16[512,128]{1,0:T(8,128)(2,1)S(1)}, u32[]{:S(2)}, u32[]{:S(2)}) collective-permute-start(bf16[512,128]{1,0:T(8,128)(2,1)S(1)} %dynamic-slice_bitcast_fusion), channel_id=1, source_target_pairs={{0,8},{2,10},{4,12},{6,14},{8,0},{10,2},{12,4},{14,6},{16,24},{18,... | collective-permute-start | bytes 393224 | tf_op jit(solution)/shard_map/ppermute | solution.py:47
  4.7 2.5 %collective-permute-start.8 = (bf16[512,128]{1,0:T(8,128)(2,1)S(1)}, bf16[512,128]{1,0:T(8,128)(2,1)S(1)}, u32[]{:S(2)}, u32[]{:S(2)}) collective-permute-start(bf16[512,128]{1,0:T(8,128)(2,1)S(1)} %dynamic-slice_bitcast_fusion), channel_id=1, source_target_pairs={{0,24},{2,26},{4,28},{6,30},{8,16},{10,18},{12,20},{14,22},{16,8},... | collective-permute-start | bytes 393224 | tf_op jit(solution)/shard_map/ppermute | solution.py:47
  10.7 2.4 %collective-permute-start.3 = (s32[1,128]{1,0:T(1,128)S(1)}, s32[1,128]{1,0:T(1,128)S(1)}, u32[]{:S(2)}, u32[]{:S(2)}) collective-permute-start(s32[1,128]{1,0:T(1,128)S(1)} %pad_bitcast_fusion.refs_0_.scalar_ref), channel_id=1, source_target_pairs={{0,6},{2,4},{4,2},{6,0},{8,14},{10,12},{12,10},{14,8},{16,22},{18,... | collective-permute-start | bytes 1544 | tf_op jit(solution)/shard_map/ppermute | solution.py:47
  15.9 3.7 %collective-permute-done.6.refs_9_ = bf16[512,128]{1,0:T(8,128)(2,1)S(1)} collective-permute-done((bf16[512,128]{1,0:T(8,128)(2,1)S(1)}, bf16[512,128]{1,0:T(8,128)(2,1)S(1)}, u32[]{:S(2)}, u32[]{:S(2)}) %collective-permute-start.6) | collective-permute-done | bytes 131104 | tf_op jit(solution)/shard_map/ppermute | solution.py:47
  27.3 3.3 %shard_map.112 = (bf16[256,128]{1,0:T(8,128)(2,1)S(1)}, bf16[256,128]{1,0:T(8,128)(2,1)S(1)}, bf16[256,128]{1,0:T(8,128)(2,1)S(1)}, bf16[256,128]{1,0:T(8,128)(2,1)S(1)}) custom-call(s32[1,128]{1,0:T(1,128)S(1)} %pad_bitcast_fusion.refs_0_.scalar_ref, s32[1,128]{1,0:T(1,128)S(1)} %collective-permute-done.1.refs_1_, ...), custom_call_target="tpu_custom_call" | custom-call | tf_op jit(solution)/shard_map/pallas_call | solution.py:427
  35.5 2.4 %collective-permute-done.12.refs_3_ = bf16[256,128]{1,0:T(8,128)(2,1)S(1)} collective-permute-done((bf16[256,128]{1,0:T(8,128)(2,1)S(1)}, bf16[256,128]{1,0:T(8,128)(2,1)S(1)}, u32[]{:S(2)}, u32[]{:S(2)}) %collective-permute-start.12) | collective-permute-done | bytes 65568 | tf_op jit(solution)/shard_map/ppermute | solution.py:47
  37.9 6.7 %shard_map.113 = (bf16[256,512]{1,0:T(8,128)(2,1)}, bf16[256,128]{1,0:T(8,128)(2,1)S(1)}, bf16[256,128]{1,0:T(8,128)(2,1)S(1)}, bf16[256,128]{1,0:T(8,128)(2,1)S...) custom-call(s32[1,128]{1,0:T(1,128)S(1)} %pad_bitcast_fusion.refs_0_, ...), custom_call_target="tpu_custom_call" | custom-call | tf_op jit(solution)/shard_map/pallas_call | solution.py:438
  44.7 2.1 %collective-permute-done.15 = bf16[128,2560]{1,0:T(8,128)(2,1)S(1)} collective-permute-done((bf16[128,2560]{1,0:T(8,128)(2,1)S(1)}, bf16[128,2560]{1,0:T(8,128)(2,1)S(1)}, u32[]{:S(2)}, u32[]{:S(2)}) %collective-permute-start.15) | collective-permute-done | bytes 655392 | tf_op jit(solution)/shard_map/ppermute | solution.py:39
  47.1 1.6 %collective-permute-start.16 = (bf16[32,2560]{1,0:T(8,128)(2,1)S(1)}, bf16[32,2560]{1,0:T(8,128)(2,1)S(1)}, u32[]{:S(2)}, u32[]{:S(2)}) collective-permute-start(bf16[32,2560]{1,0:T(8,128)(2,1)S(1)} %get-tuple-element.71), channel_id=1, source_target_pairs={{0,2},{2,0},{4,6},{6,4},{8,10},{10,8},{12,14},{14,12},{16,18},{18,... | collective-permute-start | bytes 491528 | tf_op jit(solution)/shard_map/ppermute | solution.py:47
  50.9 6.3 %collective-permute-done.19 = bf16[32,2560]{1,0:T(8,128)(2,1)S(1)} collective-permute-done((bf16[32,2560]{1,0:T(8,128)(2,1)S(1)}, bf16[32,2560]{1,0:T(8,128)(2,1)S(1)}, u32[]{:S(2)}, u32[]{:S(2)}) %collective-permute-start.19) | collective-permute-done | bytes 163872 | tf_op jit(solution)/shard_map/ppermute | solution.py:47
  63.4 1.5 %collective-permute-start.29 = (bf16[16,2560]{1,0:T(8,128)(2,1)S(1)}, bf16[16,2560]{1,0:T(8,128)(2,1)S(1)}, u32[]{:S(2)}, u32[]{:S(2)}) collective-permute-start(bf16[16,2560]{1,0:T(8,128)(2,1)S(1)} %get-tuple-element.78), channel_id=1, source_target_pairs={{0,24},{2,26},{4,28},{6,30},{8,16},{10,18},{12,20},{14,22},{16,8},... | collective-permute-start | bytes 245768 | tf_op jit(solution)/shard_map/ppermute | solution.py:47
  65.5 2.6 %collective-permute-done.26 = bf16[32,2560]{1,0:T(8,128)(2,1)S(1)} collective-permute-done((bf16[32,2560]{1,0:T(8,128)(2,1)S(1)}, bf16[32,2560]{1,0:T(8,128)(2,1)S(1)}, u32[]{:S(2)}, u32[]{:S(2)}) %collective-permute-start.26) | collective-permute-done | bytes 163872 | tf_op jit(solution)/shard_map/ppermute | solution.py:47
  69.9 4.2 %collective-permute-done.27 = bf16[16,2560]{1,0:T(8,128)(2,1)S(1)} collective-permute-done((bf16[16,2560]{1,0:T(8,128)(2,1)S(1)}, bf16[16,2560]{1,0:T(8,128)(2,1)S(1)}, u32[]{:S(2)}, u32[]{:S(2)}) %collective-permute-start.27) | collective-permute-done | bytes 81952 | tf_op jit(solution)/shard_map/ppermute | solution.py:47
  74.3 1.6 %collective-permute-start.20 = (bf16[256,128]{1,0:T(8,128)(2,1)S(1)}, bf16[256,128]{1,0:T(8,128)(2,1)S(1)}, u32[]{:S(2)}, u32[]{:S(2)}) collective-permute-start(bf16[256,128]{1,0:T(8,128)(2,1)S(1)} %get-tuple-element.58), channel_id=1, source_target_pairs={{0,2},{2,0},{4,6},{6,4},{8,10},{10,8},{12,14},{14,12},{16,18},{18,... | collective-permute-start | bytes 196616 | tf_op jit(solution)/shard_map/ppermute | solution.py:47
  81.5 2.9 %shard_map.114 = (bf16[4,512,128]{2,1,0:T(8,128)(2,1)S(1)}, bf16[4,512,128]{2,1,0:T(8,128)(2,1)S(1)}) custom-call(s32[1,128]{1,0:T(1,128)S(1)} %pad_bitcast_fusion.refs_0_.scalar_ref, s32[1,128]{1,0:T(1,128)S(1)} %collective-permute-done.1.refs_1_, s32[1,128]{1,0:T(1,128)S(1)} %collective-permute-done.2.refs_2_, ...), custom_call_target="tpu_custom_call" | custom-call | tf_op jit(solution)/shard_map/pallas_call | solution.py:514
  84.5 2.7 %collective-permute-start.38 = (bf16[16,2560]{1,0:T(8,128)(2,1)S(1)}, bf16[16,2560]{1,0:T(8,128)(2,1)S(1)}, u32[]{:S(2)}, u32[]{:S(2)}) collective-permute-start(bf16[16,2560]{1,0:T(8,128)(2,1)S(1)} %add_convert_fusion.5), channel_id=1, source_target_pairs={{0,24},{2,26},{4,28},{6,30},{8,16},{10,18},{12,20},{14,22},{16,8},... | collective-permute-start | bytes 245768 | tf_op jit(solution)/shard_map/ppermute | solution.py:47
  88.0 1.6 %collective-permute-start.36 = (bf16[32,2560]{1,0:T(8,128)(2,1)S(1)}, bf16[32,2560]{1,0:T(8,128)(2,1)S(1)}, u32[]{:S(2)}, u32[]{:S(2)}) collective-permute-start(bf16[32,2560]{1,0:T(8,128)(2,1)S(1)} %pad_maximum_fusion.refs_0_), channel_id=1, source_target_pairs={{0,6},{2,4},{4,2},{6,0},{8,14},{10,12},{12,10},{14,8},{16,22},{18,... | collective-permute-start | bytes 491528 | tf_op jit(solution)/shard_map/ppermute | solution.py:47
  90.5 5.5 %collective-permute-done.37 = bf16[16,2560]{1,0:T(8,128)(2,1)S(1)} collective-permute-done((bf16[16,2560]{1,0:T(8,128)(2,1)S(1)}, bf16[16,2560]{1,0:T(8,128)(2,1)S(1)}, u32[]{:S(2)}, u32[]{:S(2)}) %collective-permute-start.37) | collective-permute-done | bytes 81952 | tf_op jit(solution)/shard_map/ppermute | solution.py:47
  97.2 1.9 %collective-permute-start.41 = (bf16[32,2560]{1,0:T(8,128)(2,1)S(1)}, bf16[32,2560]{1,0:T(8,128)(2,1)S(1)}, u32[]{:S(2)}, u32[]{:S(2)}) collective-permute-start(bf16[32,2560]{1,0:T(8,128)(2,1)S(1)} %constant_dynamic-update-slice_fusion.refs_4_), channel_id=1, source_target_pairs={{0,6},{2,4},{4,2},{6,0},{8,14},{10,12},{12,10},{14,8},{16,22},{18,... | collective-permute-start | bytes 491528 | tf_op jit(solution)/shard_map/ppermute | solution.py:47
  101.1 2.0 %collective-permute-done.34.refs_1_ = bf16[32,2560]{1,0:T(8,128)(2,1)S(1)} collective-permute-done((bf16[32,2560]{1,0:T(8,128)(2,1)S(1)}, bf16[32,2560]{1,0:T(8,128)(2,1)S(1)}, u32[]{:S(2)}, u32[]{:S(2)}) %collective-permute-start.34) | collective-permute-done | bytes 163872 | tf_op jit(solution)/shard_map/ppermute | solution.py:47
  103.1 2.6 %collective-permute-start.33 = (bf16[512,128]{1,0:T(8,128)(2,1)S(1)}, bf16[512,128]{1,0:T(8,128)(2,1)S(1)}, u32[]{:S(2)}, u32[]{:S(2)}) collective-permute-start(bf16[512,128]{1,0:T(8,128)(2,1)S(1)} %get-tuple-element.75), channel_id=1, source_target_pairs={{0,24},{2,26},{4,28},{6,30},{8,16},{10,18},{12,20},{14,22},{16,8},... | collective-permute-start | bytes 393224 | tf_op jit(solution)/shard_map/ppermute | solution.py:47
  105.7 1.8 %collective-permute-done.41.refs_7_ = bf16[32,2560]{1,0:T(8,128)(2,1)S(1)} collective-permute-done((bf16[32,2560]{1,0:T(8,128)(2,1)S(1)}, bf16[32,2560]{1,0:T(8,128)(2,1)S(1)}, u32[]{:S(2)}, u32[]{:S(2)}) %collective-permute-start.41) | collective-permute-done | bytes 163872 | tf_op jit(solution)/shard_map/ppermute | solution.py:47
  108.8 2.3 %shard_map.115 = (f32[256,2048]{1,0:T(8,128)}, f32[256,512]{1,0:T(8,128)}) custom-call(s32[1,128]{1,0:T(1,128)S(1)} %pad_bitcast_fusion.refs_0_.scalar_ref, bf16[32,2560]{1,0:T(8,128)(2,1)S(1)} %pad_maximum_fusion.refs_0_, bf16[32,2560]{1,0:T(8,128)(2,1)S(1)} %collective-permute-done.34.refs_1_, bf16[32,2560]{1,0:T(8,128)(2,1)S(1)} %collective-permute-done.35.refs_2_, ...), custom_call_target="tpu_custom_call" | custom-call | tf_op jit(solution)/shard_map/pallas_call | solution.py:494
  111.3 4.2 %collective-permute-done.32 = bf16[512,128]{1,0:T(8,128)(2,1)S(1)} collective-permute-done((bf16[512,128]{1,0:T(8,128)(2,1)S(1)}, bf16[512,128]{1,0:T(8,128)(2,1)S(1)}, u32[]{:S(2)}, u32[]{:S(2)}) %collective-permute-start.32) | collective-permute-done | bytes 131104 | tf_op jit(solution)/shard_map/ppermute | solution.py:47
  (98 shorter events, 44.4 us)
Async XLA Ops:
  0.6 37.3 %collective-permute-start.13 = (bf16[256,2048]{1,0:T(8,128)(2,1)}, bf16[256,2048]{1,0:T(8,128)(2,1)S(1)}, u32[]{:S(2)}, u32[]{:S(2)}) collective-permute-start(bf16[256,2048]{1,0:T(8,128)(2,1)} %refs_1_.1), channel_id=1, source_target_pairs={{0,1},{1,0},{2,3},{3,2},{4,5},{5,4},{6,7},{7,6},{8,9},{9,8},{10,11... | collective-permute-start | bytes 3145736 | tf_op jit(solution)/shard_map/ppermute | solution.py:39
  2.1 8.1 %collective-permute-start = (bf16[512,128]{1,0:T(8,128)(2,1)S(1)}, bf16[512,128]{1,0:T(8,128)(2,1)S(1)}, u32[]{:S(2)}, u32[]{:S(2)}) collective-permute-start(bf16[512,128]{1,0:T(8,128)(2,1)S(1)} %dynamic-slice_bitcast_fusion), channel_id=1, source_target_pairs={{0,8},{2,10},{4,12},{6,14},{8,0},{10,2},{12,4},{14,6},{16,24},{18,... | collective-permute-start | bytes 393224 | tf_op jit(solution)/shard_map/ppermute | solution.py:47
  4.7 9.7 %collective-permute-start.8 = (bf16[512,128]{1,0:T(8,128)(2,1)S(1)}, bf16[512,128]{1,0:T(8,128)(2,1)S(1)}, u32[]{:S(2)}, u32[]{:S(2)}) collective-permute-start(bf16[512,128]{1,0:T(8,128)(2,1)S(1)} %dynamic-slice_bitcast_fusion), channel_id=1, source_target_pairs={{0,24},{2,26},{4,28},{6,30},{8,16},{10,18},{12,20},{14,22},{16,8},... | collective-permute-start | bytes 393224 | tf_op jit(solution)/shard_map/ppermute | solution.py:47
  7.2 12.4 %collective-permute-start.6 = (bf16[512,128]{1,0:T(8,128)(2,1)S(1)}, bf16[512,128]{1,0:T(8,128)(2,1)S(1)}, u32[]{:S(2)}, u32[]{:S(2)}) collective-permute-start(bf16[512,128]{1,0:T(8,128)(2,1)S(1)} %dynamic-slice_bitcast_fusion), channel_id=1, source_target_pairs={{0,16},{2,18},{4,20},{6,22},{8,24},{10,26},{12,28},{14,30},{16,0},... | collective-permute-start | bytes 393224 | tf_op jit(solution)/shard_map/ppermute | solution.py:47
  10.2 24.0 %collective-permute-start.14 = (bf16[256,512]{1,0:T(8,128)(2,1)}, bf16[256,512]{1,0:T(8,128)(2,1)S(1)}, u32[]{:S(2)}, u32[]{:S(2)}) collective-permute-start(bf16[256,512]{1,0:T(8,128)(2,1)} %refs_2_.1), channel_id=1, source_target_pairs={{0,1},{1,0},{2,3},{3,2},{4,5},{5,4},{6,7},{7,6},{8,9},{9,8},{10,11... | collective-permute-start | bytes 786440 | tf_op jit(solution)/shard_map/ppermute | solution.py:39
  10.7 14.7 %collective-permute-start.3 = (s32[1,128]{1,0:T(1,128)S(1)}, s32[1,128]{1,0:T(1,128)S(1)}, u32[]{:S(2)}, u32[]{:S(2)}) collective-permute-start(s32[1,128]{1,0:T(1,128)S(1)} %pad_bitcast_fusion.refs_0_.scalar_ref), channel_id=1, source_target_pairs={{0,6},{2,4},{4,2},{6,0},{8,14},{10,12},{12,10},{14,8},{16,22},{18,... | collective-permute-start | bytes 1544 | tf_op jit(solution)/shard_map/ppermute | solution.py:47
  14.4 11.1 %collective-permute-start.2 = (s32[1,128]{1,0:T(1,128)S(1)}, s32[1,128]{1,0:T(1,128)S(1)}, u32[]{:S(2)}, u32[]{:S(2)}) collective-permute-start(s32[1,128]{1,0:T(1,128)S(1)} %pad_bitcast_fusion.refs_0_.scalar_ref), channel_id=1, source_target_pairs={{0,4},{2,6},{4,0},{6,2},{8,12},{10,14},{12,8},{14,10},{16,20},{18,... | collective-permute-start | bytes 1544 | tf_op jit(solution)/shard_map/ppermute | solution.py:47
  47.1 11.5 %collective-permute-start.16 = (bf16[32,2560]{1,0:T(8,128)(2,1)S(1)}, bf16[32,2560]{1,0:T(8,128)(2,1)S(1)}, u32[]{:S(2)}, u32[]{:S(2)}) collective-permute-start(bf16[32,2560]{1,0:T(8,128)(2,1)S(1)} %get-tuple-element.71), channel_id=1, source_target_pairs={{0,2},{2,0},{4,6},{6,4},{8,10},{10,8},{12,14},{14,12},{16,18},{18,... | collective-permute-start | bytes 491528 | tf_op jit(solution)/shard_map/ppermute | solution.py:47
  48.7 8.5 %collective-permute-start.19 = (bf16[32,2560]{1,0:T(8,128)(2,1)S(1)}, bf16[32,2560]{1,0:T(8,128)(2,1)S(1)}, u32[]{:S(2)}, u32[]{:S(2)}) collective-permute-start(bf16[32,2560]{1,0:T(8,128)(2,1)S(1)} %get-tuple-element.72), channel_id=1, source_target_pairs={{0,6},{2,4},{4,2},{6,0},{8,14},{10,12},{12,10},{14,8},{16,22},{18,... | collective-permute-start | bytes 491528 | tf_op jit(solution)/shard_map/ppermute | solution.py:47
  49.1 9.4 %collective-permute-start.18 = (bf16[32,2560]{1,0:T(8,128)(2,1)S(1)}, bf16[32,2560]{1,0:T(8,128)(2,1)S(1)}, u32[]{:S(2)}, u32[]{:S(2)}) collective-permute-start(bf16[32,2560]{1,0:T(8,128)(2,1)S(1)} %get-tuple-element.73), channel_id=1, source_target_pairs={{0,4},{2,6},{4,0},{6,2},{8,12},{10,14},{12,8},{14,10},{16,20},{18,... | collective-permute-start | bytes 491528 | tf_op jit(solution)/shard_map/ppermute | solution.py:47
  60.1 8.1 %collective-permute-start.26 = (bf16[32,2560]{1,0:T(8,128)(2,1)S(1)}, bf16[32,2560]{1,0:T(8,128)(2,1)S(1)}, u32[]{:S(2)}, u32[]{:S(2)}) collective-permute-start(bf16[32,2560]{1,0:T(8,128)(2,1)S(1)} %get-tuple-element.69), channel_id=1, source_target_pairs={{0,6},{2,4},{4,2},{6,0},{8,14},{10,12},{12,10},{14,8},{16,22},{18,... | collective-permute-start | bytes 491528 | tf_op jit(solution)/shard_map/ppermute | solution.py:47
  61.5 8.0 %collective-permute-start.25 = (bf16[32,2560]{1,0:T(8,128)(2,1)S(1)}, bf16[32,2560]{1,0:T(8,128)(2,1)S(1)}, u32[]{:S(2)}, u32[]{:S(2)}) collective-permute-start(bf16[32,2560]{1,0:T(8,128)(2,1)S(1)} %get-tuple-element.70), channel_id=1, source_target_pairs={{0,4},{2,6},{4,0},{6,2},{8,12},{10,14},{12,8},{14,10},{16,20},{18,... | collective-permute-start | bytes 491528 | tf_op jit(solution)/shard_map/ppermute | solution.py:47
  74.2 13.8 %collective-permute-start.30 = (bf16[16,2560]{1,0:T(8,128)(2,1)S(1)}, bf16[16,2560]{1,0:T(8,128)(2,1)S(1)}, u32[]{:S(2)}, u32[]{:S(2)}) collective-permute-start(bf16[16,2560]{1,0:T(8,128)(2,1)S(1)} %add_convert_fusion.5), channel_id=1, source_target_pairs={{0,8},{2,10},{4,12},{6,14},{8,0},{10,2},{12,4},{14,6},{16,24},{18,... | collective-permute-start | bytes 245768 | tf_op jit(solution)/shard_map/ppermute | solution.py:47
  84.4 14.7 %collective-permute-start.23 = (bf16[4,512,128]{2,1,0:T(8,128)(2,1)S(1)}, bf16[4,512,128]{2,1,0:T(8,128)(2,1)S(1)}, u32[]{:S(2)}, u32[]{:S(2)}) collective-permute-start(bf16[4,512,128]{2,1,0:T(8,128)(2,1)S(1)} %get-tuple-element.64), channel_id=1, source_target_pairs={{0,1},{1,0},{2,3},{3,2},{4,5},{5,4},{6,7},{7,6},{8,9},{9,8},{10,11... | collective-permute-start | bytes 1572872 | tf_op jit(solution)/shard_map/ppermute | solution.py:39
  84.5 12.7 %collective-permute-start.38 = (bf16[16,2560]{1,0:T(8,128)(2,1)S(1)}, bf16[16,2560]{1,0:T(8,128)(2,1)S(1)}, u32[]{:S(2)}, u32[]{:S(2)}) collective-permute-start(bf16[16,2560]{1,0:T(8,128)(2,1)S(1)} %add_convert_fusion.5), channel_id=1, source_target_pairs={{0,24},{2,26},{4,28},{6,30},{8,16},{10,18},{12,20},{14,22},{16,8},... | collective-permute-start | bytes 245768 | tf_op jit(solution)/shard_map/ppermute | solution.py:47
  87.2 8.8 %collective-permute-start.37 = (bf16[16,2560]{1,0:T(8,128)(2,1)S(1)}, bf16[16,2560]{1,0:T(8,128)(2,1)S(1)}, u32[]{:S(2)}, u32[]{:S(2)}) collective-permute-start(bf16[16,2560]{1,0:T(8,128)(2,1)S(1)} %add_convert_fusion.5), channel_id=1, source_target_pairs={{0,16},{2,18},{4,20},{6,22},{8,24},{10,26},{12,28},{14,30},{16,0},... | collective-permute-start | bytes 245768 | tf_op jit(solution)/shard_map/ppermute | solution.py:47
  88.0 11.8 %collective-permute-start.36 = (bf16[32,2560]{1,0:T(8,128)(2,1)S(1)}, bf16[32,2560]{1,0:T(8,128)(2,1)S(1)}, u32[]{:S(2)}, u32[]{:S(2)}) collective-permute-start(bf16[32,2560]{1,0:T(8,128)(2,1)S(1)} %pad_maximum_fusion.refs_0_), channel_id=1, source_target_pairs={{0,6},{2,4},{4,2},{6,0},{8,14},{10,12},{12,10},{14,8},{16,22},{18,... | collective-permute-start | bytes 491528 | tf_op jit(solution)/shard_map/ppermute | solution.py:47
  89.5 11.5 %collective-permute-start.35 = (bf16[32,2560]{1,0:T(8,128)(2,1)S(1)}, bf16[32,2560]{1,0:T(8,128)(2,1)S(1)}, u32[]{:S(2)}, u32[]{:S(2)}) collective-permute-start(bf16[32,2560]{1,0:T(8,128)(2,1)S(1)} %pad_maximum_fusion.refs_0_), channel_id=1, source_target_pairs={{0,4},{2,6},{4,0},{6,2},{8,12},{10,14},{12,8},{14,10},{16,20},{18,... | collective-permute-start | bytes 491528 | tf_op jit(solution)/shard_map/ppermute | solution.py:47
  97.2 10.4 %collective-permute-start.41 = (bf16[32,2560]{1,0:T(8,128)(2,1)S(1)}, bf16[32,2560]{1,0:T(8,128)(2,1)S(1)}, u32[]{:S(2)}, u32[]{:S(2)}) collective-permute-start(bf16[32,2560]{1,0:T(8,128)(2,1)S(1)} %constant_dynamic-update-slice_fusion.refs_4_), channel_id=1, source_target_pairs={{0,6},{2,4},{4,2},{6,0},{8,14},{10,12},{12,10},{14,8},{16,22},{18,... | collective-permute-start | bytes 491528 | tf_op jit(solution)/shard_map/ppermute | solution.py:47
  99.1 8.7 %collective-permute-start.40 = (bf16[32,2560]{1,0:T(8,128)(2,1)S(1)}, bf16[32,2560]{1,0:T(8,128)(2,1)S(1)}, u32[]{:S(2)}, u32[]{:S(2)}) collective-permute-start(bf16[32,2560]{1,0:T(8,128)(2,1)S(1)} %constant_dynamic-update-slice_fusion.refs_4_), channel_id=1, source_target_pairs={{0,4},{2,6},{4,0},{6,2},{8,12},{10,14},{12,8},{14,10},{16,20},{18,... | collective-permute-start | bytes 491528 | tf_op jit(solution)/shard_map/ppermute | solution.py:47
  99.7 9.1 %collective-permute-start.39 = (bf16[32,2560]{1,0:T(8,128)(2,1)S(1)}, bf16[32,2560]{1,0:T(8,128)(2,1)S(1)}, u32[]{:S(2)}, u32[]{:S(2)}) collective-permute-start(bf16[32,2560]{1,0:T(8,128)(2,1)S(1)} %constant_dynamic-update-slice_fusion.refs_4_), channel_id=1, source_target_pairs={{0,2},{2,0},{4,6},{6,4},{8,10},{10,8},{12,14},{14,12},{16,18},{18,... | collective-permute-start | bytes 491528 | tf_op jit(solution)/shard_map/ppermute | solution.py:47
  101.0 10.1 %collective-permute-start.31 = (bf16[512,128]{1,0:T(8,128)(2,1)S(1)}, bf16[512,128]{1,0:T(8,128)(2,1)S(1)}, u32[]{:S(2)}, u32[]{:S(2)}) collective-permute-start(bf16[512,128]{1,0:T(8,128)(2,1)S(1)} %get-tuple-element.74), channel_id=1, source_target_pairs={{0,8},{2,10},{4,12},{6,14},{8,0},{10,2},{12,4},{14,6},{16,24},{18,... | collective-permute-start | bytes 393224 | tf_op jit(solution)/shard_map/ppermute | solution.py:47
  103.1 8.2 %collective-permute-start.33 = (bf16[512,128]{1,0:T(8,128)(2,1)S(1)}, bf16[512,128]{1,0:T(8,128)(2,1)S(1)}, u32[]{:S(2)}, u32[]{:S(2)}) collective-permute-start(bf16[512,128]{1,0:T(8,128)(2,1)S(1)} %get-tuple-element.75), channel_id=1, source_target_pairs={{0,24},{2,26},{4,28},{6,30},{8,16},{10,18},{12,20},{14,22},{16,8},... | collective-permute-start | bytes 393224 | tf_op jit(solution)/shard_map/ppermute | solution.py:47
  107.6 7.9 %collective-permute-start.32 = (bf16[512,128]{1,0:T(8,128)(2,1)S(1)}, bf16[512,128]{1,0:T(8,128)(2,1)S(1)}, u32[]{:S(2)}, u32[]{:S(2)}) collective-permute-start(bf16[512,128]{1,0:T(8,128)(2,1)S(1)} %get-tuple-element.76), channel_id=1, source_target_pairs={{0,16},{2,18},{4,20},{6,22},{8,24},{10,26},{12,28},{14,30},{16,0},... | collective-permute-start | bytes 393224 | tf_op jit(solution)/shard_map/ppermute | solution.py:47
  (23 other events, 91.5 us)

commit v5 on v4

--- a/solution.py
+++ b/solution.py
@@ -10,13 +10,20 @@
 HEADS = 8
 EPS = 1e-05
 LANES = 128
-ROOM = 48 * 1024 * 1024
 
 VMEM = pl.BlockSpec(memory_space=pltpu.VMEM)
 SMEM = pl.BlockSpec(memory_space=pltpu.SMEM)
 HBM = pl.BlockSpec(memory_space=pltpu.HBM)
 f32 = jnp.float32
 bf16 = jnp.bfloat16
+
+
+def room(mib):
+    return pltpu.CompilerParams(vmem_limit_bytes=mib * 1024 * 1024)
+
+
+def estimate(microseconds):
+    return pl.CostEstimate(flops=0, bytes_accessed=microseconds * 3_500_000, transcendentals=0)
 
 
 def matmul(left, right):
@@ -91,18 +98,6 @@
 
 def table_order(table_here, tables):
     return [table_here ^ step for step in range(tables)]
-
-
-def stage_kernel(*refs):
-    count = len(refs) // 2
-    copies = [
-        pltpu.make_async_copy(refs[index], refs[count + index], refs[-1].at[index])
-        for index in range(count)
-    ]
-    for copy in copies:
-        copy.start()
-    for copy in copies:
-        copy.wait()
 
 
 def lookup_kernel(groups, slots, tables, bals, *refs):
@@ -196,8 +191,7 @@
     (cot_ref,) = take(1)
     (layer_ref,) = take(1)
     grad_refs = take(groups)
-    far_refs = take(bals)
-    near_refs = take(bals)
+    term_refs = take(bals)
     (x_ref, w_in, w_out, cot_here, nt_ref, mt_ref, weights_ref, slope_ref, gate_ref, heads_ref, dsilu_ref, grads_ref, sems) = refs
 
     scalars = Scalars(scalar_ref, bals, slots)
@@ -283,24 +277,20 @@
     grad_attended = norm_back(grad_mixed * gate, normed_out, out_inverse).astype(bf16)
     grads_ref[:, :width] = (grad_mixed * normed_out * dsilu_ref[:, :width]).astype(bf16)
 
-    def owner_order(ref, turn, far):
+    def owner_order(ref, turn):
         start = (bal ^ turn) * part
         if part != groups * tables * unit:
-            half = part // 2
-            at = pl.multiple_of(start + (0 if far else half), half)
-            return ref[pl.ds(at, half), :]
-        steps = range(tables // 2, tables) if far else range(tables // 2)
+            return ref[pl.ds(pl.multiple_of(start, part), part), :]
         found = []
         for group_step in range(groups):
-            for table_step in steps:
+            for table_step in range(tables):
                 owner = (group_here ^ group_step) * tables + (table_here ^ table_step)
                 at = pl.multiple_of(start + owner * unit, unit)
                 found.append(ref[pl.ds(at, unit), :])
         return jnp.concatenate(found, axis=0)
 
     for turn in range(bals):
-        for far, out in ((True, far_refs[turn]), (False, near_refs[turn])):
-            out[:, features:] = matmul(owner_order(mt_ref, turn, far), cot).astype(bf16)
+        term_refs[turn][:, features:] = matmul(owner_order(mt_ref, turn), cot).astype(bf16)
 
     for slot in range(slots):
         here = slice(slot * slot_rows, (slot + 1) * slot_rows)
@@ -319,8 +309,7 @@
                 grads_ref[here, at] = (found * dsilu_ref[here, at]).astype(bf16)
 
     for turn in range(bals):
-        for far, out in ((True, far_refs[turn]), (False, near_refs[turn])):
-            out[:, :features] = matmul(owner_order(nt_ref, turn, far), grads_ref[...]).astype(bf16)
+        term_refs[turn][:, :features] = matmul(owner_order(nt_ref, turn), grads_ref[...]).astype(bf16)
 
     grad_normed = matmul_nt(grads_ref[...], w_in[...])
     grad_rows = (cot.astype(f32) + norm_back(grad_normed, normed_in, in_inverse)).astype(bf16)
@@ -331,22 +320,21 @@
 
 
 def place_kernel(scale, groups, slots, tables, bals, unit, scalar_ref, *refs):
-    pieces = refs[: 2 * groups]
-    in_ref, out_ref, scaled_ref, sems = refs[2 * groups :]
+    pieces = refs[:groups]
+    in_ref, out_ref, scaled_ref, sems = refs[groups:]
     _, group_here, table_here = Scalars(scalar_ref, bals, slots).place()
     features = in_ref.shape[1]
-    half = tables // 2
     copies = []
-    for index, piece in enumerate(pieces):
-        far, group_step = divmod(index, groups)
-        for inner in range(half):
-            table_step = far * half + inner
-            at = (index * half + inner) * unit
-            scaled_ref[at : at + unit, :] = piece[inner * unit : (inner + 1) * unit, :].astype(f32) * scale
+    for group_step, piece in enumerate(pieces):
+        for table_step in range(tables):
+            index = group_step * tables + table_step
+            at = index * unit
+            from_rows = slice(table_step * unit, (table_step + 1) * unit)
+            scaled_ref[at : at + unit, :] = piece[from_rows, :].astype(f32) * scale
             owner = (group_here ^ group_step) * tables + (table_here ^ table_step)
             to = pl.ds(pl.multiple_of(owner * unit, unit), unit)
             rows = scaled_ref.at[pl.ds(at, unit), :]
-            sem = sems.at[index * half + inner]
+            sem = sems.at[index]
             copies.append(
                 pltpu.make_async_copy(rows.at[:, pl.ds(0, features)], in_ref.at[to, :], sem.at[0])
             )
@@ -391,14 +379,12 @@
     group_here = emb % groups
     width, features = weight_out.shape[1], weight_in.shape[1]
     unit = weight_part // embs
-    owned = unit % 16 == 0 and tables % 2 == 0
+    owned = unit % 16 == 0
     unit = unit if owned else 0
-    params = pltpu.CompilerParams(vmem_limit_bytes=ROOM)
-    place = jnp.stack([bal, group_here, table_here]).astype(jnp.int32)
-    scalars = jnp.concatenate(
-        [surplus_slot[:, 0], helper_map[:, 0], seq_lengths[:, 0, :].reshape(-1), place]
-    )
-    scalars = jnp.pad(scalars, (0, LANES - scalars.shape[0]))[None]
+    place = [index.reshape(1, 1).astype(jnp.int32) for index in (bal, group_here, table_here)]
+    scalars = [surplus_slot.T, helper_map.T, seq_lengths[:, 0, :].reshape(1, -1)] + place
+    scalars = jnp.concatenate(scalars, axis=1)
+    scalars = jnp.pad(scalars, ((0, 0), (0, LANES - scalars.shape[1])))
 
     share = lax.dynamic_slice_in_dim(embed_tables[0], bal * part, part, 0)
     fetched = [emb_swap(share, step * groups, embs) for step in range(1, tables)]
@@ -412,36 +398,27 @@
 
     all_in = with_swapped(weight_in, bals)
     all_out = with_swapped(weight_out, bals)
-    to_stage = [embed_tables[0], weight_in, weight_out, cotangent[0]]
-    own_table, own_in, own_out, cot = pl.pallas_call(
-        stage_kernel,
-        out_shape=[jax.ShapeDtypeStruct(value.shape, value.dtype) for value in to_stage],
-        in_specs=[HBM] * len(to_stage),
-        out_specs=[VMEM] * len(to_stage),
-        scratch_shapes=[pltpu.SemaphoreType.DMA((len(to_stage),))],
-        compiler_params=params,
-    )(*to_stage)
-    fetched[-1] = after(fetched[-1], own_table)
-    pieces = [own_table] + [piece for one in fetched for piece in with_swapped(one, bals)]
+    pieces = [embed_tables[0]] + [piece for one in fetched for piece in with_swapped(one, bals)]
 
     found = pl.pallas_call(
         functools.partial(lookup_kernel, groups, slots, tables, bals),
         out_shape=[jax.ShapeDtypeStruct((rows, columns), bf16)] * groups,
         in_specs=[SMEM] * groups + [VMEM] * (bals + len(pieces)),
         out_specs=[VMEM] * groups,
-        compiler_params=params,
+        cost_estimate=estimate(3),
+        compiler_params=room(16),
     )(*plane_scalars, *plane_ids, *pieces)
     block = [found[0]] + [emb_swap(found[step], step, embs) for step in range(1, groups)]
 
     pairs = slots * HEADS // 2
-    terms = jax.ShapeDtypeStruct((weight_part // 2, features + width), bf16)
+    terms = jax.ShapeDtypeStruct((weight_part, features + width), bf16)
     results = pl.pallas_call(
         functools.partial(layer_kernel, groups, slots, tables, bals, unit),
         out_shape=[jax.ShapeDtypeStruct((rows, width), bf16)]
         + [jax.ShapeDtypeStruct((rows, columns), bf16)] * groups
-        + [terms] * (2 * bals),
+        + [terms] * bals,
         in_specs=[SMEM] + [VMEM] * groups + [HBM] * (2 * bals + 1),
-        out_specs=[VMEM] * (1 + groups + 2 * bals),
+        out_specs=[VMEM] * (1 + groups + bals),
         scratch_shapes=[
             pltpu.VMEM((groups, rows, columns), bf16),
             pltpu.VMEM((width, features), bf16),
@@ -457,72 +434,68 @@
             pltpu.VMEM((rows, features), bf16),
             pltpu.SemaphoreType.DMA((2 * bals + 1,)),
         ],
-        compiler_params=params,
-    )(scalars, *block, own_in, *all_in[1:], own_out, *all_out[1:], cot)
+        cost_estimate=estimate(7),
+        compiler_params=room(36),
+    )(scalars, *block, *all_in, *all_out, cotangent[0])
     layer_out, results = results[0], results[1:]
     grads, results = results[:groups], results[groups:]
-    far_terms, near_terms = results[:bals], results[bals:]
 
     def over_cores(parts):
-        return [parts[0]] + [bal_swap(parts[turn], turn, bals) for turn in range(1, bals)]
-
-    def over_plane(value, *others):
-        pieces = value.reshape(groups, value.shape[0] // groups, value.shape[1])
-        came = [emb_swap(pieces[step], step, embs) for step in range(1, groups)]
-        return sum_rounded([pieces[0]] + [after(piece, *others) for piece in came])
+        return sum_rounded([parts[0]] + [bal_swap(parts[turn], turn, bals) for turn in range(1, bals)])
 
     def to_plane(value):
         return [value] + [emb_swap(value, step, embs) for step in range(1, groups)]
 
-    far_terms = over_cores(far_terms)
-    near_terms = over_cores([near_terms[0]] + [after(term, far_terms[-1]) for term in near_terms[1:]])
-    far, near = sum_rounded(far_terms), sum_rounded(near_terms)
+    total = over_cores(results)
+    plane_grads = [grads[0]] + [emb_swap(grads[step], step, embs) for step in range(1, groups)]
+    sums = pl.pallas_call(
+        functools.partial(scatter_kernel, groups, slots, bals),
+        out_shape=[jax.ShapeDtypeStruct((tables, part, columns), bf16)] * bals,
+        in_specs=[SMEM] * groups + [VMEM] * (bals + groups),
+        out_specs=[VMEM] * bals,
+        cost_estimate=estimate(3),
+        compiler_params=room(16),
+    )(*plane_scalars, *plane_ids, *plane_grads)
+    own_sums = over_cores(sums)
+
     grad_scale = (rows * embs * bals) ** -0.5
     if owned:
-        half = tables // 2
-        far, near = over_plane(far, near), over_plane(near)
-        grads = [grads[0]] + [after(grad, far) for grad in grads[1:]]
-        rel = [near[at * unit : (at + 1) * unit] for at in range(half)]
-        rel += [far[at * unit : (at + 1) * unit] for at in range(half)]
+        pieces = total.reshape(groups, weight_part // groups, features + width)
+        came = [after(emb_swap(pieces[step], step, embs), sums[0]) for step in range(1, groups)]
+        mine = sum_rounded([pieces[0]] + came)
+        mine = mine.reshape(tables, unit, features + width)
         final = sum_rounded(
-            [rel[0]] + [emb_swap(rel[step], step * groups, embs) for step in range(1, tables)]
+            [mine[0]] + [emb_swap(mine[step], step * groups, embs) for step in range(1, tables)]
         )
         gathered = [final] + [emb_swap(final, step * groups, embs) for step in range(1, tables)]
-        ready = gathered[half - 1]
-        back = to_plane(jnp.concatenate(gathered[:half], axis=0))
-        back += to_plane(jnp.concatenate(gathered[half:], axis=0))
+        own_sums = after(own_sums, *gathered[1:])
+        back = to_plane(jnp.concatenate(gathered, axis=0))
+
+    table_sum = own_sums[0].astype(f32)
+    for step in range(1, tables):
+        table_sum = table_sum + emb_swap(own_sums[step], step * groups, embs).astype(f32)
+    table_scale = (distinct / (bals * item_ids.shape[1])) ** 0.5
+
+    if owned:
         total_in, total_out = pl.pallas_call(
             functools.partial(place_kernel, grad_scale, groups, slots, tables, bals, unit),
             out_shape=[
                 jax.ShapeDtypeStruct((weight_part, features), f32),
                 jax.ShapeDtypeStruct((weight_part, width), f32),
             ],
-            in_specs=[SMEM] + [VMEM] * (2 * groups),
+            in_specs=[SMEM] + [VMEM] * groups,
             out_specs=[HBM] * 2,
             scratch_shapes=[
                 pltpu.VMEM((weight_part, features + width), f32),
                 pltpu.SemaphoreType.DMA((groups * tables, 2)),
             ],
-            compiler_params=params,
+            cost_estimate=estimate(2),
+            compiler_params=room(12),
         )(scalars, *back)
     else:
-        total = lax.psum(jnp.concatenate([far, near], axis=0).astype(f32), "emb") * grad_scale
+        total = lax.psum(total.astype(f32), "emb") * grad_scale
         total_in, total_out = total[:, :features], total[:, features:]
-        ready = far
-
-    plane_grads = [grads[0]] + [emb_swap(grads[step], step, embs) for step in range(1, groups)]
-    sums = pl.pallas_call(
-        functools.partial(scatter_kernel, groups, slots, bals),
-        out_shape=[jax.ShapeDtypeStruct((tables, part, columns), bf16)] * bals,
-        in_specs=[SMEM] * groups + [VMEM] * (bals + groups),
-        out_specs=[VMEM] * bals,
-        compiler_params=params,
-    )(*plane_scalars, *plane_ids, *plane_grads)
-    own_sums = after(sum_rounded(over_cores(sums)), ready)
-    table_sum = own_sums[0].astype(f32)
-    for step in range(1, tables):
-        table_sum = table_sum + emb_swap(own_sums[step], step * groups, embs).astype(f32)
-    table_scale = (distinct / (bals * item_ids.shape[1])) ** 0.5
+
     return layer_out[None], (table_sum * table_scale)[None], total_in, total_out
 
 

time: 117 us -> 113 us (0.966)
  starting transfers between devices: 43.4 us -> 36.5 us
  waiting for transfers between devices: 47.3 us -> 52.1 us
  local copies, waits for them, and re-layouts: 6.51 us -> 5.29 us
    ppermute x33 -> x27, starting transfers between devices: 41.3 us -> 35.4 us  [emb_swap(): return lax.ppermute(value, 'emb', [(i, i ^ step) for i in range(count)])]
    ppermute x33 -> x27, waiting for transfers between devices: 44 us -> 47.7 us  [emb_swap(): return lax.ppermute(value, 'emb', [(i, i ^ step) for i in range(count)])]
    unnamed x12 -> x11, local copies, waits for them, and re-layouts: 4.6 us -> 3.37 us
    ppermute x9 -> x8, waiting for transfers between devices: 3.36 us -> 4.37 us  [bal_swap(): return lax.ppermute(value, 'bal', [(i, i ^ step) for i in range(count)])]
  transfers between devices with their start and end apart: 42 -> 35, of which waited for: 25 -> 21; matrix products, arithmetic and copies ran while one was open for 4% -> 4% of each run, Pallas kernels for 7% -> 6%
where the time goes in v5:
time: 113 us
  waiting for transfers between devices  52.1 us (46%)
  starting transfers between devices  36.5 us (32%)
  Pallas kernels  15.1 us (13%)
  local copies, waits for them, and re-layouts  5.29 us (5%)
  other arithmetic  2.81 us (2%)
    ppermute x27, waiting for transfers between devices, emb_swap(): return lax.ppermute(value, 'emb', [(i, i ^ step) for i in range(count)])  47.7 us
    ppermute x27, starting transfers between devices, emb_swap(): return lax.ppermute(value, 'emb', [(i, i ^ step) for i in range(count)])  35.4 us
    pallas_call x1, Pallas kernels, on_device(): pl.pallas_call(functools.partial(layer_kernel, groups, slots, tables, bal...  6.58 us
    ppermute x8, waiting for transfers between devices, bal_swap(): return lax.ppermute(value, 'bal', [(i, i ^ step) for i in range(count)])  4.37 us
    unnamed x11, local copies, waits for them, and re-layouts  3.37 us
    pallas_call x1, Pallas kernels, on_device(): pl.pallas_call(functools.partial(lookup_kernel, groups, slots, tables, ba...  3.3 us
    pallas_call x1, Pallas kernels, on_device(): pl.pallas_call(functools.partial(scatter_kernel, groups, slots, bals), ou...  2.9 us
    pallas_call x1, Pallas kernels, on_device(): pl.pallas_call(functools.partial(place_kernel, grad_scale, groups, slots,...  2.29 us
  transfers between devices with their start and end apart: 35, of which 21 were waited for; matrix products, arithmetic and copies ran while one was open for 4% of the time, Pallas kernels for 6%

profile of v5, /device:TPU:0, one launch (start us, length us, event | category | flops | bytes accessed | tf_op | source)
XLA Modules:
  0.0 112.7 jit_solution(4690075806685096147)
XLA Ops:
  2.1 2.7 %collective-permute-start = (bf16[512,128]{1,0:T(8,128)(2,1)S(1)}, bf16[512,128]{1,0:T(8,128)(2,1)S(1)}, u32[]{:S(2)}, u32[]{:S(2)}) collective-permute-start(bf16[512,128]{1,0:T(8,128)(2,1)S(1)} %dynamic-slice_bitcast_fusion), channel_id=1, source_target_pairs={{0,8},{2,10},{4,12},{6,14},{8,0},{10,2},{12,4},{14,6},{16,24},{18,... | collective-permute-start | bytes 393224 | tf_op jit(solution)/shard_map/ppermute | solution.py:54
  4.8 2.5 %collective-permute-start.8 = (bf16[512,128]{1,0:T(8,128)(2,1)S(1)}, bf16[512,128]{1,0:T(8,128)(2,1)S(1)}, u32[]{:S(2)}, u32[]{:S(2)}) collective-permute-start(bf16[512,128]{1,0:T(8,128)(2,1)S(1)} %dynamic-slice_bitcast_fusion), channel_id=1, source_target_pairs={{0,24},{2,26},{4,28},{6,30},{8,16},{10,18},{12,20},{14,22},{16,8},... | collective-permute-start | bytes 393224 | tf_op jit(solution)/shard_map/ppermute | solution.py:54
  11.6 2.7 %collective-permute-start.3 = (s32[1,128]{1,0:T(1,128)S(1)}, s32[1,128]{1,0:T(1,128)S(1)}, u32[]{:S(2)}, u32[]{:S(2)}) collective-permute-start(s32[1,128]{1,0:T(1,128)S(1)} %pad.4.refs_0_.scalar_ref), channel_id=1, source_target_pairs={{0,6},{2,4},{4,2},{6,0},{8,14},{10,12},{12,10},{14,8},{16,22},{18,... | collective-permute-start | bytes 1544 | tf_op jit(solution)/shard_map/ppermute | solution.py:54
  16.0 3.6 %collective-permute-done.6.refs_9_ = bf16[512,128]{1,0:T(8,128)(2,1)S(1)} collective-permute-done((bf16[512,128]{1,0:T(8,128)(2,1)S(1)}, bf16[512,128]{1,0:T(8,128)(2,1)S(1)}, u32[]{:S(2)}, u32[]{:S(2)}) %collective-permute-start.6) | collective-permute-done | bytes 131104 | tf_op jit(solution)/shard_map/ppermute | solution.py:54
  25.5 3.3 %shard_map.111 = (bf16[256,128]{1,0:T(8,128)(2,1)S(1)}, bf16[256,128]{1,0:T(8,128)(2,1)S(1)}, bf16[256,128]{1,0:T(8,128)(2,1)S(1)}, bf16[256,128]{1,0:T(8,128)(2,1)S(1)}) custom-call(s32[1,128]{1,0:T(1,128)S(1)} %pad.4.refs_0_.scalar_ref, s32[1,128]{1,0:T(1,128)S(1)} %collective-permute-done.1.refs_1_, s32[1,128]{1,0:T(1,128)S(1)} %collective-permute-done.2.refs_2_, ...), custom_call_target="tpu_custom_call" | custom-call | bytes 10500000 | tf_op jit(solution)/shard_map/pallas_call | solution.py:403
  34.6 2.4 %collective-permute-done.12.refs_3_ = bf16[256,128]{1,0:T(8,128)(2,1)S(1)} collective-permute-done((bf16[256,128]{1,0:T(8,128)(2,1)S(1)}, bf16[256,128]{1,0:T(8,128)(2,1)S(1)}, u32[]{:S(2)}, u32[]{:S(2)}) %collective-permute-start.12) | collective-permute-done | bytes 65568 | tf_op jit(solution)/shard_map/ppermute | solution.py:54
  39.0 6.6 %shard_map.112 = (bf16[256,512]{1,0:T(8,128)(2,1)}, bf16[256,128]{1,0:T(8,128)(2,1)S(1)}, bf16[256,128]{1,0:T(8,128)(2,1)S(1)}, bf16[256,128]{1,0:T(8,128)(2,1)S...) custom-call(s32[1,128]{1,0:T(1,128)S(1)} %pad.4.refs_0_.scalar_ref, ...), custom_call_target="tpu_custom_call" | custom-call | bytes 24500000 | tf_op jit(solution)/shard_map/pallas_call | solution.py:415
  45.6 3.0 %collective-permute-done.19 = bf16[256,2560]{1,0:T(8,128)(2,1)S(1)} collective-permute-done((bf16[256,2560]{1,0:T(8,128)(2,1)S(1)}, bf16[256,2560]{1,0:T(8,128)(2,1)S(1)}, u32[]{:S(2)}, u32[]{:S(2)}) %collective-permute-start.19) | collective-permute-done | bytes 1310752 | tf_op jit(solution)/shard_map/ppermute | solution.py:46
  53.7 13.7 %collective-permute-done.15.refs_7_ = bf16[256,128]{1,0:T(8,128)(2,1)S(1)} collective-permute-done((bf16[256,128]{1,0:T(8,128)(2,1)S(1)}, bf16[256,128]{1,0:T(8,128)(2,1)S(1)}, u32[]{:S(2)}, u32[]{:S(2)}) %collective-permute-start.15) | collective-permute-done | bytes 65568 | tf_op jit(solution)/shard_map/ppermute | solution.py:54
  68.7 3.8 %collective-permute-done.17.refs_9_ = bf16[256,128]{1,0:T(8,128)(2,1)S(1)} collective-permute-done((bf16[256,128]{1,0:T(8,128)(2,1)S(1)}, bf16[256,128]{1,0:T(8,128)(2,1)S(1)}, u32[]{:S(2)}, u32[]{:S(2)}) %collective-permute-start.17) | collective-permute-done | bytes 65568 | tf_op jit(solution)/shard_map/ppermute | solution.py:54
  72.5 2.9 %shard_map.113 = (bf16[4,512,128]{2,1,0:T(8,128)(2,1)S(1)}, bf16[4,512,128]{2,1,0:T(8,128)(2,1)S(1)}) custom-call(s32[1,128]{1,0:T(1,128)S(1)} %pad.4.refs_0_.scalar_ref, s32[1,128]{1,0:T(1,128)S(1)} %collective-permute-done.1.refs_1_, s32[1,128]{1,0:T(1,128)S(1)} %collective-permute-done.2.refs_2_, s32[1,128]{1,0:T(1,128)S(1)} %collective-permute-done.3.refs_3_, ...), custom_call_target="tpu_custom_call" | custom-call | bytes 10500000 | tf_op jit(solution)/shard_map/pallas_call | solution.py:451
  75.7 2.7 %collective-permute-start.25 = (bf16[16,2560]{1,0:T(8,128)(2,1)S(1)}, bf16[16,2560]{1,0:T(8,128)(2,1)S(1)}, u32[]{:S(2)}, u32[]{:S(2)}) collective-permute-start(bf16[16,2560]{1,0:T(8,128)(2,1)S(1)} %get-tuple-element.53), channel_id=1, source_target_pairs={{0,24},{2,26},{4,28},{6,30},{8,16},{10,18},{12,20},{14,22},{16,8},... | collective-permute-start | bytes 245768 | tf_op jit(solution)/shard_map/ppermute | solution.py:54
  79.2 1.6 %collective-permute-done.23 = bf16[16,2560]{1,0:T(8,128)(2,1)S(1)} collective-permute-done((bf16[16,2560]{1,0:T(8,128)(2,1)S(1)}, bf16[16,2560]{1,0:T(8,128)(2,1)S(1)}, u32[]{:S(2)}, u32[]{:S(2)}) %collective-permute-start.23) | collective-permute-done | bytes 81952 | tf_op jit(solution)/shard_map/ppermute | solution.py:54
  80.8 1.9 %collective-permute-done.25 = bf16[16,2560]{1,0:T(8,128)(2,1)S(1)} collective-permute-done((bf16[16,2560]{1,0:T(8,128)(2,1)S(1)}, bf16[16,2560]{1,0:T(8,128)(2,1)S(1)}, u32[]{:S(2)}, u32[]{:S(2)}) %collective-permute-start.25) | collective-permute-done | bytes 81952 | tf_op jit(solution)/shard_map/ppermute | solution.py:54
  82.6 3.0 %collective-permute-done.24 = bf16[16,2560]{1,0:T(8,128)(2,1)S(1)} collective-permute-done((bf16[16,2560]{1,0:T(8,128)(2,1)S(1)}, bf16[16,2560]{1,0:T(8,128)(2,1)S(1)}, u32[]{:S(2)}, u32[]{:S(2)}) %collective-permute-start.24) | collective-permute-done | bytes 81952 | tf_op jit(solution)/shard_map/ppermute | solution.py:54
  85.7 2.6 %collective-permute-start.28 = (bf16[16,2560]{1,0:T(8,128)(2,1)S(1)}, bf16[16,2560]{1,0:T(8,128)(2,1)S(1)}, u32[]{:S(2)}, u32[]{:S(2)}) collective-permute-start(bf16[16,2560]{1,0:T(8,128)(2,1)S(1)} %add_convert_fusion.3), channel_id=1, source_target_pairs={{0,24},{2,26},{4,28},{6,30},{8,16},{10,18},{12,20},{14,22},{16,8},... | collective-permute-start | bytes 245768 | tf_op jit(solution)/shard_map/ppermute | solution.py:54
  88.3 1.9 %collective-permute-start.26 = (bf16[16,2560]{1,0:T(8,128)(2,1)S(1)}, bf16[16,2560]{1,0:T(8,128)(2,1)S(1)}, u32[]{:S(2)}, u32[]{:S(2)}) collective-permute-start(bf16[16,2560]{1,0:T(8,128)(2,1)S(1)} %add_convert_fusion.3), channel_id=1, source_target_pairs={{0,8},{2,10},{4,12},{6,14},{8,0},{10,2},{12,4},{14,6},{16,24},{18,... | collective-permute-start | bytes 245768 | tf_op jit(solution)/shard_map/ppermute | solution.py:54
  90.3 1.7 %collective-permute-done.28 = bf16[16,2560]{1,0:T(8,128)(2,1)S(1)} collective-permute-done((bf16[16,2560]{1,0:T(8,128)(2,1)S(1)}, bf16[16,2560]{1,0:T(8,128)(2,1)S(1)}, u32[]{:S(2)}, u32[]{:S(2)}) %collective-permute-start.28) | collective-permute-done | bytes 81952 | tf_op jit(solution)/shard_map/ppermute | solution.py:54
  92.0 1.8 %collective-permute-done.27 = bf16[16,2560]{1,0:T(8,128)(2,1)S(1)} collective-permute-done((bf16[16,2560]{1,0:T(8,128)(2,1)S(1)}, bf16[16,2560]{1,0:T(8,128)(2,1)S(1)}, u32[]{:S(2)}, u32[]{:S(2)}) %collective-permute-start.27) | collective-permute-done | bytes 81952 | tf_op jit(solution)/shard_map/ppermute | solution.py:54
  93.9 1.7 %collective-permute-start.29 = (bf16[512,128]{1,0:T(8,128)(2,1)S(1)}, bf16[512,128]{1,0:T(8,128)(2,1)S(1)}, u32[]{:S(2)}, u32[]{:S(2)}) collective-permute-start(bf16[512,128]{1,0:T(8,128)(2,1)S(1)} %get-tuple-element.49), channel_id=1, source_target_pairs={{0,8},{2,10},{4,12},{6,14},{8,0},{10,2},{12,4},{14,6},{16,24},{18,... | collective-permute-start | bytes 393224 | tf_op jit(solution)/shard_map/ppermute | solution.py:54
  95.6 2.4 %collective-permute-start.31 = (bf16[512,128]{1,0:T(8,128)(2,1)S(1)}, bf16[512,128]{1,0:T(8,128)(2,1)S(1)}, u32[]{:S(2)}, u32[]{:S(2)}) collective-permute-start(bf16[512,128]{1,0:T(8,128)(2,1)S(1)} %get-tuple-element.50), channel_id=1, source_target_pairs={{0,24},{2,26},{4,28},{6,30},{8,16},{10,18},{12,20},{14,22},{16,8},... | collective-permute-start | bytes 393224 | tf_op jit(solution)/shard_map/ppermute | solution.py:54
  102.5 3.5 %collective-permute-done.30 = bf16[512,128]{1,0:T(8,128)(2,1)S(1)} collective-permute-done((bf16[512,128]{1,0:T(8,128)(2,1)S(1)}, bf16[512,128]{1,0:T(8,128)(2,1)S(1)}, u32[]{:S(2)}, u32[]{:S(2)}) %collective-permute-start.30) | collective-permute-done | bytes 131104 | tf_op jit(solution)/shard_map/ppermute | solution.py:54
  107.5 2.7 %collective-permute-done.33.refs_2_ = bf16[64,2560]{1,0:T(8,128)(2,1)S(1)} collective-permute-done((bf16[64,2560]{1,0:T(8,128)(2,1)S(1)}, bf16[64,2560]{1,0:T(8,128)(2,1)S(1)}, u32[]{:S(2)}, u32[]{:S(2)}) %collective-permute-start.33) | collective-permute-done | bytes 327712 | tf_op jit(solution)/shard_map/ppermute | solution.py:54
  110.2 2.3 %shard_map.114 = (f32[256,2048]{1,0:T(8,128)}, f32[256,512]{1,0:T(8,128)}) custom-call(s32[1,128]{1,0:T(1,128)S(1)} %pad.4.refs_0_.scalar_ref, bf16[64,2560]{1,0:T(8,128)(2,1)S(1)} %pad_maximum_fusion.refs_0_, bf16[64,2560]{1,0:T(8,128)(2,1)S(1)} %collective-permute-done.32.refs_1_, bf16[64,2560]{1,0:T(8,128)(2,1)S(1)} %collective-permute-done.33.refs_2_, ...), custom_call_target="tpu_custom_call" | custom-call | bytes 7000000 | tf_op jit(solution)/shard_map/pallas_call | solution.py:480
  (77 shorter events, 34.7 us)
Async XLA Ops:
  0.7 36.4 %collective-permute-start.13 = (bf16[256,2048]{1,0:T(8,128)(2,1)}, bf16[256,2048]{1,0:T(8,128)(2,1)S(1)}, u32[]{:S(2)}, u32[]{:S(2)}) collective-permute-start(bf16[256,2048]{1,0:T(8,128)(2,1)} %refs_4_.1), channel_id=1, source_target_pairs={{0,1},{1,0},{2,3},{3,2},{4,5},{5,4},{6,7},{7,6},{8,9},{9,8},{10,11... | collective-permute-start | bytes 3145736 | tf_op jit(solution)/shard_map/ppermute | solution.py:46
  2.1 6.8 %collective-permute-start = (bf16[512,128]{1,0:T(8,128)(2,1)S(1)}, bf16[512,128]{1,0:T(8,128)(2,1)S(1)}, u32[]{:S(2)}, u32[]{:S(2)}) collective-permute-start(bf16[512,128]{1,0:T(8,128)(2,1)S(1)} %dynamic-slice_bitcast_fusion), channel_id=1, source_target_pairs={{0,8},{2,10},{4,12},{6,14},{8,0},{10,2},{12,4},{14,6},{16,24},{18,... | collective-permute-start | bytes 393224 | tf_op jit(solution)/shard_map/ppermute | solution.py:54
  4.8 9.7 %collective-permute-start.8 = (bf16[512,128]{1,0:T(8,128)(2,1)S(1)}, bf16[512,128]{1,0:T(8,128)(2,1)S(1)}, u32[]{:S(2)}, u32[]{:S(2)}) collective-permute-start(bf16[512,128]{1,0:T(8,128)(2,1)S(1)} %dynamic-slice_bitcast_fusion), channel_id=1, source_target_pairs={{0,24},{2,26},{4,28},{6,30},{8,16},{10,18},{12,20},{14,22},{16,8},... | collective-permute-start | bytes 393224 | tf_op jit(solution)/shard_map/ppermute | solution.py:54
  7.3 12.3 %collective-permute-start.6 = (bf16[512,128]{1,0:T(8,128)(2,1)S(1)}, bf16[512,128]{1,0:T(8,128)(2,1)S(1)}, u32[]{:S(2)}, u32[]{:S(2)}) collective-permute-start(bf16[512,128]{1,0:T(8,128)(2,1)S(1)} %dynamic-slice_bitcast_fusion), channel_id=1, source_target_pairs={{0,16},{2,18},{4,20},{6,22},{8,24},{10,26},{12,28},{14,30},{16,0},... | collective-permute-start | bytes 393224 | tf_op jit(solution)/shard_map/ppermute | solution.py:54
  7.4 24.9 %collective-permute-start.14 = (bf16[256,512]{1,0:T(8,128)(2,1)}, bf16[256,512]{1,0:T(8,128)(2,1)S(1)}, u32[]{:S(2)}, u32[]{:S(2)}) collective-permute-start(bf16[256,512]{1,0:T(8,128)(2,1)} %refs_6_.1), channel_id=1, source_target_pairs={{0,1},{1,0},{2,3},{3,2},{4,5},{5,4},{6,7},{7,6},{8,9},{9,8},{10,11... | collective-permute-start | bytes 786440 | tf_op jit(solution)/shard_map/ppermute | solution.py:46
  11.6 9.5 %collective-permute-start.3 = (s32[1,128]{1,0:T(1,128)S(1)}, s32[1,128]{1,0:T(1,128)S(1)}, u32[]{:S(2)}, u32[]{:S(2)}) collective-permute-start(s32[1,128]{1,0:T(1,128)S(1)} %pad.4.refs_0_.scalar_ref), channel_id=1, source_target_pairs={{0,6},{2,4},{4,2},{6,0},{8,14},{10,12},{12,10},{14,8},{16,22},{18,... | collective-permute-start | bytes 1544 | tf_op jit(solution)/shard_map/ppermute | solution.py:54
  14.5 6.7 %collective-permute-start.2 = (s32[1,128]{1,0:T(1,128)S(1)}, s32[1,128]{1,0:T(1,128)S(1)}, u32[]{:S(2)}, u32[]{:S(2)}) collective-permute-start(s32[1,128]{1,0:T(1,128)S(1)} %pad.4.refs_0_.scalar_ref), channel_id=1, source_target_pairs={{0,4},{2,6},{4,0},{6,2},{8,12},{10,14},{12,8},{14,10},{16,20},{18,... | collective-permute-start | bytes 1544 | tf_op jit(solution)/shard_map/ppermute | solution.py:54
  49.0 26.4 %collective-permute-start.20 = (bf16[64,2560]{1,0:T(8,128)(2,1)S(1)}, bf16[64,2560]{1,0:T(8,128)(2,1)S(1)}, u32[]{:S(2)}, u32[]{:S(2)}) collective-permute-start(bf16[64,2560]{1,0:T(8,128)(2,1)S(1)} %get-tuple-element.46), channel_id=1, source_target_pairs={{0,2},{2,0},{4,6},{6,4},{8,10},{10,8},{12,14},{14,12},{16,18},{18,... | collective-permute-start | bytes 983048 | tf_op jit(solution)/shard_map/ppermute | solution.py:54
  49.6 25.8 %collective-permute-start.22 = (bf16[64,2560]{1,0:T(8,128)(2,1)S(1)}, bf16[64,2560]{1,0:T(8,128)(2,1)S(1)}, u32[]{:S(2)}, u32[]{:S(2)}) collective-permute-start(bf16[64,2560]{1,0:T(8,128)(2,1)S(1)} %get-tuple-element.47), channel_id=1, source_target_pairs={{0,6},{2,4},{4,2},{6,0},{8,14},{10,12},{12,10},{14,8},{16,22},{18,... | collective-permute-start | bytes 983048 | tf_op jit(solution)/shard_map/ppermute | solution.py:54
  51.1 24.3 %collective-permute-start.21 = (bf16[64,2560]{1,0:T(8,128)(2,1)S(1)}, bf16[64,2560]{1,0:T(8,128)(2,1)S(1)}, u32[]{:S(2)}, u32[]{:S(2)}) collective-permute-start(bf16[64,2560]{1,0:T(8,128)(2,1)S(1)} %get-tuple-element.48), channel_id=1, source_target_pairs={{0,4},{2,6},{4,0},{6,2},{8,12},{10,14},{12,8},{14,10},{16,20},{18,... | collective-permute-start | bytes 983048 | tf_op jit(solution)/shard_map/ppermute | solution.py:54
  52.6 14.7 %collective-permute-start.15 = (bf16[256,128]{1,0:T(8,128)(2,1)S(1)}, bf16[256,128]{1,0:T(8,128)(2,1)S(1)}, u32[]{:S(2)}, u32[]{:S(2)}) collective-permute-start(bf16[256,128]{1,0:T(8,128)(2,1)S(1)} %get-tuple-element.33), channel_id=1, source_target_pairs={{0,2},{2,0},{4,6},{6,4},{8,10},{10,8},{12,14},{14,12},{16,18},{18,... | collective-permute-start | bytes 196616 | tf_op jit(solution)/shard_map/ppermute | solution.py:54
  53.1 15.6 %collective-permute-start.16 = (bf16[256,128]{1,0:T(8,128)(2,1)S(1)}, bf16[256,128]{1,0:T(8,128)(2,1)S(1)}, u32[]{:S(2)}, u32[]{:S(2)}) collective-permute-start(bf16[256,128]{1,0:T(8,128)(2,1)S(1)} %get-tuple-element.34), channel_id=1, source_target_pairs={{0,4},{2,6},{4,0},{6,2},{8,12},{10,14},{12,8},{14,10},{16,20},{18,... | collective-permute-start | bytes 196616 | tf_op jit(solution)/shard_map/ppermute | solution.py:54
  75.7 6.9 %collective-permute-start.25 = (bf16[16,2560]{1,0:T(8,128)(2,1)S(1)}, bf16[16,2560]{1,0:T(8,128)(2,1)S(1)}, u32[]{:S(2)}, u32[]{:S(2)}) collective-permute-start(bf16[16,2560]{1,0:T(8,128)(2,1)S(1)} %get-tuple-element.53), channel_id=1, source_target_pairs={{0,24},{2,26},{4,28},{6,30},{8,16},{10,18},{12,20},{14,22},{16,8},... | collective-permute-start | bytes 245768 | tf_op jit(solution)/shard_map/ppermute | solution.py:54
  78.4 7.2 %collective-permute-start.24 = (bf16[16,2560]{1,0:T(8,128)(2,1)S(1)}, bf16[16,2560]{1,0:T(8,128)(2,1)S(1)}, u32[]{:S(2)}, u32[]{:S(2)}) collective-permute-start(bf16[16,2560]{1,0:T(8,128)(2,1)S(1)} %get-tuple-element.54), channel_id=1, source_target_pairs={{0,16},{2,18},{4,20},{6,22},{8,24},{10,26},{12,28},{14,30},{16,0},... | collective-permute-start | bytes 245768 | tf_op jit(solution)/shard_map/ppermute | solution.py:54
  79.2 11.0 %collective-permute-start.18 = (bf16[4,512,128]{2,1,0:T(8,128)(2,1)S(1)}, bf16[4,512,128]{2,1,0:T(8,128)(2,1)S(1)}, u32[]{:S(2)}, u32[]{:S(2)}) collective-permute-start(bf16[4,512,128]{2,1,0:T(8,128)(2,1)S(1)} %get-tuple-element.37), channel_id=1, source_target_pairs={{0,1},{1,0},{2,3},{3,2},{4,5},{5,4},{6,7},{7,6},{8,9},{9,8},{10,11... | collective-permute-start | bytes 1572872 | tf_op jit(solution)/shard_map/ppermute | solution.py:46
  85.7 6.3 %collective-permute-start.28 = (bf16[16,2560]{1,0:T(8,128)(2,1)S(1)}, bf16[16,2560]{1,0:T(8,128)(2,1)S(1)}, u32[]{:S(2)}, u32[]{:S(2)}) collective-permute-start(bf16[16,2560]{1,0:T(8,128)(2,1)S(1)} %add_convert_fusion.3), channel_id=1, source_target_pairs={{0,24},{2,26},{4,28},{6,30},{8,16},{10,18},{12,20},{14,22},{16,8},... | collective-permute-start | bytes 245768 | tf_op jit(solution)/shard_map/ppermute | solution.py:54
  88.3 5.5 %collective-permute-start.27 = (bf16[16,2560]{1,0:T(8,128)(2,1)S(1)}, bf16[16,2560]{1,0:T(8,128)(2,1)S(1)}, u32[]{:S(2)}, u32[]{:S(2)}) collective-permute-start(bf16[16,2560]{1,0:T(8,128)(2,1)S(1)} %add_convert_fusion.3), channel_id=1, source_target_pairs={{0,16},{2,18},{4,20},{6,22},{8,24},{10,26},{12,28},{14,30},{16,0},... | collective-permute-start | bytes 245768 | tf_op jit(solution)/shard_map/ppermute | solution.py:54
  88.3 5.5 %collective-permute-start.26 = (bf16[16,2560]{1,0:T(8,128)(2,1)S(1)}, bf16[16,2560]{1,0:T(8,128)(2,1)S(1)}, u32[]{:S(2)}, u32[]{:S(2)}) collective-permute-start(bf16[16,2560]{1,0:T(8,128)(2,1)S(1)} %add_convert_fusion.3), channel_id=1, source_target_pairs={{0,8},{2,10},{4,12},{6,14},{8,0},{10,2},{12,4},{14,6},{16,24},{18,... | collective-permute-start | bytes 245768 | tf_op jit(solution)/shard_map/ppermute | solution.py:54
  93.9 6.2 %collective-permute-start.29 = (bf16[512,128]{1,0:T(8,128)(2,1)S(1)}, bf16[512,128]{1,0:T(8,128)(2,1)S(1)}, u32[]{:S(2)}, u32[]{:S(2)}) collective-permute-start(bf16[512,128]{1,0:T(8,128)(2,1)S(1)} %get-tuple-element.49), channel_id=1, source_target_pairs={{0,8},{2,10},{4,12},{6,14},{8,0},{10,2},{12,4},{14,6},{16,24},{18,... | collective-permute-start | bytes 393224 | tf_op jit(solution)/shard_map/ppermute | solution.py:54
  95.6 6.9 %collective-permute-start.31 = (bf16[512,128]{1,0:T(8,128)(2,1)S(1)}, bf16[512,128]{1,0:T(8,128)(2,1)S(1)}, u32[]{:S(2)}, u32[]{:S(2)}) collective-permute-start(bf16[512,128]{1,0:T(8,128)(2,1)S(1)} %get-tuple-element.50), channel_id=1, source_target_pairs={{0,24},{2,26},{4,28},{6,30},{8,16},{10,18},{12,20},{14,22},{16,8},... | collective-permute-start | bytes 393224 | tf_op jit(solution)/shard_map/ppermute | solution.py:54
  98.0 8.0 %collective-permute-start.30 = (bf16[512,128]{1,0:T(8,128)(2,1)S(1)}, bf16[512,128]{1,0:T(8,128)(2,1)S(1)}, u32[]{:S(2)}, u32[]{:S(2)}) collective-permute-start(bf16[512,128]{1,0:T(8,128)(2,1)S(1)} %get-tuple-element.51), channel_id=1, source_target_pairs={{0,16},{2,18},{4,20},{6,22},{8,24},{10,26},{12,28},{14,30},{16,0},... | collective-permute-start | bytes 393224 | tf_op jit(solution)/shard_map/ppermute | solution.py:54
  98.0 9.5 %collective-permute-start.34 = (bf16[64,2560]{1,0:T(8,128)(2,1)S(1)}, bf16[64,2560]{1,0:T(8,128)(2,1)S(1)}, u32[]{:S(2)}, u32[]{:S(2)}) collective-permute-start(bf16[64,2560]{1,0:T(8,128)(2,1)S(1)} %pad_maximum_fusion.refs_0_), channel_id=1, source_target_pairs={{0,6},{2,4},{4,2},{6,0},{8,14},{10,12},{12,10},{14,8},{16,22},{18,... | collective-permute-start | bytes 983048 | tf_op jit(solution)/shard_map/ppermute | solution.py:54
  98.7 11.5 %collective-permute-start.33 = (bf16[64,2560]{1,0:T(8,128)(2,1)S(1)}, bf16[64,2560]{1,0:T(8,128)(2,1)S(1)}, u32[]{:S(2)}, u32[]{:S(2)}) collective-permute-start(bf16[64,2560]{1,0:T(8,128)(2,1)S(1)} %pad_maximum_fusion.refs_0_), channel_id=1, source_target_pairs={{0,4},{2,6},{4,0},{6,2},{8,12},{10,14},{12,8},{14,10},{16,20},{18,... | collective-permute-start | bytes 983048 | tf_op jit(solution)/shard_map/ppermute | solution.py:54
  100.1 10.1 %collective-permute-start.32 = (bf16[64,2560]{1,0:T(8,128)(2,1)S(1)}, bf16[64,2560]{1,0:T(8,128)(2,1)S(1)}, u32[]{:S(2)}, u32[]{:S(2)}) collective-permute-start(bf16[64,2560]{1,0:T(8,128)(2,1)S(1)} %pad_maximum_fusion.refs_0_), channel_id=1, source_target_pairs={{0,2},{2,0},{4,6},{6,4},{8,10},{10,8},{12,14},{14,12},{16,18},{18,... | collective-permute-start | bytes 983048 | tf_op jit(solution)/shard_map/ppermute | solution.py:54
  (16 other events, 84.9 us)

commit v6 on v5

--- a/solution.py
+++ b/solution.py
@@ -105,12 +105,10 @@
     take = lambda count: [refs.pop(0) for _ in range(count)]
     scalars = [Scalars(ref, bals, slots) for ref in take(groups)]
     ids_refs = take(bals)
-    (own_ref,) = take(1)
-    others = [take(bals) for _ in range(1, tables)]
+    pieces = [take(bals) for _ in range(tables)]
     out_refs = refs
     bal, _, table_here = scalars[0].place()
-    distinct, columns = own_ref.shape
-    part = distinct // bals
+    part, columns = pieces[0][0].shape
     slot_rows = ids_refs[0].shape[3]
     lane = lax.broadcasted_iota(jnp.int32, (LANES, LANES), 1)
     ids = pick_ids(scalars, ids_refs, slots, table_order(table_here, tables))
@@ -121,19 +119,12 @@
                 for table in range(tables):
                     row = ids[group][slot][table][:, first : first + LANES]
                     column = jnp.transpose(jnp.broadcast_to(row, (LANES, LANES)))
-                    if table == 0:
-                        pieces = [(own_ref, 0, distinct)]
-                    else:
-                        pieces = [
-                            (ref, (bal ^ turn) * part, part)
-                            for turn, ref in enumerate(others[table - 1])
-                        ]
-                    for ref, start, height in pieces:
-                        shifted = column - start
+                    for turn, ref in enumerate(pieces[table]):
+                        shifted = column - (bal ^ turn) * part
                         hot = jnp.concatenate(
                             [
                                 jnp.where(shifted == lane + at, 1.0, 0.0).astype(bf16)
-                                for at in range(0, height, LANES)
+                                for at in range(0, part, LANES)
                             ],
                             axis=1,
                         )
@@ -186,30 +177,35 @@
     refs = list(refs)
     take = lambda count: [refs.pop(0) for _ in range(count)]
     block_refs = take(groups)
-    in_refs = take(bals)
-    out_refs = take(bals)
+    weight_refs = take(bals)
     (cot_ref,) = take(1)
     (layer_ref,) = take(1)
     grad_refs = take(groups)
     term_refs = take(bals)
-    (x_ref, w_in, w_out, cot_here, nt_ref, mt_ref, weights_ref, slope_ref, gate_ref, heads_ref, dsilu_ref, grads_ref, sems) = refs
+    (x_ref, w_in, w_out, nt_ref, mt_ref, weights_ref, slope_ref, gate_ref, heads_ref, dsilu_ref, grads_ref, sems) = refs
 
     scalars = Scalars(scalar_ref, bals, slots)
     bal, group_here, table_here = scalars.place()
-    rows, width = cot_here.shape
+    rows, width = cot_ref.shape
     slot_rows = rows // slots
     head_width = width // HEADS
     score_scale = head_width**-0.5
     piece = block_refs[0].shape[1]
-    part, features = in_refs[0].shape
+    part, features = weight_refs[0].shape[0], w_in.shape[1]
 
     in_copies, out_copies = [], []
     for turn in range(bals):
         at = pl.ds(pl.multiple_of((bal ^ turn) * part, part), part)
-        in_copies.append(pltpu.make_async_copy(in_refs[turn], w_in.at[at, :], sems.at[2 * turn]))
-        out_copies.append(pltpu.make_async_copy(out_refs[turn], w_out.at[at, :], sems.at[2 * turn + 1]))
-    cot_copy = pltpu.make_async_copy(cot_ref, cot_here, sems.at[2 * bals])
-    for copy in in_copies + out_copies + [cot_copy]:
+        here = weight_refs[turn]
+        in_copies.append(
+            pltpu.make_async_copy(here.at[:, pl.ds(0, features)], w_in.at[at, :], sems.at[2 * turn])
+        )
+        out_copies.append(
+            pltpu.make_async_copy(
+                here.at[:, pl.ds(features, width)], w_out.at[at, :], sems.at[2 * turn + 1]
+            )
+        )
+    for copy in in_copies + out_copies:
         copy.start()
 
     my_slot = scalars.surplus(bal)
@@ -268,11 +264,12 @@
     gate = gate_ref[...]
     mixed = normed_out * gate
     mt_ref[...] = jnp.transpose(mixed).astype(bf16)
-    for copy in out_copies + [cot_copy]:
+    for copy in out_copies:
         copy.wait()
     layer_ref[...] = (x + matmul(mixed.astype(bf16), w_out[...])).astype(bf16)
 
-    cot = cot_here[...]
+    wide_cot = cot_ref[...]
+    cot = wide_cot.astype(bf16)
     grad_mixed = matmul_nt(cot, w_out[...])
     grad_attended = norm_back(grad_mixed * gate, normed_out, out_inverse).astype(bf16)
     grads_ref[:, :width] = (grad_mixed * normed_out * dsilu_ref[:, :width]).astype(bf16)
@@ -312,7 +309,7 @@
         term_refs[turn][:, :features] = matmul(owner_order(nt_ref, turn), grads_ref[...]).astype(bf16)
 
     grad_normed = matmul_nt(grads_ref[...], w_in[...])
-    grad_rows = (cot.astype(f32) + norm_back(grad_normed, normed_in, in_inverse)).astype(bf16)
+    grad_rows = (wide_cot + norm_back(grad_normed, normed_in, in_inverse)).astype(bf16)
     for group in range(groups):
         x_ref[group] = grad_rows[:, group * piece : (group + 1) * piece]
     for step in range(groups):
@@ -381,10 +378,17 @@
     unit = weight_part // embs
     owned = unit % 16 == 0
     unit = unit if owned else 0
-    place = [index.reshape(1, 1).astype(jnp.int32) for index in (bal, group_here, table_here)]
-    scalars = [surplus_slot.T, helper_map.T, seq_lengths[:, 0, :].reshape(1, -1)] + place
-    scalars = jnp.concatenate(scalars, axis=1)
-    scalars = jnp.pad(scalars, ((0, 0), (0, LANES - scalars.shape[1])))
+    first = bals * (2 + slots)
+    lane = lax.broadcasted_iota(jnp.int32, (1, LANES), 1)
+    scalars = jnp.where(lane == first, bal, 0)
+    scalars = jnp.where(lane == first + 1, group_here, scalars)
+    scalars = jnp.where(lane == first + 2, table_here, scalars)
+    fields = [surplus_slot.T, helper_map.T] + [seq_lengths[index] for index in range(bals)]
+    at = 0
+    for field in fields:
+        width_here = field.shape[1]
+        scalars = scalars + jnp.pad(field, ((0, 0), (at, LANES - at - width_here)))
+        at += width_here
 
     share = lax.dynamic_slice_in_dim(embed_tables[0], bal * part, part, 0)
     fetched = [emb_swap(share, step * groups, embs) for step in range(1, tables)]
@@ -393,12 +397,15 @@
         jnp.transpose(after(item_ids[0], share)), table_here * groups * rows, groups * rows, 1
     )
     plane_ids = with_swapped(ids.reshape(tables, groups * slots, 1, slot_rows), bals)
-    sent = after(scalars, fetched[0])
+    wide_cot = cotangent[0].astype(f32)
+    sent = after(scalars, share, wide_cot)
     plane_scalars = [scalars] + [emb_swap(sent, step, embs) for step in range(1, groups)]
 
-    all_in = with_swapped(weight_in, bals)
-    all_out = with_swapped(weight_out, bals)
-    pieces = [embed_tables[0]] + [piece for one in fetched for piece in with_swapped(one, bals)]
+    fetched[0] = after(fetched[0], *plane_scalars[1:])
+    pieces = [piece for one in [share] + fetched for piece in with_swapped(one, bals)]
+
+    weights = jnp.concatenate([weight_in, weight_out], axis=1)
+    weights = with_swapped(weights, bals)
 
     found = pl.pallas_call(
         functools.partial(lookup_kernel, groups, slots, tables, bals),
@@ -417,13 +424,12 @@
         out_shape=[jax.ShapeDtypeStruct((rows, width), bf16)]
         + [jax.ShapeDtypeStruct((rows, columns), bf16)] * groups
         + [terms] * bals,
-        in_specs=[SMEM] + [VMEM] * groups + [HBM] * (2 * bals + 1),
+        in_specs=[SMEM] + [VMEM] * groups + [HBM] * bals + [VMEM],
         out_specs=[VMEM] * (1 + groups + bals),
         scratch_shapes=[
             pltpu.VMEM((groups, rows, columns), bf16),
             pltpu.VMEM((width, features), bf16),
             pltpu.VMEM((width, width), bf16),
-            pltpu.VMEM((rows, width), bf16),
             pltpu.VMEM((width, rows), bf16),
             pltpu.VMEM((width, rows), bf16),
             pltpu.VMEM((pairs, 2 * slot_rows, slot_rows), bf16),
@@ -432,11 +438,11 @@
             pltpu.VMEM((rows, features - width), bf16),
             pltpu.VMEM((rows, features), f32),
             pltpu.VMEM((rows, features), bf16),
-            pltpu.SemaphoreType.DMA((2 * bals + 1,)),
+            pltpu.SemaphoreType.DMA((2 * bals,)),
         ],
         cost_estimate=estimate(7),
         compiler_params=room(36),
-    )(scalars, *block, *all_in, *all_out, cotangent[0])
+    )(scalars, *block, *weights, wide_cot)
     layer_out, results = results[0], results[1:]
     grads, results = results[:groups], results[groups:]
 
@@ -446,8 +452,8 @@
     def to_plane(value):
         return [value] + [emb_swap(value, step, embs) for step in range(1, groups)]
 
+    plane_grads = [grads[0]] + [emb_swap(grads[step], step, embs) for step in range(1, groups)]
     total = over_cores(results)
-    plane_grads = [grads[0]] + [emb_swap(grads[step], step, embs) for step in range(1, groups)]
     sums = pl.pallas_call(
         functools.partial(scatter_kernel, groups, slots, bals),
         out_shape=[jax.ShapeDtypeStruct((tables, part, columns), bf16)] * bals,
@@ -461,19 +467,22 @@
     grad_scale = (rows * embs * bals) ** -0.5
     if owned:
         pieces = total.reshape(groups, weight_part // groups, features + width)
-        came = [after(emb_swap(pieces[step], step, embs), sums[0]) for step in range(1, groups)]
+        came = [emb_swap(pieces[step], step, embs) for step in range(1, groups)]
+        came = [after(value, *plane_grads[1:]) for value in came]
         mine = sum_rounded([pieces[0]] + came)
         mine = mine.reshape(tables, unit, features + width)
-        final = sum_rounded(
-            [mine[0]] + [emb_swap(mine[step], step * groups, embs) for step in range(1, tables)]
-        )
+        came = [emb_swap(mine[step], step * groups, embs) for step in range(1, tables)]
+        final = sum_rounded([mine[0]] + [after(value, sums[0]) for value in came])
         gathered = [final] + [emb_swap(final, step * groups, embs) for step in range(1, tables)]
         own_sums = after(own_sums, *gathered[1:])
         back = to_plane(jnp.concatenate(gathered, axis=0))
 
+    swapped = [emb_swap(own_sums[step], step * groups, embs) for step in range(1, tables)]
+    if owned:
+        swapped = [after(value, *back[1:]) for value in swapped]
     table_sum = own_sums[0].astype(f32)
-    for step in range(1, tables):
-        table_sum = table_sum + emb_swap(own_sums[step], step * groups, embs).astype(f32)
+    for value in swapped:
+        table_sum = table_sum + value.astype(f32)
     table_scale = (distinct / (bals * item_ids.shape[1])) ** 0.5
 
     if owned:

time: 113 us -> 113 us (level)
  waiting for transfers between devices: 52.1 us -> 49.1 us
    ppermute x27, waiting for transfers between devices: 47.7 us -> 44.5 us  [emb_swap(): return lax.ppermute(value, 'emb', [(i, i ^ step) for i in range(count)])]
    unnamed x1 -> x0, other arithmetic: 1.34 us -> none
    add x0 -> x1, other arithmetic: none -> 1.32 us  [on_device(): scalars = scalars + jnp.pad(field, ((0, 0), (at, LANES - at - width_here)))]
    dynamic_slice x1, local copies, waits for them, and re-layouts: 0.01 us -> 1.32 us  [on_device(): lax.dynamic_slice_in_dim(jnp.transpose(after(item_ids[0], share)), table_...]
    unnamed x11 -> x21, local copies, waits for them, and re-layouts: 3.37 us -> 3.72 us
  transfers between devices with their start and end apart: 35 -> 35, of which waited for: 21 -> 22; matrix products, arithmetic and copies ran while one was open for 4% -> 4% of each run, Pallas kernels for 6% -> 6%
where the time goes in v6:
time: 113 us
  waiting for transfers between devices  49.1 us (43%)
  starting transfers between devices  36.7 us (32%)
  Pallas kernels  16 us (14%)
  local copies, waits for them, and re-layouts  5.94 us (5%)
  other arithmetic  3.87 us (3%)
    ppermute x27, waiting for transfers between devices, emb_swap(): return lax.ppermute(value, 'emb', [(i, i ^ step) for i in range(count)])  44.5 us
    ppermute x27, starting transfers between devices, emb_swap(): return lax.ppermute(value, 'emb', [(i, i ^ step) for i in range(count)])  34.8 us
    pallas_call x1, Pallas kernels, on_device(): pl.pallas_call(functools.partial(layer_kernel, groups, slots, tables, bal...  6.67 us
    ppermute x8, waiting for transfers between devices, bal_swap(): return lax.ppermute(value, 'bal', [(i, i ^ step) for i in range(count)])  4.57 us
    pallas_call x1, Pallas kernels, on_device(): pl.pallas_call(functools.partial(lookup_kernel, groups, slots, tables, ba...  3.92 us
    unnamed x21, local copies, waits for them, and re-layouts  3.72 us
    pallas_call x1, Pallas kernels, on_device(): pl.pallas_call(functools.partial(scatter_kernel, groups, slots, bals), ou...  3.02 us
    pallas_call x1, Pallas kernels, on_device(): pl.pallas_call(functools.partial(place_kernel, grad_scale, groups, slots,...  2.42 us
  transfers between devices with their start and end apart: 35, of which 22 were waited for; matrix products, arithmetic and copies ran while one was open for 4% of the time, Pallas kernels for 6%

profile of v6, /device:TPU:0, one launch (start us, length us, event | category | flops | bytes accessed | tf_op | source)
XLA Modules:
  0.0 112.7 jit_solution(10001377785687354483)
XLA Ops:
  2.6 4.7 %collective-permute-start.9 = (bf16[512,128]{1,0:T(8,128)(2,1)S(1)}, bf16[512,128]{1,0:T(8,128)(2,1)}, u32[]{:S(2)}, u32[]{:S(2)}) collective-permute-start(bf16[512,128]{1,0:T(8,128)(2,1)S(1)} %dynamic-slice_bitcast_fusion.refs_6_), channel_id=1, source_target_pairs={{0,24},{2,26},{4,28},{6,30},{8,16},{10,18},{12,20},{14,22},{16,8},... | collective-permute-start | bytes 393224 | tf_op jit(solution)/shard_map/ppermute | solution.py:54
  10.3 2.6 %collective-permute-start.2 = (s32[1,128]{1,0:T(1,128)}, s32[1,128]{1,0:T(1,128)S(1)}, u32[]{:S(2)}, u32[]{:S(2)}) collective-permute-start(s32[1,128]{1,0:T(1,128)} %pad_add_fusion.refs_0_.scalar_ref), channel_id=1, source_target_pairs={{0,6},{2,4},{4,2},{6,0},{8,14},{10,12},{12,10},{14,8},{16,22},{18,... | collective-permute-start | bytes 1544 | tf_op jit(solution)/shard_map/ppermute | solution.py:54
  12.9 1.9 %collective-permute-done.2.refs_3_ = s32[1,128]{1,0:T(1,128)S(1)} collective-permute-done((s32[1,128]{1,0:T(1,128)}, s32[1,128]{1,0:T(1,128)S(1)}, u32[]{:S(2)}, u32[]{:S(2)}) %collective-permute-start.2) | collective-permute-done | bytes 544 | tf_op jit(solution)/shard_map/ppermute | solution.py:54
  15.3 1.7 %collective-permute-start.1 = (s32[1,128]{1,0:T(1,128)}, s32[1,128]{1,0:T(1,128)S(1)}, u32[]{:S(2)}, u32[]{:S(2)}) collective-permute-start(s32[1,128]{1,0:T(1,128)} %pad_add_fusion.refs_0_.scalar_ref), channel_id=1, source_target_pairs={{0,4},{2,6},{4,0},{6,2},{8,12},{10,14},{12,8},{14,10},{16,20},{18,... | collective-permute-start | bytes 1544 | tf_op jit(solution)/shard_map/ppermute | solution.py:54
  17.0 1.9 %collective-permute-done.1.refs_2_ = s32[1,128]{1,0:T(1,128)S(1)} collective-permute-done((s32[1,128]{1,0:T(1,128)}, s32[1,128]{1,0:T(1,128)S(1)}, u32[]{:S(2)}, u32[]{:S(2)}) %collective-permute-start.1) | collective-permute-done | bytes 544 | tf_op jit(solution)/shard_map/ppermute | solution.py:54
  19.4 1.6 %collective-permute-start = (s32[1,128]{1,0:T(1,128)}, s32[1,128]{1,0:T(1,128)}, u32[]{:S(2)}, u32[]{:S(2)}) collective-permute-start(s32[1,128]{1,0:T(1,128)} %pad_add_fusion.refs_0_.scalar_ref), channel_id=1, source_target_pairs={{0,2},{2,0},{4,6},{6,4},{8,10},{10,8},{12,14},{14,12},{16,18},{18,... | collective-permute-start | bytes 1544 | tf_op jit(solution)/shard_map/ppermute | solution.py:54
  27.3 3.9 %shard_map.111 = (bf16[256,128]{1,0:T(8,128)(2,1)S(1)}, bf16[256,128]{1,0:T(8,128)(2,1)S(1)}, bf16[256,128]{1,0:T(8,128)(2,1)S(1)}, bf16[256,128]{1,0:T(8,128)(2,1)S(1)}) custom-call(s32[1,128]{1,0:T(1,128)} %pad_add_fusion.refs_0_.scalar_ref, s32[1,128]{1,0:T(1,128)} %collective-permute-done.refs_1_, s32[1,128]{1,0:T(1,128)S(1)} %copy-done.5, ...), custom_call_target="tpu_custom_call" | custom-call | bytes 10500000 | tf_op jit(solution)/shard_map/pallas_call | solution.py:410
  37.1 2.4 %collective-permute-done.13.refs_3_ = bf16[256,128]{1,0:T(8,128)(2,1)S(1)} collective-permute-done((bf16[256,128]{1,0:T(8,128)(2,1)S(1)}, bf16[256,128]{1,0:T(8,128)(2,1)S(1)}, u32[]{:S(2)}, u32[]{:S(2)}) %collective-permute-start.13) | collective-permute-done | bytes 65568 | tf_op jit(solution)/shard_map/ppermute | solution.py:54
  39.5 6.7 %shard_map.112 = (bf16[256,512]{1,0:T(8,128)(2,1)}, bf16[256,128]{1,0:T(8,128)(2,1)S(1)}, bf16[256,128]{1,0:T(8,128)(2,1)S(1)}, bf16[256,128]{1,0:T(8,128)(2,1)S...) custom-call(s32[1,128]{1,0:T(1,128)} %pad_add_fusion.refs_0_.scalar_ref, ...), custom_call_target="tpu_custom_call" | custom-call | bytes 24500000 | tf_op jit(solution)/shard_map/pallas_call | solution.py:422
  46.2 3.0 %collective-permute-done.19 = bf16[256,2560]{1,0:T(8,128)(2,1)S(1)} collective-permute-done((bf16[256,2560]{1,0:T(8,128)(2,1)S(1)}, bf16[256,2560]{1,0:T(8,128)(2,1)S(1)}, u32[]{:S(2)}, u32[]{:S(2)}) %collective-permute-start.19) | collective-permute-done | bytes 1310752 | tf_op jit(solution)/shard_map/ppermute | solution.py:46
  54.3 13.7 %collective-permute-done.15.refs_7_ = bf16[256,128]{1,0:T(8,128)(2,1)S(1)} collective-permute-done((bf16[256,128]{1,0:T(8,128)(2,1)S(1)}, bf16[256,128]{1,0:T(8,128)(2,1)S(1)}, u32[]{:S(2)}, u32[]{:S(2)}) %collective-permute-start.15) | collective-permute-done | bytes 65568 | tf_op jit(solution)/shard_map/ppermute | solution.py:54
  69.4 3.8 %collective-permute-done.17.refs_9_ = bf16[256,128]{1,0:T(8,128)(2,1)S(1)} collective-permute-done((bf16[256,128]{1,0:T(8,128)(2,1)S(1)}, bf16[256,128]{1,0:T(8,128)(2,1)S(1)}, u32[]{:S(2)}, u32[]{:S(2)}) %collective-permute-start.17) | collective-permute-done | bytes 65568 | tf_op jit(solution)/shard_map/ppermute | solution.py:54
  74.7 2.4 %collective-permute-start.25 = (bf16[16,2560]{1,0:T(8,128)(2,1)S(1)}, bf16[16,2560]{1,0:T(8,128)(2,1)S(1)}, u32[]{:S(2)}, u32[]{:S(2)}) collective-permute-start(bf16[16,2560]{1,0:T(8,128)(2,1)S(1)} %get-tuple-element.67), channel_id=1, source_target_pairs={{0,24},{2,26},{4,28},{6,30},{8,16},{10,18},{12,20},{14,22},{16,8},... | collective-permute-start | bytes 245768 | tf_op jit(solution)/shard_map/ppermute | solution.py:54
  77.7 3.0 %shard_map.113 = (bf16[4,512,128]{2,1,0:T(8,128)(2,1)S(1)}, bf16[4,512,128]{2,1,0:T(8,128)(2,1)S(1)}) custom-call(s32[1,128]{1,0:T(1,128)} %pad_add_fusion.refs_0_.scalar_ref, s32[1,128]{1,0:T(1,128)} %collective-permute-done.refs_1_, s32[1,128]{1,0:T(1,128)S(1)} %copy-done.6, s32[1,128]{1,0:T(1,128)S(1)} %copy-done.3, ...), custom_call_target="tpu_custom_call" | custom-call | bytes 10500000 | tf_op jit(solution)/shard_map/pallas_call | solution.py:457
  81.4 2.4 %collective-permute-done.24 = bf16[16,2560]{1,0:T(8,128)(2,1)S(1)} collective-permute-done((bf16[16,2560]{1,0:T(8,128)(2,1)S(1)}, bf16[16,2560]{1,0:T(8,128)(2,1)S(1)}, u32[]{:S(2)}, u32[]{:S(2)}) %collective-permute-start.24) | collective-permute-done | bytes 81952 | tf_op jit(solution)/shard_map/ppermute | solution.py:54
  83.9 2.3 %collective-permute-start.28 = (bf16[16,2560]{1,0:T(8,128)(2,1)S(1)}, bf16[16,2560]{1,0:T(8,128)(2,1)S(1)}, u32[]{:S(2)}, u32[]{:S(2)}) collective-permute-start(bf16[16,2560]{1,0:T(8,128)(2,1)S(1)} %add_convert_fusion.3), channel_id=1, source_target_pairs={{0,24},{2,26},{4,28},{6,30},{8,16},{10,18},{12,20},{14,22},{16,8},... | collective-permute-start | bytes 245768 | tf_op jit(solution)/shard_map/ppermute | solution.py:54
  86.2 2.1 %collective-permute-start.26 = (bf16[16,2560]{1,0:T(8,128)(2,1)S(1)}, bf16[16,2560]{1,0:T(8,128)(2,1)S(1)}, u32[]{:S(2)}, u32[]{:S(2)}) collective-permute-start(bf16[16,2560]{1,0:T(8,128)(2,1)S(1)} %add_convert_fusion.3), channel_id=1, source_target_pairs={{0,8},{2,10},{4,12},{6,14},{8,0},{10,2},{12,4},{14,6},{16,24},{18,... | collective-permute-start | bytes 245768 | tf_op jit(solution)/shard_map/ppermute | solution.py:54
  88.5 2.1 %collective-permute-done.28 = bf16[16,2560]{1,0:T(8,128)(2,1)S(1)} collective-permute-done((bf16[16,2560]{1,0:T(8,128)(2,1)S(1)}, bf16[16,2560]{1,0:T(8,128)(2,1)S(1)}, u32[]{:S(2)}, u32[]{:S(2)}) %collective-permute-start.28) | collective-permute-done | bytes 81952 | tf_op jit(solution)/shard_map/ppermute | solution.py:54
  90.6 1.7 %collective-permute-done.27 = bf16[16,2560]{1,0:T(8,128)(2,1)S(1)} collective-permute-done((bf16[16,2560]{1,0:T(8,128)(2,1)S(1)}, bf16[16,2560]{1,0:T(8,128)(2,1)S(1)}, u32[]{:S(2)}, u32[]{:S(2)}) %collective-permute-start.27) | collective-permute-done | bytes 81952 | tf_op jit(solution)/shard_map/ppermute | solution.py:54
  96.4 2.2 %collective-permute-start.34 = (bf16[512,128]{1,0:T(8,128)(2,1)S(1)}, bf16[512,128]{1,0:T(8,128)(2,1)S(1)}, u32[]{:S(2)}, u32[]{:S(2)}) collective-permute-start(bf16[512,128]{1,0:T(8,128)(2,1)S(1)} %get-tuple-element.64), channel_id=1, source_target_pairs={{0,24},{2,26},{4,28},{6,30},{8,16},{10,18},{12,20},{14,22},{16,8},... | collective-permute-start | bytes 393224 | tf_op jit(solution)/shard_map/ppermute | solution.py:54
  98.7 4.5 %collective-permute-done.29 = bf16[512,128]{1,0:T(8,128)(2,1)S(1)} collective-permute-done((bf16[512,128]{1,0:T(8,128)(2,1)S(1)}, bf16[512,128]{1,0:T(8,128)(2,1)S(1)}, u32[]{:S(2)}, u32[]{:S(2)}) %collective-permute-start.29) | collective-permute-done | bytes 131104 | tf_op jit(solution)/shard_map/ppermute | solution.py:54
  103.9 2.9 %collective-permute-done.31.refs_2_ = bf16[64,2560]{1,0:T(8,128)(2,1)S(1)} collective-permute-done((bf16[64,2560]{1,0:T(8,128)(2,1)S(1)}, bf16[64,2560]{1,0:T(8,128)(2,1)S(1)}, u32[]{:S(2)}, u32[]{:S(2)}) %collective-permute-start.31) | collective-permute-done | bytes 327712 | tf_op jit(solution)/shard_map/ppermute | solution.py:54
  106.8 2.5 %collective-permute-done.33 = bf16[512,128]{1,0:T(8,128)(2,1)S(1)} collective-permute-done((bf16[512,128]{1,0:T(8,128)(2,1)S(1)}, bf16[512,128]{1,0:T(8,128)(2,1)S(1)}, u32[]{:S(2)}, u32[]{:S(2)}) %collective-permute-start.33) | collective-permute-done | bytes 131104 | tf_op jit(solution)/shard_map/ppermute | solution.py:54
  110.1 2.4 %shard_map.114 = (f32[256,2048]{1,0:T(8,128)}, f32[256,512]{1,0:T(8,128)}) custom-call(s32[1,128]{1,0:T(1,128)} %pad_add_fusion.refs_0_.scalar_ref, bf16[64,2560]{1,0:T(8,128)(2,1)S(1)} %pad_maximum_fusion.refs_0_, bf16[64,2560]{1,0:T(8,128)(2,1)S(1)} %collective-permute-done.30.refs_1_, bf16[64,2560]{1,0:T(8,128)(2,1)S(1)} %collective-permute-done.31.refs_2_, ...), custom_call_target="tpu_custom_call" | custom-call | bytes 7000000 | tf_op jit(solution)/shard_map/pallas_call | solution.py:489
  (87 shorter events, 32.9 us)
Async XLA Ops:
  2.1 37.4 %collective-permute-start.14 = (bf16[256,2560]{1,0:T(8,128)(2,1)S(1)}, bf16[256,2560]{1,0:T(8,128)(2,1)S(1)}, u32[]{:S(2)}, u32[]{:S(2)}) collective-permute-start(bf16[256,2560]{1,0:T(8,128)(2,1)S(1)} %constant_dynamic-update-slice_fusion.refs_4_), channel_id=1, source_target_pairs={{0,1},{1,0},{2,3},{3,2},{4,5},{5,4},{6,7},{7,6},{8,9},{9,8},{10,11... | collective-permute-start | bytes 3932168 | tf_op jit(solution)/shard_map/ppermute | solution.py:46
  2.6 21.1 %collective-permute-start.9 = (bf16[512,128]{1,0:T(8,128)(2,1)S(1)}, bf16[512,128]{1,0:T(8,128)(2,1)}, u32[]{:S(2)}, u32[]{:S(2)}) collective-permute-start(bf16[512,128]{1,0:T(8,128)(2,1)S(1)} %dynamic-slice_bitcast_fusion.refs_6_), channel_id=1, source_target_pairs={{0,24},{2,26},{4,28},{6,30},{8,16},{10,18},{12,20},{14,22},{16,8},... | collective-permute-start | bytes 393224 | tf_op jit(solution)/shard_map/ppermute | solution.py:54
  7.3 16.5 %collective-permute-start.7 = (bf16[512,128]{1,0:T(8,128)(2,1)S(1)}, bf16[512,128]{1,0:T(8,128)(2,1)}, u32[]{:S(2)}, u32[]{:S(2)}) collective-permute-start(bf16[512,128]{1,0:T(8,128)(2,1)S(1)} %dynamic-slice_bitcast_fusion.refs_6_), channel_id=1, source_target_pairs={{0,16},{2,18},{4,20},{6,22},{8,24},{10,26},{12,28},{14,30},{16,0},... | collective-permute-start | bytes 393224 | tf_op jit(solution)/shard_map/ppermute | solution.py:54
  7.3 15.9 %collective-permute-start.5 = (bf16[512,128]{1,0:T(8,128)(2,1)S(1)}, bf16[512,128]{1,0:T(8,128)(2,1)}, u32[]{:S(2)}, u32[]{:S(2)}) collective-permute-start(bf16[512,128]{1,0:T(8,128)(2,1)S(1)} %dynamic-slice_bitcast_fusion.refs_6_), channel_id=1, source_target_pairs={{0,8},{2,10},{4,12},{6,14},{8,0},{10,2},{12,4},{14,6},{16,24},{18,... | collective-permute-start | bytes 393224 | tf_op jit(solution)/shard_map/ppermute | solution.py:54
  34.3 5.2 %collective-permute-start.13 = (bf16[256,128]{1,0:T(8,128)(2,1)S(1)}, bf16[256,128]{1,0:T(8,128)(2,1)S(1)}, u32[]{:S(2)}, u32[]{:S(2)}) collective-permute-start(bf16[256,128]{1,0:T(8,128)(2,1)S(1)} %get-tuple-element.38), channel_id=1, source_target_pairs={{0,6},{2,4},{4,2},{6,0},{8,14},{10,12},{12,10},{14,8},{16,22},{18,... | collective-permute-start | bytes 196616 | tf_op jit(solution)/shard_map/ppermute | solution.py:54
  49.7 23.5 %collective-permute-start.20 = (bf16[64,2560]{1,0:T(8,128)(2,1)S(1)}, bf16[64,2560]{1,0:T(8,128)(2,1)S(1)}, u32[]{:S(2)}, u32[]{:S(2)}) collective-permute-start(bf16[64,2560]{1,0:T(8,128)(2,1)S(1)} %get-tuple-element.60), channel_id=1, source_target_pairs={{0,2},{2,0},{4,6},{6,4},{8,10},{10,8},{12,14},{14,12},{16,18},{18,... | collective-permute-start | bytes 983048 | tf_op jit(solution)/shard_map/ppermute | solution.py:54
  50.3 22.9 %collective-permute-start.22 = (bf16[64,2560]{1,0:T(8,128)(2,1)S(1)}, bf16[64,2560]{1,0:T(8,128)(2,1)S(1)}, u32[]{:S(2)}, u32[]{:S(2)}) collective-permute-start(bf16[64,2560]{1,0:T(8,128)(2,1)S(1)} %get-tuple-element.61), channel_id=1, source_target_pairs={{0,6},{2,4},{4,2},{6,0},{8,14},{10,12},{12,10},{14,8},{16,22},{18,... | collective-permute-start | bytes 983048 | tf_op jit(solution)/shard_map/ppermute | solution.py:54
  51.8 21.4 %collective-permute-start.21 = (bf16[64,2560]{1,0:T(8,128)(2,1)S(1)}, bf16[64,2560]{1,0:T(8,128)(2,1)S(1)}, u32[]{:S(2)}, u32[]{:S(2)}) collective-permute-start(bf16[64,2560]{1,0:T(8,128)(2,1)S(1)} %get-tuple-element.62), channel_id=1, source_target_pairs={{0,4},{2,6},{4,0},{6,2},{8,12},{10,14},{12,8},{14,10},{16,20},{18,... | collective-permute-start | bytes 983048 | tf_op jit(solution)/shard_map/ppermute | solution.py:54
  53.3 14.7 %collective-permute-start.15 = (bf16[256,128]{1,0:T(8,128)(2,1)S(1)}, bf16[256,128]{1,0:T(8,128)(2,1)S(1)}, u32[]{:S(2)}, u32[]{:S(2)}) collective-permute-start(bf16[256,128]{1,0:T(8,128)(2,1)S(1)} %get-tuple-element.41), channel_id=1, source_target_pairs={{0,2},{2,0},{4,6},{6,4},{8,10},{10,8},{12,14},{14,12},{16,18},{18,... | collective-permute-start | bytes 196616 | tf_op jit(solution)/shard_map/ppermute | solution.py:54
  53.8 15.6 %collective-permute-start.16 = (bf16[256,128]{1,0:T(8,128)(2,1)S(1)}, bf16[256,128]{1,0:T(8,128)(2,1)S(1)}, u32[]{:S(2)}, u32[]{:S(2)}) collective-permute-start(bf16[256,128]{1,0:T(8,128)(2,1)S(1)} %get-tuple-element.42), channel_id=1, source_target_pairs={{0,4},{2,6},{4,0},{6,2},{8,12},{10,14},{12,8},{14,10},{16,20},{18,... | collective-permute-start | bytes 196616 | tf_op jit(solution)/shard_map/ppermute | solution.py:54
  68.0 5.2 %collective-permute-start.17 = (bf16[256,128]{1,0:T(8,128)(2,1)S(1)}, bf16[256,128]{1,0:T(8,128)(2,1)S(1)}, u32[]{:S(2)}, u32[]{:S(2)}) collective-permute-start(bf16[256,128]{1,0:T(8,128)(2,1)S(1)} %get-tuple-element.43), channel_id=1, source_target_pairs={{0,6},{2,4},{4,2},{6,0},{8,14},{10,12},{12,10},{14,8},{16,22},{18,... | collective-permute-start | bytes 196616 | tf_op jit(solution)/shard_map/ppermute | solution.py:54
  73.4 7.3 %collective-permute-start.23 = (bf16[16,2560]{1,0:T(8,128)(2,1)S(1)}, bf16[16,2560]{1,0:T(8,128)(2,1)S(1)}, u32[]{:S(2)}, u32[]{:S(2)}) collective-permute-start(bf16[16,2560]{1,0:T(8,128)(2,1)S(1)} %get-tuple-element.66), channel_id=1, source_target_pairs={{0,8},{2,10},{4,12},{6,14},{8,0},{10,2},{12,4},{14,6},{16,24},{18,... | collective-permute-start | bytes 245768 | tf_op jit(solution)/shard_map/ppermute | solution.py:54
  74.7 6.6 %collective-permute-start.25 = (bf16[16,2560]{1,0:T(8,128)(2,1)S(1)}, bf16[16,2560]{1,0:T(8,128)(2,1)S(1)}, u32[]{:S(2)}, u32[]{:S(2)}) collective-permute-start(bf16[16,2560]{1,0:T(8,128)(2,1)S(1)} %get-tuple-element.67), channel_id=1, source_target_pairs={{0,24},{2,26},{4,28},{6,30},{8,16},{10,18},{12,20},{14,22},{16,8},... | collective-permute-start | bytes 245768 | tf_op jit(solution)/shard_map/ppermute | solution.py:54
  77.2 6.6 %collective-permute-start.24 = (bf16[16,2560]{1,0:T(8,128)(2,1)S(1)}, bf16[16,2560]{1,0:T(8,128)(2,1)S(1)}, u32[]{:S(2)}, u32[]{:S(2)}) collective-permute-start(bf16[16,2560]{1,0:T(8,128)(2,1)S(1)} %get-tuple-element.68), channel_id=1, source_target_pairs={{0,16},{2,18},{4,20},{6,22},{8,24},{10,26},{12,28},{14,30},{16,0},... | collective-permute-start | bytes 245768 | tf_op jit(solution)/shard_map/ppermute | solution.py:54
  80.7 7.6 %collective-permute-start.18 = (bf16[4,512,128]{2,1,0:T(8,128)(2,1)S(1)}, bf16[4,512,128]{2,1,0:T(8,128)(2,1)S(1)}, u32[]{:S(2)}, u32[]{:S(2)}) collective-permute-start(bf16[4,512,128]{2,1,0:T(8,128)(2,1)S(1)} %get-tuple-element.45), channel_id=1, source_target_pairs={{0,1},{1,0},{2,3},{3,2},{4,5},{5,4},{6,7},{7,6},{8,9},{9,8},{10,11... | collective-permute-start | bytes 1572872 | tf_op jit(solution)/shard_map/ppermute | solution.py:46
  83.9 6.7 %collective-permute-start.28 = (bf16[16,2560]{1,0:T(8,128)(2,1)S(1)}, bf16[16,2560]{1,0:T(8,128)(2,1)S(1)}, u32[]{:S(2)}, u32[]{:S(2)}) collective-permute-start(bf16[16,2560]{1,0:T(8,128)(2,1)S(1)} %add_convert_fusion.3), channel_id=1, source_target_pairs={{0,24},{2,26},{4,28},{6,30},{8,16},{10,18},{12,20},{14,22},{16,8},... | collective-permute-start | bytes 245768 | tf_op jit(solution)/shard_map/ppermute | solution.py:54
  86.2 6.1 %collective-permute-start.27 = (bf16[16,2560]{1,0:T(8,128)(2,1)S(1)}, bf16[16,2560]{1,0:T(8,128)(2,1)S(1)}, u32[]{:S(2)}, u32[]{:S(2)}) collective-permute-start(bf16[16,2560]{1,0:T(8,128)(2,1)S(1)} %add_convert_fusion.3), channel_id=1, source_target_pairs={{0,16},{2,18},{4,20},{6,22},{8,24},{10,26},{12,28},{14,30},{16,0},... | collective-permute-start | bytes 245768 | tf_op jit(solution)/shard_map/ppermute | solution.py:54
  86.2 6.1 %collective-permute-start.26 = (bf16[16,2560]{1,0:T(8,128)(2,1)S(1)}, bf16[16,2560]{1,0:T(8,128)(2,1)S(1)}, u32[]{:S(2)}, u32[]{:S(2)}) collective-permute-start(bf16[16,2560]{1,0:T(8,128)(2,1)S(1)} %add_convert_fusion.3), channel_id=1, source_target_pairs={{0,8},{2,10},{4,12},{6,14},{8,0},{10,2},{12,4},{14,6},{16,24},{18,... | collective-permute-start | bytes 245768 | tf_op jit(solution)/shard_map/ppermute | solution.py:54
  92.3 11.6 %collective-permute-start.32 = (bf16[64,2560]{1,0:T(8,128)(2,1)S(1)}, bf16[64,2560]{1,0:T(8,128)(2,1)S(1)}, u32[]{:S(2)}, u32[]{:S(2)}) collective-permute-start(bf16[64,2560]{1,0:T(8,128)(2,1)S(1)} %pad_maximum_fusion.refs_0_), channel_id=1, source_target_pairs={{0,6},{2,4},{4,2},{6,0},{8,14},{10,12},{12,10},{14,8},{16,22},{18,... | collective-permute-start | bytes 983048 | tf_op jit(solution)/shard_map/ppermute | solution.py:54
  92.8 14.0 %collective-permute-start.31 = (bf16[64,2560]{1,0:T(8,128)(2,1)S(1)}, bf16[64,2560]{1,0:T(8,128)(2,1)S(1)}, u32[]{:S(2)}, u32[]{:S(2)}) collective-permute-start(bf16[64,2560]{1,0:T(8,128)(2,1)S(1)} %pad_maximum_fusion.refs_0_), channel_id=1, source_target_pairs={{0,4},{2,6},{4,0},{6,2},{8,12},{10,14},{12,8},{14,10},{16,20},{18,... | collective-permute-start | bytes 983048 | tf_op jit(solution)/shard_map/ppermute | solution.py:54
  94.3 12.5 %collective-permute-start.30 = (bf16[64,2560]{1,0:T(8,128)(2,1)S(1)}, bf16[64,2560]{1,0:T(8,128)(2,1)S(1)}, u32[]{:S(2)}, u32[]{:S(2)}) collective-permute-start(bf16[64,2560]{1,0:T(8,128)(2,1)S(1)} %pad_maximum_fusion.refs_0_), channel_id=1, source_target_pairs={{0,2},{2,0},{4,6},{6,4},{8,10},{10,8},{12,14},{14,12},{16,18},{18,... | collective-permute-start | bytes 983048 | tf_op jit(solution)/shard_map/ppermute | solution.py:54
  95.9 7.3 %collective-permute-start.29 = (bf16[512,128]{1,0:T(8,128)(2,1)S(1)}, bf16[512,128]{1,0:T(8,128)(2,1)S(1)}, u32[]{:S(2)}, u32[]{:S(2)}) collective-permute-start(bf16[512,128]{1,0:T(8,128)(2,1)S(1)} %get-tuple-element.63), channel_id=1, source_target_pairs={{0,8},{2,10},{4,12},{6,14},{8,0},{10,2},{12,4},{14,6},{16,24},{18,... | collective-permute-start | bytes 393224 | tf_op jit(solution)/shard_map/ppermute | solution.py:54
  96.4 10.4 %collective-permute-start.34 = (bf16[512,128]{1,0:T(8,128)(2,1)S(1)}, bf16[512,128]{1,0:T(8,128)(2,1)S(1)}, u32[]{:S(2)}, u32[]{:S(2)}) collective-permute-start(bf16[512,128]{1,0:T(8,128)(2,1)S(1)} %get-tuple-element.64), channel_id=1, source_target_pairs={{0,24},{2,26},{4,28},{6,30},{8,16},{10,18},{12,20},{14,22},{16,8},... | collective-permute-start | bytes 393224 | tf_op jit(solution)/shard_map/ppermute | solution.py:54
  103.2 6.1 %collective-permute-start.33 = (bf16[512,128]{1,0:T(8,128)(2,1)S(1)}, bf16[512,128]{1,0:T(8,128)(2,1)S(1)}, u32[]{:S(2)}, u32[]{:S(2)}) collective-permute-start(bf16[512,128]{1,0:T(8,128)(2,1)S(1)} %get-tuple-element.65), channel_id=1, source_target_pairs={{0,16},{2,18},{4,20},{6,22},{8,24},{10,26},{12,28},{14,30},{16,0},... | collective-permute-start | bytes 393224 | tf_op jit(solution)/shard_map/ppermute | solution.py:54
  (21 other events, 106.8 us)

commit v7 on v6

--- a/solution.py
+++ b/solution.py
@@ -55,24 +55,24 @@
 
 
 class Scalars:
-    def __init__(self, ref, bals, slots):
-        self.ref, self.bals, self.slots = ref, bals, slots
+    def __init__(self, ref, step, bals, slots):
+        self.ref, self.step, self.bals, self.slots = ref, step, bals, slots
 
     def surplus(self, bal):
-        return self.ref[0, bal]
+        return self.ref[self.step, bal]
 
     def source(self, bal):
         found = jnp.int32(0)
         for index in range(self.bals):
-            found = found + jnp.where(self.ref[0, self.bals + index] == bal, index, 0)
+            found = found + jnp.where(self.ref[self.step, self.bals + index] == bal, index, 0)
         return found
 
     def length(self, bal, slot):
-        return self.ref[0, 2 * self.bals + bal * self.slots + slot]
+        return self.ref[self.step, 2 * self.bals + bal * self.slots + slot]
 
     def place(self):
         first = self.bals * (2 + self.slots)
-        return self.ref[0, first], self.ref[0, first + 1], self.ref[0, first + 2]
+        return self.ref[self.step, first], self.ref[self.step, first + 1], self.ref[self.step, first + 2]
 
 
 def pick_ids(scalars, ids_refs, slots, tables):
@@ -103,7 +103,8 @@
 def lookup_kernel(groups, slots, tables, bals, *refs):
     refs = list(refs)
     take = lambda count: [refs.pop(0) for _ in range(count)]
-    scalars = [Scalars(ref, bals, slots) for ref in take(groups)]
+    (scalar_ref,) = take(1)
+    scalars = [Scalars(scalar_ref, step, bals, slots) for step in range(groups)]
     ids_refs = take(bals)
     pieces = [take(bals) for _ in range(tables)]
     out_refs = refs
@@ -136,7 +137,8 @@
 def scatter_kernel(groups, slots, bals, *refs):
     refs = list(refs)
     take = lambda count: [refs.pop(0) for _ in range(count)]
-    scalars = [Scalars(ref, bals, slots) for ref in take(groups)]
+    (scalar_ref,) = take(1)
+    scalars = [Scalars(scalar_ref, step, bals, slots) for step in range(groups)]
     ids_refs, grad_refs, out_refs = take(bals), take(groups), refs
     bal, _, table_here = scalars[0].place()
     tables, part, _ = out_refs[0].shape
@@ -144,7 +146,14 @@
     height = min(part, 256)
     iota = lax.broadcasted_iota(jnp.int32, (height, slot_rows), 0)
     ids = pick_ids(scalars, ids_refs, slots, table_order(table_here, tables))
-    grads = jnp.concatenate([ref[...] for ref in grad_refs], axis=0)
+    columns = out_refs[0].shape[2]
+
+    def rows_of(ref):
+        height = ref.shape[0]
+        first = ref.shape[1] - slots * slot_rows // height * columns
+        return [ref[:, at : at + columns] for at in range(first, ref.shape[1], columns)]
+
+    grads = jnp.concatenate([piece for ref in grad_refs for piece in rows_of(ref)], axis=0)
     for table in range(tables):
         for turn in range(bals):
             for at in range(0, part, height):
@@ -184,7 +193,7 @@
     term_refs = take(bals)
     (x_ref, w_in, w_out, nt_ref, mt_ref, weights_ref, slope_ref, gate_ref, heads_ref, dsilu_ref, grads_ref, sems) = refs
 
-    scalars = Scalars(scalar_ref, bals, slots)
+    scalars = Scalars(scalar_ref, 0, bals, slots)
     bal, group_here, table_here = scalars.place()
     rows, width = cot_ref.shape
     slot_rows = rows // slots
@@ -316,10 +325,30 @@
         grad_refs[step][...] = x_ref[group_here ^ step]
 
 
+def pieces_kernel(bals, *refs):
+    count = len(refs) - bals
+    groups = (count + 1) // 2
+    term_refs, grad_refs = refs[:bals], refs[bals : bals + groups - 1]
+    out_refs = refs[bals + groups - 1 :]
+    height, width = out_refs[0].shape
+    for step, out in enumerate(out_refs):
+        rows = slice(step * height, (step + 1) * height)
+        total = term_refs[0][rows, :].astype(f32)
+        for ref in term_refs[1:]:
+            total = total + ref[rows, :].astype(f32)
+        out[:, :width] = total.astype(bf16)
+        if step:
+            grad = grad_refs[step - 1]
+            columns = grad.shape[1]
+            for index in range(grad.shape[0] // height):
+                at = width + index * columns
+                out[:, at : at + columns] = grad[index * height : (index + 1) * height, :]
+
+
 def place_kernel(scale, groups, slots, tables, bals, unit, scalar_ref, *refs):
     pieces = refs[:groups]
     in_ref, out_ref, scaled_ref, sems = refs[groups:]
-    _, group_here, table_here = Scalars(scalar_ref, bals, slots).place()
+    _, group_here, table_here = Scalars(scalar_ref, 0, bals, slots).place()
     features = in_ref.shape[1]
     copies = []
     for group_step, piece in enumerate(pieces):
@@ -398,23 +427,23 @@
     )
     plane_ids = with_swapped(ids.reshape(tables, groups * slots, 1, slot_rows), bals)
     wide_cot = cotangent[0].astype(f32)
-    sent = after(scalars, share, wide_cot)
-    plane_scalars = [scalars] + [emb_swap(sent, step, embs) for step in range(1, groups)]
-
-    fetched[0] = after(fetched[0], *plane_scalars[1:])
+    scalars = after(scalars, share, wide_cot)
+    for bit in range((groups - 1).bit_length()):
+        scalars = jnp.concatenate([scalars, emb_swap(scalars, 1 << bit, embs)], axis=0)
+
+    fetched[0] = after(fetched[0], scalars)
     pieces = [piece for one in [share] + fetched for piece in with_swapped(one, bals)]
-
-    weights = jnp.concatenate([weight_in, weight_out], axis=1)
-    weights = with_swapped(weights, bals)
 
     found = pl.pallas_call(
         functools.partial(lookup_kernel, groups, slots, tables, bals),
         out_shape=[jax.ShapeDtypeStruct((rows, columns), bf16)] * groups,
-        in_specs=[SMEM] * groups + [VMEM] * (bals + len(pieces)),
+        in_specs=[SMEM] + [VMEM] * (bals + len(pieces)),
         out_specs=[VMEM] * groups,
         cost_estimate=estimate(3),
         compiler_params=room(16),
-    )(*plane_scalars, *plane_ids, *pieces)
+    )(scalars, *plane_ids, *pieces)
+    weights = jnp.concatenate([weight_in, weight_out], axis=1)
+    weights = with_swapped(after(weights, found[0]), bals)
     block = [found[0]] + [emb_swap(found[step], step, embs) for step in range(1, groups)]
 
     pairs = slots * HEADS // 2
@@ -452,34 +481,44 @@
     def to_plane(value):
         return [value] + [emb_swap(value, step, embs) for step in range(1, groups)]
 
-    plane_grads = [grads[0]] + [emb_swap(grads[step], step, embs) for step in range(1, groups)]
-    total = over_cores(results)
-    sums = pl.pallas_call(
-        functools.partial(scatter_kernel, groups, slots, bals),
-        out_shape=[jax.ShapeDtypeStruct((tables, part, columns), bf16)] * bals,
-        in_specs=[SMEM] * groups + [VMEM] * (bals + groups),
-        out_specs=[VMEM] * bals,
-        cost_estimate=estimate(3),
-        compiler_params=room(16),
-    )(*plane_scalars, *plane_ids, *plane_grads)
-    own_sums = over_cores(sums)
+    def table_sums(plane_grads):
+        return pl.pallas_call(
+            functools.partial(scatter_kernel, groups, slots, bals),
+            out_shape=[jax.ShapeDtypeStruct((tables, part, columns), bf16)] * bals,
+            in_specs=[SMEM] + [VMEM] * (bals + groups),
+            out_specs=[VMEM] * bals,
+            cost_estimate=estimate(3),
+            compiler_params=room(16),
+        )(scalars, *plane_ids, *plane_grads)
 
     grad_scale = (rows * embs * bals) ** -0.5
     if owned:
-        pieces = total.reshape(groups, weight_part // groups, features + width)
+        height, wide = weight_part // groups, features + width
+        terms = [results[0]] + [bal_swap(results[turn], turn, bals) for turn in range(1, bals)]
+        pieces = pl.pallas_call(
+            functools.partial(pieces_kernel, bals),
+            out_shape=[jax.ShapeDtypeStruct((height, wide), bf16)]
+            + [jax.ShapeDtypeStruct((height, wide + rows // height * columns), bf16)] * (groups - 1),
+            in_specs=[VMEM] * (bals + groups - 1),
+            out_specs=[VMEM] * groups,
+            compiler_params=room(12),
+        )(*terms, *grads[1:])
         came = [emb_swap(pieces[step], step, embs) for step in range(1, groups)]
-        came = [after(value, *plane_grads[1:]) for value in came]
-        mine = sum_rounded([pieces[0]] + came)
-        mine = mine.reshape(tables, unit, features + width)
+        mine = sum_rounded([pieces[0]] + [value[:, :wide] for value in came])
+        mine = mine.reshape(tables, unit, wide)
+        sums = table_sums([grads[0]] + came)
+        own_sums = over_cores(sums)
         came = [emb_swap(mine[step], step * groups, embs) for step in range(1, tables)]
-        final = sum_rounded([mine[0]] + [after(value, sums[0]) for value in came])
+        final = sum_rounded([mine[0]] + came)
         gathered = [final] + [emb_swap(final, step * groups, embs) for step in range(1, tables)]
-        own_sums = after(own_sums, *gathered[1:])
         back = to_plane(jnp.concatenate(gathered, axis=0))
-
-    swapped = [emb_swap(own_sums[step], step * groups, embs) for step in range(1, tables)]
-    if owned:
+        later = after(own_sums, *gathered[1:])
+        swapped = [emb_swap(later[step], step * groups, embs) for step in range(1, tables)]
         swapped = [after(value, *back[1:]) for value in swapped]
+    else:
+        sums = table_sums([grads[0]] + [emb_swap(grads[step], step, embs) for step in range(1, groups)])
+        own_sums = over_cores(sums)
+        swapped = [emb_swap(own_sums[step], step * groups, embs) for step in range(1, tables)]
     table_sum = own_sums[0].astype(f32)
     for value in swapped:
         table_sum = table_sum + value.astype(f32)
@@ -502,7 +541,7 @@
             compiler_params=room(12),
         )(scalars, *back)
     else:
-        total = lax.psum(total.astype(f32), "emb") * grad_scale
+        total = lax.psum(over_cores(results).astype(f32), "emb") * grad_scale
         total_in, total_out = total[:, :features], total[:, features:]
 
     return layer_out[None], (table_sum * table_scale)[None], total_in, total_out

time: 113 us -> 102 us (0.903)
  starting transfers between devices: 36.7 us -> 32.7 us
  local copies, waits for them, and re-layouts: 5.94 us -> 2.42 us
  waiting for transfers between devices: 49.1 us -> 46.3 us
    ppermute x27 -> x23, starting transfers between devices: 34.8 us -> 31.3 us  [emb_swap(): return lax.ppermute(value, 'emb', [(i, i ^ step) for i in range(count)])]
    unnamed x21 -> x4, local copies, waits for them, and re-layouts: 3.72 us -> 0.94 us
    ppermute x8, waiting for transfers between devices: 4.57 us -> 3.06 us  [bal_swap(): return lax.ppermute(value, 'bal', [(i, i ^ step) for i in range(count)])]
    ppermute x27 -> x23, waiting for transfers between devices: 44.5 us -> 43.3 us  [emb_swap(): return lax.ppermute(value, 'emb', [(i, i ^ step) for i in range(count)])]
    pallas_call x1 -> x2, Pallas kernels: 3.02 us -> 3.21 us  [the longest x1 2.91 us: table_sums(): pl.pallas_call(functools.partial(scatter_kernel, groups, slots, bals), ou...]
  transfers between devices with their start and end apart: 35 -> 31, of which waited for: 22 -> 15; matrix products, arithmetic and copies ran while one was open for 4% -> 4% of each run, Pallas kernels for 6% -> 5%
where the time goes in v7:
time: 102 us
  waiting for transfers between devices  46.3 us (45%)
  starting transfers between devices  32.7 us (32%)
  Pallas kernels  15.6 us (15%)
  other arithmetic  3.96 us (4%)
  local copies, waits for them, and re-layouts  2.42 us (2%)
    ppermute x23, waiting for transfers between devices, emb_swap(): return lax.ppermute(value, 'emb', [(i, i ^ step) for i in range(count)])  43.3 us
    ppermute x23, starting transfers between devices, emb_swap(): return lax.ppermute(value, 'emb', [(i, i ^ step) for i in range(count)])  31.3 us
    pallas_call x1, Pallas kernels, on_device(): pl.pallas_call(functools.partial(layer_kernel, groups, slots, tables, bal...  6.56 us
    pallas_call x1, Pallas kernels, on_device(): pl.pallas_call(functools.partial(lookup_kernel, groups, slots, tables, ba...  3.46 us
    ppermute x8, waiting for transfers between devices, bal_swap(): return lax.ppermute(value, 'bal', [(i, i ^ step) for i in range(count)])  3.06 us
    pallas_call x1, Pallas kernels, table_sums(): pl.pallas_call(functools.partial(scatter_kernel, groups, slots, bals), ou...  2.91 us
    pallas_call x1, Pallas kernels, on_device(): pl.pallas_call(functools.partial(place_kernel, grad_scale, groups, slots,...  2.32 us
  transfers between devices with their start and end apart: 31, of which 15 were waited for; matrix products, arithmetic and copies ran while one was open for 4% of the time, Pallas kernels for 5%

profile of v7, /device:TPU:0, one launch (start us, length us, event | category | flops | bytes accessed | tf_op | source)
XLA Modules:
  0.0 101.8 jit_solution(14917928180025336567)
XLA Ops:
  1.6 5.1 %collective-permute-start.8 = (bf16[512,128]{1,0:T(8,128)(2,1)S(1)}, bf16[512,128]{1,0:T(8,128)(2,1)S(1)}, u32[]{:S(2)}, u32[]{:S(2)}) collective-permute-start(bf16[512,128]{1,0:T(8,128)(2,1)S(1)} %dynamic-slice_bitcast_fusion.refs_3_), channel_id=1, source_target_pairs={{0,24},{2,26},{4,28},{6,30},{8,16},{10,18},{12,20},{14,22},{16,8},... | collective-permute-start | bytes 393224 | tf_op jit(solution)/shard_map/ppermute | solution.py:54
  9.8 1.6 %collective-permute-start = (s32[1,128]{1,0:T(1,128)S(1)}, s32[1,128]{1,0:T(1,128)S(1)}, u32[]{:S(2)}, u32[]{:S(2)}) collective-permute-start(s32[1,128]{1,0:T(1,128)S(1)} %pad_add_fusion.2), channel_id=1, source_target_pairs={{0,2},{2,0},{4,6},{6,4},{8,10},{10,8},{12,14},{14,12},{16,18},{18,... | collective-permute-start | bytes 1544 | tf_op jit(solution)/shard_map/ppermute | solution.py:54
  11.4 1.9 %collective-permute-done = s32[1,128]{1,0:T(1,128)S(1)} collective-permute-done((s32[1,128]{1,0:T(1,128)S(1)}, s32[1,128]{1,0:T(1,128)S(1)}, u32[]{:S(2)}, u32[]{:S(2)}) %collective-permute-start) | collective-permute-done | bytes 544 | tf_op jit(solution)/shard_map/ppermute | solution.py:54
  13.4 1.7 %collective-permute-start.1 = (s32[2,128]{1,0:T(2,128)S(1)}, s32[2,128]{1,0:T(2,128)S(1)}, u32[]{:S(2)}, u32[]{:S(2)}) collective-permute-start(s32[2,128]{1,0:T(2,128)S(1)} %pad_add_fusion.1), channel_id=1, source_target_pairs={{0,4},{2,6},{4,0},{6,2},{8,12},{10,14},{12,8},{14,10},{16,20},{18,... | collective-permute-start | bytes 3080 | tf_op jit(solution)/shard_map/ppermute | solution.py:54
  19.1 3.5 %shard_map.111 = (bf16[256,128]{1,0:T(8,128)(2,1)S(1)}, bf16[256,128]{1,0:T(8,128)(2,1)S(1)}, bf16[256,128]{1,0:T(8,128)(2,1)S(1)}, bf16[256,128]{1,0:T(8,128)(2,1)S(1)}) custom-call(s32[4,128]{1,0:T(4,128)S(1)} %pad_add_fusion.refs_0_.scalar_ref, s32[4,8,1,128]{3,2,1,0:T(1,128)S(1)} %reshape.61.refs_1_, ...), custom_call_target="tpu_custom_call" | custom-call | bytes 10500000 | tf_op jit(solution)/shard_map/pallas_call | solution.py:437
  22.9 1.6 %collective-permute-start.10 = (bf16[256,128]{1,0:T(8,128)(2,1)S(1)}, bf16[256,128]{1,0:T(8,128)(2,1)S(1)}, u32[]{:S(2)}, u32[]{:S(2)}) collective-permute-start(bf16[256,128]{1,0:T(8,128)(2,1)S(1)} %get-tuple-element.35), channel_id=1, source_target_pairs={{0,2},{2,0},{4,6},{6,4},{8,10},{10,8},{12,14},{14,12},{16,18},{18,... | collective-permute-start | bytes 196616 | tf_op jit(solution)/shard_map/ppermute | solution.py:54
  27.2 1.6 %collective-permute-done.11.refs_2_ = bf16[256,128]{1,0:T(8,128)(2,1)S(1)} collective-permute-done((bf16[256,128]{1,0:T(8,128)(2,1)S(1)}, bf16[256,128]{1,0:T(8,128)(2,1)S(1)}, u32[]{:S(2)}, u32[]{:S(2)}) %collective-permute-start.11) | collective-permute-done | bytes 65568 | tf_op jit(solution)/shard_map/ppermute | solution.py:54
  28.8 2.4 %collective-permute-done.12.refs_3_ = bf16[256,128]{1,0:T(8,128)(2,1)S(1)} collective-permute-done((bf16[256,128]{1,0:T(8,128)(2,1)S(1)}, bf16[256,128]{1,0:T(8,128)(2,1)S(1)}, u32[]{:S(2)}, u32[]{:S(2)}) %collective-permute-start.12) | collective-permute-done | bytes 65568 | tf_op jit(solution)/shard_map/ppermute | solution.py:54
  31.2 6.6 %shard_map.112 = (bf16[256,512]{1,0:T(8,128)(2,1)}, bf16[256,128]{1,0:T(8,128)(2,1)S(1)}, bf16[256,128]{1,0:T(8,128)(2,1)S(1)}, bf16[256,128]{1,0:T(8,128)(2,1)S...) custom-call(s32[4,128]{1,0:T(4,128)S(1)} %pad_add_fusion.refs_0_.scalar_ref, ...), custom_call_target="tpu_custom_call" | custom-call | bytes 24500000 | tf_op jit(solution)/shard_map/pallas_call | solution.py:451
  37.9 3.0 %collective-permute-done.14.refs_1_ = bf16[256,2560]{1,0:T(8,128)(2,1)S(1)} collective-permute-done((bf16[256,2560]{1,0:T(8,128)(2,1)S(1)}, bf16[256,2560]{1,0:T(8,128)(2,1)S(1)}, u32[]{:S(2)}, u32[]{:S(2)}) %collective-permute-start.14) | collective-permute-done | bytes 1310752 | tf_op jit(solution)/shard_map/ppermute | solution.py:46
  42.3 2.4 %collective-permute-start.17 = (bf16[64,3072]{1,0:T(8,128)(2,1)S(1)}, bf16[64,3072]{1,0:T(8,128)(2,1)S(1)}, u32[]{:S(2)}, u32[]{:S(2)}) collective-permute-start(bf16[64,3072]{1,0:T(8,128)(2,1)S(1)} %get-tuple-element.48), channel_id=1, source_target_pairs={{0,6},{2,4},{4,2},{6,0},{8,14},{10,12},{12,10},{14,8},{16,22},{18,... | collective-permute-start | bytes 1179656 | tf_op jit(solution)/shard_map/ppermute | solution.py:54
  44.8 8.5 %collective-permute-done.15.refs_4_ = bf16[64,3072]{1,0:T(8,128)(2,1)S(1)} collective-permute-done((bf16[64,3072]{1,0:T(8,128)(2,1)S(1)}, bf16[64,3072]{1,0:T(8,128)(2,1)S(1)}, u32[]{:S(2)}, u32[]{:S(2)}) %collective-permute-start.15) | collective-permute-done | bytes 393248 | tf_op jit(solution)/shard_map/ppermute | solution.py:54
  53.2 7.9 %collective-permute-done.16.refs_5_ = bf16[64,3072]{1,0:T(8,128)(2,1)S(1)} collective-permute-done((bf16[64,3072]{1,0:T(8,128)(2,1)S(1)}, bf16[64,3072]{1,0:T(8,128)(2,1)S(1)}, u32[]{:S(2)}, u32[]{:S(2)}) %collective-permute-start.16) | collective-permute-done | bytes 393248 | tf_op jit(solution)/shard_map/ppermute | solution.py:54
  62.6 2.4 %collective-permute-start.21 = (bf16[16,2560]{1,0:T(8,128)(2,1)S(1)}, bf16[16,2560]{1,0:T(8,128)(2,1)S(1)}, u32[]{:S(2)}, u32[]{:S(2)}) collective-permute-start(bf16[16,2560]{1,0:T(8,128)(2,1)S(1)} %get-tuple-element.62), channel_id=1, source_target_pairs={{0,24},{2,26},{4,28},{6,30},{8,16},{10,18},{12,20},{14,22},{16,8},... | collective-permute-start | bytes 245768 | tf_op jit(solution)/shard_map/ppermute | solution.py:54
  65.6 2.9 %shard_map.114 = (bf16[4,512,128]{2,1,0:T(8,128)(2,1)S(1)}, bf16[4,512,128]{2,1,0:T(8,128)(2,1)S(1)}) custom-call(s32[4,128]{1,0:T(4,128)S(1)} %pad_add_fusion.refs_0_.scalar_ref, s32[4,8,1,128]{3,2,1,0:T(1,128)S(1)} %reshape.61.refs_1_, s32[4,8,1,128]{3,2,1,0:T(1,128)S(1)} %collective-permute-done.2.refs_2_, ...), custom_call_target="tpu_custom_call" | custom-call | bytes 10500000 | tf_op jit(solution)/shard_map/pallas_call | solution.py:485
  69.4 3.0 %collective-permute-done.20 = bf16[16,2560]{1,0:T(8,128)(2,1)S(1)} collective-permute-done((bf16[16,2560]{1,0:T(8,128)(2,1)S(1)}, bf16[16,2560]{1,0:T(8,128)(2,1)S(1)}, u32[]{:S(2)}, u32[]{:S(2)}) %collective-permute-start.20) | collective-permute-done | bytes 81952 | tf_op jit(solution)/shard_map/ppermute | solution.py:54
  72.4 2.5 %collective-permute-start.24 = (bf16[16,2560]{1,0:T(8,128)(2,1)S(1)}, bf16[16,2560]{1,0:T(8,128)(2,1)S(1)}, u32[]{:S(2)}, u32[]{:S(2)}) collective-permute-start(bf16[16,2560]{1,0:T(8,128)(2,1)S(1)} %add_convert_fusion.2), channel_id=1, source_target_pairs={{0,24},{2,26},{4,28},{6,30},{8,16},{10,18},{12,20},{14,22},{16,8},... | collective-permute-start | bytes 245768 | tf_op jit(solution)/shard_map/ppermute | solution.py:54
  74.9 1.9 %collective-permute-start.22 = (bf16[16,2560]{1,0:T(8,128)(2,1)S(1)}, bf16[16,2560]{1,0:T(8,128)(2,1)S(1)}, u32[]{:S(2)}, u32[]{:S(2)}) collective-permute-start(bf16[16,2560]{1,0:T(8,128)(2,1)S(1)} %add_convert_fusion.2), channel_id=1, source_target_pairs={{0,8},{2,10},{4,12},{6,14},{8,0},{10,2},{12,4},{14,6},{16,24},{18,... | collective-permute-start | bytes 245768 | tf_op jit(solution)/shard_map/ppermute | solution.py:54
  76.9 2.8 %collective-permute-done.24 = bf16[16,2560]{1,0:T(8,128)(2,1)S(1)} collective-permute-done((bf16[16,2560]{1,0:T(8,128)(2,1)S(1)}, bf16[16,2560]{1,0:T(8,128)(2,1)S(1)}, u32[]{:S(2)}, u32[]{:S(2)}) %collective-permute-start.24) | collective-permute-done | bytes 81952 | tf_op jit(solution)/shard_map/ppermute | solution.py:54
  79.7 1.9 %collective-permute-done.23 = bf16[16,2560]{1,0:T(8,128)(2,1)S(1)} collective-permute-done((bf16[16,2560]{1,0:T(8,128)(2,1)S(1)}, bf16[16,2560]{1,0:T(8,128)(2,1)S(1)}, u32[]{:S(2)}, u32[]{:S(2)}) %collective-permute-start.23) | collective-permute-done | bytes 81952 | tf_op jit(solution)/shard_map/ppermute | solution.py:54
  85.7 2.0 %collective-permute-start.30 = (bf16[512,128]{1,0:T(8,128)(2,1)S(1)}, bf16[512,128]{1,0:T(8,128)(2,1)S(1)}, u32[]{:S(2)}, u32[]{:S(2)}) collective-permute-start(bf16[512,128]{1,0:T(8,128)(2,1)S(1)} %get-tuple-element.59), channel_id=1, source_target_pairs={{0,24},{2,26},{4,28},{6,30},{8,16},{10,18},{12,20},{14,22},{16,8},... | collective-permute-start | bytes 393224 | tf_op jit(solution)/shard_map/ppermute | solution.py:54
  87.7 5.6 %collective-permute-done.28.refs_3_ = bf16[64,2560]{1,0:T(8,128)(2,1)S(1)} collective-permute-done((bf16[64,2560]{1,0:T(8,128)(2,1)S(1)}, bf16[64,2560]{1,0:T(8,128)(2,1)S(1)}, u32[]{:S(2)}, u32[]{:S(2)}) %collective-permute-start.28) | collective-permute-done | bytes 327712 | tf_op jit(solution)/shard_map/ppermute | solution.py:54
  93.9 4.7 %collective-permute-done.27.refs_2_ = bf16[64,2560]{1,0:T(8,128)(2,1)S(1)} collective-permute-done((bf16[64,2560]{1,0:T(8,128)(2,1)S(1)}, bf16[64,2560]{1,0:T(8,128)(2,1)S(1)}, u32[]{:S(2)}, u32[]{:S(2)}) %collective-permute-start.27) | collective-permute-done | bytes 327712 | tf_op jit(solution)/shard_map/ppermute | solution.py:54
  98.7 2.3 %shard_map.115 = (f32[256,2048]{1,0:T(8,128)}, f32[256,512]{1,0:T(8,128)}) custom-call(s32[4,128]{1,0:T(4,128)S(1)} %pad_add_fusion.refs_0_.scalar_ref, bf16[64,2560]{1,0:T(8,128)(2,1)S(1)} %pad_maximum_fusion.1.refs_0_, bf16[64,2560]{1,0:T(8,128)(2,1)S(1)} %collective-permute-done.26.refs_1_, bf16[64,2560]{1,0:T(8,128)(2,1)S(1)} %collective-permute-done.27.refs_2_, ...), custom_call_target="tpu_custom_call" | custom-call | bytes 7000000 | tf_op jit(solution)/shard_map/pallas_call | solution.py:528
  (63 shorter events, 21.0 us)
Async XLA Ops:
  1.6 15.9 %collective-permute-start.8 = (bf16[512,128]{1,0:T(8,128)(2,1)S(1)}, bf16[512,128]{1,0:T(8,128)(2,1)S(1)}, u32[]{:S(2)}, u32[]{:S(2)}) collective-permute-start(bf16[512,128]{1,0:T(8,128)(2,1)S(1)} %dynamic-slice_bitcast_fusion.refs_3_), channel_id=1, source_target_pairs={{0,24},{2,26},{4,28},{6,30},{8,16},{10,18},{12,20},{14,22},{16,8},... | collective-permute-start | bytes 393224 | tf_op jit(solution)/shard_map/ppermute | solution.py:54
  6.7 11.1 %collective-permute-start.6 = (bf16[512,128]{1,0:T(8,128)(2,1)S(1)}, bf16[512,128]{1,0:T(8,128)(2,1)S(1)}, u32[]{:S(2)}, u32[]{:S(2)}) collective-permute-start(bf16[512,128]{1,0:T(8,128)(2,1)S(1)} %dynamic-slice_bitcast_fusion.refs_3_), channel_id=1, source_target_pairs={{0,16},{2,18},{4,20},{6,22},{8,24},{10,26},{12,28},{14,30},{16,0},... | collective-permute-start | bytes 393224 | tf_op jit(solution)/shard_map/ppermute | solution.py:54
  6.7 10.2 %collective-permute-start.4 = (bf16[512,128]{1,0:T(8,128)(2,1)S(1)}, bf16[512,128]{1,0:T(8,128)(2,1)S(1)}, u32[]{:S(2)}, u32[]{:S(2)}) collective-permute-start(bf16[512,128]{1,0:T(8,128)(2,1)S(1)} %dynamic-slice_bitcast_fusion.refs_3_), channel_id=1, source_target_pairs={{0,8},{2,10},{4,12},{6,14},{8,0},{10,2},{12,4},{14,6},{16,24},{18,... | collective-permute-start | bytes 393224 | tf_op jit(solution)/shard_map/ppermute | solution.py:54
  11.4 7.7 %collective-permute-start.3 = (bf16[512,128]{1,0:T(8,128)(2,1)S(1)}, bf16[512,128]{1,0:T(8,128)(2,1)S(1)}, u32[]{:S(2)}, u32[]{:S(2)}) collective-permute-start(bf16[512,128]{1,0:T(8,128)(2,1)S(1)} %dynamic-slice_bitcast_fusion.refs_3_), channel_id=1, source_target_pairs={{0,1},{1,0},{2,3},{3,2},{4,5},{5,4},{6,7},{7,6},{8,9},{9,8},{10,11... | collective-permute-start | bytes 393224 | tf_op jit(solution)/shard_map/ppermute | solution.py:46
  22.6 8.6 %collective-permute-start.13 = (bf16[256,2560]{1,0:T(8,128)(2,1)S(1)}, bf16[256,2560]{1,0:T(8,128)(2,1)S(1)}, u32[]{:S(2)}, u32[]{:S(2)}) collective-permute-start(bf16[256,2560]{1,0:T(8,128)(2,1)S(1)} %pad_maximum_fusion.refs_4_), channel_id=1, source_target_pairs={{0,1},{1,0},{2,3},{3,2},{4,5},{5,4},{6,7},{7,6},{8,9},{9,8},{10,11... | collective-permute-start | bytes 3932168 | tf_op jit(solution)/shard_map/ppermute | solution.py:46
  22.9 4.3 %collective-permute-start.10 = (bf16[256,128]{1,0:T(8,128)(2,1)S(1)}, bf16[256,128]{1,0:T(8,128)(2,1)S(1)}, u32[]{:S(2)}, u32[]{:S(2)}) collective-permute-start(bf16[256,128]{1,0:T(8,128)(2,1)S(1)} %get-tuple-element.35), channel_id=1, source_target_pairs={{0,2},{2,0},{4,6},{6,4},{8,10},{10,8},{12,14},{14,12},{16,18},{18,... | collective-permute-start | bytes 196616 | tf_op jit(solution)/shard_map/ppermute | solution.py:54
  24.6 4.3 %collective-permute-start.11 = (bf16[256,128]{1,0:T(8,128)(2,1)S(1)}, bf16[256,128]{1,0:T(8,128)(2,1)S(1)}, u32[]{:S(2)}, u32[]{:S(2)}) collective-permute-start(bf16[256,128]{1,0:T(8,128)(2,1)S(1)} %get-tuple-element.36), channel_id=1, source_target_pairs={{0,4},{2,6},{4,0},{6,2},{8,12},{10,14},{12,8},{14,10},{16,20},{18,... | collective-permute-start | bytes 196616 | tf_op jit(solution)/shard_map/ppermute | solution.py:54
  26.1 5.2 %collective-permute-start.12 = (bf16[256,128]{1,0:T(8,128)(2,1)S(1)}, bf16[256,128]{1,0:T(8,128)(2,1)S(1)}, u32[]{:S(2)}, u32[]{:S(2)}) collective-permute-start(bf16[256,128]{1,0:T(8,128)(2,1)S(1)} %get-tuple-element.37), channel_id=1, source_target_pairs={{0,6},{2,4},{4,2},{6,0},{8,14},{10,12},{12,10},{14,8},{16,22},{18,... | collective-permute-start | bytes 196616 | tf_op jit(solution)/shard_map/ppermute | solution.py:54
  41.2 12.0 %collective-permute-start.15 = (bf16[64,3072]{1,0:T(8,128)(2,1)S(1)}, bf16[64,3072]{1,0:T(8,128)(2,1)S(1)}, u32[]{:S(2)}, u32[]{:S(2)}) collective-permute-start(bf16[64,3072]{1,0:T(8,128)(2,1)S(1)} %get-tuple-element.46), channel_id=1, source_target_pairs={{0,2},{2,0},{4,6},{6,4},{8,10},{10,8},{12,14},{14,12},{16,18},{18,... | collective-permute-start | bytes 1179656 | tf_op jit(solution)/shard_map/ppermute | solution.py:54
  41.8 19.3 %collective-permute-start.16 = (bf16[64,3072]{1,0:T(8,128)(2,1)S(1)}, bf16[64,3072]{1,0:T(8,128)(2,1)S(1)}, u32[]{:S(2)}, u32[]{:S(2)}) collective-permute-start(bf16[64,3072]{1,0:T(8,128)(2,1)S(1)} %get-tuple-element.47), channel_id=1, source_target_pairs={{0,4},{2,6},{4,0},{6,2},{8,12},{10,14},{12,8},{14,10},{16,20},{18,... | collective-permute-start | bytes 1179656 | tf_op jit(solution)/shard_map/ppermute | solution.py:54
  42.3 18.8 %collective-permute-start.17 = (bf16[64,3072]{1,0:T(8,128)(2,1)S(1)}, bf16[64,3072]{1,0:T(8,128)(2,1)S(1)}, u32[]{:S(2)}, u32[]{:S(2)}) collective-permute-start(bf16[64,3072]{1,0:T(8,128)(2,1)S(1)} %get-tuple-element.48), channel_id=1, source_target_pairs={{0,6},{2,4},{4,2},{6,0},{8,14},{10,12},{12,10},{14,8},{16,22},{18,... | collective-permute-start | bytes 1179656 | tf_op jit(solution)/shard_map/ppermute | solution.py:54
  61.3 7.2 %collective-permute-start.19 = (bf16[16,2560]{1,0:T(8,128)(2,1)S(1)}, bf16[16,2560]{1,0:T(8,128)(2,1)S(1)}, u32[]{:S(2)}, u32[]{:S(2)}) collective-permute-start(bf16[16,2560]{1,0:T(8,128)(2,1)S(1)} %get-tuple-element.61), channel_id=1, source_target_pairs={{0,8},{2,10},{4,12},{6,14},{8,0},{10,2},{12,4},{14,6},{16,24},{18,... | collective-permute-start | bytes 245768 | tf_op jit(solution)/shard_map/ppermute | solution.py:54
  62.6 6.7 %collective-permute-start.21 = (bf16[16,2560]{1,0:T(8,128)(2,1)S(1)}, bf16[16,2560]{1,0:T(8,128)(2,1)S(1)}, u32[]{:S(2)}, u32[]{:S(2)}) collective-permute-start(bf16[16,2560]{1,0:T(8,128)(2,1)S(1)} %get-tuple-element.62), channel_id=1, source_target_pairs={{0,24},{2,26},{4,28},{6,30},{8,16},{10,18},{12,20},{14,22},{16,8},... | collective-permute-start | bytes 245768 | tf_op jit(solution)/shard_map/ppermute | solution.py:54
  65.1 7.3 %collective-permute-start.20 = (bf16[16,2560]{1,0:T(8,128)(2,1)S(1)}, bf16[16,2560]{1,0:T(8,128)(2,1)S(1)}, u32[]{:S(2)}, u32[]{:S(2)}) collective-permute-start(bf16[16,2560]{1,0:T(8,128)(2,1)S(1)} %get-tuple-element.63), channel_id=1, source_target_pairs={{0,16},{2,18},{4,20},{6,22},{8,24},{10,26},{12,28},{14,30},{16,0},... | collective-permute-start | bytes 245768 | tf_op jit(solution)/shard_map/ppermute | solution.py:54
  68.5 16.7 %collective-permute-start.18 = (bf16[4,512,128]{2,1,0:T(8,128)(2,1)S(1)}, bf16[4,512,128]{2,1,0:T(8,128)(2,1)S(1)}, u32[]{:S(2)}, u32[]{:S(2)}) collective-permute-start(bf16[4,512,128]{2,1,0:T(8,128)(2,1)S(1)} %get-tuple-element.50), channel_id=1, source_target_pairs={{0,1},{1,0},{2,3},{3,2},{4,5},{5,4},{6,7},{7,6},{8,9},{9,8},{10,11... | collective-permute-start | bytes 1572872 | tf_op jit(solution)/shard_map/ppermute | solution.py:46
  72.4 7.3 %collective-permute-start.24 = (bf16[16,2560]{1,0:T(8,128)(2,1)S(1)}, bf16[16,2560]{1,0:T(8,128)(2,1)S(1)}, u32[]{:S(2)}, u32[]{:S(2)}) collective-permute-start(bf16[16,2560]{1,0:T(8,128)(2,1)S(1)} %add_convert_fusion.2), channel_id=1, source_target_pairs={{0,24},{2,26},{4,28},{6,30},{8,16},{10,18},{12,20},{14,22},{16,8},... | collective-permute-start | bytes 245768 | tf_op jit(solution)/shard_map/ppermute | solution.py:54
  74.9 6.7 %collective-permute-start.23 = (bf16[16,2560]{1,0:T(8,128)(2,1)S(1)}, bf16[16,2560]{1,0:T(8,128)(2,1)S(1)}, u32[]{:S(2)}, u32[]{:S(2)}) collective-permute-start(bf16[16,2560]{1,0:T(8,128)(2,1)S(1)} %add_convert_fusion.2), channel_id=1, source_target_pairs={{0,16},{2,18},{4,20},{6,22},{8,24},{10,26},{12,28},{14,30},{16,0},... | collective-permute-start | bytes 245768 | tf_op jit(solution)/shard_map/ppermute | solution.py:54
  74.9 6.7 %collective-permute-start.22 = (bf16[16,2560]{1,0:T(8,128)(2,1)S(1)}, bf16[16,2560]{1,0:T(8,128)(2,1)S(1)}, u32[]{:S(2)}, u32[]{:S(2)}) collective-permute-start(bf16[16,2560]{1,0:T(8,128)(2,1)S(1)} %add_convert_fusion.2), channel_id=1, source_target_pairs={{0,8},{2,10},{4,12},{6,14},{8,0},{10,2},{12,4},{14,6},{16,24},{18,... | collective-permute-start | bytes 245768 | tf_op jit(solution)/shard_map/ppermute | solution.py:54
  81.6 11.7 %collective-permute-start.28 = (bf16[64,2560]{1,0:T(8,128)(2,1)S(1)}, bf16[64,2560]{1,0:T(8,128)(2,1)S(1)}, u32[]{:S(2)}, u32[]{:S(2)}) collective-permute-start(bf16[64,2560]{1,0:T(8,128)(2,1)S(1)} %pad_maximum_fusion.1.refs_0_), channel_id=1, source_target_pairs={{0,6},{2,4},{4,2},{6,0},{8,14},{10,12},{12,10},{14,8},{16,22},{18,... | collective-permute-start | bytes 983048 | tf_op jit(solution)/shard_map/ppermute | solution.py:54
  83.2 15.5 %collective-permute-start.27 = (bf16[64,2560]{1,0:T(8,128)(2,1)S(1)}, bf16[64,2560]{1,0:T(8,128)(2,1)S(1)}, u32[]{:S(2)}, u32[]{:S(2)}) collective-permute-start(bf16[64,2560]{1,0:T(8,128)(2,1)S(1)} %pad_maximum_fusion.1.refs_0_), channel_id=1, source_target_pairs={{0,4},{2,6},{4,0},{6,2},{8,12},{10,14},{12,8},{14,10},{16,20},{18,... | collective-permute-start | bytes 983048 | tf_op jit(solution)/shard_map/ppermute | solution.py:54
  84.6 14.1 %collective-permute-start.26 = (bf16[64,2560]{1,0:T(8,128)(2,1)S(1)}, bf16[64,2560]{1,0:T(8,128)(2,1)S(1)}, u32[]{:S(2)}, u32[]{:S(2)}) collective-permute-start(bf16[64,2560]{1,0:T(8,128)(2,1)S(1)} %pad_maximum_fusion.1.refs_0_), channel_id=1, source_target_pairs={{0,2},{2,0},{4,6},{6,4},{8,10},{10,8},{12,14},{14,12},{16,18},{18,... | collective-permute-start | bytes 983048 | tf_op jit(solution)/shard_map/ppermute | solution.py:54
  85.4 15.7 %collective-permute-start.25 = (bf16[512,128]{1,0:T(8,128)(2,1)S(1)}, bf16[512,128]{1,0:T(8,128)(2,1)S(1)}, u32[]{:S(2)}, u32[]{:S(2)}) collective-permute-start(bf16[512,128]{1,0:T(8,128)(2,1)S(1)} %get-tuple-element.58), channel_id=1, source_target_pairs={{0,8},{2,10},{4,12},{6,14},{8,0},{10,2},{12,4},{14,6},{16,24},{18,... | collective-permute-start | bytes 393224 | tf_op jit(solution)/shard_map/ppermute | solution.py:54
  85.7 15.3 %collective-permute-start.30 = (bf16[512,128]{1,0:T(8,128)(2,1)S(1)}, bf16[512,128]{1,0:T(8,128)(2,1)S(1)}, u32[]{:S(2)}, u32[]{:S(2)}) collective-permute-start(bf16[512,128]{1,0:T(8,128)(2,1)S(1)} %get-tuple-element.59), channel_id=1, source_target_pairs={{0,24},{2,26},{4,28},{6,30},{8,16},{10,18},{12,20},{14,22},{16,8},... | collective-permute-start | bytes 393224 | tf_op jit(solution)/shard_map/ppermute | solution.py:54
  93.3 7.8 %collective-permute-start.29 = (bf16[512,128]{1,0:T(8,128)(2,1)S(1)}, bf16[512,128]{1,0:T(8,128)(2,1)S(1)}, u32[]{:S(2)}, u32[]{:S(2)}) collective-permute-start(bf16[512,128]{1,0:T(8,128)(2,1)S(1)} %get-tuple-element.60), channel_id=1, source_target_pairs={{0,16},{2,18},{4,20},{6,22},{8,24},{10,26},{12,28},{14,30},{16,0},... | collective-permute-start | bytes 393224 | tf_op jit(solution)/shard_map/ppermute | solution.py:54
  (9 other events, 35.8 us)

commit v8 on v7

--- a/solution.py
+++ b/solution.py
@@ -325,24 +325,34 @@
         grad_refs[step][...] = x_ref[group_here ^ step]
 
 
-def pieces_kernel(bals, *refs):
-    count = len(refs) - bals
-    groups = (count + 1) // 2
+def pieces_kernel(tables, groups, bals, *refs):
     term_refs, grad_refs = refs[:bals], refs[bals : bals + groups - 1]
-    out_refs = refs[bals + groups - 1 :]
-    height, width = out_refs[0].shape
-    for step, out in enumerate(out_refs):
+    plane_refs = refs[bals + groups - 1 : bals + 2 * groups - 1]
+    table_refs = refs[bals + 2 * groups - 1 :]
+    height, width = plane_refs[0].shape
+    unit = height // tables
+
+    def total(rows, columns):
+        found = term_refs[0][rows, columns].astype(f32)
+        for ref in term_refs[1:]:
+            found = found + ref[rows, columns].astype(f32)
+        return found.astype(bf16)
+
+    for step, out in enumerate(plane_refs):
         rows = slice(step * height, (step + 1) * height)
-        total = term_refs[0][rows, :].astype(f32)
-        for ref in term_refs[1:]:
-            total = total + ref[rows, :].astype(f32)
-        out[:, :width] = total.astype(bf16)
+        out[:, :width] = total(rows, slice(0, width))
         if step:
             grad = grad_refs[step - 1]
             columns = grad.shape[1]
             for index in range(grad.shape[0] // height):
                 at = width + index * columns
                 out[:, at : at + columns] = grad[index * height : (index + 1) * height, :]
+    for table_step, out in enumerate(table_refs):
+        for step in range(groups):
+            first = step * height + table_step * unit
+            rows = slice(first, first + unit)
+            columns = slice(width, width + out.shape[1])
+            out[step * unit : (step + 1) * unit, :] = total(rows, columns)
 
 
 def place_kernel(scale, groups, slots, tables, bals, unit, scalar_ref, *refs):
@@ -427,11 +437,12 @@
     )
     plane_ids = with_swapped(ids.reshape(tables, groups * slots, 1, slot_rows), bals)
     wide_cot = cotangent[0].astype(f32)
-    scalars = after(scalars, share, wide_cot)
+    weights = jnp.concatenate([weight_in, weight_out], axis=1)
+    scalars = after(scalars, share, wide_cot, weights)
     for bit in range((groups - 1).bit_length()):
         scalars = jnp.concatenate([scalars, emb_swap(scalars, 1 << bit, embs)], axis=0)
 
-    fetched[0] = after(fetched[0], scalars)
+    fetched[0] = after(fetched[0], scalars, *plane_ids[1:])
     pieces = [piece for one in [share] + fetched for piece in with_swapped(one, bals)]
 
     found = pl.pallas_call(
@@ -442,7 +453,6 @@
         cost_estimate=estimate(3),
         compiler_params=room(16),
     )(scalars, *plane_ids, *pieces)
-    weights = jnp.concatenate([weight_in, weight_out], axis=1)
     weights = with_swapped(after(weights, found[0]), bals)
     block = [found[0]] + [emb_swap(found[step], step, embs) for step in range(1, groups)]
 
@@ -494,22 +504,29 @@
     grad_scale = (rows * embs * bals) ** -0.5
     if owned:
         height, wide = weight_part // groups, features + width
+        last = wide // 2
+        first = wide - last
         terms = [results[0]] + [bal_swap(results[turn], turn, bals) for turn in range(1, bals)]
         pieces = pl.pallas_call(
-            functools.partial(pieces_kernel, bals),
-            out_shape=[jax.ShapeDtypeStruct((height, wide), bf16)]
-            + [jax.ShapeDtypeStruct((height, wide + rows // height * columns), bf16)] * (groups - 1),
+            functools.partial(pieces_kernel, tables, groups, bals),
+            out_shape=[jax.ShapeDtypeStruct((height, first), bf16)]
+            + [jax.ShapeDtypeStruct((height, first + rows // height * columns), bf16)] * (groups - 1)
+            + [jax.ShapeDtypeStruct((groups * unit, last), bf16)] * tables,
             in_specs=[VMEM] * (bals + groups - 1),
-            out_specs=[VMEM] * groups,
+            out_specs=[VMEM] * (groups + tables),
             compiler_params=room(12),
         )(*terms, *grads[1:])
-        came = [emb_swap(pieces[step], step, embs) for step in range(1, groups)]
-        mine = sum_rounded([pieces[0]] + [value[:, :wide] for value in came])
-        mine = mine.reshape(tables, unit, wide)
+        plane_pieces, table_pieces = pieces[:groups], pieces[groups:]
+        came = [emb_swap(plane_pieces[step], step, embs) for step in range(1, groups)]
+        mine = sum_rounded([plane_pieces[0]] + [value[:, :first] for value in came])
+        mine = mine.reshape(tables, unit, first)
         sums = table_sums([grads[0]] + came)
+        other = [emb_swap(table_pieces[step], step * groups, embs) for step in range(1, tables)]
+        other = sum_rounded([table_pieces[0]] + other).reshape(groups, unit, last)
         own_sums = over_cores(sums)
         came = [emb_swap(mine[step], step * groups, embs) for step in range(1, tables)]
-        final = sum_rounded([mine[0]] + came)
+        other = [other[0]] + [emb_swap(other[step], step, embs) for step in range(1, groups)]
+        final = jnp.concatenate([sum_rounded([mine[0]] + came), sum_rounded(other)], axis=1)
         gathered = [final] + [emb_swap(final, step * groups, embs) for step in range(1, tables)]
         back = to_plane(jnp.concatenate(gathered, axis=0))
         later = after(own_sums, *gathered[1:])

time: 102 us -> 103 us (level)
  starting transfers between devices: 32.7 us -> 39.2 us
  waiting for transfers between devices: 46.3 us -> 41.4 us
  other arithmetic: 3.96 us -> 2.31 us
  local copies, waits for them, and re-layouts: 2.42 us -> 3.77 us
    ppermute x23 -> x29, waiting for transfers between devices: 43.3 us -> 36 us  [emb_swap(): return lax.ppermute(value, 'emb', [(i, i ^ step) for i in range(count)])]
    ppermute x23 -> x29, starting transfers between devices: 31.3 us -> 38.1 us  [emb_swap(): return lax.ppermute(value, 'emb', [(i, i ^ step) for i in range(count)])]
    ppermute x8, waiting for transfers between devices: 3.06 us -> 5.38 us  [bal_swap(): return lax.ppermute(value, 'bal', [(i, i ^ step) for i in range(count)])]
    unnamed x4 -> x9, local copies, waits for them, and re-layouts: 0.94 us -> 2.27 us
    concatenate x1, other arithmetic: 1.04 us -> 0.01 us  [on_device(): jnp.concatenate([sum_rounded([mine[0]] + came), sum_rounded(other)], axis=1)]
  transfers between devices with their start and end apart: 31 -> 37, of which waited for: 15 -> 18; matrix products, arithmetic and copies ran while one was open for 4% -> 4% of each run, Pallas kernels for 5% -> 5%
where the time goes in v8:
time: 103 us
  waiting for transfers between devices  41.4 us (40%)
  starting transfers between devices  39.2 us (38%)
  Pallas kernels  15.6 us (15%)
  local copies, waits for them, and re-layouts  3.77 us (4%)
  other arithmetic  2.31 us (2%)
    ppermute x29, starting transfers between devices, emb_swap(): return lax.ppermute(value, 'emb', [(i, i ^ step) for i in range(count)])  38.1 us
    ppermute x29, waiting for transfers between devices, emb_swap(): return lax.ppermute(value, 'emb', [(i, i ^ step) for i in range(count)])  36 us
    pallas_call x1, Pallas kernels, on_device(): pl.pallas_call(functools.partial(layer_kernel, groups, slots, tables, bal...  6.6 us
    ppermute x8, waiting for transfers between devices, bal_swap(): return lax.ppermute(value, 'bal', [(i, i ^ step) for i in range(count)])  5.38 us
    pallas_call x1, Pallas kernels, on_device(): pl.pallas_call(functools.partial(lookup_kernel, groups, slots, tables, ba...  3.5 us
    pallas_call x1, Pallas kernels, table_sums(): pl.pallas_call(functools.partial(scatter_kernel, groups, slots, bals), ou...  2.91 us
    pallas_call x1, Pallas kernels, on_device(): pl.pallas_call(functools.partial(place_kernel, grad_scale, groups, slots,...  2.32 us
    unnamed x9, local copies, waits for them, and re-layouts  2.27 us
  transfers between devices with their start and end apart: 37, of which 18 were waited for; matrix products, arithmetic and copies ran while one was open for 4% of the time, Pallas kernels for 5%

profile of v8, /device:TPU:0, one launch (start us, length us, event | category | flops | bytes accessed | tf_op | source)
XLA Modules:
  0.0 103.2 jit_solution(14821061844219608640)
XLA Ops:
  1.6 5.1 %collective-permute-start.8 = (bf16[512,128]{1,0:T(8,128)(2,1)S(1)}, bf16[512,128]{1,0:T(8,128)(2,1)S(1)}, u32[]{:S(2)}, u32[]{:S(2)}) collective-permute-start(bf16[512,128]{1,0:T(8,128)(2,1)S(1)} %dynamic-slice_bitcast_fusion.refs_3_), channel_id=1, source_target_pairs={{0,24},{2,26},{4,28},{6,30},{8,16},{10,18},{12,20},{14,22},{16,8},... | collective-permute-start | bytes 393224 | tf_op jit(solution)/shard_map/ppermute | solution.py:54
  10.6 1.6 %collective-permute-start = (s32[1,128]{1,0:T(1,128)S(1)}, s32[1,128]{1,0:T(1,128)S(1)}, u32[]{:S(2)}, u32[]{:S(2)}) collective-permute-start(s32[1,128]{1,0:T(1,128)S(1)} %pad_add_fusion.2), channel_id=1, source_target_pairs={{0,2},{2,0},{4,6},{6,4},{8,10},{10,8},{12,14},{14,12},{16,18},{18,... | collective-permute-start | bytes 1544 | tf_op jit(solution)/shard_map/ppermute | solution.py:54
  12.2 1.9 %collective-permute-done = s32[1,128]{1,0:T(1,128)S(1)} collective-permute-done((s32[1,128]{1,0:T(1,128)S(1)}, s32[1,128]{1,0:T(1,128)S(1)}, u32[]{:S(2)}, u32[]{:S(2)}) %collective-permute-start) | collective-permute-done | bytes 544 | tf_op jit(solution)/shard_map/ppermute | solution.py:54
  14.1 1.7 %collective-permute-start.1 = (s32[2,128]{1,0:T(2,128)S(1)}, s32[2,128]{1,0:T(2,128)S(1)}, u32[]{:S(2)}, u32[]{:S(2)}) collective-permute-start(s32[2,128]{1,0:T(2,128)S(1)} %pad_add_fusion.1), channel_id=1, source_target_pairs={{0,4},{2,6},{4,0},{6,2},{8,12},{10,14},{12,8},{14,10},{16,20},{18,... | collective-permute-start | bytes 3080 | tf_op jit(solution)/shard_map/ppermute | solution.py:54
  20.8 3.5 %shard_map.111 = (bf16[256,128]{1,0:T(8,128)(2,1)S(1)}, bf16[256,128]{1,0:T(8,128)(2,1)S(1)}, bf16[256,128]{1,0:T(8,128)(2,1)S(1)}, bf16[256,128]{1,0:T(8,128)(2,1)S(1)}) custom-call(s32[4,128]{1,0:T(4,128)S(1)} %pad_add_fusion.refs_0_.scalar_ref, s32[4,8,1,128]{3,2,1,0:T(1,128)S(1)} %reshape.70.refs_1_, ...), custom_call_target="tpu_custom_call" | custom-call | bytes 10500000 | tf_op jit(solution)/shard_map/pallas_call | solution.py:448
  24.5 1.6 %collective-permute-start.10 = (bf16[256,128]{1,0:T(8,128)(2,1)S(1)}, bf16[256,128]{1,0:T(8,128)(2,1)S(1)}, u32[]{:S(2)}, u32[]{:S(2)}) collective-permute-start(bf16[256,128]{1,0:T(8,128)(2,1)S(1)} %get-tuple-element.39), channel_id=1, source_target_pairs={{0,2},{2,0},{4,6},{6,4},{8,10},{10,8},{12,14},{14,12},{16,18},{18,... | collective-permute-start | bytes 196616 | tf_op jit(solution)/shard_map/ppermute | solution.py:54
  28.8 1.6 %collective-permute-done.11.refs_2_ = bf16[256,128]{1,0:T(8,128)(2,1)S(1)} collective-permute-done((bf16[256,128]{1,0:T(8,128)(2,1)S(1)}, bf16[256,128]{1,0:T(8,128)(2,1)S(1)}, u32[]{:S(2)}, u32[]{:S(2)}) %collective-permute-start.11) | collective-permute-done | bytes 65568 | tf_op jit(solution)/shard_map/ppermute | solution.py:54
  30.4 2.4 %collective-permute-done.12.refs_3_ = bf16[256,128]{1,0:T(8,128)(2,1)S(1)} collective-permute-done((bf16[256,128]{1,0:T(8,128)(2,1)S(1)}, bf16[256,128]{1,0:T(8,128)(2,1)S(1)}, u32[]{:S(2)}, u32[]{:S(2)}) %collective-permute-start.12) | collective-permute-done | bytes 65568 | tf_op jit(solution)/shard_map/ppermute | solution.py:54
  32.8 6.6 %shard_map.112 = (bf16[256,512]{1,0:T(8,128)(2,1)}, bf16[256,128]{1,0:T(8,128)(2,1)S(1)}, bf16[256,128]{1,0:T(8,128)(2,1)S(1)}, bf16[256,128]{1,0:T(8,128)(2,1)S...) custom-call(s32[4,128]{1,0:T(4,128)S(1)} %pad_add_fusion.refs_0_.scalar_ref, ...), custom_call_target="tpu_custom_call" | custom-call | bytes 24500000 | tf_op jit(solution)/shard_map/pallas_call | solution.py:461
  39.5 3.0 %collective-permute-done.14.refs_1_ = bf16[256,2560]{1,0:T(8,128)(2,1)S(1)} collective-permute-done((bf16[256,2560]{1,0:T(8,128)(2,1)S(1)}, bf16[256,2560]{1,0:T(8,128)(2,1)S(1)}, u32[]{:S(2)}, u32[]{:S(2)}) %collective-permute-start.14) | collective-permute-done | bytes 1310752 | tf_op jit(solution)/shard_map/ppermute | solution.py:46
  44.1 2.9 %collective-permute-start.23 = (bf16[64,1280]{1,0:T(8,128)(2,1)S(1)}, bf16[64,1280]{1,0:T(8,128)(2,1)S(1)}, u32[]{:S(2)}, u32[]{:S(2)}) collective-permute-start(bf16[64,1280]{1,0:T(8,128)(2,1)S(1)} %get-tuple-element.58), channel_id=1, source_target_pairs={{0,16},{2,18},{4,20},{6,22},{8,24},{10,26},{12,28},{14,30},{16,0},... | collective-permute-start | bytes 491528 | tf_op jit(solution)/shard_map/ppermute | solution.py:54
  48.3 3.8 %collective-permute-done.22 = bf16[64,1280]{1,0:T(8,128)(2,1)S(1)} collective-permute-done((bf16[64,1280]{1,0:T(8,128)(2,1)S(1)}, bf16[64,1280]{1,0:T(8,128)(2,1)S(1)}, u32[]{:S(2)}, u32[]{:S(2)}) %collective-permute-start.22) | collective-permute-done | bytes 163872 | tf_op jit(solution)/shard_map/ppermute | solution.py:54
  52.6 6.5 %collective-permute-done.23 = bf16[64,1280]{1,0:T(8,128)(2,1)S(1)} collective-permute-done((bf16[64,1280]{1,0:T(8,128)(2,1)S(1)}, bf16[64,1280]{1,0:T(8,128)(2,1)S(1)}, u32[]{:S(2)}, u32[]{:S(2)}) %collective-permute-start.23) | collective-permute-done | bytes 163872 | tf_op jit(solution)/shard_map/ppermute | solution.py:54
  62.9 3.3 %collective-permute-start.19 = (bf16[16,1280]{1,0:T(8,128)(2,1)S(1)}, bf16[16,1280]{1,0:T(8,128)(2,1)S(1)}, u32[]{:S(2)}, u32[]{:S(2)}) collective-permute-start(bf16[16,1280]{1,0:T(8,128)(2,1)S(1)} %get-tuple-element.69), channel_id=1, source_target_pairs={{0,8},{2,10},{4,12},{6,14},{8,0},{10,2},{12,4},{14,6},{16,24},{18,... | collective-permute-start | bytes 122888 | tf_op jit(solution)/shard_map/ppermute | solution.py:54
  66.3 2.4 %collective-permute-start.21 = (bf16[16,1280]{1,0:T(8,128)(2,1)S(1)}, bf16[16,1280]{1,0:T(8,128)(2,1)S(1)}, u32[]{:S(2)}, u32[]{:S(2)}) collective-permute-start(bf16[16,1280]{1,0:T(8,128)(2,1)S(1)} %get-tuple-element.70), channel_id=1, source_target_pairs={{0,24},{2,26},{4,28},{6,30},{8,16},{10,18},{12,20},{14,22},{16,8},... | collective-permute-start | bytes 122888 | tf_op jit(solution)/shard_map/ppermute | solution.py:54
  68.8 2.9 %shard_map.114 = (bf16[4,512,128]{2,1,0:T(8,128)(2,1)S(1)}, bf16[4,512,128]{2,1,0:T(8,128)(2,1)S(1)}) custom-call(s32[4,128]{1,0:T(4,128)S(1)} %pad_add_fusion.refs_0_.scalar_ref, s32[4,8,1,128]{3,2,1,0:T(1,128)S(1)} %reshape.70.refs_1_, s32[4,8,1,128]{3,2,1,0:T(1,128)S(1)} %collective-permute-done.2.refs_2_, ...), custom_call_target="tpu_custom_call" | custom-call | bytes 10500000 | tf_op jit(solution)/shard_map/pallas_call | solution.py:495
  73.6 1.8 %collective-permute-start.30 = (bf16[16,2560]{1,0:T(8,128)(2,1)S(1)}, bf16[16,2560]{1,0:T(8,128)(2,1)S(1)}, u32[]{:S(2)}, u32[]{:S(2)}) collective-permute-start(bf16[16,2560]{1,0:T(8,128)(2,1)S(1)} %pad_maximum_fusion.1), channel_id=1, source_target_pairs={{0,24},{2,26},{4,28},{6,30},{8,16},{10,18},{12,20},{14,22},{16,8},... | collective-permute-start | bytes 245768 | tf_op jit(solution)/shard_map/ppermute | solution.py:54
  75.5 2.6 %collective-permute-start.28 = (bf16[16,2560]{1,0:T(8,128)(2,1)S(1)}, bf16[16,2560]{1,0:T(8,128)(2,1)S(1)}, u32[]{:S(2)}, u32[]{:S(2)}) collective-permute-start(bf16[16,2560]{1,0:T(8,128)(2,1)S(1)} %pad_maximum_fusion.1), channel_id=1, source_target_pairs={{0,8},{2,10},{4,12},{6,14},{8,0},{10,2},{12,4},{14,6},{16,24},{18,... | collective-permute-start | bytes 245768 | tf_op jit(solution)/shard_map/ppermute | solution.py:54
  78.1 2.7 %collective-permute-done.30 = bf16[16,2560]{1,0:T(8,128)(2,1)S(1)} collective-permute-done((bf16[16,2560]{1,0:T(8,128)(2,1)S(1)}, bf16[16,2560]{1,0:T(8,128)(2,1)S(1)}, u32[]{:S(2)}, u32[]{:S(2)}) %collective-permute-start.30) | collective-permute-done | bytes 81952 | tf_op jit(solution)/shard_map/ppermute | solution.py:54
  80.8 2.5 %collective-permute-done.29 = bf16[16,2560]{1,0:T(8,128)(2,1)S(1)} collective-permute-done((bf16[16,2560]{1,0:T(8,128)(2,1)S(1)}, bf16[16,2560]{1,0:T(8,128)(2,1)S(1)}, u32[]{:S(2)}, u32[]{:S(2)}) %collective-permute-start.29) | collective-permute-done | bytes 81952 | tf_op jit(solution)/shard_map/ppermute | solution.py:54
  87.2 2.0 %collective-permute-start.36 = (bf16[512,128]{1,0:T(8,128)(2,1)S(1)}, bf16[512,128]{1,0:T(8,128)(2,1)S(1)}, u32[]{:S(2)}, u32[]{:S(2)}) collective-permute-start(bf16[512,128]{1,0:T(8,128)(2,1)S(1)} %get-tuple-element.67), channel_id=1, source_target_pairs={{0,24},{2,26},{4,28},{6,30},{8,16},{10,18},{12,20},{14,22},{16,8},... | collective-permute-start | bytes 393224 | tf_op jit(solution)/shard_map/ppermute | solution.py:54
  89.2 5.8 %collective-permute-done.34.refs_3_ = bf16[64,2560]{1,0:T(8,128)(2,1)S(1)} collective-permute-done((bf16[64,2560]{1,0:T(8,128)(2,1)S(1)}, bf16[64,2560]{1,0:T(8,128)(2,1)S(1)}, u32[]{:S(2)}, u32[]{:S(2)}) %collective-permute-start.34) | collective-permute-done | bytes 327712 | tf_op jit(solution)/shard_map/ppermute | solution.py:54
  95.1 4.9 %collective-permute-done.33.refs_2_ = bf16[64,2560]{1,0:T(8,128)(2,1)S(1)} collective-permute-done((bf16[64,2560]{1,0:T(8,128)(2,1)S(1)}, bf16[64,2560]{1,0:T(8,128)(2,1)S(1)}, u32[]{:S(2)}, u32[]{:S(2)}) %collective-permute-start.33) | collective-permute-done | bytes 327712 | tf_op jit(solution)/shard_map/ppermute | solution.py:54
  100.0 2.3 %shard_map.115 = (f32[256,2048]{1,0:T(8,128)}, f32[256,512]{1,0:T(8,128)}) custom-call(s32[4,128]{1,0:T(4,128)S(1)} %pad_add_fusion.refs_0_.scalar_ref, bf16[64,2560]{1,0:T(8,128)(2,1)S(1)} %pad_maximum_fusion.refs_0_, bf16[64,2560]{1,0:T(8,128)(2,1)S(1)} %collective-permute-done.32.refs_1_, bf16[64,2560]{1,0:T(8,128)(2,1)S(1)} %collective-permute-done.33.refs_2_, ...), custom_call_target="tpu_custom_call" | custom-call | bytes 7000000 | tf_op jit(solution)/shard_map/pallas_call | solution.py:545
  (84 shorter events, 26.6 us)
Async XLA Ops:
  1.6 17.3 %collective-permute-start.8 = (bf16[512,128]{1,0:T(8,128)(2,1)S(1)}, bf16[512,128]{1,0:T(8,128)(2,1)S(1)}, u32[]{:S(2)}, u32[]{:S(2)}) collective-permute-start(bf16[512,128]{1,0:T(8,128)(2,1)S(1)} %dynamic-slice_bitcast_fusion.refs_3_), channel_id=1, source_target_pairs={{0,24},{2,26},{4,28},{6,30},{8,16},{10,18},{12,20},{14,22},{16,8},... | collective-permute-start | bytes 393224 | tf_op jit(solution)/shard_map/ppermute | solution.py:54
  6.7 12.3 %collective-permute-start.6 = (bf16[512,128]{1,0:T(8,128)(2,1)S(1)}, bf16[512,128]{1,0:T(8,128)(2,1)S(1)}, u32[]{:S(2)}, u32[]{:S(2)}) collective-permute-start(bf16[512,128]{1,0:T(8,128)(2,1)S(1)} %dynamic-slice_bitcast_fusion.refs_3_), channel_id=1, source_target_pairs={{0,16},{2,18},{4,20},{6,22},{8,24},{10,26},{12,28},{14,30},{16,0},... | collective-permute-start | bytes 393224 | tf_op jit(solution)/shard_map/ppermute | solution.py:54
  6.7 12.2 %collective-permute-start.4 = (bf16[512,128]{1,0:T(8,128)(2,1)S(1)}, bf16[512,128]{1,0:T(8,128)(2,1)S(1)}, u32[]{:S(2)}, u32[]{:S(2)}) collective-permute-start(bf16[512,128]{1,0:T(8,128)(2,1)S(1)} %dynamic-slice_bitcast_fusion.refs_3_), channel_id=1, source_target_pairs={{0,8},{2,10},{4,12},{6,14},{8,0},{10,2},{12,4},{14,6},{16,24},{18,... | collective-permute-start | bytes 393224 | tf_op jit(solution)/shard_map/ppermute | solution.py:54
  12.2 7.4 %collective-permute-start.3 = (bf16[512,128]{1,0:T(8,128)(2,1)S(1)}, bf16[512,128]{1,0:T(8,128)(2,1)S(1)}, u32[]{:S(2)}, u32[]{:S(2)}) collective-permute-start(bf16[512,128]{1,0:T(8,128)(2,1)S(1)} %dynamic-slice_bitcast_fusion.refs_3_), channel_id=1, source_target_pairs={{0,1},{1,0},{2,3},{3,2},{4,5},{5,4},{6,7},{7,6},{8,9},{9,8},{10,11... | collective-permute-start | bytes 393224 | tf_op jit(solution)/shard_map/ppermute | solution.py:46
  24.3 8.6 %collective-permute-start.13 = (bf16[256,2560]{1,0:T(8,128)(2,1)S(1)}, bf16[256,2560]{1,0:T(8,128)(2,1)S(1)}, u32[]{:S(2)}, u32[]{:S(2)}) collective-permute-start(bf16[256,2560]{1,0:T(8,128)(2,1)S(1)} %constant_dynamic-update-slice_fusion.refs_4_), channel_id=1, source_target_pairs={{0,1},{1,0},{2,3},{3,2},{4,5},{5,4},{6,7},{7,6},{8,9},{9,8},{10,11... | collective-permute-start | bytes 3932168 | tf_op jit(solution)/shard_map/ppermute | solution.py:46
  42.8 9.3 %collective-permute-start.22 = (bf16[64,1280]{1,0:T(8,128)(2,1)S(1)}, bf16[64,1280]{1,0:T(8,128)(2,1)S(1)}, u32[]{:S(2)}, u32[]{:S(2)}) collective-permute-start(bf16[64,1280]{1,0:T(8,128)(2,1)S(1)} %get-tuple-element.57), channel_id=1, source_target_pairs={{0,8},{2,10},{4,12},{6,14},{8,0},{10,2},{12,4},{14,6},{16,24},{18,... | collective-permute-start | bytes 491528 | tf_op jit(solution)/shard_map/ppermute | solution.py:54
  44.1 15.0 %collective-permute-start.23 = (bf16[64,1280]{1,0:T(8,128)(2,1)S(1)}, bf16[64,1280]{1,0:T(8,128)(2,1)S(1)}, u32[]{:S(2)}, u32[]{:S(2)}) collective-permute-start(bf16[64,1280]{1,0:T(8,128)(2,1)S(1)} %get-tuple-element.58), channel_id=1, source_target_pairs={{0,16},{2,18},{4,20},{6,22},{8,24},{10,26},{12,28},{14,30},{16,0},... | collective-permute-start | bytes 491528 | tf_op jit(solution)/shard_map/ppermute | solution.py:54
  47.1 12.1 %collective-permute-start.24 = (bf16[64,1280]{1,0:T(8,128)(2,1)S(1)}, bf16[64,1280]{1,0:T(8,128)(2,1)S(1)}, u32[]{:S(2)}, u32[]{:S(2)}) collective-permute-start(bf16[64,1280]{1,0:T(8,128)(2,1)S(1)} %get-tuple-element.59), channel_id=1, source_target_pairs={{0,24},{2,26},{4,28},{6,30},{8,16},{10,18},{12,20},{14,22},{16,8},... | collective-permute-start | bytes 491528 | tf_op jit(solution)/shard_map/ppermute | solution.py:54
  47.3 14.0 %collective-permute-start.15 = (bf16[64,1792]{1,0:T(8,128)(2,1)S(1)}, bf16[64,1792]{1,0:T(8,128)(2,1)S(1)}, u32[]{:S(2)}, u32[]{:S(2)}) collective-permute-start(bf16[64,1792]{1,0:T(8,128)(2,1)S(1)} %get-tuple-element.50), channel_id=1, source_target_pairs={{0,2},{2,0},{4,6},{6,4},{8,10},{10,8},{12,14},{14,12},{16,18},{18,... | collective-permute-start | bytes 688136 | tf_op jit(solution)/shard_map/ppermute | solution.py:54
  47.8 15.0 %collective-permute-start.16 = (bf16[64,1792]{1,0:T(8,128)(2,1)S(1)}, bf16[64,1792]{1,0:T(8,128)(2,1)S(1)}, u32[]{:S(2)}, u32[]{:S(2)}) collective-permute-start(bf16[64,1792]{1,0:T(8,128)(2,1)S(1)} %get-tuple-element.51), channel_id=1, source_target_pairs={{0,4},{2,6},{4,0},{6,2},{8,12},{10,14},{12,8},{14,10},{16,20},{18,... | collective-permute-start | bytes 688136 | tf_op jit(solution)/shard_map/ppermute | solution.py:54
  52.1 10.7 %collective-permute-start.17 = (bf16[64,1792]{1,0:T(8,128)(2,1)S(1)}, bf16[64,1792]{1,0:T(8,128)(2,1)S(1)}, u32[]{:S(2)}, u32[]{:S(2)}) collective-permute-start(bf16[64,1792]{1,0:T(8,128)(2,1)S(1)} %get-tuple-element.52), channel_id=1, source_target_pairs={{0,6},{2,4},{4,2},{6,0},{8,14},{10,12},{12,10},{14,8},{16,22},{18,... | collective-permute-start | bytes 688136 | tf_op jit(solution)/shard_map/ppermute | solution.py:54
  59.3 9.4 %collective-permute-start.25 = (bf16[16,1280]{1,0:T(8,128)(2,1)S(1)}, bf16[16,1280]{1,0:T(8,128)(2,1)S(1)}, u32[]{:S(2)}, u32[]{:S(2)}) collective-permute-start(bf16[16,1280]{1,0:T(8,128)(2,1)S(1)} %get-tuple-element.72), channel_id=1, source_target_pairs={{0,2},{2,0},{4,6},{6,4},{8,10},{10,8},{12,14},{14,12},{16,18},{18,... | collective-permute-start | bytes 122888 | tf_op jit(solution)/shard_map/ppermute | solution.py:54
  59.9 8.8 %collective-permute-start.27 = (bf16[16,1280]{1,0:T(8,128)(2,1)S(1)}, bf16[16,1280]{1,0:T(8,128)(2,1)S(1)}, u32[]{:S(2)}, u32[]{:S(2)}) collective-permute-start(bf16[16,1280]{1,0:T(8,128)(2,1)S(1)} %get-tuple-element.73), channel_id=1, source_target_pairs={{0,6},{2,4},{4,2},{6,0},{8,14},{10,12},{12,10},{14,8},{16,22},{18,... | collective-permute-start | bytes 122888 | tf_op jit(solution)/shard_map/ppermute | solution.py:54
  61.3 7.4 %collective-permute-start.26 = (bf16[16,1280]{1,0:T(8,128)(2,1)S(1)}, bf16[16,1280]{1,0:T(8,128)(2,1)S(1)}, u32[]{:S(2)}, u32[]{:S(2)}) collective-permute-start(bf16[16,1280]{1,0:T(8,128)(2,1)S(1)} %get-tuple-element.74), channel_id=1, source_target_pairs={{0,4},{2,6},{4,0},{6,2},{8,12},{10,14},{12,8},{14,10},{16,20},{18,... | collective-permute-start | bytes 122888 | tf_op jit(solution)/shard_map/ppermute | solution.py:54
  62.9 8.8 %collective-permute-start.19 = (bf16[16,1280]{1,0:T(8,128)(2,1)S(1)}, bf16[16,1280]{1,0:T(8,128)(2,1)S(1)}, u32[]{:S(2)}, u32[]{:S(2)}) collective-permute-start(bf16[16,1280]{1,0:T(8,128)(2,1)S(1)} %get-tuple-element.69), channel_id=1, source_target_pairs={{0,8},{2,10},{4,12},{6,14},{8,0},{10,2},{12,4},{14,6},{16,24},{18,... | collective-permute-start | bytes 122888 | tf_op jit(solution)/shard_map/ppermute | solution.py:54
  71.7 15.3 %collective-permute-start.18 = (bf16[4,512,128]{2,1,0:T(8,128)(2,1)S(1)}, bf16[4,512,128]{2,1,0:T(8,128)(2,1)S(1)}, u32[]{:S(2)}, u32[]{:S(2)}) collective-permute-start(bf16[4,512,128]{2,1,0:T(8,128)(2,1)S(1)} %get-tuple-element.54), channel_id=1, source_target_pairs={{0,1},{1,0},{2,3},{3,2},{4,5},{5,4},{6,7},{7,6},{8,9},{9,8},{10,11... | collective-permute-start | bytes 1572872 | tf_op jit(solution)/shard_map/ppermute | solution.py:46
  75.5 7.9 %collective-permute-start.29 = (bf16[16,2560]{1,0:T(8,128)(2,1)S(1)}, bf16[16,2560]{1,0:T(8,128)(2,1)S(1)}, u32[]{:S(2)}, u32[]{:S(2)}) collective-permute-start(bf16[16,2560]{1,0:T(8,128)(2,1)S(1)} %pad_maximum_fusion.1), channel_id=1, source_target_pairs={{0,16},{2,18},{4,20},{6,22},{8,24},{10,26},{12,28},{14,30},{16,0},... | collective-permute-start | bytes 245768 | tf_op jit(solution)/shard_map/ppermute | solution.py:54
  75.5 7.9 %collective-permute-start.28 = (bf16[16,2560]{1,0:T(8,128)(2,1)S(1)}, bf16[16,2560]{1,0:T(8,128)(2,1)S(1)}, u32[]{:S(2)}, u32[]{:S(2)}) collective-permute-start(bf16[16,2560]{1,0:T(8,128)(2,1)S(1)} %pad_maximum_fusion.1), channel_id=1, source_target_pairs={{0,8},{2,10},{4,12},{6,14},{8,0},{10,2},{12,4},{14,6},{16,24},{18,... | collective-permute-start | bytes 245768 | tf_op jit(solution)/shard_map/ppermute | solution.py:54
  83.4 11.6 %collective-permute-start.34 = (bf16[64,2560]{1,0:T(8,128)(2,1)S(1)}, bf16[64,2560]{1,0:T(8,128)(2,1)S(1)}, u32[]{:S(2)}, u32[]{:S(2)}) collective-permute-start(bf16[64,2560]{1,0:T(8,128)(2,1)S(1)} %pad_maximum_fusion.refs_0_), channel_id=1, source_target_pairs={{0,6},{2,4},{4,2},{6,0},{8,14},{10,12},{12,10},{14,8},{16,22},{18,... | collective-permute-start | bytes 983048 | tf_op jit(solution)/shard_map/ppermute | solution.py:54
  84.0 16.1 %collective-permute-start.33 = (bf16[64,2560]{1,0:T(8,128)(2,1)S(1)}, bf16[64,2560]{1,0:T(8,128)(2,1)S(1)}, u32[]{:S(2)}, u32[]{:S(2)}) collective-permute-start(bf16[64,2560]{1,0:T(8,128)(2,1)S(1)} %pad_maximum_fusion.refs_0_), channel_id=1, source_target_pairs={{0,4},{2,6},{4,0},{6,2},{8,12},{10,14},{12,8},{14,10},{16,20},{18,... | collective-permute-start | bytes 983048 | tf_op jit(solution)/shard_map/ppermute | solution.py:54
  85.5 14.6 %collective-permute-start.32 = (bf16[64,2560]{1,0:T(8,128)(2,1)S(1)}, bf16[64,2560]{1,0:T(8,128)(2,1)S(1)}, u32[]{:S(2)}, u32[]{:S(2)}) collective-permute-start(bf16[64,2560]{1,0:T(8,128)(2,1)S(1)} %pad_maximum_fusion.refs_0_), channel_id=1, source_target_pairs={{0,2},{2,0},{4,6},{6,4},{8,10},{10,8},{12,14},{14,12},{16,18},{18,... | collective-permute-start | bytes 983048 | tf_op jit(solution)/shard_map/ppermute | solution.py:54
  87.1 15.2 %collective-permute-start.31 = (bf16[512,128]{1,0:T(8,128)(2,1)S(1)}, bf16[512,128]{1,0:T(8,128)(2,1)S(1)}, u32[]{:S(2)}, u32[]{:S(2)}) collective-permute-start(bf16[512,128]{1,0:T(8,128)(2,1)S(1)} %get-tuple-element.66), channel_id=1, source_target_pairs={{0,8},{2,10},{4,12},{6,14},{8,0},{10,2},{12,4},{14,6},{16,24},{18,... | collective-permute-start | bytes 393224 | tf_op jit(solution)/shard_map/ppermute | solution.py:54
  87.2 15.1 %collective-permute-start.36 = (bf16[512,128]{1,0:T(8,128)(2,1)S(1)}, bf16[512,128]{1,0:T(8,128)(2,1)S(1)}, u32[]{:S(2)}, u32[]{:S(2)}) collective-permute-start(bf16[512,128]{1,0:T(8,128)(2,1)S(1)} %get-tuple-element.67), channel_id=1, source_target_pairs={{0,24},{2,26},{4,28},{6,30},{8,16},{10,18},{12,20},{14,22},{16,8},... | collective-permute-start | bytes 393224 | tf_op jit(solution)/shard_map/ppermute | solution.py:54
  95.0 7.4 %collective-permute-start.35 = (bf16[512,128]{1,0:T(8,128)(2,1)S(1)}, bf16[512,128]{1,0:T(8,128)(2,1)S(1)}, u32[]{:S(2)}, u32[]{:S(2)}) collective-permute-start(bf16[512,128]{1,0:T(8,128)(2,1)S(1)} %get-tuple-element.68), channel_id=1, source_target_pairs={{0,16},{2,18},{4,20},{6,22},{8,24},{10,26},{12,28},{14,30},{16,0},... | collective-permute-start | bytes 393224 | tf_op jit(solution)/shard_map/ppermute | solution.py:54
  (17 other events, 53.2 us)

commit v9 on v7

--- a/solution.py
+++ b/solution.py
@@ -139,7 +139,7 @@
     take = lambda count: [refs.pop(0) for _ in range(count)]
     (scalar_ref,) = take(1)
     scalars = [Scalars(scalar_ref, step, bals, slots) for step in range(groups)]
-    ids_refs, grad_refs, out_refs = take(bals), take(groups), refs
+    ids_refs, grad_refs, out_refs = take(bals), take(groups)[::-1], refs
     bal, _, table_here = scalars[0].place()
     tables, part, _ = out_refs[0].shape
     slot_rows = ids_refs[0].shape[3]
@@ -185,13 +185,13 @@
 def layer_kernel(groups, slots, tables, bals, unit, scalar_ref, *refs):
     refs = list(refs)
     take = lambda count: [refs.pop(0) for _ in range(count)]
-    block_refs = take(groups)
+    block_refs = take(groups)[::-1]
     weight_refs = take(bals)
     (cot_ref,) = take(1)
     (layer_ref,) = take(1)
     grad_refs = take(groups)
     term_refs = take(bals)
-    (x_ref, w_in, w_out, nt_ref, mt_ref, weights_ref, slope_ref, gate_ref, heads_ref, dsilu_ref, grads_ref, sems) = refs
+    (x_ref, halves_ref, wide_ref, nt_ref, mt_ref, weights_ref, slope_ref, gate_ref, heads_ref, dsilu_ref, grads_ref) = refs
 
     scalars = Scalars(scalar_ref, 0, bals, slots)
     bal, group_here, table_here = scalars.place()
@@ -200,22 +200,20 @@
     head_width = width // HEADS
     score_scale = head_width**-0.5
     piece = block_refs[0].shape[1]
-    part, features = weight_refs[0].shape[0], w_in.shape[1]
-
-    in_copies, out_copies = [], []
-    for turn in range(bals):
-        at = pl.ds(pl.multiple_of((bal ^ turn) * part, part), part)
-        here = weight_refs[turn]
-        in_copies.append(
-            pltpu.make_async_copy(here.at[:, pl.ds(0, features)], w_in.at[at, :], sems.at[2 * turn])
-        )
-        out_copies.append(
-            pltpu.make_async_copy(
-                here.at[:, pl.ds(features, width)], w_out.at[at, :], sems.at[2 * turn + 1]
-            )
-        )
-    for copy in in_copies + out_copies:
-        copy.start()
+    part, features = weight_refs[0].shape[0], weight_refs[0].shape[1] - width
+
+    def times_parts(value, first, last):
+        for index in range(bals):
+            halves_ref[index] = value[:, index * part : (index + 1) * part]
+        found = matmul(halves_ref[bal], weight_refs[0][:, first:last])
+        for turn in range(1, bals):
+            found = found + matmul(halves_ref[bal ^ turn], weight_refs[turn][:, first:last])
+        return found
+
+    def times_parts_nt(value, first, last):
+        for turn in range(bals):
+            wide_ref[bal ^ turn] = matmul_nt(value, weight_refs[turn][:, first:last])
+        return jnp.concatenate([wide_ref[index] for index in range(bals)], axis=1)
 
     my_slot = scalars.surplus(bal)
     source = scalars.source(bal)
@@ -227,9 +225,7 @@
     x = jnp.concatenate([x_ref[group] for group in range(groups)], axis=1).astype(f32)
     normed_in, in_inverse = norm(x)
     nt_ref[...] = jnp.transpose(normed_in).astype(bf16)
-    for copy in in_copies:
-        copy.wait()
-    projected = matmul(normed_in.astype(bf16), w_in[...])
+    projected = times_parts(normed_in.astype(bf16), 0, features)
     logistic = sigmoid(projected)
     active = projected * logistic
     dsilu_ref[...] = logistic + active * (1.0 - logistic)
@@ -273,13 +269,11 @@
     gate = gate_ref[...]
     mixed = normed_out * gate
     mt_ref[...] = jnp.transpose(mixed).astype(bf16)
-    for copy in out_copies:
-        copy.wait()
-    layer_ref[...] = (x + matmul(mixed.astype(bf16), w_out[...])).astype(bf16)
+    layer_ref[...] = (x + times_parts(mixed.astype(bf16), features, features + width)).astype(bf16)
 
     wide_cot = cot_ref[...]
     cot = wide_cot.astype(bf16)
-    grad_mixed = matmul_nt(cot, w_out[...])
+    grad_mixed = times_parts_nt(cot, features, features + width)
     grad_attended = norm_back(grad_mixed * gate, normed_out, out_inverse).astype(bf16)
     grads_ref[:, :width] = (grad_mixed * normed_out * dsilu_ref[:, :width]).astype(bf16)
 
@@ -317,7 +311,7 @@
     for turn in range(bals):
         term_refs[turn][:, :features] = matmul(owner_order(nt_ref, turn), grads_ref[...]).astype(bf16)
 
-    grad_normed = matmul_nt(grads_ref[...], w_in[...])
+    grad_normed = times_parts_nt(grads_ref[...], 0, features)
     grad_rows = (wide_cot + norm_back(grad_normed, normed_in, in_inverse)).astype(bf16)
     for group in range(groups):
         x_ref[group] = grad_rows[:, group * piece : (group + 1) * piece]
@@ -345,15 +339,15 @@
                 out[:, at : at + columns] = grad[index * height : (index + 1) * height, :]
 
 
-def place_kernel(scale, groups, slots, tables, bals, unit, scalar_ref, *refs):
-    pieces = refs[:groups]
-    in_ref, out_ref, scaled_ref, sems = refs[groups:]
+def place_kernel(scale, steps, slots, tables, bals, unit, scalar_ref, *refs):
+    pieces = refs[: len(steps)]
+    in_ref, out_ref, scaled_ref, sems = refs[-4:]
     _, group_here, table_here = Scalars(scalar_ref, 0, bals, slots).place()
     features = in_ref.shape[1]
     copies = []
-    for group_step, piece in enumerate(pieces):
+    for number, (group_step, piece) in enumerate(zip(steps, pieces)):
         for table_step in range(tables):
-            index = group_step * tables + table_step
+            index = number * tables + table_step
             at = index * unit
             from_rows = slice(table_step * unit, (table_step + 1) * unit)
             scaled_ref[at : at + unit, :] = piece[from_rows, :].astype(f32) * scale
@@ -453,12 +447,12 @@
         out_shape=[jax.ShapeDtypeStruct((rows, width), bf16)]
         + [jax.ShapeDtypeStruct((rows, columns), bf16)] * groups
         + [terms] * bals,
-        in_specs=[SMEM] + [VMEM] * groups + [HBM] * bals + [VMEM],
+        in_specs=[SMEM] + [VMEM] * (groups + bals + 1),
         out_specs=[VMEM] * (1 + groups + bals),
         scratch_shapes=[
             pltpu.VMEM((groups, rows, columns), bf16),
-            pltpu.VMEM((width, features), bf16),
-            pltpu.VMEM((width, width), bf16),
+            pltpu.VMEM((bals, rows, weight_part), bf16),
+            pltpu.VMEM((bals, rows, weight_part), f32),
             pltpu.VMEM((width, rows), bf16),
             pltpu.VMEM((width, rows), bf16),
             pltpu.VMEM((pairs, 2 * slot_rows, slot_rows), bf16),
@@ -467,11 +461,10 @@
             pltpu.VMEM((rows, features - width), bf16),
             pltpu.VMEM((rows, features), f32),
             pltpu.VMEM((rows, features), bf16),
-            pltpu.SemaphoreType.DMA((2 * bals,)),
         ],
         cost_estimate=estimate(7),
         compiler_params=room(36),
-    )(scalars, *block, *weights, wide_cot)
+    )(scalars, *block[::-1], *weights, wide_cot)
     layer_out, results = results[0], results[1:]
     grads, results = results[:groups], results[groups:]
 
@@ -489,7 +482,7 @@
             out_specs=[VMEM] * bals,
             cost_estimate=estimate(3),
             compiler_params=room(16),
-        )(scalars, *plane_ids, *plane_grads)
+        )(scalars, *plane_ids, *plane_grads[::-1])
 
     grad_scale = (rows * embs * bals) ** -0.5
     if owned:
@@ -504,12 +497,12 @@
             compiler_params=room(12),
         )(*terms, *grads[1:])
         came = [emb_swap(pieces[step], step, embs) for step in range(1, groups)]
-        mine = sum_rounded([pieces[0]] + [value[:, :wide] for value in came])
+        mine = sum_rounded([value[:, :wide] for value in came[::-1]] + [pieces[0]])
         mine = mine.reshape(tables, unit, wide)
         sums = table_sums([grads[0]] + came)
         own_sums = over_cores(sums)
         came = [emb_swap(mine[step], step * groups, embs) for step in range(1, tables)]
-        final = sum_rounded([mine[0]] + came)
+        final = sum_rounded(came[-1:] + came[:-1] + [mine[0]])
         gathered = [final] + [emb_swap(final, step * groups, embs) for step in range(1, tables)]
         back = to_plane(jnp.concatenate(gathered, axis=0))
         later = after(own_sums, *gathered[1:])
@@ -519,27 +512,33 @@
         sums = table_sums([grads[0]] + [emb_swap(grads[step], step, embs) for step in range(1, groups)])
         own_sums = over_cores(sums)
         swapped = [emb_swap(own_sums[step], step * groups, embs) for step in range(1, tables)]
-    table_sum = own_sums[0].astype(f32)
-    for value in swapped:
+    table_sum = swapped[-1].astype(f32)
+    for value in swapped[:-1] + [own_sums[0]]:
         table_sum = table_sum + value.astype(f32)
     table_scale = (distinct / (bals * item_ids.shape[1])) ** 0.5
 
     if owned:
-        total_in, total_out = pl.pallas_call(
-            functools.partial(place_kernel, grad_scale, groups, slots, tables, bals, unit),
-            out_shape=[
-                jax.ShapeDtypeStruct((weight_part, features), f32),
-                jax.ShapeDtypeStruct((weight_part, width), f32),
-            ],
-            in_specs=[SMEM] + [VMEM] * groups,
-            out_specs=[HBM] * 2,
-            scratch_shapes=[
-                pltpu.VMEM((weight_part, features + width), f32),
-                pltpu.SemaphoreType.DMA((groups * tables, 2)),
-            ],
-            cost_estimate=estimate(2),
-            compiler_params=room(12),
-        )(scalars, *back)
+        totals = []
+        for steps in ([0] + list(range(groups - 1, 1, -1))[: groups // 2 - 1], None):
+            steps = steps or [step for step in range(1, groups) if step not in done]
+            done = steps
+            totals = pl.pallas_call(
+                functools.partial(place_kernel, grad_scale, steps, slots, tables, bals, unit),
+                out_shape=[
+                    jax.ShapeDtypeStruct((weight_part, features), f32),
+                    jax.ShapeDtypeStruct((weight_part, width), f32),
+                ],
+                in_specs=[SMEM] + [VMEM] * len(steps) + [HBM] * len(totals),
+                out_specs=[HBM] * 2,
+                scratch_shapes=[
+                    pltpu.VMEM((len(steps) * tables * unit, features + width), f32),
+                    pltpu.SemaphoreType.DMA((len(steps) * tables, 2)),
+                ],
+                input_output_aliases={1 + len(steps) + index: index for index in range(len(totals))},
+                cost_estimate=estimate(1),
+                compiler_params=room(12),
+            )(scalars, *[back[step] for step in steps], *totals)
+        total_in, total_out = totals
     else:
         total = lax.psum(over_cores(results).astype(f32), "emb") * grad_scale
         total_in, total_out = total[:, :features], total[:, features:]

time: 102 us -> 101 us (level)
    pallas_call x1 -> x2, Pallas kernels: 2.32 us -> 3.5 us  [on_device(): pl.pallas_call(functools.partial(place_kernel, grad_scale, steps, slots,...]
    ppermute x23, starting transfers between devices: 31.3 us -> 30.3 us  [emb_swap(): return lax.ppermute(value, 'emb', [(i, i ^ step) for i in range(count)])]
  transfers between devices with their start and end apart: 31 -> 31, of which waited for: 15 -> 15; matrix products, arithmetic and copies ran while one was open for 4% -> 4% of each run, Pallas kernels for 5% -> 6%
where the time goes in v9:
time: 101 us
  waiting for transfers between devices  45.5 us (45%)
  starting transfers between devices  31.7 us (31%)
  Pallas kernels  16.5 us (16%)
  other arithmetic  3.96 us (4%)
  local copies, waits for them, and re-layouts  2.42 us (2%)
    ppermute x23, waiting for transfers between devices, emb_swap(): return lax.ppermute(value, 'emb', [(i, i ^ step) for i in range(count)])  42.5 us
    ppermute x23, starting transfers between devices, emb_swap(): return lax.ppermute(value, 'emb', [(i, i ^ step) for i in range(count)])  30.3 us
    pallas_call x1, Pallas kernels, on_device(): pl.pallas_call(functools.partial(layer_kernel, groups, slots, tables, bal...  6.29 us
    pallas_call x2, Pallas kernels, on_device(): pl.pallas_call(functools.partial(place_kernel, grad_scale, steps, slots,...  3.5 us
    pallas_call x1, Pallas kernels, on_device(): pl.pallas_call(functools.partial(lookup_kernel, groups, slots, tables, ba...  3.46 us
    ppermute x8, waiting for transfers between devices, bal_swap(): return lax.ppermute(value, 'bal', [(i, i ^ step) for i in range(count)])  3.06 us
    pallas_call x1, Pallas kernels, table_sums(): pl.pallas_call(functools.partial(scatter_kernel, groups, slots, bals), ou...  2.91 us
  transfers between devices with their start and end apart: 31, of which 15 were waited for; matrix products, arithmetic and copies ran while one was open for 4% of the time, Pallas kernels for 6%

profile of v9, /device:TPU:0, one launch (start us, length us, event | category | flops | bytes accessed | tf_op | source)
XLA Modules:
  0.0 100.9 jit_solution(11993144714412376713)
XLA Ops:
  1.6 5.1 %collective-permute-start.8 = (bf16[512,128]{1,0:T(8,128)(2,1)S(1)}, bf16[512,128]{1,0:T(8,128)(2,1)S(1)}, u32[]{:S(2)}, u32[]{:S(2)}) collective-permute-start(bf16[512,128]{1,0:T(8,128)(2,1)S(1)} %dynamic-slice_bitcast_fusion.refs_3_), channel_id=1, source_target_pairs={{0,24},{2,26},{4,28},{6,30},{8,16},{10,18},{12,20},{14,22},{16,8},... | collective-permute-start | bytes 393224 | tf_op jit(solution)/shard_map/ppermute | solution.py:54
  9.8 1.6 %collective-permute-start = (s32[1,128]{1,0:T(1,128)S(1)}, s32[1,128]{1,0:T(1,128)S(1)}, u32[]{:S(2)}, u32[]{:S(2)}) collective-permute-start(s32[1,128]{1,0:T(1,128)S(1)} %pad_add_fusion.2), channel_id=1, source_target_pairs={{0,2},{2,0},{4,6},{6,4},{8,10},{10,8},{12,14},{14,12},{16,18},{18,... | collective-permute-start | bytes 1544 | tf_op jit(solution)/shard_map/ppermute | solution.py:54
  11.4 1.9 %collective-permute-done = s32[1,128]{1,0:T(1,128)S(1)} collective-permute-done((s32[1,128]{1,0:T(1,128)S(1)}, s32[1,128]{1,0:T(1,128)S(1)}, u32[]{:S(2)}, u32[]{:S(2)}) %collective-permute-start) | collective-permute-done | bytes 544 | tf_op jit(solution)/shard_map/ppermute | solution.py:54
  13.4 1.7 %collective-permute-start.1 = (s32[2,128]{1,0:T(2,128)S(1)}, s32[2,128]{1,0:T(2,128)S(1)}, u32[]{:S(2)}, u32[]{:S(2)}) collective-permute-start(s32[2,128]{1,0:T(2,128)S(1)} %pad_add_fusion.1), channel_id=1, source_target_pairs={{0,4},{2,6},{4,0},{6,2},{8,12},{10,14},{12,8},{14,10},{16,20},{18,... | collective-permute-start | bytes 3080 | tf_op jit(solution)/shard_map/ppermute | solution.py:54
  19.1 3.5 %shard_map.111 = (bf16[256,128]{1,0:T(8,128)(2,1)S(1)}, bf16[256,128]{1,0:T(8,128)(2,1)S(1)}, bf16[256,128]{1,0:T(8,128)(2,1)S(1)}, bf16[256,128]{1,0:T(8,128)(2,1)S(1)}) custom-call(s32[4,128]{1,0:T(4,128)S(1)} %pad_add_fusion.refs_0_.scalar_ref, s32[4,8,1,128]{3,2,1,0:T(1,128)S(1)} %reshape.61.refs_1_, ...), custom_call_target="tpu_custom_call" | custom-call | bytes 10500000 | tf_op jit(solution)/shard_map/pallas_call | solution.py:431
  22.9 2.6 %collective-permute-start.10 = (bf16[256,128]{1,0:T(8,128)(2,1)S(1)}, bf16[256,128]{1,0:T(8,128)(2,1)S(1)}, u32[]{:S(2)}, u32[]{:S(2)}) collective-permute-start(bf16[256,128]{1,0:T(8,128)(2,1)S(1)} %get-tuple-element.36), channel_id=1, source_target_pairs={{0,6},{2,4},{4,2},{6,0},{8,14},{10,12},{12,10},{14,8},{16,22},{18,... | collective-permute-start | bytes 196616 | tf_op jit(solution)/shard_map/ppermute | solution.py:54
  26.4 1.7 %collective-permute-done.10.refs_0_ = bf16[256,128]{1,0:T(8,128)(2,1)S(1)} collective-permute-done((bf16[256,128]{1,0:T(8,128)(2,1)S(1)}, bf16[256,128]{1,0:T(8,128)(2,1)S(1)}, u32[]{:S(2)}, u32[]{:S(2)}) %collective-permute-start.10) | collective-permute-done | bytes 65568 | tf_op jit(solution)/shard_map/ppermute | solution.py:54
  28.1 1.7 %collective-permute-done.11.refs_1_ = bf16[256,128]{1,0:T(8,128)(2,1)S(1)} collective-permute-done((bf16[256,128]{1,0:T(8,128)(2,1)S(1)}, bf16[256,128]{1,0:T(8,128)(2,1)S(1)}, u32[]{:S(2)}, u32[]{:S(2)}) %collective-permute-start.11) | collective-permute-done | bytes 65568 | tf_op jit(solution)/shard_map/ppermute | solution.py:54
  30.3 6.3 %shard_map.112 = (bf16[256,512]{1,0:T(8,128)(2,1)}, bf16[256,128]{1,0:T(8,128)(2,1)S(1)}, bf16[256,128]{1,0:T(8,128)(2,1)S(1)}, bf16[256,128]{1,0:T(8,128)(2,1)S...) custom-call(s32[4,128]{1,0:T(4,128)S(1)} %pad_add_fusion.refs_0_.scalar_ref, ...), custom_call_target="tpu_custom_call" | custom-call | bytes 24500000 | tf_op jit(solution)/shard_map/pallas_call | solution.py:445
  36.7 3.0 %collective-permute-done.14.refs_1_ = bf16[256,2560]{1,0:T(8,128)(2,1)S(1)} collective-permute-done((bf16[256,2560]{1,0:T(8,128)(2,1)S(1)}, bf16[256,2560]{1,0:T(8,128)(2,1)S(1)}, u32[]{:S(2)}, u32[]{:S(2)}) %collective-permute-start.14) | collective-permute-done | bytes 1310752 | tf_op jit(solution)/shard_map/ppermute | solution.py:46
  43.6 9.4 %collective-permute-done.15.refs_3_ = bf16[64,3072]{1,0:T(8,128)(2,1)S(1)} collective-permute-done((bf16[64,3072]{1,0:T(8,128)(2,1)S(1)}, bf16[64,3072]{1,0:T(8,128)(2,1)S(1)}, u32[]{:S(2)}, u32[]{:S(2)}) %collective-permute-start.15) | collective-permute-done | bytes 393248 | tf_op jit(solution)/shard_map/ppermute | solution.py:54
  53.0 7.6 %collective-permute-done.16.refs_4_ = bf16[64,3072]{1,0:T(8,128)(2,1)S(1)} collective-permute-done((bf16[64,3072]{1,0:T(8,128)(2,1)S(1)}, bf16[64,3072]{1,0:T(8,128)(2,1)S(1)}, u32[]{:S(2)}, u32[]{:S(2)}) %collective-permute-start.16) | collective-permute-done | bytes 393248 | tf_op jit(solution)/shard_map/ppermute | solution.py:54
  60.8 3.7 %collective-permute-start.19 = (bf16[16,2560]{1,0:T(8,128)(2,1)S(1)}, bf16[16,2560]{1,0:T(8,128)(2,1)S(1)}, u32[]{:S(2)}, u32[]{:S(2)}) collective-permute-start(bf16[16,2560]{1,0:T(8,128)(2,1)S(1)} %get-tuple-element.65), channel_id=1, source_target_pairs={{0,24},{2,26},{4,28},{6,30},{8,16},{10,18},{12,20},{14,22},{16,8},... | collective-permute-start | bytes 245768 | tf_op jit(solution)/shard_map/ppermute | solution.py:54
  65.3 2.9 %shard_map.114 = (bf16[4,512,128]{2,1,0:T(8,128)(2,1)S(1)}, bf16[4,512,128]{2,1,0:T(8,128)(2,1)S(1)}) custom-call(s32[4,128]{1,0:T(4,128)S(1)} %pad_add_fusion.refs_0_.scalar_ref, s32[4,8,1,128]{3,2,1,0:T(1,128)S(1)} %reshape.61.refs_1_, s32[4,8,1,128]{3,2,1,0:T(1,128)S(1)} %collective-permute-done.2.refs_2_, ...), custom_call_target="tpu_custom_call" | custom-call | bytes 10500000 | tf_op jit(solution)/shard_map/pallas_call | solution.py:478
  68.3 3.0 %collective-permute-done.21 = bf16[16,2560]{1,0:T(8,128)(2,1)S(1)} collective-permute-done((bf16[16,2560]{1,0:T(8,128)(2,1)S(1)}, bf16[16,2560]{1,0:T(8,128)(2,1)S(1)}, u32[]{:S(2)}, u32[]{:S(2)}) %collective-permute-start.21) | collective-permute-done | bytes 81952 | tf_op jit(solution)/shard_map/ppermute | solution.py:54
  71.3 2.4 %collective-permute-start.24 = (bf16[16,2560]{1,0:T(8,128)(2,1)S(1)}, bf16[16,2560]{1,0:T(8,128)(2,1)S(1)}, u32[]{:S(2)}, u32[]{:S(2)}) collective-permute-start(bf16[16,2560]{1,0:T(8,128)(2,1)S(1)} %add_convert_fusion.2), channel_id=1, source_target_pairs={{0,24},{2,26},{4,28},{6,30},{8,16},{10,18},{12,20},{14,22},{16,8},... | collective-permute-start | bytes 245768 | tf_op jit(solution)/shard_map/ppermute | solution.py:54
  73.9 1.9 %collective-permute-start.22 = (bf16[16,2560]{1,0:T(8,128)(2,1)S(1)}, bf16[16,2560]{1,0:T(8,128)(2,1)S(1)}, u32[]{:S(2)}, u32[]{:S(2)}) collective-permute-start(bf16[16,2560]{1,0:T(8,128)(2,1)S(1)} %add_convert_fusion.2), channel_id=1, source_target_pairs={{0,8},{2,10},{4,12},{6,14},{8,0},{10,2},{12,4},{14,6},{16,24},{18,... | collective-permute-start | bytes 245768 | tf_op jit(solution)/shard_map/ppermute | solution.py:54
  75.8 2.7 %collective-permute-done.24 = bf16[16,2560]{1,0:T(8,128)(2,1)S(1)} collective-permute-done((bf16[16,2560]{1,0:T(8,128)(2,1)S(1)}, bf16[16,2560]{1,0:T(8,128)(2,1)S(1)}, u32[]{:S(2)}, u32[]{:S(2)}) %collective-permute-start.24) | collective-permute-done | bytes 81952 | tf_op jit(solution)/shard_map/ppermute | solution.py:54
  78.5 2.9 %collective-permute-done.23 = bf16[16,2560]{1,0:T(8,128)(2,1)S(1)} collective-permute-done((bf16[16,2560]{1,0:T(8,128)(2,1)S(1)}, bf16[16,2560]{1,0:T(8,128)(2,1)S(1)}, u32[]{:S(2)}, u32[]{:S(2)}) %collective-permute-start.23) | collective-permute-done | bytes 81952 | tf_op jit(solution)/shard_map/ppermute | solution.py:54
  85.2 1.7 %collective-permute-start.25 = (bf16[512,128]{1,0:T(8,128)(2,1)S(1)}, bf16[512,128]{1,0:T(8,128)(2,1)S(1)}, u32[]{:S(2)}, u32[]{:S(2)}) collective-permute-start(bf16[512,128]{1,0:T(8,128)(2,1)S(1)} %get-tuple-element.62), channel_id=1, source_target_pairs={{0,24},{2,26},{4,28},{6,30},{8,16},{10,18},{12,20},{14,22},{16,8},... | collective-permute-start | bytes 393224 | tf_op jit(solution)/shard_map/ppermute | solution.py:54
  86.9 6.2 %collective-permute-done.28.refs_1_ = bf16[64,2560]{1,0:T(8,128)(2,1)S(1)} collective-permute-done((bf16[64,2560]{1,0:T(8,128)(2,1)S(1)}, bf16[64,2560]{1,0:T(8,128)(2,1)S(1)}, u32[]{:S(2)}, u32[]{:S(2)}) %collective-permute-start.28) | collective-permute-done | bytes 327712 | tf_op jit(solution)/shard_map/ppermute | solution.py:54
  93.1 1.8 %shard_map.115 = (f32[256,2048]{1,0:T(8,128)}, f32[256,512]{1,0:T(8,128)}) custom-call(s32[4,128]{1,0:T(4,128)S(1)} %pad_add_fusion.refs_0_.scalar_ref, bf16[64,2560]{1,0:T(8,128)(2,1)S(1)} %pad_maximum_fusion.1.refs_0_, bf16[64,2560]{1,0:T(8,128)(2,1)S(1)} %collective-permute-done.28.refs_1_), custom_call_target="tpu_custom_call" | custom-call | bytes 3500000 | tf_op jit(solution)/shard_map/pallas_call | solution.py:525
  94.8 3.5 %collective-permute-done.27.refs_1_ = bf16[64,2560]{1,0:T(8,128)(2,1)S(1)} collective-permute-done((bf16[64,2560]{1,0:T(8,128)(2,1)S(1)}, bf16[64,2560]{1,0:T(8,128)(2,1)S(1)}, u32[]{:S(2)}, u32[]{:S(2)}) %collective-permute-start.27) | collective-permute-done | bytes 327712 | tf_op jit(solution)/shard_map/ppermute | solution.py:54
  98.3 1.8 %shard_map.116 = (f32[256,2048]{1,0:T(8,128)}, f32[256,512]{1,0:T(8,128)}) custom-call(s32[4,128]{1,0:T(4,128)S(1)} %pad_add_fusion.refs_0_.scalar_ref, bf16[64,2560]{1,0:T(8,128)(2,1)S(1)} %collective-permute-done.26.refs_0_, bf16[64,2560]{1,0:T(8,128)(2,1)S(1)} %collective-permute-done.27.refs_1_, ...), custom_call_target="tpu_custom_call", output_to_operand_aliasing={{0}: (3, {}), {1}: (4, {})} | custom-call | bytes 3500000 | tf_op jit(solution)/shard_map/pallas_call | solution.py:525
  (64 shorter events, 19.6 us)
Async XLA Ops:
  1.6 15.9 %collective-permute-start.8 = (bf16[512,128]{1,0:T(8,128)(2,1)S(1)}, bf16[512,128]{1,0:T(8,128)(2,1)S(1)}, u32[]{:S(2)}, u32[]{:S(2)}) collective-permute-start(bf16[512,128]{1,0:T(8,128)(2,1)S(1)} %dynamic-slice_bitcast_fusion.refs_3_), channel_id=1, source_target_pairs={{0,24},{2,26},{4,28},{6,30},{8,16},{10,18},{12,20},{14,22},{16,8},... | collective-permute-start | bytes 393224 | tf_op jit(solution)/shard_map/ppermute | solution.py:54
  6.7 11.1 %collective-permute-start.6 = (bf16[512,128]{1,0:T(8,128)(2,1)S(1)}, bf16[512,128]{1,0:T(8,128)(2,1)S(1)}, u32[]{:S(2)}, u32[]{:S(2)}) collective-permute-start(bf16[512,128]{1,0:T(8,128)(2,1)S(1)} %dynamic-slice_bitcast_fusion.refs_3_), channel_id=1, source_target_pairs={{0,16},{2,18},{4,20},{6,22},{8,24},{10,26},{12,28},{14,30},{16,0},... | collective-permute-start | bytes 393224 | tf_op jit(solution)/shard_map/ppermute | solution.py:54
  6.7 10.2 %collective-permute-start.4 = (bf16[512,128]{1,0:T(8,128)(2,1)S(1)}, bf16[512,128]{1,0:T(8,128)(2,1)S(1)}, u32[]{:S(2)}, u32[]{:S(2)}) collective-permute-start(bf16[512,128]{1,0:T(8,128)(2,1)S(1)} %dynamic-slice_bitcast_fusion.refs_3_), channel_id=1, source_target_pairs={{0,8},{2,10},{4,12},{6,14},{8,0},{10,2},{12,4},{14,6},{16,24},{18,... | collective-permute-start | bytes 393224 | tf_op jit(solution)/shard_map/ppermute | solution.py:54
  11.4 7.7 %collective-permute-start.3 = (bf16[512,128]{1,0:T(8,128)(2,1)S(1)}, bf16[512,128]{1,0:T(8,128)(2,1)S(1)}, u32[]{:S(2)}, u32[]{:S(2)}) collective-permute-start(bf16[512,128]{1,0:T(8,128)(2,1)S(1)} %dynamic-slice_bitcast_fusion.refs_3_), channel_id=1, source_target_pairs={{0,1},{1,0},{2,3},{3,2},{4,5},{5,4},{6,7},{7,6},{8,9},{9,8},{10,11... | collective-permute-start | bytes 393224 | tf_op jit(solution)/shard_map/ppermute | solution.py:46
  22.6 7.7 %collective-permute-start.13 = (bf16[256,2560]{1,0:T(8,128)(2,1)S(1)}, bf16[256,2560]{1,0:T(8,128)(2,1)S(1)}, u32[]{:S(2)}, u32[]{:S(2)}) collective-permute-start(bf16[256,2560]{1,0:T(8,128)(2,1)S(1)} %pad_maximum_fusion.refs_4_), channel_id=1, source_target_pairs={{0,1},{1,0},{2,3},{3,2},{4,5},{5,4},{6,7},{7,6},{8,9},{9,8},{10,11... | collective-permute-start | bytes 3932168 | tf_op jit(solution)/shard_map/ppermute | solution.py:46
  22.9 5.2 %collective-permute-start.10 = (bf16[256,128]{1,0:T(8,128)(2,1)S(1)}, bf16[256,128]{1,0:T(8,128)(2,1)S(1)}, u32[]{:S(2)}, u32[]{:S(2)}) collective-permute-start(bf16[256,128]{1,0:T(8,128)(2,1)S(1)} %get-tuple-element.36), channel_id=1, source_target_pairs={{0,6},{2,4},{4,2},{6,0},{8,14},{10,12},{12,10},{14,8},{16,22},{18,... | collective-permute-start | bytes 196616 | tf_op jit(solution)/shard_map/ppermute | solution.py:54
  25.5 4.3 %collective-permute-start.11 = (bf16[256,128]{1,0:T(8,128)(2,1)S(1)}, bf16[256,128]{1,0:T(8,128)(2,1)S(1)}, u32[]{:S(2)}, u32[]{:S(2)}) collective-permute-start(bf16[256,128]{1,0:T(8,128)(2,1)S(1)} %get-tuple-element.37), channel_id=1, source_target_pairs={{0,4},{2,6},{4,0},{6,2},{8,12},{10,14},{12,8},{14,10},{16,20},{18,... | collective-permute-start | bytes 196616 | tf_op jit(solution)/shard_map/ppermute | solution.py:54
  26.0 4.3 %collective-permute-start.12 = (bf16[256,128]{1,0:T(8,128)(2,1)S(1)}, bf16[256,128]{1,0:T(8,128)(2,1)S(1)}, u32[]{:S(2)}, u32[]{:S(2)}) collective-permute-start(bf16[256,128]{1,0:T(8,128)(2,1)S(1)} %get-tuple-element.38), channel_id=1, source_target_pairs={{0,2},{2,0},{4,6},{6,4},{8,10},{10,8},{12,14},{14,12},{16,18},{18,... | collective-permute-start | bytes 196616 | tf_op jit(solution)/shard_map/ppermute | solution.py:54
  40.0 13.0 %collective-permute-start.15 = (bf16[64,3072]{1,0:T(8,128)(2,1)S(1)}, bf16[64,3072]{1,0:T(8,128)(2,1)S(1)}, u32[]{:S(2)}, u32[]{:S(2)}) collective-permute-start(bf16[64,3072]{1,0:T(8,128)(2,1)S(1)} %get-tuple-element.47), channel_id=1, source_target_pairs={{0,6},{2,4},{4,2},{6,0},{8,14},{10,12},{12,10},{14,8},{16,22},{18,... | collective-permute-start | bytes 1179656 | tf_op jit(solution)/shard_map/ppermute | solution.py:54
  41.5 19.0 %collective-permute-start.16 = (bf16[64,3072]{1,0:T(8,128)(2,1)S(1)}, bf16[64,3072]{1,0:T(8,128)(2,1)S(1)}, u32[]{:S(2)}, u32[]{:S(2)}) collective-permute-start(bf16[64,3072]{1,0:T(8,128)(2,1)S(1)} %get-tuple-element.48), channel_id=1, source_target_pairs={{0,4},{2,6},{4,0},{6,2},{8,12},{10,14},{12,8},{14,10},{16,20},{18,... | collective-permute-start | bytes 1179656 | tf_op jit(solution)/shard_map/ppermute | solution.py:54
  42.4 18.2 %collective-permute-start.17 = (bf16[64,3072]{1,0:T(8,128)(2,1)S(1)}, bf16[64,3072]{1,0:T(8,128)(2,1)S(1)}, u32[]{:S(2)}, u32[]{:S(2)}) collective-permute-start(bf16[64,3072]{1,0:T(8,128)(2,1)S(1)} %get-tuple-element.49), channel_id=1, source_target_pairs={{0,2},{2,0},{4,6},{6,4},{8,10},{10,8},{12,14},{14,12},{16,18},{18,... | collective-permute-start | bytes 1179656 | tf_op jit(solution)/shard_map/ppermute | solution.py:54
  60.8 7.5 %collective-permute-start.19 = (bf16[16,2560]{1,0:T(8,128)(2,1)S(1)}, bf16[16,2560]{1,0:T(8,128)(2,1)S(1)}, u32[]{:S(2)}, u32[]{:S(2)}) collective-permute-start(bf16[16,2560]{1,0:T(8,128)(2,1)S(1)} %get-tuple-element.65), channel_id=1, source_target_pairs={{0,24},{2,26},{4,28},{6,30},{8,16},{10,18},{12,20},{14,22},{16,8},... | collective-permute-start | bytes 245768 | tf_op jit(solution)/shard_map/ppermute | solution.py:54
  64.5 6.8 %collective-permute-start.21 = (bf16[16,2560]{1,0:T(8,128)(2,1)S(1)}, bf16[16,2560]{1,0:T(8,128)(2,1)S(1)}, u32[]{:S(2)}, u32[]{:S(2)}) collective-permute-start(bf16[16,2560]{1,0:T(8,128)(2,1)S(1)} %get-tuple-element.66), channel_id=1, source_target_pairs={{0,16},{2,18},{4,20},{6,22},{8,24},{10,26},{12,28},{14,30},{16,0},... | collective-permute-start | bytes 245768 | tf_op jit(solution)/shard_map/ppermute | solution.py:54
  64.5 6.8 %collective-permute-start.20 = (bf16[16,2560]{1,0:T(8,128)(2,1)S(1)}, bf16[16,2560]{1,0:T(8,128)(2,1)S(1)}, u32[]{:S(2)}, u32[]{:S(2)}) collective-permute-start(bf16[16,2560]{1,0:T(8,128)(2,1)S(1)} %get-tuple-element.67), channel_id=1, source_target_pairs={{0,8},{2,10},{4,12},{6,14},{8,0},{10,2},{12,4},{14,6},{16,24},{18,... | collective-permute-start | bytes 245768 | tf_op jit(solution)/shard_map/ppermute | solution.py:54
  68.2 16.8 %collective-permute-start.18 = (bf16[4,512,128]{2,1,0:T(8,128)(2,1)S(1)}, bf16[4,512,128]{2,1,0:T(8,128)(2,1)S(1)}, u32[]{:S(2)}, u32[]{:S(2)}) collective-permute-start(bf16[4,512,128]{2,1,0:T(8,128)(2,1)S(1)} %get-tuple-element.52), channel_id=1, source_target_pairs={{0,1},{1,0},{2,3},{3,2},{4,5},{5,4},{6,7},{7,6},{8,9},{9,8},{10,11... | collective-permute-start | bytes 1572872 | tf_op jit(solution)/shard_map/ppermute | solution.py:46
  71.3 7.1 %collective-permute-start.24 = (bf16[16,2560]{1,0:T(8,128)(2,1)S(1)}, bf16[16,2560]{1,0:T(8,128)(2,1)S(1)}, u32[]{:S(2)}, u32[]{:S(2)}) collective-permute-start(bf16[16,2560]{1,0:T(8,128)(2,1)S(1)} %add_convert_fusion.2), channel_id=1, source_target_pairs={{0,24},{2,26},{4,28},{6,30},{8,16},{10,18},{12,20},{14,22},{16,8},... | collective-permute-start | bytes 245768 | tf_op jit(solution)/shard_map/ppermute | solution.py:54
  73.8 7.6 %collective-permute-start.23 = (bf16[16,2560]{1,0:T(8,128)(2,1)S(1)}, bf16[16,2560]{1,0:T(8,128)(2,1)S(1)}, u32[]{:S(2)}, u32[]{:S(2)}) collective-permute-start(bf16[16,2560]{1,0:T(8,128)(2,1)S(1)} %add_convert_fusion.2), channel_id=1, source_target_pairs={{0,16},{2,18},{4,20},{6,22},{8,24},{10,26},{12,28},{14,30},{16,0},... | collective-permute-start | bytes 245768 | tf_op jit(solution)/shard_map/ppermute | solution.py:54
  73.9 7.5 %collective-permute-start.22 = (bf16[16,2560]{1,0:T(8,128)(2,1)S(1)}, bf16[16,2560]{1,0:T(8,128)(2,1)S(1)}, u32[]{:S(2)}, u32[]{:S(2)}) collective-permute-start(bf16[16,2560]{1,0:T(8,128)(2,1)S(1)} %add_convert_fusion.2), channel_id=1, source_target_pairs={{0,8},{2,10},{4,12},{6,14},{8,0},{10,2},{12,4},{14,6},{16,24},{18,... | collective-permute-start | bytes 245768 | tf_op jit(solution)/shard_map/ppermute | solution.py:54
  81.4 11.7 %collective-permute-start.28 = (bf16[64,2560]{1,0:T(8,128)(2,1)S(1)}, bf16[64,2560]{1,0:T(8,128)(2,1)S(1)}, u32[]{:S(2)}, u32[]{:S(2)}) collective-permute-start(bf16[64,2560]{1,0:T(8,128)(2,1)S(1)} %pad_maximum_fusion.1.refs_0_), channel_id=1, source_target_pairs={{0,6},{2,4},{4,2},{6,0},{8,14},{10,12},{12,10},{14,8},{16,22},{18,... | collective-permute-start | bytes 983048 | tf_op jit(solution)/shard_map/ppermute | solution.py:54
  83.0 15.3 %collective-permute-start.27 = (bf16[64,2560]{1,0:T(8,128)(2,1)S(1)}, bf16[64,2560]{1,0:T(8,128)(2,1)S(1)}, u32[]{:S(2)}, u32[]{:S(2)}) collective-permute-start(bf16[64,2560]{1,0:T(8,128)(2,1)S(1)} %pad_maximum_fusion.1.refs_0_), channel_id=1, source_target_pairs={{0,4},{2,6},{4,0},{6,2},{8,12},{10,14},{12,8},{14,10},{16,20},{18,... | collective-permute-start | bytes 983048 | tf_op jit(solution)/shard_map/ppermute | solution.py:54
  83.9 14.5 %collective-permute-start.26 = (bf16[64,2560]{1,0:T(8,128)(2,1)S(1)}, bf16[64,2560]{1,0:T(8,128)(2,1)S(1)}, u32[]{:S(2)}, u32[]{:S(2)}) collective-permute-start(bf16[64,2560]{1,0:T(8,128)(2,1)S(1)} %pad_maximum_fusion.1.refs_0_), channel_id=1, source_target_pairs={{0,2},{2,0},{4,6},{6,4},{8,10},{10,8},{12,14},{14,12},{16,18},{18,... | collective-permute-start | bytes 983048 | tf_op jit(solution)/shard_map/ppermute | solution.py:54
  85.2 14.9 %collective-permute-start.25 = (bf16[512,128]{1,0:T(8,128)(2,1)S(1)}, bf16[512,128]{1,0:T(8,128)(2,1)S(1)}, u32[]{:S(2)}, u32[]{:S(2)}) collective-permute-start(bf16[512,128]{1,0:T(8,128)(2,1)S(1)} %get-tuple-element.62), channel_id=1, source_target_pairs={{0,24},{2,26},{4,28},{6,30},{8,16},{10,18},{12,20},{14,22},{16,8},... | collective-permute-start | bytes 393224 | tf_op jit(solution)/shard_map/ppermute | solution.py:54
  86.9 13.2 %collective-permute-start.30 = (bf16[512,128]{1,0:T(8,128)(2,1)S(1)}, bf16[512,128]{1,0:T(8,128)(2,1)S(1)}, u32[]{:S(2)}, u32[]{:S(2)}) collective-permute-start(bf16[512,128]{1,0:T(8,128)(2,1)S(1)} %get-tuple-element.63), channel_id=1, source_target_pairs={{0,16},{2,18},{4,20},{6,22},{8,24},{10,26},{12,28},{14,30},{16,0},... | collective-permute-start | bytes 393224 | tf_op jit(solution)/shard_map/ppermute | solution.py:54
  93.1 7.0 %collective-permute-start.29 = (bf16[512,128]{1,0:T(8,128)(2,1)S(1)}, bf16[512,128]{1,0:T(8,128)(2,1)S(1)}, u32[]{:S(2)}, u32[]{:S(2)}) collective-permute-start(bf16[512,128]{1,0:T(8,128)(2,1)S(1)} %get-tuple-element.64), channel_id=1, source_target_pairs={{0,8},{2,10},{4,12},{6,14},{8,0},{10,2},{12,4},{14,6},{16,24},{18,... | collective-permute-start | bytes 393224 | tf_op jit(solution)/shard_map/ppermute | solution.py:54
  (9 other events, 35.8 us)

commit v10 on v9

--- a/solution.py
+++ b/solution.py
@@ -113,25 +113,26 @@
     slot_rows = ids_refs[0].shape[3]
     lane = lax.broadcasted_iota(jnp.int32, (LANES, LANES), 1)
     ids = pick_ids(scalars, ids_refs, slots, table_order(table_here, tables))
+    rows = out_refs[0].shape[0]
+    total = jnp.zeros((groups * rows, columns), f32)
+    for table in range(tables):
+        found = []
+        for group in range(groups):
+            for slot in range(slots):
+                for first in range(0, slot_rows, LANES):
+                    row = ids[group][slot][table][:, first : first + LANES]
+                    found.append(jnp.transpose(jnp.broadcast_to(row, (LANES, LANES))))
+        column = jnp.concatenate(found, axis=0)
+        for turn, ref in enumerate(pieces[table]):
+            shifted = column - (bal ^ turn) * part
+            hot = []
+            for at in range(0, part, LANES):
+                here = [shifted[row : row + LANES] == lane + at for row in range(0, groups * rows, LANES)]
+                here = [jnp.where(one, 1.0, 0.0).astype(bf16) for one in here]
+                hot.append(jnp.concatenate(here, axis=0))
+            total = total + matmul(jnp.concatenate(hot, axis=1), ref[...])
     for group in range(groups):
-        for slot in range(slots):
-            for first in range(0, slot_rows, LANES):
-                total = jnp.zeros((LANES, columns), f32)
-                for table in range(tables):
-                    row = ids[group][slot][table][:, first : first + LANES]
-                    column = jnp.transpose(jnp.broadcast_to(row, (LANES, LANES)))
-                    for turn, ref in enumerate(pieces[table]):
-                        shifted = column - (bal ^ turn) * part
-                        hot = jnp.concatenate(
-                            [
-                                jnp.where(shifted == lane + at, 1.0, 0.0).astype(bf16)
-                                for at in range(0, part, LANES)
-                            ],
-                            axis=1,
-                        )
-                        total = total + matmul(hot, ref[...])
-                at = slot * slot_rows + first
-                out_refs[group][at : at + LANES, :] = total.astype(bf16)
+        out_refs[group][...] = total[group * rows : (group + 1) * rows].astype(bf16)
 
 
 def scatter_kernel(groups, slots, bals, *refs):
@@ -289,8 +290,14 @@
                 found.append(ref[pl.ds(at, unit), :])
         return jnp.concatenate(found, axis=0)
 
-    for turn in range(bals):
-        term_refs[turn][:, features:] = matmul(owner_order(mt_ref, turn), cot).astype(bf16)
+    def emit_terms(ref, right, first):
+        left = jnp.concatenate([owner_order(ref, turn) for turn in range(bals)], axis=0)
+        found = matmul(left, right).astype(bf16)
+        for turn in range(bals):
+            rows_here = slice(turn * part, (turn + 1) * part)
+            term_refs[turn][:, first : first + right.shape[1]] = found[rows_here]
+
+    emit_terms(mt_ref, cot, features)
 
     for slot in range(slots):
         here = slice(slot * slot_rows, (slot + 1) * slot_rows)
@@ -308,8 +315,7 @@
                 at = slice(first, first + pair_width)
                 grads_ref[here, at] = (found * dsilu_ref[here, at]).astype(bf16)
 
-    for turn in range(bals):
-        term_refs[turn][:, :features] = matmul(owner_order(nt_ref, turn), grads_ref[...]).astype(bf16)
+    emit_terms(nt_ref, grads_ref[...], 0)
 
     grad_normed = times_parts_nt(grads_ref[...], 0, features)
     grad_rows = (wide_cot + norm_back(grad_normed, normed_in, in_inverse)).astype(bf16)
@@ -537,7 +543,7 @@
                 input_output_aliases={1 + len(steps) + index: index for index in range(len(totals))},
                 cost_estimate=estimate(1),
                 compiler_params=room(12),
-            )(scalars, *[back[step] for step in steps], *totals)
+            )(after(scalars, table_sum) if totals else scalars, *[back[step] for step in steps], *totals)
         total_in, total_out = totals
     else:
         total = lax.psum(over_cores(results).astype(f32), "emb") * grad_scale

time: 101 us -> 101 us (level)
  transfers between devices with their start and end apart: 31 -> 31, of which waited for: 15 -> 16; matrix products, arithmetic and copies ran while one was open for 4% -> 4% of each run, Pallas kernels for 6% -> 5%
where the time goes in v10:
time: 101 us
  waiting for transfers between devices  46.3 us (46%)
  starting transfers between devices  31.7 us (31%)
  Pallas kernels  16.1 us (16%)
  other arithmetic  3.96 us (4%)
  local copies, waits for them, and re-layouts  2.42 us (2%)
    ppermute x23, waiting for transfers between devices, emb_swap(): return lax.ppermute(value, 'emb', [(i, i ^ step) for i in range(count)])  43.2 us
    ppermute x23, starting transfers between devices, emb_swap(): return lax.ppermute(value, 'emb', [(i, i ^ step) for i in range(count)])  30.3 us
    pallas_call x1, Pallas kernels, on_device(): pl.pallas_call(functools.partial(layer_kernel, groups, slots, tables, bal...  6.28 us
    pallas_call x2, Pallas kernels, on_device(): pl.pallas_call(functools.partial(place_kernel, grad_scale, steps, slots,...  3.5 us
    pallas_call x1, Pallas kernels, on_device(): pl.pallas_call(functools.partial(lookup_kernel, groups, slots, tables, ba...  3.08 us
    ppermute x8, waiting for transfers between devices, bal_swap(): return lax.ppermute(value, 'bal', [(i, i ^ step) for i in range(count)])  3.06 us
    pallas_call x1, Pallas kernels, table_sums(): pl.pallas_call(functools.partial(scatter_kernel, groups, slots, bals), ou...  2.91 us
  transfers between devices with their start and end apart: 31, of which 16 were waited for; matrix products, arithmetic and copies ran while one was open for 4% of the time, Pallas kernels for 5%

profile of v10, /device:TPU:0, one launch (start us, length us, event | category | flops | bytes accessed | tf_op | source)
XLA Modules:
  0.0 101.2 jit_solution(7201946982584246014)
XLA Ops:
  1.6 5.1 %collective-permute-start.8 = (bf16[512,128]{1,0:T(8,128)(2,1)S(1)}, bf16[512,128]{1,0:T(8,128)(2,1)S(1)}, u32[]{:S(2)}, u32[]{:S(2)}) collective-permute-start(bf16[512,128]{1,0:T(8,128)(2,1)S(1)} %dynamic-slice_bitcast_fusion.refs_3_), channel_id=1, source_target_pairs={{0,24},{2,26},{4,28},{6,30},{8,16},{10,18},{12,20},{14,22},{16,8},... | collective-permute-start | bytes 393224 | tf_op jit(solution)/shard_map/ppermute | solution.py:54
  9.8 1.6 %collective-permute-start = (s32[1,128]{1,0:T(1,128)S(1)}, s32[1,128]{1,0:T(1,128)S(1)}, u32[]{:S(2)}, u32[]{:S(2)}) collective-permute-start(s32[1,128]{1,0:T(1,128)S(1)} %pad_add_fusion.2), channel_id=1, source_target_pairs={{0,2},{2,0},{4,6},{6,4},{8,10},{10,8},{12,14},{14,12},{16,18},{18,... | collective-permute-start | bytes 1544 | tf_op jit(solution)/shard_map/ppermute | solution.py:54
  11.4 1.9 %collective-permute-done = s32[1,128]{1,0:T(1,128)S(1)} collective-permute-done((s32[1,128]{1,0:T(1,128)S(1)}, s32[1,128]{1,0:T(1,128)S(1)}, u32[]{:S(2)}, u32[]{:S(2)}) %collective-permute-start) | collective-permute-done | bytes 544 | tf_op jit(solution)/shard_map/ppermute | solution.py:54
  13.4 1.7 %collective-permute-start.1 = (s32[2,128]{1,0:T(2,128)S(1)}, s32[2,128]{1,0:T(2,128)S(1)}, u32[]{:S(2)}, u32[]{:S(2)}) collective-permute-start(s32[2,128]{1,0:T(2,128)S(1)} %pad_add_fusion.1), channel_id=1, source_target_pairs={{0,4},{2,6},{4,0},{6,2},{8,12},{10,14},{12,8},{14,10},{16,20},{18,... | collective-permute-start | bytes 3080 | tf_op jit(solution)/shard_map/ppermute | solution.py:54
  19.1 3.1 %shard_map.111 = (bf16[256,128]{1,0:T(8,128)(2,1)S(1)}, bf16[256,128]{1,0:T(8,128)(2,1)S(1)}, bf16[256,128]{1,0:T(8,128)(2,1)S(1)}, bf16[256,128]{1,0:T(8,128)(2,1)S(1)}) custom-call(s32[4,128]{1,0:T(4,128)S(1)} %pad_add_fusion.refs_0_.scalar_ref, s32[4,8,1,128]{3,2,1,0:T(1,128)S(1)} %reshape.61.refs_1_, ...), custom_call_target="tpu_custom_call" | custom-call | bytes 10500000 | tf_op jit(solution)/shard_map/pallas_call | solution.py:437
  22.5 2.6 %collective-permute-start.10 = (bf16[256,128]{1,0:T(8,128)(2,1)S(1)}, bf16[256,128]{1,0:T(8,128)(2,1)S(1)}, u32[]{:S(2)}, u32[]{:S(2)}) collective-permute-start(bf16[256,128]{1,0:T(8,128)(2,1)S(1)} %get-tuple-element.37), channel_id=1, source_target_pairs={{0,6},{2,4},{4,2},{6,0},{8,14},{10,12},{12,10},{14,8},{16,22},{18,... | collective-permute-start | bytes 196616 | tf_op jit(solution)/shard_map/ppermute | solution.py:54
  26.0 1.7 %collective-permute-done.10.refs_0_ = bf16[256,128]{1,0:T(8,128)(2,1)S(1)} collective-permute-done((bf16[256,128]{1,0:T(8,128)(2,1)S(1)}, bf16[256,128]{1,0:T(8,128)(2,1)S(1)}, u32[]{:S(2)}, u32[]{:S(2)}) %collective-permute-start.10) | collective-permute-done | bytes 65568 | tf_op jit(solution)/shard_map/ppermute | solution.py:54
  27.7 1.7 %collective-permute-done.11.refs_1_ = bf16[256,128]{1,0:T(8,128)(2,1)S(1)} collective-permute-done((bf16[256,128]{1,0:T(8,128)(2,1)S(1)}, bf16[256,128]{1,0:T(8,128)(2,1)S(1)}, u32[]{:S(2)}, u32[]{:S(2)}) %collective-permute-start.11) | collective-permute-done | bytes 65568 | tf_op jit(solution)/shard_map/ppermute | solution.py:54
  29.9 6.3 %shard_map.112 = (bf16[256,512]{1,0:T(8,128)(2,1)}, bf16[256,128]{1,0:T(8,128)(2,1)S(1)}, bf16[256,128]{1,0:T(8,128)(2,1)S(1)}, bf16[256,128]{1,0:T(8,128)(2,1)S...) custom-call(s32[4,128]{1,0:T(4,128)S(1)} %pad_add_fusion.refs_0_.scalar_ref, ...), custom_call_target="tpu_custom_call" | custom-call | bytes 24500000 | tf_op jit(solution)/shard_map/pallas_call | solution.py:451
  36.2 3.0 %collective-permute-done.14.refs_1_ = bf16[256,2560]{1,0:T(8,128)(2,1)S(1)} collective-permute-done((bf16[256,2560]{1,0:T(8,128)(2,1)S(1)}, bf16[256,2560]{1,0:T(8,128)(2,1)S(1)}, u32[]{:S(2)}, u32[]{:S(2)}) %collective-permute-start.14) | collective-permute-done | bytes 1310752 | tf_op jit(solution)/shard_map/ppermute | solution.py:46
  43.1 9.4 %collective-permute-done.15.refs_3_ = bf16[64,3072]{1,0:T(8,128)(2,1)S(1)} collective-permute-done((bf16[64,3072]{1,0:T(8,128)(2,1)S(1)}, bf16[64,3072]{1,0:T(8,128)(2,1)S(1)}, u32[]{:S(2)}, u32[]{:S(2)}) %collective-permute-start.15) | collective-permute-done | bytes 393248 | tf_op jit(solution)/shard_map/ppermute | solution.py:54
  52.6 7.6 %collective-permute-done.16.refs_4_ = bf16[64,3072]{1,0:T(8,128)(2,1)S(1)} collective-permute-done((bf16[64,3072]{1,0:T(8,128)(2,1)S(1)}, bf16[64,3072]{1,0:T(8,128)(2,1)S(1)}, u32[]{:S(2)}, u32[]{:S(2)}) %collective-permute-start.16) | collective-permute-done | bytes 393248 | tf_op jit(solution)/shard_map/ppermute | solution.py:54
  60.4 3.7 %collective-permute-start.19 = (bf16[16,2560]{1,0:T(8,128)(2,1)S(1)}, bf16[16,2560]{1,0:T(8,128)(2,1)S(1)}, u32[]{:S(2)}, u32[]{:S(2)}) collective-permute-start(bf16[16,2560]{1,0:T(8,128)(2,1)S(1)} %get-tuple-element.69), channel_id=1, source_target_pairs={{0,24},{2,26},{4,28},{6,30},{8,16},{10,18},{12,20},{14,22},{16,8},... | collective-permute-start | bytes 245768 | tf_op jit(solution)/shard_map/ppermute | solution.py:54
  64.9 2.9 %shard_map.114 = (bf16[4,512,128]{2,1,0:T(8,128)(2,1)S(1)}, bf16[4,512,128]{2,1,0:T(8,128)(2,1)S(1)}) custom-call(s32[4,128]{1,0:T(4,128)S(1)} %pad_add_fusion.refs_0_.scalar_ref, s32[4,8,1,128]{3,2,1,0:T(1,128)S(1)} %reshape.61.refs_1_, s32[4,8,1,128]{3,2,1,0:T(1,128)S(1)} %collective-permute-done.2.refs_2_, ...), custom_call_target="tpu_custom_call" | custom-call | bytes 10500000 | tf_op jit(solution)/shard_map/pallas_call | solution.py:484
  67.9 3.0 %collective-permute-done.21 = bf16[16,2560]{1,0:T(8,128)(2,1)S(1)} collective-permute-done((bf16[16,2560]{1,0:T(8,128)(2,1)S(1)}, bf16[16,2560]{1,0:T(8,128)(2,1)S(1)}, u32[]{:S(2)}, u32[]{:S(2)}) %collective-permute-start.21) | collective-permute-done | bytes 81952 | tf_op jit(solution)/shard_map/ppermute | solution.py:54
  70.9 2.4 %collective-permute-start.24 = (bf16[16,2560]{1,0:T(8,128)(2,1)S(1)}, bf16[16,2560]{1,0:T(8,128)(2,1)S(1)}, u32[]{:S(2)}, u32[]{:S(2)}) collective-permute-start(bf16[16,2560]{1,0:T(8,128)(2,1)S(1)} %add_convert_fusion.2), channel_id=1, source_target_pairs={{0,24},{2,26},{4,28},{6,30},{8,16},{10,18},{12,20},{14,22},{16,8},... | collective-permute-start | bytes 245768 | tf_op jit(solution)/shard_map/ppermute | solution.py:54
  73.5 1.9 %collective-permute-start.22 = (bf16[16,2560]{1,0:T(8,128)(2,1)S(1)}, bf16[16,2560]{1,0:T(8,128)(2,1)S(1)}, u32[]{:S(2)}, u32[]{:S(2)}) collective-permute-start(bf16[16,2560]{1,0:T(8,128)(2,1)S(1)} %add_convert_fusion.2), channel_id=1, source_target_pairs={{0,8},{2,10},{4,12},{6,14},{8,0},{10,2},{12,4},{14,6},{16,24},{18,... | collective-permute-start | bytes 245768 | tf_op jit(solution)/shard_map/ppermute | solution.py:54
  75.4 2.7 %collective-permute-done.24 = bf16[16,2560]{1,0:T(8,128)(2,1)S(1)} collective-permute-done((bf16[16,2560]{1,0:T(8,128)(2,1)S(1)}, bf16[16,2560]{1,0:T(8,128)(2,1)S(1)}, u32[]{:S(2)}, u32[]{:S(2)}) %collective-permute-start.24) | collective-permute-done | bytes 81952 | tf_op jit(solution)/shard_map/ppermute | solution.py:54
  78.1 2.9 %collective-permute-done.23 = bf16[16,2560]{1,0:T(8,128)(2,1)S(1)} collective-permute-done((bf16[16,2560]{1,0:T(8,128)(2,1)S(1)}, bf16[16,2560]{1,0:T(8,128)(2,1)S(1)}, u32[]{:S(2)}, u32[]{:S(2)}) %collective-permute-start.23) | collective-permute-done | bytes 81952 | tf_op jit(solution)/shard_map/ppermute | solution.py:54
  84.8 1.7 %collective-permute-start.25 = (bf16[512,128]{1,0:T(8,128)(2,1)S(1)}, bf16[512,128]{1,0:T(8,128)(2,1)S(1)}, u32[]{:S(2)}, u32[]{:S(2)}) collective-permute-start(bf16[512,128]{1,0:T(8,128)(2,1)S(1)} %get-tuple-element.66), channel_id=1, source_target_pairs={{0,24},{2,26},{4,28},{6,30},{8,16},{10,18},{12,20},{14,22},{16,8},... | collective-permute-start | bytes 393224 | tf_op jit(solution)/shard_map/ppermute | solution.py:54
  86.5 6.2 %collective-permute-done.28.refs_1_ = bf16[64,2560]{1,0:T(8,128)(2,1)S(1)} collective-permute-done((bf16[64,2560]{1,0:T(8,128)(2,1)S(1)}, bf16[64,2560]{1,0:T(8,128)(2,1)S(1)}, u32[]{:S(2)}, u32[]{:S(2)}) %collective-permute-start.28) | collective-permute-done | bytes 327712 | tf_op jit(solution)/shard_map/ppermute | solution.py:54
  92.7 1.8 %shard_map.115 = (f32[256,2048]{1,0:T(8,128)}, f32[256,512]{1,0:T(8,128)}) custom-call(s32[4,128]{1,0:T(4,128)S(1)} %pad_add_fusion.refs_0_.scalar_ref, bf16[64,2560]{1,0:T(8,128)(2,1)S(1)} %pad_maximum_fusion.1.refs_0_, bf16[64,2560]{1,0:T(8,128)(2,1)S(1)} %collective-permute-done.28.refs_1_), custom_call_target="tpu_custom_call" | custom-call | bytes 3500000 | tf_op jit(solution)/shard_map/pallas_call | solution.py:531
  94.5 3.5 %collective-permute-done.27.refs_1_ = bf16[64,2560]{1,0:T(8,128)(2,1)S(1)} collective-permute-done((bf16[64,2560]{1,0:T(8,128)(2,1)S(1)}, bf16[64,2560]{1,0:T(8,128)(2,1)S(1)}, u32[]{:S(2)}, u32[]{:S(2)}) %collective-permute-start.27) | collective-permute-done | bytes 327712 | tf_op jit(solution)/shard_map/ppermute | solution.py:54
  99.5 1.8 %shard_map.116 = (f32[256,2048]{1,0:T(8,128)}, f32[256,512]{1,0:T(8,128)}) custom-call(s32[4,128]{1,0:T(4,128)S(1)} %pad_add_fusion.refs_0_.scalar_ref, bf16[64,2560]{1,0:T(8,128)(2,1)S(1)} %collective-permute-done.26.refs_0_, bf16[64,2560]{1,0:T(8,128)(2,1)S(1)} %collective-permute-done.27.refs_1_, ...), custom_call_target="tpu_custom_call", output_to_operand_aliasing={{0}: (3, {}), {1}: (4, {})} | custom-call | bytes 3500000 | tf_op jit(solution)/shard_map/pallas_call | solution.py:531
  (64 shorter events, 20.4 us)
Async XLA Ops:
  1.6 15.9 %collective-permute-start.8 = (bf16[512,128]{1,0:T(8,128)(2,1)S(1)}, bf16[512,128]{1,0:T(8,128)(2,1)S(1)}, u32[]{:S(2)}, u32[]{:S(2)}) collective-permute-start(bf16[512,128]{1,0:T(8,128)(2,1)S(1)} %dynamic-slice_bitcast_fusion.refs_3_), channel_id=1, source_target_pairs={{0,24},{2,26},{4,28},{6,30},{8,16},{10,18},{12,20},{14,22},{16,8},... | collective-permute-start | bytes 393224 | tf_op jit(solution)/shard_map/ppermute | solution.py:54
  6.7 11.1 %collective-permute-start.6 = (bf16[512,128]{1,0:T(8,128)(2,1)S(1)}, bf16[512,128]{1,0:T(8,128)(2,1)S(1)}, u32[]{:S(2)}, u32[]{:S(2)}) collective-permute-start(bf16[512,128]{1,0:T(8,128)(2,1)S(1)} %dynamic-slice_bitcast_fusion.refs_3_), channel_id=1, source_target_pairs={{0,16},{2,18},{4,20},{6,22},{8,24},{10,26},{12,28},{14,30},{16,0},... | collective-permute-start | bytes 393224 | tf_op jit(solution)/shard_map/ppermute | solution.py:54
  6.7 10.2 %collective-permute-start.4 = (bf16[512,128]{1,0:T(8,128)(2,1)S(1)}, bf16[512,128]{1,0:T(8,128)(2,1)S(1)}, u32[]{:S(2)}, u32[]{:S(2)}) collective-permute-start(bf16[512,128]{1,0:T(8,128)(2,1)S(1)} %dynamic-slice_bitcast_fusion.refs_3_), channel_id=1, source_target_pairs={{0,8},{2,10},{4,12},{6,14},{8,0},{10,2},{12,4},{14,6},{16,24},{18,... | collective-permute-start | bytes 393224 | tf_op jit(solution)/shard_map/ppermute | solution.py:54
  11.4 7.7 %collective-permute-start.3 = (bf16[512,128]{1,0:T(8,128)(2,1)S(1)}, bf16[512,128]{1,0:T(8,128)(2,1)S(1)}, u32[]{:S(2)}, u32[]{:S(2)}) collective-permute-start(bf16[512,128]{1,0:T(8,128)(2,1)S(1)} %dynamic-slice_bitcast_fusion.refs_3_), channel_id=1, source_target_pairs={{0,1},{1,0},{2,3},{3,2},{4,5},{5,4},{6,7},{7,6},{8,9},{9,8},{10,11... | collective-permute-start | bytes 393224 | tf_op jit(solution)/shard_map/ppermute | solution.py:46
  22.2 7.7 %collective-permute-start.13 = (bf16[256,2560]{1,0:T(8,128)(2,1)S(1)}, bf16[256,2560]{1,0:T(8,128)(2,1)S(1)}, u32[]{:S(2)}, u32[]{:S(2)}) collective-permute-start(bf16[256,2560]{1,0:T(8,128)(2,1)S(1)} %pad_maximum_fusion.refs_4_), channel_id=1, source_target_pairs={{0,1},{1,0},{2,3},{3,2},{4,5},{5,4},{6,7},{7,6},{8,9},{9,8},{10,11... | collective-permute-start | bytes 3932168 | tf_op jit(solution)/shard_map/ppermute | solution.py:46
  22.5 5.2 %collective-permute-start.10 = (bf16[256,128]{1,0:T(8,128)(2,1)S(1)}, bf16[256,128]{1,0:T(8,128)(2,1)S(1)}, u32[]{:S(2)}, u32[]{:S(2)}) collective-permute-start(bf16[256,128]{1,0:T(8,128)(2,1)S(1)} %get-tuple-element.37), channel_id=1, source_target_pairs={{0,6},{2,4},{4,2},{6,0},{8,14},{10,12},{12,10},{14,8},{16,22},{18,... | collective-permute-start | bytes 196616 | tf_op jit(solution)/shard_map/ppermute | solution.py:54
  25.1 4.3 %collective-permute-start.11 = (bf16[256,128]{1,0:T(8,128)(2,1)S(1)}, bf16[256,128]{1,0:T(8,128)(2,1)S(1)}, u32[]{:S(2)}, u32[]{:S(2)}) collective-permute-start(bf16[256,128]{1,0:T(8,128)(2,1)S(1)} %get-tuple-element.38), channel_id=1, source_target_pairs={{0,4},{2,6},{4,0},{6,2},{8,12},{10,14},{12,8},{14,10},{16,20},{18,... | collective-permute-start | bytes 196616 | tf_op jit(solution)/shard_map/ppermute | solution.py:54
  25.6 4.3 %collective-permute-start.12 = (bf16[256,128]{1,0:T(8,128)(2,1)S(1)}, bf16[256,128]{1,0:T(8,128)(2,1)S(1)}, u32[]{:S(2)}, u32[]{:S(2)}) collective-permute-start(bf16[256,128]{1,0:T(8,128)(2,1)S(1)} %get-tuple-element.39), channel_id=1, source_target_pairs={{0,2},{2,0},{4,6},{6,4},{8,10},{10,8},{12,14},{14,12},{16,18},{18,... | collective-permute-start | bytes 196616 | tf_op jit(solution)/shard_map/ppermute | solution.py:54
  39.6 13.0 %collective-permute-start.15 = (bf16[64,3072]{1,0:T(8,128)(2,1)S(1)}, bf16[64,3072]{1,0:T(8,128)(2,1)S(1)}, u32[]{:S(2)}, u32[]{:S(2)}) collective-permute-start(bf16[64,3072]{1,0:T(8,128)(2,1)S(1)} %get-tuple-element.48), channel_id=1, source_target_pairs={{0,6},{2,4},{4,2},{6,0},{8,14},{10,12},{12,10},{14,8},{16,22},{18,... | collective-permute-start | bytes 1179656 | tf_op jit(solution)/shard_map/ppermute | solution.py:54
  41.1 19.0 %collective-permute-start.16 = (bf16[64,3072]{1,0:T(8,128)(2,1)S(1)}, bf16[64,3072]{1,0:T(8,128)(2,1)S(1)}, u32[]{:S(2)}, u32[]{:S(2)}) collective-permute-start(bf16[64,3072]{1,0:T(8,128)(2,1)S(1)} %get-tuple-element.49), channel_id=1, source_target_pairs={{0,4},{2,6},{4,0},{6,2},{8,12},{10,14},{12,8},{14,10},{16,20},{18,... | collective-permute-start | bytes 1179656 | tf_op jit(solution)/shard_map/ppermute | solution.py:54
  42.0 18.2 %collective-permute-start.17 = (bf16[64,3072]{1,0:T(8,128)(2,1)S(1)}, bf16[64,3072]{1,0:T(8,128)(2,1)S(1)}, u32[]{:S(2)}, u32[]{:S(2)}) collective-permute-start(bf16[64,3072]{1,0:T(8,128)(2,1)S(1)} %get-tuple-element.50), channel_id=1, source_target_pairs={{0,2},{2,0},{4,6},{6,4},{8,10},{10,8},{12,14},{14,12},{16,18},{18,... | collective-permute-start | bytes 1179656 | tf_op jit(solution)/shard_map/ppermute | solution.py:54
  60.4 7.5 %collective-permute-start.19 = (bf16[16,2560]{1,0:T(8,128)(2,1)S(1)}, bf16[16,2560]{1,0:T(8,128)(2,1)S(1)}, u32[]{:S(2)}, u32[]{:S(2)}) collective-permute-start(bf16[16,2560]{1,0:T(8,128)(2,1)S(1)} %get-tuple-element.69), channel_id=1, source_target_pairs={{0,24},{2,26},{4,28},{6,30},{8,16},{10,18},{12,20},{14,22},{16,8},... | collective-permute-start | bytes 245768 | tf_op jit(solution)/shard_map/ppermute | solution.py:54
  64.1 6.8 %collective-permute-start.21 = (bf16[16,2560]{1,0:T(8,128)(2,1)S(1)}, bf16[16,2560]{1,0:T(8,128)(2,1)S(1)}, u32[]{:S(2)}, u32[]{:S(2)}) collective-permute-start(bf16[16,2560]{1,0:T(8,128)(2,1)S(1)} %get-tuple-element.70), channel_id=1, source_target_pairs={{0,16},{2,18},{4,20},{6,22},{8,24},{10,26},{12,28},{14,30},{16,0},... | collective-permute-start | bytes 245768 | tf_op jit(solution)/shard_map/ppermute | solution.py:54
  64.1 6.8 %collective-permute-start.20 = (bf16[16,2560]{1,0:T(8,128)(2,1)S(1)}, bf16[16,2560]{1,0:T(8,128)(2,1)S(1)}, u32[]{:S(2)}, u32[]{:S(2)}) collective-permute-start(bf16[16,2560]{1,0:T(8,128)(2,1)S(1)} %get-tuple-element.71), channel_id=1, source_target_pairs={{0,8},{2,10},{4,12},{6,14},{8,0},{10,2},{12,4},{14,6},{16,24},{18,... | collective-permute-start | bytes 245768 | tf_op jit(solution)/shard_map/ppermute | solution.py:54
  67.8 16.8 %collective-permute-start.18 = (bf16[4,512,128]{2,1,0:T(8,128)(2,1)S(1)}, bf16[4,512,128]{2,1,0:T(8,128)(2,1)S(1)}, u32[]{:S(2)}, u32[]{:S(2)}) collective-permute-start(bf16[4,512,128]{2,1,0:T(8,128)(2,1)S(1)} %get-tuple-element.53), channel_id=1, source_target_pairs={{0,1},{1,0},{2,3},{3,2},{4,5},{5,4},{6,7},{7,6},{8,9},{9,8},{10,11... | collective-permute-start | bytes 1572872 | tf_op jit(solution)/shard_map/ppermute | solution.py:46
  70.9 7.1 %collective-permute-start.24 = (bf16[16,2560]{1,0:T(8,128)(2,1)S(1)}, bf16[16,2560]{1,0:T(8,128)(2,1)S(1)}, u32[]{:S(2)}, u32[]{:S(2)}) collective-permute-start(bf16[16,2560]{1,0:T(8,128)(2,1)S(1)} %add_convert_fusion.2), channel_id=1, source_target_pairs={{0,24},{2,26},{4,28},{6,30},{8,16},{10,18},{12,20},{14,22},{16,8},... | collective-permute-start | bytes 245768 | tf_op jit(solution)/shard_map/ppermute | solution.py:54
  73.4 7.6 %collective-permute-start.23 = (bf16[16,2560]{1,0:T(8,128)(2,1)S(1)}, bf16[16,2560]{1,0:T(8,128)(2,1)S(1)}, u32[]{:S(2)}, u32[]{:S(2)}) collective-permute-start(bf16[16,2560]{1,0:T(8,128)(2,1)S(1)} %add_convert_fusion.2), channel_id=1, source_target_pairs={{0,16},{2,18},{4,20},{6,22},{8,24},{10,26},{12,28},{14,30},{16,0},... | collective-permute-start | bytes 245768 | tf_op jit(solution)/shard_map/ppermute | solution.py:54
  73.5 7.5 %collective-permute-start.22 = (bf16[16,2560]{1,0:T(8,128)(2,1)S(1)}, bf16[16,2560]{1,0:T(8,128)(2,1)S(1)}, u32[]{:S(2)}, u32[]{:S(2)}) collective-permute-start(bf16[16,2560]{1,0:T(8,128)(2,1)S(1)} %add_convert_fusion.2), channel_id=1, source_target_pairs={{0,8},{2,10},{4,12},{6,14},{8,0},{10,2},{12,4},{14,6},{16,24},{18,... | collective-permute-start | bytes 245768 | tf_op jit(solution)/shard_map/ppermute | solution.py:54
  81.0 11.7 %collective-permute-start.28 = (bf16[64,2560]{1,0:T(8,128)(2,1)S(1)}, bf16[64,2560]{1,0:T(8,128)(2,1)S(1)}, u32[]{:S(2)}, u32[]{:S(2)}) collective-permute-start(bf16[64,2560]{1,0:T(8,128)(2,1)S(1)} %pad_maximum_fusion.1.refs_0_), channel_id=1, source_target_pairs={{0,6},{2,4},{4,2},{6,0},{8,14},{10,12},{12,10},{14,8},{16,22},{18,... | collective-permute-start | bytes 983048 | tf_op jit(solution)/shard_map/ppermute | solution.py:54
  82.6 15.4 %collective-permute-start.27 = (bf16[64,2560]{1,0:T(8,128)(2,1)S(1)}, bf16[64,2560]{1,0:T(8,128)(2,1)S(1)}, u32[]{:S(2)}, u32[]{:S(2)}) collective-permute-start(bf16[64,2560]{1,0:T(8,128)(2,1)S(1)} %pad_maximum_fusion.1.refs_0_), channel_id=1, source_target_pairs={{0,4},{2,6},{4,0},{6,2},{8,12},{10,14},{12,8},{14,10},{16,20},{18,... | collective-permute-start | bytes 983048 | tf_op jit(solution)/shard_map/ppermute | solution.py:54
  83.5 14.5 %collective-permute-start.26 = (bf16[64,2560]{1,0:T(8,128)(2,1)S(1)}, bf16[64,2560]{1,0:T(8,128)(2,1)S(1)}, u32[]{:S(2)}, u32[]{:S(2)}) collective-permute-start(bf16[64,2560]{1,0:T(8,128)(2,1)S(1)} %pad_maximum_fusion.1.refs_0_), channel_id=1, source_target_pairs={{0,2},{2,0},{4,6},{6,4},{8,10},{10,8},{12,14},{14,12},{16,18},{18,... | collective-permute-start | bytes 983048 | tf_op jit(solution)/shard_map/ppermute | solution.py:54
  84.8 13.2 %collective-permute-start.25 = (bf16[512,128]{1,0:T(8,128)(2,1)S(1)}, bf16[512,128]{1,0:T(8,128)(2,1)S(1)}, u32[]{:S(2)}, u32[]{:S(2)}) collective-permute-start(bf16[512,128]{1,0:T(8,128)(2,1)S(1)} %get-tuple-element.66), channel_id=1, source_target_pairs={{0,24},{2,26},{4,28},{6,30},{8,16},{10,18},{12,20},{14,22},{16,8},... | collective-permute-start | bytes 393224 | tf_op jit(solution)/shard_map/ppermute | solution.py:54
  86.5 11.5 %collective-permute-start.30 = (bf16[512,128]{1,0:T(8,128)(2,1)S(1)}, bf16[512,128]{1,0:T(8,128)(2,1)S(1)}, u32[]{:S(2)}, u32[]{:S(2)}) collective-permute-start(bf16[512,128]{1,0:T(8,128)(2,1)S(1)} %get-tuple-element.67), channel_id=1, source_target_pairs={{0,16},{2,18},{4,20},{6,22},{8,24},{10,26},{12,28},{14,30},{16,0},... | collective-permute-start | bytes 393224 | tf_op jit(solution)/shard_map/ppermute | solution.py:54
  92.7 6.0 %collective-permute-start.29 = (bf16[512,128]{1,0:T(8,128)(2,1)S(1)}, bf16[512,128]{1,0:T(8,128)(2,1)S(1)}, u32[]{:S(2)}, u32[]{:S(2)}) collective-permute-start(bf16[512,128]{1,0:T(8,128)(2,1)S(1)} %get-tuple-element.68), channel_id=1, source_target_pairs={{0,8},{2,10},{4,12},{6,14},{8,0},{10,2},{12,4},{14,6},{16,24},{18,... | collective-permute-start | bytes 393224 | tf_op jit(solution)/shard_map/ppermute | solution.py:54
  (9 other events, 35.8 us)

commit v11 on v10

--- a/solution.py
+++ b/solution.py
@@ -135,12 +135,12 @@
         out_refs[group][...] = total[group * rows : (group + 1) * rows].astype(bf16)
 
 
-def scatter_kernel(groups, slots, bals, *refs):
+def scatter_kernel(groups, slots, bals, waits, *refs):
     refs = list(refs)
     take = lambda count: [refs.pop(0) for _ in range(count)]
     (scalar_ref,) = take(1)
     scalars = [Scalars(scalar_ref, step, bals, slots) for step in range(groups)]
-    ids_refs, grad_refs, out_refs = take(bals), take(groups)[::-1], refs
+    ids_refs, grad_refs, _, out_refs = take(bals), take(groups)[::-1], take(waits), refs
     bal, _, table_here = scalars[0].place()
     tables, part, _ = out_refs[0].shape
     slot_rows = ids_refs[0].shape[3]
@@ -325,24 +325,69 @@
         grad_refs[step][...] = x_ref[group_here ^ step]
 
 
-def pieces_kernel(bals, *refs):
-    count = len(refs) - bals
-    groups = (count + 1) // 2
+def pieces_kernel(tables, groups, bals, *refs):
     term_refs, grad_refs = refs[:bals], refs[bals : bals + groups - 1]
-    out_refs = refs[bals + groups - 1 :]
-    height, width = out_refs[0].shape
-    for step, out in enumerate(out_refs):
+    plane_refs = refs[bals + groups - 1 : bals + 2 * groups - 1]
+    table_refs = refs[bals + 2 * groups - 1 :]
+    height, width = plane_refs[0].shape
+    unit = height // tables
+
+    def total(rows, columns):
+        found = term_refs[0][rows, columns].astype(f32)
+        for ref in term_refs[1:]:
+            found = found + ref[rows, columns].astype(f32)
+        return found.astype(bf16)
+
+    for step, out in enumerate(plane_refs):
         rows = slice(step * height, (step + 1) * height)
-        total = term_refs[0][rows, :].astype(f32)
-        for ref in term_refs[1:]:
-            total = total + ref[rows, :].astype(f32)
-        out[:, :width] = total.astype(bf16)
+        out[:, :width] = total(rows, slice(0, width))
         if step:
             grad = grad_refs[step - 1]
             columns = grad.shape[1]
             for index in range(grad.shape[0] // height):
                 at = width + index * columns
                 out[:, at : at + columns] = grad[index * height : (index + 1) * height, :]
+    for table_step, out in enumerate(table_refs):
+        for step in range(groups):
+            first = step * height + table_step * unit
+            rows = slice(first, first + unit)
+            columns = slice(width, width + out.shape[1])
+            out[step * unit : (step + 1) * unit, :] = total(rows, columns)
+
+
+def ordered(plane, table, first):
+    rest = [("plane", step) for step in plane] + [("table", step) for step in table]
+    rest.remove(first)
+    rest.sort(key=lambda one: (-one[1], one[0] if first[0] == "table" else one[0] != "table"))
+    return [first] + rest
+
+
+def first_sums_kernel(order, tables, groups, plane_ref, table_ref, *refs):
+    came, outs = refs[: len(order)], refs[len(order) :]
+    unit, width = outs[0].shape
+    plane, table = plane_ref[...].astype(f32), table_ref[...].astype(f32)
+    for (kind, _), ref in zip(order, came):
+        if kind == "plane":
+            plane = plane + ref[:, :width].astype(f32)
+        else:
+            table = table + ref[...].astype(f32)
+    for step in range(tables):
+        outs[step][...] = plane[step * unit : (step + 1) * unit].astype(bf16)
+    for step in range(groups):
+        outs[tables + step][...] = table[step * unit : (step + 1) * unit].astype(bf16)
+
+
+def second_sums_kernel(order, first_ref, last_ref, *refs):
+    came, out = refs[:-1], refs[-1]
+    width = first_ref.shape[1]
+    first, last = first_ref[...].astype(f32), last_ref[...].astype(f32)
+    for (kind, _), ref in zip(order, came):
+        if kind == "table":
+            first = first + ref[...].astype(f32)
+        else:
+            last = last + ref[...].astype(f32)
+    out[:, :width] = first.astype(bf16)
+    out[:, width:] = last.astype(bf16)
 
 
 def place_kernel(scale, steps, slots, tables, bals, unit, scalar_ref, *refs):
@@ -419,6 +464,7 @@
         scalars = scalars + jnp.pad(field, ((0, 0), (at, LANES - at - width_here)))
         at += width_here
 
+    plane_steps, table_steps = range(1, groups), range(1, tables)
     share = lax.dynamic_slice_in_dim(embed_tables[0], bal * part, part, 0)
     fetched = [emb_swap(share, step * groups, embs) for step in range(1, tables)]
 
@@ -480,35 +526,57 @@
     def to_plane(value):
         return [value] + [emb_swap(value, step, embs) for step in range(1, groups)]
 
-    def table_sums(plane_grads):
+    def table_sums(plane_grads, *others):
         return pl.pallas_call(
-            functools.partial(scatter_kernel, groups, slots, bals),
+            functools.partial(scatter_kernel, groups, slots, bals, len(others)),
             out_shape=[jax.ShapeDtypeStruct((tables, part, columns), bf16)] * bals,
-            in_specs=[SMEM] + [VMEM] * (bals + groups),
+            in_specs=[SMEM] + [VMEM] * (bals + groups) + [HBM] * len(others),
             out_specs=[VMEM] * bals,
             cost_estimate=estimate(3),
             compiler_params=room(16),
-        )(scalars, *plane_ids, *plane_grads[::-1])
+        )(scalars, *plane_ids, *plane_grads[::-1], *others)
 
     grad_scale = (rows * embs * bals) ** -0.5
     if owned:
         height, wide = weight_part // groups, features + width
         terms = [results[0]] + [bal_swap(results[turn], turn, bals) for turn in range(1, bals)]
+        last = 2 * width
+        first = wide - last
+        shape = lambda *dims: jax.ShapeDtypeStruct(dims, bf16)
         pieces = pl.pallas_call(
-            functools.partial(pieces_kernel, bals),
-            out_shape=[jax.ShapeDtypeStruct((height, wide), bf16)]
-            + [jax.ShapeDtypeStruct((height, wide + rows // height * columns), bf16)] * (groups - 1),
+            functools.partial(pieces_kernel, tables, groups, bals),
+            out_shape=[shape(height, first)]
+            + [shape(height, first + rows // height * columns)] * (groups - 1)
+            + [shape(height, last)] * tables,
             in_specs=[VMEM] * (bals + groups - 1),
-            out_specs=[VMEM] * groups,
+            out_specs=[VMEM] * (groups + tables),
             compiler_params=room(12),
         )(*terms, *grads[1:])
-        came = [emb_swap(pieces[step], step, embs) for step in range(1, groups)]
-        mine = sum_rounded([value[:, :wide] for value in came[::-1]] + [pieces[0]])
-        mine = mine.reshape(tables, unit, wide)
-        sums = table_sums([grads[0]] + came)
-        own_sums = over_cores(sums)
-        came = [emb_swap(mine[step], step * groups, embs) for step in range(1, tables)]
-        final = sum_rounded(came[-1:] + came[:-1] + [mine[0]])
+        plane_pieces, table_pieces = pieces[:groups], pieces[groups:]
+        order = ordered(plane_steps, table_steps, ("table", 1))
+        came = {("plane", step): emb_swap(plane_pieces[step], step, embs) for step in plane_steps}
+        for step in table_steps:
+            came["table", step] = emb_swap(table_pieces[step], step * groups, embs)
+        mine = pl.pallas_call(
+            functools.partial(first_sums_kernel, order, tables, groups),
+            out_shape=[shape(unit, first)] * tables + [shape(unit, last)] * groups,
+            in_specs=[VMEM] * (2 + len(order)),
+            out_specs=[VMEM] * (tables + groups),
+            compiler_params=room(12),
+        )(plane_pieces[0], table_pieces[0], *[came[one] for one in order])
+        plane_grads = [grads[0]] + [came["plane", step] for step in range(1, groups)]
+        order = ordered(plane_steps, table_steps, ("plane", 1))
+        came = {("plane", step): emb_swap(mine[tables + step], step, embs) for step in plane_steps}
+        for step in table_steps:
+            came["table", step] = emb_swap(mine[step], step * groups, embs)
+        final = pl.pallas_call(
+            functools.partial(second_sums_kernel, order),
+            out_shape=shape(unit, wide),
+            in_specs=[VMEM] * (2 + len(order)),
+            out_specs=VMEM,
+            compiler_params=room(12),
+        )(mine[0], mine[tables], *[came[one] for one in order])
+        own_sums = over_cores(table_sums(plane_grads, final))
         gathered = [final] + [emb_swap(final, step * groups, embs) for step in range(1, tables)]
         back = to_plane(jnp.concatenate(gathered, axis=0))
         later = after(own_sums, *gathered[1:])

time: 101 us -> 104 us (1.030)
  starting transfers between devices: 31.7 us -> 41.5 us
  waiting for transfers between devices: 46.3 us -> 39.3 us
    ppermute x23 -> x29, starting transfers between devices: 30.3 us -> 40.2 us  [emb_swap(): return lax.ppermute(value, 'emb', [(i, i ^ step) for i in range(count)])]
    ppermute x23 -> x29, waiting for transfers between devices: 43.2 us -> 36.2 us  [emb_swap(): return lax.ppermute(value, 'emb', [(i, i ^ step) for i in range(count)])]
    pallas_call x2 -> x4, Pallas kernels: 3.22 us -> 3.43 us  [the longest x1 2.91 us: table_sums(): pl.pallas_call(functools.partial(scatter_kernel, groups, slots, bals, len...]
  transfers between devices with their start and end apart: 31 -> 37, of which waited for: 16 -> 16; matrix products, arithmetic and copies ran while one was open for 4% -> 4% of each run, Pallas kernels for 5% -> 2%
where the time goes in v11:
time: 104 us
  starting transfers between devices  41.5 us (40%)
  waiting for transfers between devices  39.3 us (38%)
  Pallas kernels  16.3 us (16%)
  other arithmetic  3.75 us (4%)
  local copies, waits for them, and re-layouts  2.4 us (2%)
    ppermute x29, starting transfers between devices, emb_swap(): return lax.ppermute(value, 'emb', [(i, i ^ step) for i in range(count)])  40.2 us
    ppermute x29, waiting for transfers between devices, emb_swap(): return lax.ppermute(value, 'emb', [(i, i ^ step) for i in range(count)])  36.2 us
    pallas_call x1, Pallas kernels, on_device(): pl.pallas_call(functools.partial(layer_kernel, groups, slots, tables, bal...  6.28 us
    pallas_call x2, Pallas kernels, on_device(): pl.pallas_call(functools.partial(place_kernel, grad_scale, steps, slots,...  3.5 us
    pallas_call x1, Pallas kernels, on_device(): pl.pallas_call(functools.partial(lookup_kernel, groups, slots, tables, ba...  3.08 us
    ppermute x8, waiting for transfers between devices, bal_swap(): return lax.ppermute(value, 'bal', [(i, i ^ step) for i in range(count)])  3.06 us
    pallas_call x1, Pallas kernels, table_sums(): pl.pallas_call(functools.partial(scatter_kernel, groups, slots, bals, len...  2.91 us
  transfers between devices with their start and end apart: 37, of which 16 were waited for; matrix products, arithmetic and copies ran while one was open for 4% of the time, Pallas kernels for 2%

profile of v11, /device:TPU:0, one launch (start us, length us, event | category | flops | bytes accessed | tf_op | source)
XLA Modules:
  0.0 104.1 jit_solution(7176403488580449504)
XLA Ops:
  1.6 5.1 %collective-permute-start.8 = (bf16[512,128]{1,0:T(8,128)(2,1)S(1)}, bf16[512,128]{1,0:T(8,128)(2,1)S(1)}, u32[]{:S(2)}, u32[]{:S(2)}) collective-permute-start(bf16[512,128]{1,0:T(8,128)(2,1)S(1)} %dynamic-slice_bitcast_fusion.refs_3_), channel_id=1, source_target_pairs={{0,24},{2,26},{4,28},{6,30},{8,16},{10,18},{12,20},{14,22},{16,8},... | collective-permute-start | bytes 393224 | tf_op jit(solution)/shard_map/ppermute | solution.py:54
  11.4 1.9 %collective-permute-done = s32[1,128]{1,0:T(1,128)S(1)} collective-permute-done((s32[1,128]{1,0:T(1,128)S(1)}, s32[1,128]{1,0:T(1,128)S(1)}, u32[]{:S(2)}, u32[]{:S(2)}) %collective-permute-start) | collective-permute-done | bytes 544 | tf_op jit(solution)/shard_map/ppermute | solution.py:54
  19.1 3.1 %shard_map.111 = (bf16[256,128]{1,0:T(8,128)(2,1)S(1)}, bf16[256,128]{1,0:T(8,128)(2,1)S(1)}, bf16[256,128]{1,0:T(8,128)(2,1)S(1)}, bf16[256,128]{1,0:T(8,128)(2,1)S(1)}) custom-call(s32[4,128]{1,0:T(4,128)S(1)} %pad_add_fusion.refs_0_.scalar_ref, s32[4,8,1,128]{3,2,1,0:T(1,128)S(1)} %reshape.52.refs_1_, ...), custom_call_target="tpu_custom_call" | custom-call | bytes 10500000 | tf_op jit(solution)/shard_map/pallas_call | solution.py:483
  22.5 2.6 %collective-permute-start.10 = (bf16[256,128]{1,0:T(8,128)(2,1)S(1)}, bf16[256,128]{1,0:T(8,128)(2,1)S(1)}, u32[]{:S(2)}, u32[]{:S(2)}) collective-permute-start(bf16[256,128]{1,0:T(8,128)(2,1)S(1)} %get-tuple-element.49), channel_id=1, source_target_pairs={{0,6},{2,4},{4,2},{6,0},{8,14},{10,12},{12,10},{14,8},{16,22},{18,... | collective-permute-start | bytes 196616 | tf_op jit(solution)/shard_map/ppermute | solution.py:54
  26.0 1.7 %collective-permute-done.10.refs_0_ = bf16[256,128]{1,0:T(8,128)(2,1)S(1)} collective-permute-done((bf16[256,128]{1,0:T(8,128)(2,1)S(1)}, bf16[256,128]{1,0:T(8,128)(2,1)S(1)}, u32[]{:S(2)}, u32[]{:S(2)}) %collective-permute-start.10) | collective-permute-done | bytes 65568 | tf_op jit(solution)/shard_map/ppermute | solution.py:54
  29.9 6.3 %shard_map.112 = (bf16[256,512]{1,0:T(8,128)(2,1)}, bf16[256,128]{1,0:T(8,128)(2,1)S(1)}, bf16[256,128]{1,0:T(8,128)(2,1)S(1)}, bf16[256,128]{1,0:T(8,128)(2,1)S...) custom-call(s32[4,128]{1,0:T(4,128)S(1)} %pad_add_fusion.refs_0_.scalar_ref, ...), custom_call_target="tpu_custom_call" | custom-call | bytes 24500000 | tf_op jit(solution)/shard_map/pallas_call | solution.py:497
  36.2 3.0 %collective-permute-done.14.refs_1_ = bf16[256,2560]{1,0:T(8,128)(2,1)S(1)} collective-permute-done((bf16[256,2560]{1,0:T(8,128)(2,1)S(1)}, bf16[256,2560]{1,0:T(8,128)(2,1)S(1)}, u32[]{:S(2)}, u32[]{:S(2)}) %collective-permute-start.14) | collective-permute-done | bytes 1310752 | tf_op jit(solution)/shard_map/ppermute | solution.py:46
  44.4 2.4 %collective-permute-start.19 = (bf16[64,1024]{1,0:T(8,128)(2,1)S(1)}, bf16[64,1024]{1,0:T(8,128)(2,1)S(1)}, u32[]{:S(2)}, u32[]{:S(2)}) collective-permute-start(bf16[64,1024]{1,0:T(8,128)(2,1)S(1)} %get-tuple-element.67), channel_id=1, source_target_pairs={{0,24},{2,26},{4,28},{6,30},{8,16},{10,18},{12,20},{14,22},{16,8},... | collective-permute-start | bytes 393224 | tf_op jit(solution)/shard_map/ppermute | solution.py:54
  47.6 4.8 %collective-permute-done.19.refs_2_ = bf16[64,1024]{1,0:T(8,128)(2,1)S(1)} collective-permute-done((bf16[64,1024]{1,0:T(8,128)(2,1)S(1)}, bf16[64,1024]{1,0:T(8,128)(2,1)S(1)}, u32[]{:S(2)}, u32[]{:S(2)}) %collective-permute-start.19) | collective-permute-done | bytes 131104 | tf_op jit(solution)/shard_map/ppermute | solution.py:54
  52.4 6.0 %collective-permute-done.20.refs_4_ = bf16[64,1024]{1,0:T(8,128)(2,1)S(1)} collective-permute-done((bf16[64,1024]{1,0:T(8,128)(2,1)S(1)}, bf16[64,1024]{1,0:T(8,128)(2,1)S(1)}, u32[]{:S(2)}, u32[]{:S(2)}) %collective-permute-start.20) | collective-permute-done | bytes 131104 | tf_op jit(solution)/shard_map/ppermute | solution.py:54
  59.6 2.6 %collective-permute-start.22 = (bf16[16,1536]{1,0:T(8,128)(2,1)S(1)}, bf16[16,1536]{1,0:T(8,128)(2,1)S(1)}, u32[]{:S(2)}, u32[]{:S(2)}) collective-permute-start(bf16[16,1536]{1,0:T(8,128)(2,1)S(1)} %get-tuple-element.72), channel_id=1, source_target_pairs={{0,24},{2,26},{4,28},{6,30},{8,16},{10,18},{12,20},{14,22},{16,8},... | collective-permute-start | bytes 147464 | tf_op jit(solution)/shard_map/ppermute | solution.py:54
  62.2 1.7 %collective-permute-start.26 = (bf16[16,1536]{1,0:T(8,128)(2,1)S(1)}, bf16[16,1536]{1,0:T(8,128)(2,1)S(1)}, u32[]{:S(2)}, u32[]{:S(2)}) collective-permute-start(bf16[16,1536]{1,0:T(8,128)(2,1)S(1)} %get-tuple-element.76), channel_id=1, source_target_pairs={{0,8},{2,10},{4,12},{6,14},{8,0},{10,2},{12,4},{14,6},{16,24},{18,... | collective-permute-start | bytes 147464 | tf_op jit(solution)/shard_map/ppermute | solution.py:54
  63.9 2.1 %collective-permute-start.23 = (bf16[16,1024]{1,0:T(8,128)(2,1)S(1)}, bf16[16,1024]{1,0:T(8,128)(2,1)S(1)}, u32[]{:S(2)}, u32[]{:S(2)}) collective-permute-start(bf16[16,1024]{1,0:T(8,128)(2,1)S(1)} %get-tuple-element.73), channel_id=1, source_target_pairs={{0,6},{2,4},{4,2},{6,0},{8,14},{10,12},{12,10},{14,8},{16,22},{18,... | collective-permute-start | bytes 98312 | tf_op jit(solution)/shard_map/ppermute | solution.py:54
  66.5 2.2 %collective-permute-done.23.refs_2_ = bf16[16,1024]{1,0:T(8,128)(2,1)S(1)} collective-permute-done((bf16[16,1024]{1,0:T(8,128)(2,1)S(1)}, bf16[16,1024]{1,0:T(8,128)(2,1)S(1)}, u32[]{:S(2)}, u32[]{:S(2)}) %collective-permute-start.23) | collective-permute-done | bytes 32800 | tf_op jit(solution)/shard_map/ppermute | solution.py:54
  70.0 2.9 %shard_map.116 = (bf16[4,512,128]{2,1,0:T(8,128)(2,1)S(1)}, bf16[4,512,128]{2,1,0:T(8,128)(2,1)S(1)}) custom-call(s32[4,128]{1,0:T(4,128)S(1)} %pad_add_fusion.refs_0_.scalar_ref, s32[4,8,1,128]{3,2,1,0:T(1,128)S(1)} %reshape.52.refs_1_, s32[4,8,1,128]{3,2,1,0:T(1,128)S(1)} %collective-permute-done.2.refs_2_, ...), custom_call_target="tpu_custom_call" | custom-call | bytes 10500000 | tf_op jit(solution)/shard_map/pallas_call | solution.py:530
  73.0 2.7 %collective-permute-start.30 = (bf16[16,2560]{1,0:T(8,128)(2,1)S(1)}, bf16[16,2560]{1,0:T(8,128)(2,1)S(1)}, u32[]{:S(2)}, u32[]{:S(2)}) collective-permute-start(bf16[16,2560]{1,0:T(8,128)(2,1)S(1)} %shard_map.115.refs_7_), channel_id=1, source_target_pairs={{0,24},{2,26},{4,28},{6,30},{8,16},{10,18},{12,20},{14,22},{16,8},... | collective-permute-start | bytes 245768 | tf_op jit(solution)/shard_map/ppermute | solution.py:54
  75.7 1.7 %collective-permute-start.28 = (bf16[16,2560]{1,0:T(8,128)(2,1)S(1)}, bf16[16,2560]{1,0:T(8,128)(2,1)S(1)}, u32[]{:S(2)}, u32[]{:S(2)}) collective-permute-start(bf16[16,2560]{1,0:T(8,128)(2,1)S(1)} %shard_map.115.refs_7_), channel_id=1, source_target_pairs={{0,8},{2,10},{4,12},{6,14},{8,0},{10,2},{12,4},{14,6},{16,24},{18,... | collective-permute-start | bytes 245768 | tf_op jit(solution)/shard_map/ppermute | solution.py:54
  77.5 2.7 %collective-permute-done.30 = bf16[16,2560]{1,0:T(8,128)(2,1)S(1)} collective-permute-done((bf16[16,2560]{1,0:T(8,128)(2,1)S(1)}, bf16[16,2560]{1,0:T(8,128)(2,1)S(1)}, u32[]{:S(2)}, u32[]{:S(2)}) %collective-permute-start.30) | collective-permute-done | bytes 81952 | tf_op jit(solution)/shard_map/ppermute | solution.py:54
  80.2 3.0 %collective-permute-done.29 = bf16[16,2560]{1,0:T(8,128)(2,1)S(1)} collective-permute-done((bf16[16,2560]{1,0:T(8,128)(2,1)S(1)}, bf16[16,2560]{1,0:T(8,128)(2,1)S(1)}, u32[]{:S(2)}, u32[]{:S(2)}) %collective-permute-start.29) | collective-permute-done | bytes 81952 | tf_op jit(solution)/shard_map/ppermute | solution.py:54
  86.9 2.7 %collective-permute-start.31 = (bf16[512,128]{1,0:T(8,128)(2,1)S(1)}, bf16[512,128]{1,0:T(8,128)(2,1)S(1)}, u32[]{:S(2)}, u32[]{:S(2)}) collective-permute-start(bf16[512,128]{1,0:T(8,128)(2,1)S(1)} %get-tuple-element.90), channel_id=1, source_target_pairs={{0,24},{2,26},{4,28},{6,30},{8,16},{10,18},{12,20},{14,22},{16,8},... | collective-permute-start | bytes 393224 | tf_op jit(solution)/shard_map/ppermute | solution.py:54
  89.7 5.1 %collective-permute-done.34.refs_1_ = bf16[64,2560]{1,0:T(8,128)(2,1)S(1)} collective-permute-done((bf16[64,2560]{1,0:T(8,128)(2,1)S(1)}, bf16[64,2560]{1,0:T(8,128)(2,1)S(1)}, u32[]{:S(2)}, u32[]{:S(2)}) %collective-permute-start.34) | collective-permute-done | bytes 327712 | tf_op jit(solution)/shard_map/ppermute | solution.py:54
  95.7 1.8 %shard_map.117 = (f32[256,2048]{1,0:T(8,128)}, f32[256,512]{1,0:T(8,128)}) custom-call(s32[4,128]{1,0:T(4,128)S(1)} %pad_add_fusion.refs_0_.scalar_ref, bf16[64,2560]{1,0:T(8,128)(2,1)S(1)} %pad_maximum_fusion.1.refs_0_, bf16[64,2560]{1,0:T(8,128)(2,1)S(1)} %collective-permute-done.34.refs_1_), custom_call_target="tpu_custom_call" | custom-call | bytes 3500000 | tf_op jit(solution)/shard_map/pallas_call | solution.py:599
  97.5 3.4 %collective-permute-done.33.refs_1_ = bf16[64,2560]{1,0:T(8,128)(2,1)S(1)} collective-permute-done((bf16[64,2560]{1,0:T(8,128)(2,1)S(1)}, bf16[64,2560]{1,0:T(8,128)(2,1)S(1)}, u32[]{:S(2)}, u32[]{:S(2)}) %collective-permute-start.33) | collective-permute-done | bytes 327712 | tf_op jit(solution)/shard_map/ppermute | solution.py:54
  102.3 1.8 %shard_map.118 = (f32[256,2048]{1,0:T(8,128)}, f32[256,512]{1,0:T(8,128)}) custom-call(s32[4,128]{1,0:T(4,128)S(1)} %pad_add_fusion.refs_0_.scalar_ref, bf16[64,2560]{1,0:T(8,128)(2,1)S(1)} %collective-permute-done.32.refs_0_, bf16[64,2560]{1,0:T(8,128)(2,1)S(1)} %collective-permute-done.33.refs_1_, ...), custom_call_target="tpu_custom_call", output_to_operand_aliasing={{0}: (3, {}), {1}: (4, {})} | custom-call | bytes 3500000 | tf_op jit(solution)/shard_map/pallas_call | solution.py:599
  (75 shorter events, 29.9 us)
Async XLA Ops:
  1.6 15.9 %collective-permute-start.8 = (bf16[512,128]{1,0:T(8,128)(2,1)S(1)}, bf16[512,128]{1,0:T(8,128)(2,1)S(1)}, u32[]{:S(2)}, u32[]{:S(2)}) collective-permute-start(bf16[512,128]{1,0:T(8,128)(2,1)S(1)} %dynamic-slice_bitcast_fusion.refs_3_), channel_id=1, source_target_pairs={{0,24},{2,26},{4,28},{6,30},{8,16},{10,18},{12,20},{14,22},{16,8},... | collective-permute-start | bytes 393224 | tf_op jit(solution)/shard_map/ppermute | solution.py:54
  6.7 11.1 %collective-permute-start.6 = (bf16[512,128]{1,0:T(8,128)(2,1)S(1)}, bf16[512,128]{1,0:T(8,128)(2,1)S(1)}, u32[]{:S(2)}, u32[]{:S(2)}) collective-permute-start(bf16[512,128]{1,0:T(8,128)(2,1)S(1)} %dynamic-slice_bitcast_fusion.refs_3_), channel_id=1, source_target_pairs={{0,16},{2,18},{4,20},{6,22},{8,24},{10,26},{12,28},{14,30},{16,0},... | collective-permute-start | bytes 393224 | tf_op jit(solution)/shard_map/ppermute | solution.py:54
  6.7 10.2 %collective-permute-start.4 = (bf16[512,128]{1,0:T(8,128)(2,1)S(1)}, bf16[512,128]{1,0:T(8,128)(2,1)S(1)}, u32[]{:S(2)}, u32[]{:S(2)}) collective-permute-start(bf16[512,128]{1,0:T(8,128)(2,1)S(1)} %dynamic-slice_bitcast_fusion.refs_3_), channel_id=1, source_target_pairs={{0,8},{2,10},{4,12},{6,14},{8,0},{10,2},{12,4},{14,6},{16,24},{18,... | collective-permute-start | bytes 393224 | tf_op jit(solution)/shard_map/ppermute | solution.py:54
  11.4 7.7 %collective-permute-start.3 = (bf16[512,128]{1,0:T(8,128)(2,1)S(1)}, bf16[512,128]{1,0:T(8,128)(2,1)S(1)}, u32[]{:S(2)}, u32[]{:S(2)}) collective-permute-start(bf16[512,128]{1,0:T(8,128)(2,1)S(1)} %dynamic-slice_bitcast_fusion.refs_3_), channel_id=1, source_target_pairs={{0,1},{1,0},{2,3},{3,2},{4,5},{5,4},{6,7},{7,6},{8,9},{9,8},{10,11... | collective-permute-start | bytes 393224 | tf_op jit(solution)/shard_map/ppermute | solution.py:46
  22.2 7.7 %collective-permute-start.13 = (bf16[256,2560]{1,0:T(8,128)(2,1)S(1)}, bf16[256,2560]{1,0:T(8,128)(2,1)S(1)}, u32[]{:S(2)}, u32[]{:S(2)}) collective-permute-start(bf16[256,2560]{1,0:T(8,128)(2,1)S(1)} %pad_maximum_fusion.refs_4_), channel_id=1, source_target_pairs={{0,1},{1,0},{2,3},{3,2},{4,5},{5,4},{6,7},{7,6},{8,9},{9,8},{10,11... | collective-permute-start | bytes 3932168 | tf_op jit(solution)/shard_map/ppermute | solution.py:46
  39.6 7.2 %collective-permute-start.18 = (bf16[64,1024]{1,0:T(8,128)(2,1)S(1)}, bf16[64,1024]{1,0:T(8,128)(2,1)S(1)}, u32[]{:S(2)}, u32[]{:S(2)}) collective-permute-start(bf16[64,1024]{1,0:T(8,128)(2,1)S(1)} %get-tuple-element.66), channel_id=1, source_target_pairs={{0,8},{2,10},{4,12},{6,14},{8,0},{10,2},{12,4},{14,6},{16,24},{18,... | collective-permute-start | bytes 393224 | tf_op jit(solution)/shard_map/ppermute | solution.py:54
  40.9 17.5 %collective-permute-start.15 = (bf16[64,2048]{1,0:T(8,128)(2,1)S(1)}, bf16[64,2048]{1,0:T(8,128)(2,1)S(1)}, u32[]{:S(2)}, u32[]{:S(2)}) collective-permute-start(bf16[64,2048]{1,0:T(8,128)(2,1)S(1)} %get-tuple-element.60), channel_id=1, source_target_pairs={{0,6},{2,4},{4,2},{6,0},{8,14},{10,12},{12,10},{14,8},{16,22},{18,... | collective-permute-start | bytes 786440 | tf_op jit(solution)/shard_map/ppermute | solution.py:54
  42.4 16.0 %collective-permute-start.16 = (bf16[64,2048]{1,0:T(8,128)(2,1)S(1)}, bf16[64,2048]{1,0:T(8,128)(2,1)S(1)}, u32[]{:S(2)}, u32[]{:S(2)}) collective-permute-start(bf16[64,2048]{1,0:T(8,128)(2,1)S(1)} %get-tuple-element.61), channel_id=1, source_target_pairs={{0,4},{2,6},{4,0},{6,2},{8,12},{10,14},{12,8},{14,10},{16,20},{18,... | collective-permute-start | bytes 786440 | tf_op jit(solution)/shard_map/ppermute | solution.py:54
  43.3 15.2 %collective-permute-start.17 = (bf16[64,2048]{1,0:T(8,128)(2,1)S(1)}, bf16[64,2048]{1,0:T(8,128)(2,1)S(1)}, u32[]{:S(2)}, u32[]{:S(2)}) collective-permute-start(bf16[64,2048]{1,0:T(8,128)(2,1)S(1)} %get-tuple-element.62), channel_id=1, source_target_pairs={{0,2},{2,0},{4,6},{6,4},{8,10},{10,8},{12,14},{14,12},{16,18},{18,... | collective-permute-start | bytes 786440 | tf_op jit(solution)/shard_map/ppermute | solution.py:54
  44.4 8.0 %collective-permute-start.19 = (bf16[64,1024]{1,0:T(8,128)(2,1)S(1)}, bf16[64,1024]{1,0:T(8,128)(2,1)S(1)}, u32[]{:S(2)}, u32[]{:S(2)}) collective-permute-start(bf16[64,1024]{1,0:T(8,128)(2,1)S(1)} %get-tuple-element.67), channel_id=1, source_target_pairs={{0,24},{2,26},{4,28},{6,30},{8,16},{10,18},{12,20},{14,22},{16,8},... | collective-permute-start | bytes 393224 | tf_op jit(solution)/shard_map/ppermute | solution.py:54
  46.8 11.6 %collective-permute-start.20 = (bf16[64,1024]{1,0:T(8,128)(2,1)S(1)}, bf16[64,1024]{1,0:T(8,128)(2,1)S(1)}, u32[]{:S(2)}, u32[]{:S(2)}) collective-permute-start(bf16[64,1024]{1,0:T(8,128)(2,1)S(1)} %get-tuple-element.68), channel_id=1, source_target_pairs={{0,16},{2,18},{4,20},{6,22},{8,24},{10,26},{12,28},{14,30},{16,0},... | collective-permute-start | bytes 393224 | tf_op jit(solution)/shard_map/ppermute | solution.py:54
  58.6 7.4 %collective-permute-start.21 = (bf16[16,1024]{1,0:T(8,128)(2,1)S(1)}, bf16[16,1024]{1,0:T(8,128)(2,1)S(1)}, u32[]{:S(2)}, u32[]{:S(2)}) collective-permute-start(bf16[16,1024]{1,0:T(8,128)(2,1)S(1)} %get-tuple-element.71), channel_id=1, source_target_pairs={{0,2},{2,0},{4,6},{6,4},{8,10},{10,8},{12,14},{14,12},{16,18},{18,... | collective-permute-start | bytes 98312 | tf_op jit(solution)/shard_map/ppermute | solution.py:54
  59.6 10.4 %collective-permute-start.22 = (bf16[16,1536]{1,0:T(8,128)(2,1)S(1)}, bf16[16,1536]{1,0:T(8,128)(2,1)S(1)}, u32[]{:S(2)}, u32[]{:S(2)}) collective-permute-start(bf16[16,1536]{1,0:T(8,128)(2,1)S(1)} %get-tuple-element.72), channel_id=1, source_target_pairs={{0,24},{2,26},{4,28},{6,30},{8,16},{10,18},{12,20},{14,22},{16,8},... | collective-permute-start | bytes 147464 | tf_op jit(solution)/shard_map/ppermute | solution.py:54
  62.2 7.8 %collective-permute-start.24 = (bf16[16,1536]{1,0:T(8,128)(2,1)S(1)}, bf16[16,1536]{1,0:T(8,128)(2,1)S(1)}, u32[]{:S(2)}, u32[]{:S(2)}) collective-permute-start(bf16[16,1536]{1,0:T(8,128)(2,1)S(1)} %get-tuple-element.74), channel_id=1, source_target_pairs={{0,16},{2,18},{4,20},{6,22},{8,24},{10,26},{12,28},{14,30},{16,0},... | collective-permute-start | bytes 147464 | tf_op jit(solution)/shard_map/ppermute | solution.py:54
  62.2 7.8 %collective-permute-start.26 = (bf16[16,1536]{1,0:T(8,128)(2,1)S(1)}, bf16[16,1536]{1,0:T(8,128)(2,1)S(1)}, u32[]{:S(2)}, u32[]{:S(2)}) collective-permute-start(bf16[16,1536]{1,0:T(8,128)(2,1)S(1)} %get-tuple-element.76), channel_id=1, source_target_pairs={{0,8},{2,10},{4,12},{6,14},{8,0},{10,2},{12,4},{14,6},{16,24},{18,... | collective-permute-start | bytes 147464 | tf_op jit(solution)/shard_map/ppermute | solution.py:54
  72.9 13.8 %collective-permute-start.27 = (bf16[4,512,128]{2,1,0:T(8,128)(2,1)S(1)}, bf16[4,512,128]{2,1,0:T(8,128)(2,1)S(1)}, u32[]{:S(2)}, u32[]{:S(2)}) collective-permute-start(bf16[4,512,128]{2,1,0:T(8,128)(2,1)S(1)} %get-tuple-element.78), channel_id=1, source_target_pairs={{0,1},{1,0},{2,3},{3,2},{4,5},{5,4},{6,7},{7,6},{8,9},{9,8},{10,11... | collective-permute-start | bytes 1572872 | tf_op jit(solution)/shard_map/ppermute | solution.py:46
  73.0 7.2 %collective-permute-start.30 = (bf16[16,2560]{1,0:T(8,128)(2,1)S(1)}, bf16[16,2560]{1,0:T(8,128)(2,1)S(1)}, u32[]{:S(2)}, u32[]{:S(2)}) collective-permute-start(bf16[16,2560]{1,0:T(8,128)(2,1)S(1)} %shard_map.115.refs_7_), channel_id=1, source_target_pairs={{0,24},{2,26},{4,28},{6,30},{8,16},{10,18},{12,20},{14,22},{16,8},... | collective-permute-start | bytes 245768 | tf_op jit(solution)/shard_map/ppermute | solution.py:54
  75.7 7.5 %collective-permute-start.29 = (bf16[16,2560]{1,0:T(8,128)(2,1)S(1)}, bf16[16,2560]{1,0:T(8,128)(2,1)S(1)}, u32[]{:S(2)}, u32[]{:S(2)}) collective-permute-start(bf16[16,2560]{1,0:T(8,128)(2,1)S(1)} %shard_map.115.refs_7_), channel_id=1, source_target_pairs={{0,16},{2,18},{4,20},{6,22},{8,24},{10,26},{12,28},{14,30},{16,0},... | collective-permute-start | bytes 245768 | tf_op jit(solution)/shard_map/ppermute | solution.py:54
  75.7 7.5 %collective-permute-start.28 = (bf16[16,2560]{1,0:T(8,128)(2,1)S(1)}, bf16[16,2560]{1,0:T(8,128)(2,1)S(1)}, u32[]{:S(2)}, u32[]{:S(2)}) collective-permute-start(bf16[16,2560]{1,0:T(8,128)(2,1)S(1)} %shard_map.115.refs_7_), channel_id=1, source_target_pairs={{0,8},{2,10},{4,12},{6,14},{8,0},{10,2},{12,4},{14,6},{16,24},{18,... | collective-permute-start | bytes 245768 | tf_op jit(solution)/shard_map/ppermute | solution.py:54
  83.2 11.6 %collective-permute-start.34 = (bf16[64,2560]{1,0:T(8,128)(2,1)S(1)}, bf16[64,2560]{1,0:T(8,128)(2,1)S(1)}, u32[]{:S(2)}, u32[]{:S(2)}) collective-permute-start(bf16[64,2560]{1,0:T(8,128)(2,1)S(1)} %pad_maximum_fusion.1.refs_0_), channel_id=1, source_target_pairs={{0,6},{2,4},{4,2},{6,0},{8,14},{10,12},{12,10},{14,8},{16,22},{18,... | collective-permute-start | bytes 983048 | tf_op jit(solution)/shard_map/ppermute | solution.py:54
  84.5 16.4 %collective-permute-start.33 = (bf16[64,2560]{1,0:T(8,128)(2,1)S(1)}, bf16[64,2560]{1,0:T(8,128)(2,1)S(1)}, u32[]{:S(2)}, u32[]{:S(2)}) collective-permute-start(bf16[64,2560]{1,0:T(8,128)(2,1)S(1)} %pad_maximum_fusion.1.refs_0_), channel_id=1, source_target_pairs={{0,4},{2,6},{4,0},{6,2},{8,12},{10,14},{12,8},{14,10},{16,20},{18,... | collective-permute-start | bytes 983048 | tf_op jit(solution)/shard_map/ppermute | solution.py:54
  85.3 15.6 %collective-permute-start.32 = (bf16[64,2560]{1,0:T(8,128)(2,1)S(1)}, bf16[64,2560]{1,0:T(8,128)(2,1)S(1)}, u32[]{:S(2)}, u32[]{:S(2)}) collective-permute-start(bf16[64,2560]{1,0:T(8,128)(2,1)S(1)} %pad_maximum_fusion.1.refs_0_), channel_id=1, source_target_pairs={{0,2},{2,0},{4,6},{6,4},{8,10},{10,8},{12,14},{14,12},{16,18},{18,... | collective-permute-start | bytes 983048 | tf_op jit(solution)/shard_map/ppermute | solution.py:54
  86.9 13.9 %collective-permute-start.31 = (bf16[512,128]{1,0:T(8,128)(2,1)S(1)}, bf16[512,128]{1,0:T(8,128)(2,1)S(1)}, u32[]{:S(2)}, u32[]{:S(2)}) collective-permute-start(bf16[512,128]{1,0:T(8,128)(2,1)S(1)} %get-tuple-element.90), channel_id=1, source_target_pairs={{0,24},{2,26},{4,28},{6,30},{8,16},{10,18},{12,20},{14,22},{16,8},... | collective-permute-start | bytes 393224 | tf_op jit(solution)/shard_map/ppermute | solution.py:54
  89.7 11.2 %collective-permute-start.36 = (bf16[512,128]{1,0:T(8,128)(2,1)S(1)}, bf16[512,128]{1,0:T(8,128)(2,1)S(1)}, u32[]{:S(2)}, u32[]{:S(2)}) collective-permute-start(bf16[512,128]{1,0:T(8,128)(2,1)S(1)} %get-tuple-element.91), channel_id=1, source_target_pairs={{0,16},{2,18},{4,20},{6,22},{8,24},{10,26},{12,28},{14,30},{16,0},... | collective-permute-start | bytes 393224 | tf_op jit(solution)/shard_map/ppermute | solution.py:54
  (15 other events, 65.0 us)

commit v12 on v10

--- a/solution.py
+++ b/solution.py
@@ -183,6 +183,12 @@
     return inverse * (incoming - first - normed * second)
 
 
+def times_parts_nt(value, weight_refs, first, last, bal, wide_ref):
+    for turn, ref in enumerate(weight_refs):
+        wide_ref[bal ^ turn] = matmul_nt(value, ref[:, first:last])
+    return jnp.concatenate([wide_ref[index] for index in range(len(weight_refs))], axis=1)
+
+
 def layer_kernel(groups, slots, tables, bals, unit, scalar_ref, *refs):
     refs = list(refs)
     take = lambda count: [refs.pop(0) for _ in range(count)]
@@ -190,9 +196,9 @@
     weight_refs = take(bals)
     (cot_ref,) = take(1)
     (layer_ref,) = take(1)
-    grad_refs = take(groups)
+    grads_ref, normed_ref, inverse_ref = take(3)
     term_refs = take(bals)
-    (x_ref, halves_ref, wide_ref, nt_ref, mt_ref, weights_ref, slope_ref, gate_ref, heads_ref, dsilu_ref, grads_ref) = refs
+    (x_ref, halves_ref, wide_ref, nt_ref, mt_ref, weights_ref, slope_ref, gate_ref, heads_ref, dsilu_ref) = refs
 
     scalars = Scalars(scalar_ref, 0, bals, slots)
     bal, group_here, table_here = scalars.place()
@@ -211,11 +217,6 @@
             found = found + matmul(halves_ref[bal ^ turn], weight_refs[turn][:, first:last])
         return found
 
-    def times_parts_nt(value, first, last):
-        for turn in range(bals):
-            wide_ref[bal ^ turn] = matmul_nt(value, weight_refs[turn][:, first:last])
-        return jnp.concatenate([wide_ref[index] for index in range(bals)], axis=1)
-
     my_slot = scalars.surplus(bal)
     source = scalars.source(bal)
     moved = scalars.length(source, scalars.surplus(source))
@@ -225,6 +226,8 @@
         x_ref[group_here ^ step] = block_refs[step][...]
     x = jnp.concatenate([x_ref[group] for group in range(groups)], axis=1).astype(f32)
     normed_in, in_inverse = norm(x)
+    normed_ref[...] = normed_in
+    inverse_ref[...] = jnp.broadcast_to(in_inverse, inverse_ref.shape)
     nt_ref[...] = jnp.transpose(normed_in).astype(bf16)
     projected = times_parts(normed_in.astype(bf16), 0, features)
     logistic = sigmoid(projected)
@@ -274,7 +277,7 @@
 
     wide_cot = cot_ref[...]
     cot = wide_cot.astype(bf16)
-    grad_mixed = times_parts_nt(cot, features, features + width)
+    grad_mixed = times_parts_nt(cot, weight_refs, features, features + width, bal, wide_ref)
     grad_attended = norm_back(grad_mixed * gate, normed_out, out_inverse).astype(bf16)
     grads_ref[:, :width] = (grad_mixed * normed_out * dsilu_ref[:, :width]).astype(bf16)
 
@@ -317,8 +320,19 @@
 
     emit_terms(nt_ref, grads_ref[...], 0)
 
-    grad_normed = times_parts_nt(grads_ref[...], 0, features)
-    grad_rows = (wide_cot + norm_back(grad_normed, normed_in, in_inverse)).astype(bf16)
+
+def rows_kernel(groups, slots, bals, scalar_ref, *refs):
+    refs = list(refs)
+    take = lambda count: [refs.pop(0) for _ in range(count)]
+    grads_ref, normed_ref, inverse_ref, cot_ref = take(4)
+    weight_refs, grad_refs = take(bals), take(groups)
+    x_ref, wide_ref = refs
+    bal, group_here, _ = Scalars(scalar_ref, 0, bals, slots).place()
+    features = grads_ref.shape[1]
+    piece = grad_refs[0].shape[1]
+    grad_normed = times_parts_nt(grads_ref[...], weight_refs, 0, features, bal, wide_ref)
+    back = norm_back(grad_normed, normed_ref[...], inverse_ref[:, :1])
+    grad_rows = (cot_ref[...] + back).astype(bf16)
     for group in range(groups):
         x_ref[group] = grad_rows[:, group * piece : (group + 1) * piece]
     for step in range(groups):
@@ -451,10 +465,11 @@
     results = pl.pallas_call(
         functools.partial(layer_kernel, groups, slots, tables, bals, unit),
         out_shape=[jax.ShapeDtypeStruct((rows, width), bf16)]
-        + [jax.ShapeDtypeStruct((rows, columns), bf16)] * groups
+        + [jax.ShapeDtypeStruct((rows, features), bf16)]
+        + [jax.ShapeDtypeStruct((rows, columns_here), f32) for columns_here in (width, LANES)]
         + [terms] * bals,
         in_specs=[SMEM] + [VMEM] * (groups + bals + 1),
-        out_specs=[VMEM] * (1 + groups + bals),
+        out_specs=[VMEM] * (4 + bals),
         scratch_shapes=[
             pltpu.VMEM((groups, rows, columns), bf16),
             pltpu.VMEM((bals, rows, weight_part), bf16),
@@ -466,13 +481,23 @@
             pltpu.VMEM((rows, width), f32),
             pltpu.VMEM((rows, features - width), bf16),
             pltpu.VMEM((rows, features), f32),
-            pltpu.VMEM((rows, features), bf16),
         ],
         cost_estimate=estimate(7),
         compiler_params=room(36),
     )(scalars, *block[::-1], *weights, wide_cot)
-    layer_out, results = results[0], results[1:]
-    grads, results = results[:groups], results[groups:]
+    layer_out, for_rows, results = results[0], results[1:4], results[4:]
+    grads = pl.pallas_call(
+        functools.partial(rows_kernel, groups, slots, bals),
+        out_shape=[jax.ShapeDtypeStruct((rows, columns), bf16)] * groups,
+        in_specs=[SMEM] + [VMEM] * (4 + bals),
+        out_specs=[VMEM] * groups,
+        scratch_shapes=[
+            pltpu.VMEM((groups, rows, columns), bf16),
+            pltpu.VMEM((bals, rows, weight_part), f32),
+        ],
+        cost_estimate=estimate(2),
+        compiler_params=room(16),
+    )(scalars, *for_rows, wide_cot, *weights)
 
     def over_cores(parts):
         return sum_rounded([parts[0]] + [bal_swap(parts[turn], turn, bals) for turn in range(1, bals)])
@@ -543,7 +568,7 @@
                 input_output_aliases={1 + len(steps) + index: index for index in range(len(totals))},
                 cost_estimate=estimate(1),
                 compiler_params=room(12),
-            )(after(scalars, table_sum) if totals else scalars, *[back[step] for step in steps], *totals)
+            )(scalars, *[back[step] for step in steps], *totals)
         total_in, total_out = totals
     else:
         total = lax.psum(over_cores(results).astype(f32), "emb") * grad_scale

time: 101 us -> 100 us (0.990)
  waiting for transfers between devices: 46.3 us -> 44 us
  Pallas kernels: 16.1 us -> 17.4 us
    pallas_call x0 -> x1, Pallas kernels: none -> 1.58 us  [on_device(): pl.pallas_call(functools.partial(rows_kernel, groups, slots, bals), out_s...]
    ppermute x8, waiting for transfers between devices: 3.06 us -> 1.48 us  [bal_swap(): return lax.ppermute(value, 'bal', [(i, i ^ step) for i in range(count)])]
  transfers between devices with their start and end apart: 31 -> 31, of which waited for: 16 -> 15; matrix products, arithmetic and copies ran while one was open for 4% -> 4% of each run, Pallas kernels for 5% -> 8%
where the time goes in v12:
time: 100 us
  waiting for transfers between devices  44 us (44%)
  starting transfers between devices  31.6 us (32%)
  Pallas kernels  17.4 us (17%)
  other arithmetic  3.96 us (4%)
  local copies, waits for them, and re-layouts  2.42 us (2%)
    ppermute x23, waiting for transfers between devices, emb_swap(): return lax.ppermute(value, 'emb', [(i, i ^ step) for i in range(count)])  42.5 us
    ppermute x23, starting transfers between devices, emb_swap(): return lax.ppermute(value, 'emb', [(i, i ^ step) for i in range(count)])  30.3 us
    pallas_call x1, Pallas kernels, on_device(): pl.pallas_call(functools.partial(layer_kernel, groups, slots, tables, bal...  6.03 us
    pallas_call x2, Pallas kernels, on_device(): pl.pallas_call(functools.partial(place_kernel, grad_scale, steps, slots,...  3.5 us
    pallas_call x1, Pallas kernels, on_device(): pl.pallas_call(functools.partial(lookup_kernel, groups, slots, tables, ba...  3.07 us
    pallas_call x1, Pallas kernels, table_sums(): pl.pallas_call(functools.partial(scatter_kernel, groups, slots, bals), ou...  2.9 us
  transfers between devices with their start and end apart: 31, of which 15 were waited for; matrix products, arithmetic and copies ran while one was open for 4% of the time, Pallas kernels for 8%

profile of v12, /device:TPU:0, one launch (start us, length us, event | category | flops | bytes accessed | tf_op | source)
XLA Modules:
  0.0 100.2 jit_solution(4558187040279701975)
XLA Ops:
  1.6 5.1 %collective-permute-start.8 = (bf16[512,128]{1,0:T(8,128)(2,1)S(1)}, bf16[512,128]{1,0:T(8,128)(2,1)S(1)}, u32[]{:S(2)}, u32[]{:S(2)}) collective-permute-start(bf16[512,128]{1,0:T(8,128)(2,1)S(1)} %dynamic-slice_bitcast_fusion.refs_3_), channel_id=1, source_target_pairs={{0,24},{2,26},{4,28},{6,30},{8,16},{10,18},{12,20},{14,22},{16,8},... | collective-permute-start | bytes 393224 | tf_op jit(solution)/shard_map/ppermute | solution.py:54
  9.8 1.6 %collective-permute-start = (s32[1,128]{1,0:T(1,128)S(1)}, s32[1,128]{1,0:T(1,128)S(1)}, u32[]{:S(2)}, u32[]{:S(2)}) collective-permute-start(s32[1,128]{1,0:T(1,128)S(1)} %pad_add_fusion.2), channel_id=1, source_target_pairs={{0,2},{2,0},{4,6},{6,4},{8,10},{10,8},{12,14},{14,12},{16,18},{18,... | collective-permute-start | bytes 1544 | tf_op jit(solution)/shard_map/ppermute | solution.py:54
  11.4 1.9 %collective-permute-done = s32[1,128]{1,0:T(1,128)S(1)} collective-permute-done((s32[1,128]{1,0:T(1,128)S(1)}, s32[1,128]{1,0:T(1,128)S(1)}, u32[]{:S(2)}, u32[]{:S(2)}) %collective-permute-start) | collective-permute-done | bytes 544 | tf_op jit(solution)/shard_map/ppermute | solution.py:54
  13.4 1.7 %collective-permute-start.1 = (s32[2,128]{1,0:T(2,128)S(1)}, s32[2,128]{1,0:T(2,128)S(1)}, u32[]{:S(2)}, u32[]{:S(2)}) collective-permute-start(s32[2,128]{1,0:T(2,128)S(1)} %pad_add_fusion.1), channel_id=1, source_target_pairs={{0,4},{2,6},{4,0},{6,2},{8,12},{10,14},{12,8},{14,10},{16,20},{18,... | collective-permute-start | bytes 3080 | tf_op jit(solution)/shard_map/ppermute | solution.py:54
  19.1 3.1 %shard_map.111 = (bf16[256,128]{1,0:T(8,128)(2,1)S(1)}, bf16[256,128]{1,0:T(8,128)(2,1)S(1)}, bf16[256,128]{1,0:T(8,128)(2,1)S(1)}, bf16[256,128]{1,0:T(8,128)(2,1)S(1)}) custom-call(s32[4,128]{1,0:T(4,128)S(1)} %pad_add_fusion.refs_0_.scalar_ref, s32[4,8,1,128]{3,2,1,0:T(1,128)S(1)} %reshape.61.refs_1_, ...), custom_call_target="tpu_custom_call" | custom-call | bytes 10500000 | tf_op jit(solution)/shard_map/pallas_call | solution.py:451
  22.5 2.6 %collective-permute-start.10 = (bf16[256,128]{1,0:T(8,128)(2,1)S(1)}, bf16[256,128]{1,0:T(8,128)(2,1)S(1)}, u32[]{:S(2)}, u32[]{:S(2)}) collective-permute-start(bf16[256,128]{1,0:T(8,128)(2,1)S(1)} %get-tuple-element.39), channel_id=1, source_target_pairs={{0,6},{2,4},{4,2},{6,0},{8,14},{10,12},{12,10},{14,8},{16,22},{18,... | collective-permute-start | bytes 196616 | tf_op jit(solution)/shard_map/ppermute | solution.py:54
  26.0 1.7 %collective-permute-done.10.refs_0_ = bf16[256,128]{1,0:T(8,128)(2,1)S(1)} collective-permute-done((bf16[256,128]{1,0:T(8,128)(2,1)S(1)}, bf16[256,128]{1,0:T(8,128)(2,1)S(1)}, u32[]{:S(2)}, u32[]{:S(2)}) %collective-permute-start.10) | collective-permute-done | bytes 65568 | tf_op jit(solution)/shard_map/ppermute | solution.py:54
  27.7 1.7 %collective-permute-done.11.refs_1_ = bf16[256,128]{1,0:T(8,128)(2,1)S(1)} collective-permute-done((bf16[256,128]{1,0:T(8,128)(2,1)S(1)}, bf16[256,128]{1,0:T(8,128)(2,1)S(1)}, u32[]{:S(2)}, u32[]{:S(2)}) %collective-permute-start.11) | collective-permute-done | bytes 65568 | tf_op jit(solution)/shard_map/ppermute | solution.py:54
  29.9 6.0 %shard_map.112 = (bf16[256,512]{1,0:T(8,128)(2,1)}, bf16[256,2048]{1,0:T(8,128)(2,1)S(1)}, f32[256,512]{1,0:T(8,128)S(1)}, f32[256,128]{1,0:T(8,128)S(1)}, bf16[...) custom-call(s32[4,128]{1,0:T(4,128)S(1)} %pad_add_fusion.refs_0_.scalar_ref, ...), custom_call_target="tpu_custom_call" | custom-call | bytes 24500000 | tf_op jit(solution)/shard_map/pallas_call | solution.py:465
  35.9 1.6 %shard_map.113 = (bf16[256,128]{1,0:T(8,128)(2,1)S(1)}, bf16[256,128]{1,0:T(8,128)(2,1)S(1)}, bf16[256,128]{1,0:T(8,128)(2,1)S(1)}, bf16[256,128]{1,0:T(8,128)(2,1)S(1)}) custom-call(s32[4,128]{1,0:T(4,128)S(1)} %pad_add_fusion.refs_0_.scalar_ref, bf16[256,2048]{1,0:T(8,128)(2,1)S(1)} %get-tuple-element.47.refs_0_, ...), custom_call_target="tpu_custom_call" | custom-call | bytes 7000000 | tf_op jit(solution)/shard_map/pallas_call | solution.py:489
  42.8 9.4 %collective-permute-done.15.refs_3_ = bf16[64,3072]{1,0:T(8,128)(2,1)S(1)} collective-permute-done((bf16[64,3072]{1,0:T(8,128)(2,1)S(1)}, bf16[64,3072]{1,0:T(8,128)(2,1)S(1)}, u32[]{:S(2)}, u32[]{:S(2)}) %collective-permute-start.15) | collective-permute-done | bytes 393248 | tf_op jit(solution)/shard_map/ppermute | solution.py:54
  52.2 7.6 %collective-permute-done.16.refs_4_ = bf16[64,3072]{1,0:T(8,128)(2,1)S(1)} collective-permute-done((bf16[64,3072]{1,0:T(8,128)(2,1)S(1)}, bf16[64,3072]{1,0:T(8,128)(2,1)S(1)}, u32[]{:S(2)}, u32[]{:S(2)}) %collective-permute-start.16) | collective-permute-done | bytes 393248 | tf_op jit(solution)/shard_map/ppermute | solution.py:54
  60.1 3.7 %collective-permute-start.19 = (bf16[16,2560]{1,0:T(8,128)(2,1)S(1)}, bf16[16,2560]{1,0:T(8,128)(2,1)S(1)}, u32[]{:S(2)}, u32[]{:S(2)}) collective-permute-start(bf16[16,2560]{1,0:T(8,128)(2,1)S(1)} %get-tuple-element.71), channel_id=1, source_target_pairs={{0,24},{2,26},{4,28},{6,30},{8,16},{10,18},{12,20},{14,22},{16,8},... | collective-permute-start | bytes 245768 | tf_op jit(solution)/shard_map/ppermute | solution.py:54
  64.6 2.9 %shard_map.115 = (bf16[4,512,128]{2,1,0:T(8,128)(2,1)S(1)}, bf16[4,512,128]{2,1,0:T(8,128)(2,1)S(1)}) custom-call(s32[4,128]{1,0:T(4,128)S(1)} %pad_add_fusion.refs_0_.scalar_ref, s32[4,8,1,128]{3,2,1,0:T(1,128)S(1)} %reshape.61.refs_1_, s32[4,8,1,128]{3,2,1,0:T(1,128)S(1)} %collective-permute-done.2.refs_2_, ...), custom_call_target="tpu_custom_call" | custom-call | bytes 10500000 | tf_op jit(solution)/shard_map/pallas_call | solution.py:509
  67.6 3.0 %collective-permute-done.21 = bf16[16,2560]{1,0:T(8,128)(2,1)S(1)} collective-permute-done((bf16[16,2560]{1,0:T(8,128)(2,1)S(1)}, bf16[16,2560]{1,0:T(8,128)(2,1)S(1)}, u32[]{:S(2)}, u32[]{:S(2)}) %collective-permute-start.21) | collective-permute-done | bytes 81952 | tf_op jit(solution)/shard_map/ppermute | solution.py:54
  70.6 2.4 %collective-permute-start.24 = (bf16[16,2560]{1,0:T(8,128)(2,1)S(1)}, bf16[16,2560]{1,0:T(8,128)(2,1)S(1)}, u32[]{:S(2)}, u32[]{:S(2)}) collective-permute-start(bf16[16,2560]{1,0:T(8,128)(2,1)S(1)} %add_convert_fusion.2), channel_id=1, source_target_pairs={{0,24},{2,26},{4,28},{6,30},{8,16},{10,18},{12,20},{14,22},{16,8},... | collective-permute-start | bytes 245768 | tf_op jit(solution)/shard_map/ppermute | solution.py:54
  73.2 1.9 %collective-permute-start.22 = (bf16[16,2560]{1,0:T(8,128)(2,1)S(1)}, bf16[16,2560]{1,0:T(8,128)(2,1)S(1)}, u32[]{:S(2)}, u32[]{:S(2)}) collective-permute-start(bf16[16,2560]{1,0:T(8,128)(2,1)S(1)} %add_convert_fusion.2), channel_id=1, source_target_pairs={{0,8},{2,10},{4,12},{6,14},{8,0},{10,2},{12,4},{14,6},{16,24},{18,... | collective-permute-start | bytes 245768 | tf_op jit(solution)/shard_map/ppermute | solution.py:54
  75.1 2.7 %collective-permute-done.24 = bf16[16,2560]{1,0:T(8,128)(2,1)S(1)} collective-permute-done((bf16[16,2560]{1,0:T(8,128)(2,1)S(1)}, bf16[16,2560]{1,0:T(8,128)(2,1)S(1)}, u32[]{:S(2)}, u32[]{:S(2)}) %collective-permute-start.24) | collective-permute-done | bytes 81952 | tf_op jit(solution)/shard_map/ppermute | solution.py:54
  77.8 2.9 %collective-permute-done.23 = bf16[16,2560]{1,0:T(8,128)(2,1)S(1)} collective-permute-done((bf16[16,2560]{1,0:T(8,128)(2,1)S(1)}, bf16[16,2560]{1,0:T(8,128)(2,1)S(1)}, u32[]{:S(2)}, u32[]{:S(2)}) %collective-permute-start.23) | collective-permute-done | bytes 81952 | tf_op jit(solution)/shard_map/ppermute | solution.py:54
  84.5 1.7 %collective-permute-start.25 = (bf16[512,128]{1,0:T(8,128)(2,1)S(1)}, bf16[512,128]{1,0:T(8,128)(2,1)S(1)}, u32[]{:S(2)}, u32[]{:S(2)}) collective-permute-start(bf16[512,128]{1,0:T(8,128)(2,1)S(1)} %get-tuple-element.68), channel_id=1, source_target_pairs={{0,24},{2,26},{4,28},{6,30},{8,16},{10,18},{12,20},{14,22},{16,8},... | collective-permute-start | bytes 393224 | tf_op jit(solution)/shard_map/ppermute | solution.py:54
  86.2 6.2 %collective-permute-done.28.refs_1_ = bf16[64,2560]{1,0:T(8,128)(2,1)S(1)} collective-permute-done((bf16[64,2560]{1,0:T(8,128)(2,1)S(1)}, bf16[64,2560]{1,0:T(8,128)(2,1)S(1)}, u32[]{:S(2)}, u32[]{:S(2)}) %collective-permute-start.28) | collective-permute-done | bytes 327712 | tf_op jit(solution)/shard_map/ppermute | solution.py:54
  92.4 1.8 %shard_map.116 = (f32[256,2048]{1,0:T(8,128)}, f32[256,512]{1,0:T(8,128)}) custom-call(s32[4,128]{1,0:T(4,128)S(1)} %pad_add_fusion.refs_0_.scalar_ref, bf16[64,2560]{1,0:T(8,128)(2,1)S(1)} %pad_maximum_fusion.1.refs_0_, bf16[64,2560]{1,0:T(8,128)(2,1)S(1)} %collective-permute-done.28.refs_1_), custom_call_target="tpu_custom_call" | custom-call | bytes 3500000 | tf_op jit(solution)/shard_map/pallas_call | solution.py:556
  94.2 3.5 %collective-permute-done.27.refs_1_ = bf16[64,2560]{1,0:T(8,128)(2,1)S(1)} collective-permute-done((bf16[64,2560]{1,0:T(8,128)(2,1)S(1)}, bf16[64,2560]{1,0:T(8,128)(2,1)S(1)}, u32[]{:S(2)}, u32[]{:S(2)}) %collective-permute-start.27) | collective-permute-done | bytes 327712 | tf_op jit(solution)/shard_map/ppermute | solution.py:54
  97.6 1.8 %shard_map.117 = (f32[256,2048]{1,0:T(8,128)}, f32[256,512]{1,0:T(8,128)}) custom-call(s32[4,128]{1,0:T(4,128)S(1)} %pad_add_fusion.refs_0_.scalar_ref, bf16[64,2560]{1,0:T(8,128)(2,1)S(1)} %collective-permute-done.26.refs_0_, bf16[64,2560]{1,0:T(8,128)(2,1)S(1)} %collective-permute-done.27.refs_1_, ...), custom_call_target="tpu_custom_call", output_to_operand_aliasing={{0}: (3, {}), {1}: (4, {})} | custom-call | bytes 3500000 | tf_op jit(solution)/shard_map/pallas_call | solution.py:556
  (65 shorter events, 21.0 us)
Async XLA Ops:
  1.6 15.9 %collective-permute-start.8 = (bf16[512,128]{1,0:T(8,128)(2,1)S(1)}, bf16[512,128]{1,0:T(8,128)(2,1)S(1)}, u32[]{:S(2)}, u32[]{:S(2)}) collective-permute-start(bf16[512,128]{1,0:T(8,128)(2,1)S(1)} %dynamic-slice_bitcast_fusion.refs_3_), channel_id=1, source_target_pairs={{0,24},{2,26},{4,28},{6,30},{8,16},{10,18},{12,20},{14,22},{16,8},... | collective-permute-start | bytes 393224 | tf_op jit(solution)/shard_map/ppermute | solution.py:54
  6.7 11.1 %collective-permute-start.6 = (bf16[512,128]{1,0:T(8,128)(2,1)S(1)}, bf16[512,128]{1,0:T(8,128)(2,1)S(1)}, u32[]{:S(2)}, u32[]{:S(2)}) collective-permute-start(bf16[512,128]{1,0:T(8,128)(2,1)S(1)} %dynamic-slice_bitcast_fusion.refs_3_), channel_id=1, source_target_pairs={{0,16},{2,18},{4,20},{6,22},{8,24},{10,26},{12,28},{14,30},{16,0},... | collective-permute-start | bytes 393224 | tf_op jit(solution)/shard_map/ppermute | solution.py:54
  6.7 10.2 %collective-permute-start.4 = (bf16[512,128]{1,0:T(8,128)(2,1)S(1)}, bf16[512,128]{1,0:T(8,128)(2,1)S(1)}, u32[]{:S(2)}, u32[]{:S(2)}) collective-permute-start(bf16[512,128]{1,0:T(8,128)(2,1)S(1)} %dynamic-slice_bitcast_fusion.refs_3_), channel_id=1, source_target_pairs={{0,8},{2,10},{4,12},{6,14},{8,0},{10,2},{12,4},{14,6},{16,24},{18,... | collective-permute-start | bytes 393224 | tf_op jit(solution)/shard_map/ppermute | solution.py:54
  11.4 7.7 %collective-permute-start.3 = (bf16[512,128]{1,0:T(8,128)(2,1)S(1)}, bf16[512,128]{1,0:T(8,128)(2,1)S(1)}, u32[]{:S(2)}, u32[]{:S(2)}) collective-permute-start(bf16[512,128]{1,0:T(8,128)(2,1)S(1)} %dynamic-slice_bitcast_fusion.refs_3_), channel_id=1, source_target_pairs={{0,1},{1,0},{2,3},{3,2},{4,5},{5,4},{6,7},{7,6},{8,9},{9,8},{10,11... | collective-permute-start | bytes 393224 | tf_op jit(solution)/shard_map/ppermute | solution.py:46
  22.2 7.7 %collective-permute-start.13 = (bf16[256,2560]{1,0:T(8,128)(2,1)S(1)}, bf16[256,2560]{1,0:T(8,128)(2,1)S(1)}, u32[]{:S(2)}, u32[]{:S(2)}) collective-permute-start(bf16[256,2560]{1,0:T(8,128)(2,1)S(1)} %pad_maximum_fusion.refs_4_), channel_id=1, source_target_pairs={{0,1},{1,0},{2,3},{3,2},{4,5},{5,4},{6,7},{7,6},{8,9},{9,8},{10,11... | collective-permute-start | bytes 3932168 | tf_op jit(solution)/shard_map/ppermute | solution.py:46
  22.5 5.2 %collective-permute-start.10 = (bf16[256,128]{1,0:T(8,128)(2,1)S(1)}, bf16[256,128]{1,0:T(8,128)(2,1)S(1)}, u32[]{:S(2)}, u32[]{:S(2)}) collective-permute-start(bf16[256,128]{1,0:T(8,128)(2,1)S(1)} %get-tuple-element.39), channel_id=1, source_target_pairs={{0,6},{2,4},{4,2},{6,0},{8,14},{10,12},{12,10},{14,8},{16,22},{18,... | collective-permute-start | bytes 196616 | tf_op jit(solution)/shard_map/ppermute | solution.py:54
  25.1 4.3 %collective-permute-start.11 = (bf16[256,128]{1,0:T(8,128)(2,1)S(1)}, bf16[256,128]{1,0:T(8,128)(2,1)S(1)}, u32[]{:S(2)}, u32[]{:S(2)}) collective-permute-start(bf16[256,128]{1,0:T(8,128)(2,1)S(1)} %get-tuple-element.40), channel_id=1, source_target_pairs={{0,4},{2,6},{4,0},{6,2},{8,12},{10,14},{12,8},{14,10},{16,20},{18,... | collective-permute-start | bytes 196616 | tf_op jit(solution)/shard_map/ppermute | solution.py:54
  25.6 4.3 %collective-permute-start.12 = (bf16[256,128]{1,0:T(8,128)(2,1)S(1)}, bf16[256,128]{1,0:T(8,128)(2,1)S(1)}, u32[]{:S(2)}, u32[]{:S(2)}) collective-permute-start(bf16[256,128]{1,0:T(8,128)(2,1)S(1)} %get-tuple-element.41), channel_id=1, source_target_pairs={{0,2},{2,0},{4,6},{6,4},{8,10},{10,8},{12,14},{14,12},{16,18},{18,... | collective-permute-start | bytes 196616 | tf_op jit(solution)/shard_map/ppermute | solution.py:54
  39.3 13.0 %collective-permute-start.15 = (bf16[64,3072]{1,0:T(8,128)(2,1)S(1)}, bf16[64,3072]{1,0:T(8,128)(2,1)S(1)}, u32[]{:S(2)}, u32[]{:S(2)}) collective-permute-start(bf16[64,3072]{1,0:T(8,128)(2,1)S(1)} %get-tuple-element.53), channel_id=1, source_target_pairs={{0,6},{2,4},{4,2},{6,0},{8,14},{10,12},{12,10},{14,8},{16,22},{18,... | collective-permute-start | bytes 1179656 | tf_op jit(solution)/shard_map/ppermute | solution.py:54
  40.8 19.0 %collective-permute-start.16 = (bf16[64,3072]{1,0:T(8,128)(2,1)S(1)}, bf16[64,3072]{1,0:T(8,128)(2,1)S(1)}, u32[]{:S(2)}, u32[]{:S(2)}) collective-permute-start(bf16[64,3072]{1,0:T(8,128)(2,1)S(1)} %get-tuple-element.54), channel_id=1, source_target_pairs={{0,4},{2,6},{4,0},{6,2},{8,12},{10,14},{12,8},{14,10},{16,20},{18,... | collective-permute-start | bytes 1179656 | tf_op jit(solution)/shard_map/ppermute | solution.py:54
  41.7 18.2 %collective-permute-start.17 = (bf16[64,3072]{1,0:T(8,128)(2,1)S(1)}, bf16[64,3072]{1,0:T(8,128)(2,1)S(1)}, u32[]{:S(2)}, u32[]{:S(2)}) collective-permute-start(bf16[64,3072]{1,0:T(8,128)(2,1)S(1)} %get-tuple-element.55), channel_id=1, source_target_pairs={{0,2},{2,0},{4,6},{6,4},{8,10},{10,8},{12,14},{14,12},{16,18},{18,... | collective-permute-start | bytes 1179656 | tf_op jit(solution)/shard_map/ppermute | solution.py:54
  60.1 7.4 %collective-permute-start.19 = (bf16[16,2560]{1,0:T(8,128)(2,1)S(1)}, bf16[16,2560]{1,0:T(8,128)(2,1)S(1)}, u32[]{:S(2)}, u32[]{:S(2)}) collective-permute-start(bf16[16,2560]{1,0:T(8,128)(2,1)S(1)} %get-tuple-element.71), channel_id=1, source_target_pairs={{0,24},{2,26},{4,28},{6,30},{8,16},{10,18},{12,20},{14,22},{16,8},... | collective-permute-start | bytes 245768 | tf_op jit(solution)/shard_map/ppermute | solution.py:54
  63.8 6.8 %collective-permute-start.21 = (bf16[16,2560]{1,0:T(8,128)(2,1)S(1)}, bf16[16,2560]{1,0:T(8,128)(2,1)S(1)}, u32[]{:S(2)}, u32[]{:S(2)}) collective-permute-start(bf16[16,2560]{1,0:T(8,128)(2,1)S(1)} %get-tuple-element.72), channel_id=1, source_target_pairs={{0,16},{2,18},{4,20},{6,22},{8,24},{10,26},{12,28},{14,30},{16,0},... | collective-permute-start | bytes 245768 | tf_op jit(solution)/shard_map/ppermute | solution.py:54
  63.8 6.8 %collective-permute-start.20 = (bf16[16,2560]{1,0:T(8,128)(2,1)S(1)}, bf16[16,2560]{1,0:T(8,128)(2,1)S(1)}, u32[]{:S(2)}, u32[]{:S(2)}) collective-permute-start(bf16[16,2560]{1,0:T(8,128)(2,1)S(1)} %get-tuple-element.73), channel_id=1, source_target_pairs={{0,8},{2,10},{4,12},{6,14},{8,0},{10,2},{12,4},{14,6},{16,24},{18,... | collective-permute-start | bytes 245768 | tf_op jit(solution)/shard_map/ppermute | solution.py:54
  67.5 16.8 %collective-permute-start.18 = (bf16[4,512,128]{2,1,0:T(8,128)(2,1)S(1)}, bf16[4,512,128]{2,1,0:T(8,128)(2,1)S(1)}, u32[]{:S(2)}, u32[]{:S(2)}) collective-permute-start(bf16[4,512,128]{2,1,0:T(8,128)(2,1)S(1)} %get-tuple-element.58), channel_id=1, source_target_pairs={{0,1},{1,0},{2,3},{3,2},{4,5},{5,4},{6,7},{7,6},{8,9},{9,8},{10,11... | collective-permute-start | bytes 1572872 | tf_op jit(solution)/shard_map/ppermute | solution.py:46
  70.6 7.2 %collective-permute-start.24 = (bf16[16,2560]{1,0:T(8,128)(2,1)S(1)}, bf16[16,2560]{1,0:T(8,128)(2,1)S(1)}, u32[]{:S(2)}, u32[]{:S(2)}) collective-permute-start(bf16[16,2560]{1,0:T(8,128)(2,1)S(1)} %add_convert_fusion.2), channel_id=1, source_target_pairs={{0,24},{2,26},{4,28},{6,30},{8,16},{10,18},{12,20},{14,22},{16,8},... | collective-permute-start | bytes 245768 | tf_op jit(solution)/shard_map/ppermute | solution.py:54
  73.0 7.7 %collective-permute-start.23 = (bf16[16,2560]{1,0:T(8,128)(2,1)S(1)}, bf16[16,2560]{1,0:T(8,128)(2,1)S(1)}, u32[]{:S(2)}, u32[]{:S(2)}) collective-permute-start(bf16[16,2560]{1,0:T(8,128)(2,1)S(1)} %add_convert_fusion.2), channel_id=1, source_target_pairs={{0,16},{2,18},{4,20},{6,22},{8,24},{10,26},{12,28},{14,30},{16,0},... | collective-permute-start | bytes 245768 | tf_op jit(solution)/shard_map/ppermute | solution.py:54
  73.2 7.5 %collective-permute-start.22 = (bf16[16,2560]{1,0:T(8,128)(2,1)S(1)}, bf16[16,2560]{1,0:T(8,128)(2,1)S(1)}, u32[]{:S(2)}, u32[]{:S(2)}) collective-permute-start(bf16[16,2560]{1,0:T(8,128)(2,1)S(1)} %add_convert_fusion.2), channel_id=1, source_target_pairs={{0,8},{2,10},{4,12},{6,14},{8,0},{10,2},{12,4},{14,6},{16,24},{18,... | collective-permute-start | bytes 245768 | tf_op jit(solution)/shard_map/ppermute | solution.py:54
  80.7 11.7 %collective-permute-start.28 = (bf16[64,2560]{1,0:T(8,128)(2,1)S(1)}, bf16[64,2560]{1,0:T(8,128)(2,1)S(1)}, u32[]{:S(2)}, u32[]{:S(2)}) collective-permute-start(bf16[64,2560]{1,0:T(8,128)(2,1)S(1)} %pad_maximum_fusion.1.refs_0_), channel_id=1, source_target_pairs={{0,6},{2,4},{4,2},{6,0},{8,14},{10,12},{12,10},{14,8},{16,22},{18,... | collective-permute-start | bytes 983048 | tf_op jit(solution)/shard_map/ppermute | solution.py:54
  82.3 15.3 %collective-permute-start.27 = (bf16[64,2560]{1,0:T(8,128)(2,1)S(1)}, bf16[64,2560]{1,0:T(8,128)(2,1)S(1)}, u32[]{:S(2)}, u32[]{:S(2)}) collective-permute-start(bf16[64,2560]{1,0:T(8,128)(2,1)S(1)} %pad_maximum_fusion.1.refs_0_), channel_id=1, source_target_pairs={{0,4},{2,6},{4,0},{6,2},{8,12},{10,14},{12,8},{14,10},{16,20},{18,... | collective-permute-start | bytes 983048 | tf_op jit(solution)/shard_map/ppermute | solution.py:54
  83.2 14.5 %collective-permute-start.26 = (bf16[64,2560]{1,0:T(8,128)(2,1)S(1)}, bf16[64,2560]{1,0:T(8,128)(2,1)S(1)}, u32[]{:S(2)}, u32[]{:S(2)}) collective-permute-start(bf16[64,2560]{1,0:T(8,128)(2,1)S(1)} %pad_maximum_fusion.1.refs_0_), channel_id=1, source_target_pairs={{0,2},{2,0},{4,6},{6,4},{8,10},{10,8},{12,14},{14,12},{16,18},{18,... | collective-permute-start | bytes 983048 | tf_op jit(solution)/shard_map/ppermute | solution.py:54
  84.5 14.9 %collective-permute-start.25 = (bf16[512,128]{1,0:T(8,128)(2,1)S(1)}, bf16[512,128]{1,0:T(8,128)(2,1)S(1)}, u32[]{:S(2)}, u32[]{:S(2)}) collective-permute-start(bf16[512,128]{1,0:T(8,128)(2,1)S(1)} %get-tuple-element.68), channel_id=1, source_target_pairs={{0,24},{2,26},{4,28},{6,30},{8,16},{10,18},{12,20},{14,22},{16,8},... | collective-permute-start | bytes 393224 | tf_op jit(solution)/shard_map/ppermute | solution.py:54
  86.2 13.2 %collective-permute-start.30 = (bf16[512,128]{1,0:T(8,128)(2,1)S(1)}, bf16[512,128]{1,0:T(8,128)(2,1)S(1)}, u32[]{:S(2)}, u32[]{:S(2)}) collective-permute-start(bf16[512,128]{1,0:T(8,128)(2,1)S(1)} %get-tuple-element.69), channel_id=1, source_target_pairs={{0,16},{2,18},{4,20},{6,22},{8,24},{10,26},{12,28},{14,30},{16,0},... | collective-permute-start | bytes 393224 | tf_op jit(solution)/shard_map/ppermute | solution.py:54
  92.4 7.0 %collective-permute-start.29 = (bf16[512,128]{1,0:T(8,128)(2,1)S(1)}, bf16[512,128]{1,0:T(8,128)(2,1)S(1)}, u32[]{:S(2)}, u32[]{:S(2)}) collective-permute-start(bf16[512,128]{1,0:T(8,128)(2,1)S(1)} %get-tuple-element.70), channel_id=1, source_target_pairs={{0,8},{2,10},{4,12},{6,14},{8,0},{10,2},{12,4},{14,6},{16,24},{18,... | collective-permute-start | bytes 393224 | tf_op jit(solution)/shard_map/ppermute | solution.py:54
  (9 other events, 35.8 us)

commit v13 on v12

--- a/solution.py
+++ b/solution.py
@@ -10,6 +10,8 @@
 HEADS = 8
 EPS = 1e-05
 LANES = 128
+BLOCK_ROWS = 64
+BLOCK_COLUMNS = 256
 
 VMEM = pl.BlockSpec(memory_space=pltpu.VMEM)
 SMEM = pl.BlockSpec(memory_space=pltpu.SMEM)
@@ -198,7 +200,7 @@
     (layer_ref,) = take(1)
     grads_ref, normed_ref, inverse_ref = take(3)
     term_refs = take(bals)
-    (x_ref, halves_ref, wide_ref, nt_ref, mt_ref, weights_ref, slope_ref, gate_ref, heads_ref, dsilu_ref) = refs
+    (x_ref, halves_ref, wide_ref, nt_ref, mt_ref, weights_ref, slope_ref, gate_ref, heads_ref, dsilu_ref, out_ref, mixed_ref, back_ref) = refs
 
     scalars = Scalars(scalar_ref, 0, bals, slots)
     bal, group_here, table_here = scalars.place()
@@ -209,9 +211,13 @@
     piece = block_refs[0].shape[1]
     part, features = weight_refs[0].shape[0], weight_refs[0].shape[1] - width
 
-    def times_parts(value, first, last):
+    blocks = [slice(at, at + BLOCK_ROWS) for at in range(0, rows, BLOCK_ROWS)]
+
+    def keep_parts(here, value):
         for index in range(bals):
-            halves_ref[index] = value[:, index * part : (index + 1) * part]
+            halves_ref[index, here, :] = value[:, index * part : (index + 1) * part].astype(bf16)
+
+    def times_parts(first, last):
         found = matmul(halves_ref[bal], weight_refs[0][:, first:last])
         for turn in range(1, bals):
             found = found + matmul(halves_ref[bal ^ turn], weight_refs[turn][:, first:last])
@@ -224,17 +230,29 @@
 
     for step in range(groups):
         x_ref[group_here ^ step] = block_refs[step][...]
-    x = jnp.concatenate([x_ref[group] for group in range(groups)], axis=1).astype(f32)
-    normed_in, in_inverse = norm(x)
-    normed_ref[...] = normed_in
-    inverse_ref[...] = jnp.broadcast_to(in_inverse, inverse_ref.shape)
-    nt_ref[...] = jnp.transpose(normed_in).astype(bf16)
-    projected = times_parts(normed_in.astype(bf16), 0, features)
-    logistic = sigmoid(projected)
-    active = projected * logistic
-    dsilu_ref[...] = logistic + active * (1.0 - logistic)
-    gate_ref[...] = active[:, :width]
-    heads_ref[...] = active[:, width:].astype(bf16)
+
+    def x_rows(here):
+        return jnp.concatenate([x_ref[group, here, :] for group in range(groups)], axis=1).astype(f32)
+
+    for here in blocks:
+        normed, inverse = norm(x_rows(here))
+        normed_ref[here, :] = normed
+        inverse_ref[here, :] = jnp.broadcast_to(inverse, (BLOCK_ROWS, inverse_ref.shape[1]))
+        keep_parts(here, normed)
+    for at in range(0, features, width):
+        dsilu_ref[:, at : at + width] = times_parts(at, at + width)
+        for here in blocks:
+            for first in range(at, at + width, BLOCK_COLUMNS):
+                columns = slice(first, first + BLOCK_COLUMNS)
+                projected = dsilu_ref[here, columns]
+                logistic = sigmoid(projected)
+                active = projected * logistic
+                dsilu_ref[here, columns] = logistic + active * (1.0 - logistic)
+                if at < width:
+                    gate_ref[here, columns] = active
+                else:
+                    heads_ref[here, first - width : first - width + BLOCK_COLUMNS] = active.astype(bf16)
+    nt_ref[...] = jnp.transpose(normed_ref[...]).astype(bf16)
 
     pair_width = 2 * head_width
     low = lax.broadcasted_iota(jnp.int32, (slot_rows, pair_width), 1) < head_width
@@ -253,33 +271,39 @@
         return heads_ref[slot * slot_rows : (slot + 1) * slot_rows, first : first + pair_width]
 
     pairs = HEADS // 2
-    attended = []
     for slot in range(slots):
         live = (col_at <= row_at) & (row_at < lengths[slot])
         allowed = jnp.where(live, 1.0 / slot_rows, 0.0)
-        allowed = jnp.concatenate([allowed, allowed], axis=0)
-        across = []
+        slot_here = slice(slot * slot_rows, (slot + 1) * slot_rows)
         for pair in range(pairs):
             value, query, key = (part_of(slot, pair, which) for which in range(3))
             scores = matmul_nt(split(query), key) * score_scale
-            q = sigmoid(scores)
-            sq = scores * q
-            weights = (sq * allowed).astype(bf16)
-            weights_ref[slot * pairs + pair] = weights
-            slope_ref[slot * pairs + pair] = allowed * (q + sq * (1.0 - q))
-            across.append(matmul(side_by_side(weights), split(value)))
-        attended.append(jnp.concatenate(across, axis=1))
-    normed_out, out_inverse = norm(jnp.concatenate(attended, axis=0))
-    gate = gate_ref[...]
-    mixed = normed_out * gate
-    mt_ref[...] = jnp.transpose(mixed).astype(bf16)
-    layer_ref[...] = (x + times_parts(mixed.astype(bf16), features, features + width)).astype(bf16)
-
-    wide_cot = cot_ref[...]
-    cot = wide_cot.astype(bf16)
-    grad_mixed = times_parts_nt(cot, weight_refs, features, features + width, bal, wide_ref)
-    grad_attended = norm_back(grad_mixed * gate, normed_out, out_inverse).astype(bf16)
-    grads_ref[:, :width] = (grad_mixed * normed_out * dsilu_ref[:, :width]).astype(bf16)
+            both = []
+            for head in range(2):
+                half = slice(head * slot_rows, (head + 1) * slot_rows)
+                q = sigmoid(scores[half])
+                sq = scores[half] * q
+                both.append((sq * allowed).astype(bf16))
+                weights_ref[slot * pairs + pair, half, :] = both[-1]
+                slope_ref[slot * pairs + pair, half, :] = allowed * (q + sq * (1.0 - q))
+            lanes = slice(pair * pair_width, (pair + 1) * pair_width)
+            out_ref[slot_here, lanes] = matmul(jnp.concatenate(both, axis=1), split(value))
+
+    cot = cot_ref[...].astype(bf16)
+    mixed_ref[...] = times_parts_nt(cot, weight_refs, features, features + width, bal, wide_ref)
+    for here in blocks:
+        normed, inverse = norm(out_ref[here, :])
+        gate = gate_ref[here, :]
+        grad_mixed = mixed_ref[here, :]
+        back_ref[here, :] = norm_back(grad_mixed * gate, normed, inverse).astype(bf16)
+        grads_ref[here, :width] = (grad_mixed * normed * dsilu_ref[here, :width]).astype(bf16)
+        mixed = normed * gate
+        mixed_ref[here, :] = mixed
+        keep_parts(here, mixed)
+    mt_ref[...] = jnp.transpose(mixed_ref[...]).astype(bf16)
+    mixed_ref[...] = times_parts(features, features + width)
+    for here in blocks:
+        layer_ref[here, :] = (x_rows(here) + mixed_ref[here, :]).astype(bf16)
 
     def owner_order(ref, turn):
         start = (bal ^ turn) * part
@@ -307,7 +331,7 @@
         for pair in range(pairs):
             value, query, key = (part_of(slot, pair, which) for which in range(3))
             lanes = slice(pair * pair_width, (pair + 1) * pair_width)
-            upper = split(grad_attended[here, lanes])
+            upper = split(back_ref[here, lanes])
             grad_weights = matmul_nt(upper, value)
             grad_scores = (grad_weights * slope_ref[slot * pairs + pair]).astype(bf16)
             grad_value = matmul_tn(weights_ref[slot * pairs + pair], upper)
@@ -481,6 +505,9 @@
             pltpu.VMEM((rows, width), f32),
             pltpu.VMEM((rows, features - width), bf16),
             pltpu.VMEM((rows, features), f32),
+            pltpu.VMEM((rows, width), f32),
+            pltpu.VMEM((rows, width), f32),
+            pltpu.VMEM((rows, width), bf16),
         ],
         cost_estimate=estimate(7),
         compiler_params=room(36),

time: 100 us -> 100 us (level)
  no operation moved by 1% of the time
where the time goes in v13:
time: 100 us; the launch traced here: 99.8 us
  waiting for transfers between devices  44 us (44%)
  starting transfers between devices  31.6 us (32%)
  Pallas kernels  17 us (17%)
  other arithmetic  3.96 us (4%)
  local copies, waits for them, and re-layouts  2.42 us (2%)
    ppermute x23, waiting for transfers between devices, emb_swap(): return lax.ppermute(value, 'emb', [(i, i ^ step) for i in range(count)])  42.5 us
    ppermute x23, starting transfers between devices, emb_swap(): return lax.ppermute(value, 'emb', [(i, i ^ step) for i in range(count)])  30.3 us
    pallas_call x1, Pallas kernels, on_device(): pl.pallas_call(functools.partial(layer_kernel, groups, slots, tables, bal...  5.6 us
    pallas_call x2, Pallas kernels, on_device(): pl.pallas_call(functools.partial(place_kernel, grad_scale, steps, slots,...  3.5 us
    pallas_call x1, Pallas kernels, on_device(): pl.pallas_call(functools.partial(lookup_kernel, groups, slots, tables, ba...  3.08 us
    pallas_call x1, Pallas kernels, table_sums(): pl.pallas_call(functools.partial(scatter_kernel, groups, slots, bals), ou...  2.9 us
  transfers between devices with their start and end apart: 31, of which 15 were waited for; matrix products, arithmetic and copies ran while one was open for 4% of the time, Pallas kernels for 8%

profile of v13, /device:TPU:0, one launch (start us, length us, event | category | flops | bytes accessed | tf_op | source)
XLA Modules:
  0.0 99.8 jit_solution(13471851734583326519)
XLA Ops:
  1.6 5.1 %collective-permute-start.8 = (bf16[512,128]{1,0:T(8,128)(2,1)S(1)}, bf16[512,128]{1,0:T(8,128)(2,1)S(1)}, u32[]{:S(2)}, u32[]{:S(2)}) collective-permute-start(bf16[512,128]{1,0:T(8,128)(2,1)S(1)} %dynamic-slice_bitcast_fusion.refs_3_), channel_id=1, source_target_pairs={{0,24},{2,26},{4,28},{6,30},{8,16},{10,18},{12,20},{14,22},{16,8},... | collective-permute-start | bytes 393224 | tf_op jit(solution)/shard_map/ppermute | solution.py:56
  9.8 1.6 %collective-permute-start = (s32[1,128]{1,0:T(1,128)S(1)}, s32[1,128]{1,0:T(1,128)S(1)}, u32[]{:S(2)}, u32[]{:S(2)}) collective-permute-start(s32[1,128]{1,0:T(1,128)S(1)} %pad_add_fusion.2), channel_id=1, source_target_pairs={{0,2},{2,0},{4,6},{6,4},{8,10},{10,8},{12,14},{14,12},{16,18},{18,... | collective-permute-start | bytes 1544 | tf_op jit(solution)/shard_map/ppermute | solution.py:56
  11.4 1.9 %collective-permute-done = s32[1,128]{1,0:T(1,128)S(1)} collective-permute-done((s32[1,128]{1,0:T(1,128)S(1)}, s32[1,128]{1,0:T(1,128)S(1)}, u32[]{:S(2)}, u32[]{:S(2)}) %collective-permute-start) | collective-permute-done | bytes 544 | tf_op jit(solution)/shard_map/ppermute | solution.py:56
  13.4 1.7 %collective-permute-start.1 = (s32[2,128]{1,0:T(2,128)S(1)}, s32[2,128]{1,0:T(2,128)S(1)}, u32[]{:S(2)}, u32[]{:S(2)}) collective-permute-start(s32[2,128]{1,0:T(2,128)S(1)} %pad_add_fusion.1), channel_id=1, source_target_pairs={{0,4},{2,6},{4,0},{6,2},{8,12},{10,14},{12,8},{14,10},{16,20},{18,... | collective-permute-start | bytes 3080 | tf_op jit(solution)/shard_map/ppermute | solution.py:56
  19.1 3.1 %shard_map.111 = (bf16[256,128]{1,0:T(8,128)(2,1)S(1)}, bf16[256,128]{1,0:T(8,128)(2,1)S(1)}, bf16[256,128]{1,0:T(8,128)(2,1)S(1)}, bf16[256,128]{1,0:T(8,128)(2,1)S(1)}) custom-call(s32[4,128]{1,0:T(4,128)S(1)} %pad_add_fusion.refs_0_.scalar_ref, s32[4,8,1,128]{3,2,1,0:T(1,128)S(1)} %reshape.61.refs_1_, ...), custom_call_target="tpu_custom_call" | custom-call | bytes 10500000 | tf_op jit(solution)/shard_map/pallas_call | solution.py:475
  22.5 2.6 %collective-permute-start.10 = (bf16[256,128]{1,0:T(8,128)(2,1)S(1)}, bf16[256,128]{1,0:T(8,128)(2,1)S(1)}, u32[]{:S(2)}, u32[]{:S(2)}) collective-permute-start(bf16[256,128]{1,0:T(8,128)(2,1)S(1)} %get-tuple-element.39), channel_id=1, source_target_pairs={{0,6},{2,4},{4,2},{6,0},{8,14},{10,12},{12,10},{14,8},{16,22},{18,... | collective-permute-start | bytes 196616 | tf_op jit(solution)/shard_map/ppermute | solution.py:56
  26.0 1.7 %collective-permute-done.10.refs_0_ = bf16[256,128]{1,0:T(8,128)(2,1)S(1)} collective-permute-done((bf16[256,128]{1,0:T(8,128)(2,1)S(1)}, bf16[256,128]{1,0:T(8,128)(2,1)S(1)}, u32[]{:S(2)}, u32[]{:S(2)}) %collective-permute-start.10) | collective-permute-done | bytes 65568 | tf_op jit(solution)/shard_map/ppermute | solution.py:56
  27.7 1.7 %collective-permute-done.11.refs_1_ = bf16[256,128]{1,0:T(8,128)(2,1)S(1)} collective-permute-done((bf16[256,128]{1,0:T(8,128)(2,1)S(1)}, bf16[256,128]{1,0:T(8,128)(2,1)S(1)}, u32[]{:S(2)}, u32[]{:S(2)}) %collective-permute-start.11) | collective-permute-done | bytes 65568 | tf_op jit(solution)/shard_map/ppermute | solution.py:56
  29.9 5.6 %shard_map.112 = (bf16[256,512]{1,0:T(8,128)(2,1)}, bf16[256,2048]{1,0:T(8,128)(2,1)S(1)}, f32[256,512]{1,0:T(8,128)S(1)}, f32[256,128]{1,0:T(8,128)S(1)}, bf16[...) custom-call(s32[4,128]{1,0:T(4,128)S(1)} %pad_add_fusion.refs_0_.scalar_ref, ...), custom_call_target="tpu_custom_call" | custom-call | bytes 24500000 | tf_op jit(solution)/shard_map/pallas_call | solution.py:489
  35.5 1.6 %shard_map.113 = (bf16[256,128]{1,0:T(8,128)(2,1)S(1)}, bf16[256,128]{1,0:T(8,128)(2,1)S(1)}, bf16[256,128]{1,0:T(8,128)(2,1)S(1)}, bf16[256,128]{1,0:T(8,128)(2,1)S(1)}) custom-call(s32[4,128]{1,0:T(4,128)S(1)} %pad_add_fusion.refs_0_.scalar_ref, bf16[256,2048]{1,0:T(8,128)(2,1)S(1)} %get-tuple-element.47.refs_0_, ...), custom_call_target="tpu_custom_call" | custom-call | bytes 7000000 | tf_op jit(solution)/shard_map/pallas_call | solution.py:516
  42.4 9.4 %collective-permute-done.15.refs_3_ = bf16[64,3072]{1,0:T(8,128)(2,1)S(1)} collective-permute-done((bf16[64,3072]{1,0:T(8,128)(2,1)S(1)}, bf16[64,3072]{1,0:T(8,128)(2,1)S(1)}, u32[]{:S(2)}, u32[]{:S(2)}) %collective-permute-start.15) | collective-permute-done | bytes 393248 | tf_op jit(solution)/shard_map/ppermute | solution.py:56
  51.8 7.6 %collective-permute-done.16.refs_4_ = bf16[64,3072]{1,0:T(8,128)(2,1)S(1)} collective-permute-done((bf16[64,3072]{1,0:T(8,128)(2,1)S(1)}, bf16[64,3072]{1,0:T(8,128)(2,1)S(1)}, u32[]{:S(2)}, u32[]{:S(2)}) %collective-permute-start.16) | collective-permute-done | bytes 393248 | tf_op jit(solution)/shard_map/ppermute | solution.py:56
  59.7 3.7 %collective-permute-start.19 = (bf16[16,2560]{1,0:T(8,128)(2,1)S(1)}, bf16[16,2560]{1,0:T(8,128)(2,1)S(1)}, u32[]{:S(2)}, u32[]{:S(2)}) collective-permute-start(bf16[16,2560]{1,0:T(8,128)(2,1)S(1)} %get-tuple-element.71), channel_id=1, source_target_pairs={{0,24},{2,26},{4,28},{6,30},{8,16},{10,18},{12,20},{14,22},{16,8},... | collective-permute-start | bytes 245768 | tf_op jit(solution)/shard_map/ppermute | solution.py:56
  64.1 2.9 %shard_map.115 = (bf16[4,512,128]{2,1,0:T(8,128)(2,1)S(1)}, bf16[4,512,128]{2,1,0:T(8,128)(2,1)S(1)}) custom-call(s32[4,128]{1,0:T(4,128)S(1)} %pad_add_fusion.refs_0_.scalar_ref, s32[4,8,1,128]{3,2,1,0:T(1,128)S(1)} %reshape.61.refs_1_, s32[4,8,1,128]{3,2,1,0:T(1,128)S(1)} %collective-permute-done.2.refs_2_, ...), custom_call_target="tpu_custom_call" | custom-call | bytes 10500000 | tf_op jit(solution)/shard_map/pallas_call | solution.py:536
  67.1 3.0 %collective-permute-done.21 = bf16[16,2560]{1,0:T(8,128)(2,1)S(1)} collective-permute-done((bf16[16,2560]{1,0:T(8,128)(2,1)S(1)}, bf16[16,2560]{1,0:T(8,128)(2,1)S(1)}, u32[]{:S(2)}, u32[]{:S(2)}) %collective-permute-start.21) | collective-permute-done | bytes 81952 | tf_op jit(solution)/shard_map/ppermute | solution.py:56
  70.2 2.4 %collective-permute-start.24 = (bf16[16,2560]{1,0:T(8,128)(2,1)S(1)}, bf16[16,2560]{1,0:T(8,128)(2,1)S(1)}, u32[]{:S(2)}, u32[]{:S(2)}) collective-permute-start(bf16[16,2560]{1,0:T(8,128)(2,1)S(1)} %add_convert_fusion.2), channel_id=1, source_target_pairs={{0,24},{2,26},{4,28},{6,30},{8,16},{10,18},{12,20},{14,22},{16,8},... | collective-permute-start | bytes 245768 | tf_op jit(solution)/shard_map/ppermute | solution.py:56
  72.8 1.9 %collective-permute-start.22 = (bf16[16,2560]{1,0:T(8,128)(2,1)S(1)}, bf16[16,2560]{1,0:T(8,128)(2,1)S(1)}, u32[]{:S(2)}, u32[]{:S(2)}) collective-permute-start(bf16[16,2560]{1,0:T(8,128)(2,1)S(1)} %add_convert_fusion.2), channel_id=1, source_target_pairs={{0,8},{2,10},{4,12},{6,14},{8,0},{10,2},{12,4},{14,6},{16,24},{18,... | collective-permute-start | bytes 245768 | tf_op jit(solution)/shard_map/ppermute | solution.py:56
  74.7 2.7 %collective-permute-done.24 = bf16[16,2560]{1,0:T(8,128)(2,1)S(1)} collective-permute-done((bf16[16,2560]{1,0:T(8,128)(2,1)S(1)}, bf16[16,2560]{1,0:T(8,128)(2,1)S(1)}, u32[]{:S(2)}, u32[]{:S(2)}) %collective-permute-start.24) | collective-permute-done | bytes 81952 | tf_op jit(solution)/shard_map/ppermute | solution.py:56
  77.4 2.9 %collective-permute-done.23 = bf16[16,2560]{1,0:T(8,128)(2,1)S(1)} collective-permute-done((bf16[16,2560]{1,0:T(8,128)(2,1)S(1)}, bf16[16,2560]{1,0:T(8,128)(2,1)S(1)}, u32[]{:S(2)}, u32[]{:S(2)}) %collective-permute-start.23) | collective-permute-done | bytes 81952 | tf_op jit(solution)/shard_map/ppermute | solution.py:56
  84.0 1.7 %collective-permute-start.25 = (bf16[512,128]{1,0:T(8,128)(2,1)S(1)}, bf16[512,128]{1,0:T(8,128)(2,1)S(1)}, u32[]{:S(2)}, u32[]{:S(2)}) collective-permute-start(bf16[512,128]{1,0:T(8,128)(2,1)S(1)} %get-tuple-element.68), channel_id=1, source_target_pairs={{0,24},{2,26},{4,28},{6,30},{8,16},{10,18},{12,20},{14,22},{16,8},... | collective-permute-start | bytes 393224 | tf_op jit(solution)/shard_map/ppermute | solution.py:56
  85.8 6.2 %collective-permute-done.28.refs_1_ = bf16[64,2560]{1,0:T(8,128)(2,1)S(1)} collective-permute-done((bf16[64,2560]{1,0:T(8,128)(2,1)S(1)}, bf16[64,2560]{1,0:T(8,128)(2,1)S(1)}, u32[]{:S(2)}, u32[]{:S(2)}) %collective-permute-start.28) | collective-permute-done | bytes 327712 | tf_op jit(solution)/shard_map/ppermute | solution.py:56
  92.0 1.8 %shard_map.116 = (f32[256,2048]{1,0:T(8,128)}, f32[256,512]{1,0:T(8,128)}) custom-call(s32[4,128]{1,0:T(4,128)S(1)} %pad_add_fusion.refs_0_.scalar_ref, bf16[64,2560]{1,0:T(8,128)(2,1)S(1)} %pad_maximum_fusion.1.refs_0_, bf16[64,2560]{1,0:T(8,128)(2,1)S(1)} %collective-permute-done.28.refs_1_), custom_call_target="tpu_custom_call" | custom-call | bytes 3500000 | tf_op jit(solution)/shard_map/pallas_call | solution.py:583
  93.7 3.5 %collective-permute-done.27.refs_1_ = bf16[64,2560]{1,0:T(8,128)(2,1)S(1)} collective-permute-done((bf16[64,2560]{1,0:T(8,128)(2,1)S(1)}, bf16[64,2560]{1,0:T(8,128)(2,1)S(1)}, u32[]{:S(2)}, u32[]{:S(2)}) %collective-permute-start.27) | collective-permute-done | bytes 327712 | tf_op jit(solution)/shard_map/ppermute | solution.py:56
  97.2 1.8 %shard_map.117 = (f32[256,2048]{1,0:T(8,128)}, f32[256,512]{1,0:T(8,128)}) custom-call(s32[4,128]{1,0:T(4,128)S(1)} %pad_add_fusion.refs_0_.scalar_ref, bf16[64,2560]{1,0:T(8,128)(2,1)S(1)} %collective-permute-done.26.refs_0_, bf16[64,2560]{1,0:T(8,128)(2,1)S(1)} %collective-permute-done.27.refs_1_, ...), custom_call_target="tpu_custom_call", output_to_operand_aliasing={{0}: (3, {}), {1}: (4, {})} | custom-call | bytes 3500000 | tf_op jit(solution)/shard_map/pallas_call | solution.py:583
  (65 shorter events, 21.0 us)
Async XLA Ops:
  1.6 15.9 %collective-permute-start.8 = (bf16[512,128]{1,0:T(8,128)(2,1)S(1)}, bf16[512,128]{1,0:T(8,128)(2,1)S(1)}, u32[]{:S(2)}, u32[]{:S(2)}) collective-permute-start(bf16[512,128]{1,0:T(8,128)(2,1)S(1)} %dynamic-slice_bitcast_fusion.refs_3_), channel_id=1, source_target_pairs={{0,24},{2,26},{4,28},{6,30},{8,16},{10,18},{12,20},{14,22},{16,8},... | collective-permute-start | bytes 393224 | tf_op jit(solution)/shard_map/ppermute | solution.py:56
  6.7 11.1 %collective-permute-start.6 = (bf16[512,128]{1,0:T(8,128)(2,1)S(1)}, bf16[512,128]{1,0:T(8,128)(2,1)S(1)}, u32[]{:S(2)}, u32[]{:S(2)}) collective-permute-start(bf16[512,128]{1,0:T(8,128)(2,1)S(1)} %dynamic-slice_bitcast_fusion.refs_3_), channel_id=1, source_target_pairs={{0,16},{2,18},{4,20},{6,22},{8,24},{10,26},{12,28},{14,30},{16,0},... | collective-permute-start | bytes 393224 | tf_op jit(solution)/shard_map/ppermute | solution.py:56
  6.7 10.2 %collective-permute-start.4 = (bf16[512,128]{1,0:T(8,128)(2,1)S(1)}, bf16[512,128]{1,0:T(8,128)(2,1)S(1)}, u32[]{:S(2)}, u32[]{:S(2)}) collective-permute-start(bf16[512,128]{1,0:T(8,128)(2,1)S(1)} %dynamic-slice_bitcast_fusion.refs_3_), channel_id=1, source_target_pairs={{0,8},{2,10},{4,12},{6,14},{8,0},{10,2},{12,4},{14,6},{16,24},{18,... | collective-permute-start | bytes 393224 | tf_op jit(solution)/shard_map/ppermute | solution.py:56
  11.4 7.7 %collective-permute-start.3 = (bf16[512,128]{1,0:T(8,128)(2,1)S(1)}, bf16[512,128]{1,0:T(8,128)(2,1)S(1)}, u32[]{:S(2)}, u32[]{:S(2)}) collective-permute-start(bf16[512,128]{1,0:T(8,128)(2,1)S(1)} %dynamic-slice_bitcast_fusion.refs_3_), channel_id=1, source_target_pairs={{0,1},{1,0},{2,3},{3,2},{4,5},{5,4},{6,7},{7,6},{8,9},{9,8},{10,11... | collective-permute-start | bytes 393224 | tf_op jit(solution)/shard_map/ppermute | solution.py:48
  22.2 7.7 %collective-permute-start.13 = (bf16[256,2560]{1,0:T(8,128)(2,1)S(1)}, bf16[256,2560]{1,0:T(8,128)(2,1)S(1)}, u32[]{:S(2)}, u32[]{:S(2)}) collective-permute-start(bf16[256,2560]{1,0:T(8,128)(2,1)S(1)} %pad_maximum_fusion.refs_4_), channel_id=1, source_target_pairs={{0,1},{1,0},{2,3},{3,2},{4,5},{5,4},{6,7},{7,6},{8,9},{9,8},{10,11... | collective-permute-start | bytes 3932168 | tf_op jit(solution)/shard_map/ppermute | solution.py:48
  22.5 5.2 %collective-permute-start.10 = (bf16[256,128]{1,0:T(8,128)(2,1)S(1)}, bf16[256,128]{1,0:T(8,128)(2,1)S(1)}, u32[]{:S(2)}, u32[]{:S(2)}) collective-permute-start(bf16[256,128]{1,0:T(8,128)(2,1)S(1)} %get-tuple-element.39), channel_id=1, source_target_pairs={{0,6},{2,4},{4,2},{6,0},{8,14},{10,12},{12,10},{14,8},{16,22},{18,... | collective-permute-start | bytes 196616 | tf_op jit(solution)/shard_map/ppermute | solution.py:56
  25.1 4.3 %collective-permute-start.11 = (bf16[256,128]{1,0:T(8,128)(2,1)S(1)}, bf16[256,128]{1,0:T(8,128)(2,1)S(1)}, u32[]{:S(2)}, u32[]{:S(2)}) collective-permute-start(bf16[256,128]{1,0:T(8,128)(2,1)S(1)} %get-tuple-element.40), channel_id=1, source_target_pairs={{0,4},{2,6},{4,0},{6,2},{8,12},{10,14},{12,8},{14,10},{16,20},{18,... | collective-permute-start | bytes 196616 | tf_op jit(solution)/shard_map/ppermute | solution.py:56
  25.6 4.3 %collective-permute-start.12 = (bf16[256,128]{1,0:T(8,128)(2,1)S(1)}, bf16[256,128]{1,0:T(8,128)(2,1)S(1)}, u32[]{:S(2)}, u32[]{:S(2)}) collective-permute-start(bf16[256,128]{1,0:T(8,128)(2,1)S(1)} %get-tuple-element.41), channel_id=1, source_target_pairs={{0,2},{2,0},{4,6},{6,4},{8,10},{10,8},{12,14},{14,12},{16,18},{18,... | collective-permute-start | bytes 196616 | tf_op jit(solution)/shard_map/ppermute | solution.py:56
  38.8 13.0 %collective-permute-start.15 = (bf16[64,3072]{1,0:T(8,128)(2,1)S(1)}, bf16[64,3072]{1,0:T(8,128)(2,1)S(1)}, u32[]{:S(2)}, u32[]{:S(2)}) collective-permute-start(bf16[64,3072]{1,0:T(8,128)(2,1)S(1)} %get-tuple-element.53), channel_id=1, source_target_pairs={{0,6},{2,4},{4,2},{6,0},{8,14},{10,12},{12,10},{14,8},{16,22},{18,... | collective-permute-start | bytes 1179656 | tf_op jit(solution)/shard_map/ppermute | solution.py:56
  40.4 19.0 %collective-permute-start.16 = (bf16[64,3072]{1,0:T(8,128)(2,1)S(1)}, bf16[64,3072]{1,0:T(8,128)(2,1)S(1)}, u32[]{:S(2)}, u32[]{:S(2)}) collective-permute-start(bf16[64,3072]{1,0:T(8,128)(2,1)S(1)} %get-tuple-element.54), channel_id=1, source_target_pairs={{0,4},{2,6},{4,0},{6,2},{8,12},{10,14},{12,8},{14,10},{16,20},{18,... | collective-permute-start | bytes 1179656 | tf_op jit(solution)/shard_map/ppermute | solution.py:56
  41.3 18.2 %collective-permute-start.17 = (bf16[64,3072]{1,0:T(8,128)(2,1)S(1)}, bf16[64,3072]{1,0:T(8,128)(2,1)S(1)}, u32[]{:S(2)}, u32[]{:S(2)}) collective-permute-start(bf16[64,3072]{1,0:T(8,128)(2,1)S(1)} %get-tuple-element.55), channel_id=1, source_target_pairs={{0,2},{2,0},{4,6},{6,4},{8,10},{10,8},{12,14},{14,12},{16,18},{18,... | collective-permute-start | bytes 1179656 | tf_op jit(solution)/shard_map/ppermute | solution.py:56
  59.7 7.4 %collective-permute-start.19 = (bf16[16,2560]{1,0:T(8,128)(2,1)S(1)}, bf16[16,2560]{1,0:T(8,128)(2,1)S(1)}, u32[]{:S(2)}, u32[]{:S(2)}) collective-permute-start(bf16[16,2560]{1,0:T(8,128)(2,1)S(1)} %get-tuple-element.71), channel_id=1, source_target_pairs={{0,24},{2,26},{4,28},{6,30},{8,16},{10,18},{12,20},{14,22},{16,8},... | collective-permute-start | bytes 245768 | tf_op jit(solution)/shard_map/ppermute | solution.py:56
  63.4 6.8 %collective-permute-start.21 = (bf16[16,2560]{1,0:T(8,128)(2,1)S(1)}, bf16[16,2560]{1,0:T(8,128)(2,1)S(1)}, u32[]{:S(2)}, u32[]{:S(2)}) collective-permute-start(bf16[16,2560]{1,0:T(8,128)(2,1)S(1)} %get-tuple-element.72), channel_id=1, source_target_pairs={{0,16},{2,18},{4,20},{6,22},{8,24},{10,26},{12,28},{14,30},{16,0},... | collective-permute-start | bytes 245768 | tf_op jit(solution)/shard_map/ppermute | solution.py:56
  63.4 6.8 %collective-permute-start.20 = (bf16[16,2560]{1,0:T(8,128)(2,1)S(1)}, bf16[16,2560]{1,0:T(8,128)(2,1)S(1)}, u32[]{:S(2)}, u32[]{:S(2)}) collective-permute-start(bf16[16,2560]{1,0:T(8,128)(2,1)S(1)} %get-tuple-element.73), channel_id=1, source_target_pairs={{0,8},{2,10},{4,12},{6,14},{8,0},{10,2},{12,4},{14,6},{16,24},{18,... | collective-permute-start | bytes 245768 | tf_op jit(solution)/shard_map/ppermute | solution.py:56
  67.1 16.8 %collective-permute-start.18 = (bf16[4,512,128]{2,1,0:T(8,128)(2,1)S(1)}, bf16[4,512,128]{2,1,0:T(8,128)(2,1)S(1)}, u32[]{:S(2)}, u32[]{:S(2)}) collective-permute-start(bf16[4,512,128]{2,1,0:T(8,128)(2,1)S(1)} %get-tuple-element.58), channel_id=1, source_target_pairs={{0,1},{1,0},{2,3},{3,2},{4,5},{5,4},{6,7},{7,6},{8,9},{9,8},{10,11... | collective-permute-start | bytes 1572872 | tf_op jit(solution)/shard_map/ppermute | solution.py:48
  70.2 7.2 %collective-permute-start.24 = (bf16[16,2560]{1,0:T(8,128)(2,1)S(1)}, bf16[16,2560]{1,0:T(8,128)(2,1)S(1)}, u32[]{:S(2)}, u32[]{:S(2)}) collective-permute-start(bf16[16,2560]{1,0:T(8,128)(2,1)S(1)} %add_convert_fusion.2), channel_id=1, source_target_pairs={{0,24},{2,26},{4,28},{6,30},{8,16},{10,18},{12,20},{14,22},{16,8},... | collective-permute-start | bytes 245768 | tf_op jit(solution)/shard_map/ppermute | solution.py:56
  72.6 7.7 %collective-permute-start.23 = (bf16[16,2560]{1,0:T(8,128)(2,1)S(1)}, bf16[16,2560]{1,0:T(8,128)(2,1)S(1)}, u32[]{:S(2)}, u32[]{:S(2)}) collective-permute-start(bf16[16,2560]{1,0:T(8,128)(2,1)S(1)} %add_convert_fusion.2), channel_id=1, source_target_pairs={{0,16},{2,18},{4,20},{6,22},{8,24},{10,26},{12,28},{14,30},{16,0},... | collective-permute-start | bytes 245768 | tf_op jit(solution)/shard_map/ppermute | solution.py:56
  72.8 7.5 %collective-permute-start.22 = (bf16[16,2560]{1,0:T(8,128)(2,1)S(1)}, bf16[16,2560]{1,0:T(8,128)(2,1)S(1)}, u32[]{:S(2)}, u32[]{:S(2)}) collective-permute-start(bf16[16,2560]{1,0:T(8,128)(2,1)S(1)} %add_convert_fusion.2), channel_id=1, source_target_pairs={{0,8},{2,10},{4,12},{6,14},{8,0},{10,2},{12,4},{14,6},{16,24},{18,... | collective-permute-start | bytes 245768 | tf_op jit(solution)/shard_map/ppermute | solution.py:56
  80.3 11.7 %collective-permute-start.28 = (bf16[64,2560]{1,0:T(8,128)(2,1)S(1)}, bf16[64,2560]{1,0:T(8,128)(2,1)S(1)}, u32[]{:S(2)}, u32[]{:S(2)}) collective-permute-start(bf16[64,2560]{1,0:T(8,128)(2,1)S(1)} %pad_maximum_fusion.1.refs_0_), channel_id=1, source_target_pairs={{0,6},{2,4},{4,2},{6,0},{8,14},{10,12},{12,10},{14,8},{16,22},{18,... | collective-permute-start | bytes 983048 | tf_op jit(solution)/shard_map/ppermute | solution.py:56
  81.9 15.3 %collective-permute-start.27 = (bf16[64,2560]{1,0:T(8,128)(2,1)S(1)}, bf16[64,2560]{1,0:T(8,128)(2,1)S(1)}, u32[]{:S(2)}, u32[]{:S(2)}) collective-permute-start(bf16[64,2560]{1,0:T(8,128)(2,1)S(1)} %pad_maximum_fusion.1.refs_0_), channel_id=1, source_target_pairs={{0,4},{2,6},{4,0},{6,2},{8,12},{10,14},{12,8},{14,10},{16,20},{18,... | collective-permute-start | bytes 983048 | tf_op jit(solution)/shard_map/ppermute | solution.py:56
  82.7 14.5 %collective-permute-start.26 = (bf16[64,2560]{1,0:T(8,128)(2,1)S(1)}, bf16[64,2560]{1,0:T(8,128)(2,1)S(1)}, u32[]{:S(2)}, u32[]{:S(2)}) collective-permute-start(bf16[64,2560]{1,0:T(8,128)(2,1)S(1)} %pad_maximum_fusion.1.refs_0_), channel_id=1, source_target_pairs={{0,2},{2,0},{4,6},{6,4},{8,10},{10,8},{12,14},{14,12},{16,18},{18,... | collective-permute-start | bytes 983048 | tf_op jit(solution)/shard_map/ppermute | solution.py:56
  84.0 14.9 %collective-permute-start.25 = (bf16[512,128]{1,0:T(8,128)(2,1)S(1)}, bf16[512,128]{1,0:T(8,128)(2,1)S(1)}, u32[]{:S(2)}, u32[]{:S(2)}) collective-permute-start(bf16[512,128]{1,0:T(8,128)(2,1)S(1)} %get-tuple-element.68), channel_id=1, source_target_pairs={{0,24},{2,26},{4,28},{6,30},{8,16},{10,18},{12,20},{14,22},{16,8},... | collective-permute-start | bytes 393224 | tf_op jit(solution)/shard_map/ppermute | solution.py:56
  85.8 13.2 %collective-permute-start.30 = (bf16[512,128]{1,0:T(8,128)(2,1)S(1)}, bf16[512,128]{1,0:T(8,128)(2,1)S(1)}, u32[]{:S(2)}, u32[]{:S(2)}) collective-permute-start(bf16[512,128]{1,0:T(8,128)(2,1)S(1)} %get-tuple-element.69), channel_id=1, source_target_pairs={{0,16},{2,18},{4,20},{6,22},{8,24},{10,26},{12,28},{14,30},{16,0},... | collective-permute-start | bytes 393224 | tf_op jit(solution)/shard_map/ppermute | solution.py:56
  92.0 7.0 %collective-permute-start.29 = (bf16[512,128]{1,0:T(8,128)(2,1)S(1)}, bf16[512,128]{1,0:T(8,128)(2,1)S(1)}, u32[]{:S(2)}, u32[]{:S(2)}) collective-permute-start(bf16[512,128]{1,0:T(8,128)(2,1)S(1)} %get-tuple-element.70), channel_id=1, source_target_pairs={{0,8},{2,10},{4,12},{6,14},{8,0},{10,2},{12,4},{14,6},{16,24},{18,... | collective-permute-start | bytes 393224 | tf_op jit(solution)/shard_map/ppermute | solution.py:56
  (9 other events, 35.8 us)

commit v14 on v13

--- a/solution.py
+++ b/solution.py
@@ -197,8 +197,7 @@
     block_refs = take(groups)[::-1]
     weight_refs = take(bals)
     (cot_ref,) = take(1)
-    (layer_ref,) = take(1)
-    grads_ref, normed_ref, inverse_ref = take(3)
+    grads_ref, normed_ref, inverse_ref, keep_mixed_ref = take(4)
     term_refs = take(bals)
     (x_ref, halves_ref, wide_ref, nt_ref, mt_ref, weights_ref, slope_ref, gate_ref, heads_ref, dsilu_ref, out_ref, mixed_ref, back_ref) = refs
 
@@ -299,11 +298,8 @@
         grads_ref[here, :width] = (grad_mixed * normed * dsilu_ref[here, :width]).astype(bf16)
         mixed = normed * gate
         mixed_ref[here, :] = mixed
-        keep_parts(here, mixed)
+        keep_mixed_ref[here, :] = mixed.astype(bf16)
     mt_ref[...] = jnp.transpose(mixed_ref[...]).astype(bf16)
-    mixed_ref[...] = times_parts(features, features + width)
-    for here in blocks:
-        layer_ref[here, :] = (x_rows(here) + mixed_ref[here, :]).astype(bf16)
 
     def owner_order(ref, turn):
         start = (bal ^ turn) * part
@@ -348,12 +344,23 @@
 def rows_kernel(groups, slots, bals, scalar_ref, *refs):
     refs = list(refs)
     take = lambda count: [refs.pop(0) for _ in range(count)]
-    grads_ref, normed_ref, inverse_ref, cot_ref = take(4)
-    weight_refs, grad_refs = take(bals), take(groups)
-    x_ref, wide_ref = refs
+    grads_ref, normed_ref, inverse_ref, mixed_ref, cot_ref = take(5)
+    weight_refs, block_refs = take(bals), take(groups)
+    (layer_ref,) = take(1)
+    grad_refs = take(groups)
+    x_ref, wide_ref, halves_ref = refs
     bal, group_here, _ = Scalars(scalar_ref, 0, bals, slots).place()
     features = grads_ref.shape[1]
     piece = grad_refs[0].shape[1]
+    part = weight_refs[0].shape[0]
+    for step in range(groups):
+        x_ref[group_here ^ step] = block_refs[step][...]
+    x = jnp.concatenate([x_ref[group] for group in range(groups)], axis=1).astype(f32)
+    for index in range(bals):
+        halves_ref[index] = mixed_ref[:, index * part : (index + 1) * part]
+    for turn in range(bals):
+        x = x + matmul(halves_ref[bal ^ turn], weight_refs[turn][:, features:])
+    layer_ref[...] = x.astype(bf16)
     grad_normed = times_parts_nt(grads_ref[...], weight_refs, 0, features, bal, wide_ref)
     back = norm_back(grad_normed, normed_ref[...], inverse_ref[:, :1])
     grad_rows = (cot_ref[...] + back).astype(bf16)
@@ -389,25 +396,20 @@
     _, group_here, table_here = Scalars(scalar_ref, 0, bals, slots).place()
     features = in_ref.shape[1]
     copies = []
+    height = tables * unit
     for number, (group_step, piece) in enumerate(zip(steps, pieces)):
         for table_step in range(tables):
-            index = number * tables + table_step
-            at = index * unit
-            from_rows = slice(table_step * unit, (table_step + 1) * unit)
-            scaled_ref[at : at + unit, :] = piece[from_rows, :].astype(f32) * scale
-            owner = (group_here ^ group_step) * tables + (table_here ^ table_step)
-            to = pl.ds(pl.multiple_of(owner * unit, unit), unit)
-            rows = scaled_ref.at[pl.ds(at, unit), :]
-            sem = sems.at[index]
-            copies.append(
-                pltpu.make_async_copy(rows.at[:, pl.ds(0, features)], in_ref.at[to, :], sem.at[0])
-            )
+            to = pl.multiple_of(number * height + (table_here ^ table_step) * unit, unit)
+            value = piece[table_step * unit : (table_step + 1) * unit, :]
+            scaled_ref[pl.ds(to, unit), :] = value.astype(f32) * scale
+        from_rows = scaled_ref.at[pl.ds(number * height, height), :]
+        to = pl.ds(pl.multiple_of((group_here ^ group_step) * height, height), height)
+        for index, (first, out) in enumerate(((0, in_ref), (features, out_ref))):
             copies.append(
                 pltpu.make_async_copy(
-                    rows.at[:, pl.ds(features, out_ref.shape[1])], out_ref.at[to, :], sem.at[1]
+                    from_rows.at[:, pl.ds(first, out.shape[1])], out.at[to, :], sems.at[number, index]
                 )
             )
-            copies[-2].start()
             copies[-1].start()
     for copy in copies:
         copy.wait()
@@ -488,9 +490,9 @@
     terms = jax.ShapeDtypeStruct((weight_part, features + width), bf16)
     results = pl.pallas_call(
         functools.partial(layer_kernel, groups, slots, tables, bals, unit),
-        out_shape=[jax.ShapeDtypeStruct((rows, width), bf16)]
-        + [jax.ShapeDtypeStruct((rows, features), bf16)]
+        out_shape=[jax.ShapeDtypeStruct((rows, features), bf16)]
         + [jax.ShapeDtypeStruct((rows, columns_here), f32) for columns_here in (width, LANES)]
+        + [jax.ShapeDtypeStruct((rows, width), bf16)]
         + [terms] * bals,
         in_specs=[SMEM] + [VMEM] * (groups + bals + 1),
         out_specs=[VMEM] * (4 + bals),
@@ -512,19 +514,21 @@
         cost_estimate=estimate(7),
         compiler_params=room(36),
     )(scalars, *block[::-1], *weights, wide_cot)
-    layer_out, for_rows, results = results[0], results[1:4], results[4:]
-    grads = pl.pallas_call(
+    for_rows, results = results[:4], results[4:]
+    layer_out, *grads = pl.pallas_call(
         functools.partial(rows_kernel, groups, slots, bals),
-        out_shape=[jax.ShapeDtypeStruct((rows, columns), bf16)] * groups,
-        in_specs=[SMEM] + [VMEM] * (4 + bals),
-        out_specs=[VMEM] * groups,
+        out_shape=[jax.ShapeDtypeStruct((rows, width), bf16)]
+        + [jax.ShapeDtypeStruct((rows, columns), bf16)] * groups,
+        in_specs=[SMEM] + [VMEM] * (5 + bals + groups),
+        out_specs=[VMEM] * (1 + groups),
         scratch_shapes=[
             pltpu.VMEM((groups, rows, columns), bf16),
             pltpu.VMEM((bals, rows, weight_part), f32),
+            pltpu.VMEM((bals, rows, weight_part), bf16),
         ],
         cost_estimate=estimate(2),
         compiler_params=room(16),
-    )(scalars, *for_rows, wide_cot, *weights)
+    )(scalars, *for_rows, wide_cot, *weights, *block)
 
     def over_cores(parts):
         return sum_rounded([parts[0]] + [bal_swap(parts[turn], turn, bals) for turn in range(1, bals)])
@@ -590,7 +594,7 @@
                 out_specs=[HBM] * 2,
                 scratch_shapes=[
                     pltpu.VMEM((len(steps) * tables * unit, features + width), f32),
-                    pltpu.SemaphoreType.DMA((len(steps) * tables, 2)),
+                    pltpu.SemaphoreType.DMA((len(steps), 2)),
                 ],
                 input_output_aliases={1 + len(steps) + index: index for index in range(len(totals))},
                 cost_estimate=estimate(1),

time: 100 us -> 99.4 us (level)
  transfers between devices with their start and end apart: 31 -> 31, of which waited for: 15 -> 15; matrix products, arithmetic and copies ran while one was open for 4% -> 5% of each run, Pallas kernels for 8% -> 9%
where the time goes in v14:
time: 99.4 us; the launch traced here: 99.2 us
  waiting for transfers between devices  43.5 us (44%)
  starting transfers between devices  31.7 us (32%)
  Pallas kernels  16.8 us (17%)
  other arithmetic  3.96 us (4%)
  local copies, waits for them, and re-layouts  2.42 us (2%)
    ppermute x23, waiting for transfers between devices, emb_swap(): return lax.ppermute(value, 'emb', [(i, i ^ step) for i in range(count)])  42.5 us
    ppermute x23, starting transfers between devices, emb_swap(): return lax.ppermute(value, 'emb', [(i, i ^ step) for i in range(count)])  30.3 us
    pallas_call x1, Pallas kernels, on_device(): pl.pallas_call(functools.partial(layer_kernel, groups, slots, tables, bal...  4.98 us
    pallas_call x2, Pallas kernels, on_device(): pl.pallas_call(functools.partial(place_kernel, grad_scale, steps, slots,...  3.39 us
    pallas_call x1, Pallas kernels, on_device(): pl.pallas_call(functools.partial(lookup_kernel, groups, slots, tables, ba...  3.08 us
    pallas_call x1, Pallas kernels, table_sums(): pl.pallas_call(functools.partial(scatter_kernel, groups, slots, bals), ou...  2.91 us
    pallas_call x1, Pallas kernels, on_device(): pl.pallas_call(functools.partial(rows_kernel, groups, slots, bals), out_s...  2.15 us
  transfers between devices with their start and end apart: 31, of which 15 were waited for; matrix products, arithmetic and copies ran while one was open for 5% of the time, Pallas kernels for 9%

profile of v14, /device:TPU:0, one launch (start us, length us, event | category | flops | bytes accessed | tf_op | source)
XLA Modules:
  0.0 99.2 jit_solution(12023665367158464713)
XLA Ops:
  1.6 5.1 %collective-permute-start.8 = (bf16[512,128]{1,0:T(8,128)(2,1)S(1)}, bf16[512,128]{1,0:T(8,128)(2,1)S(1)}, u32[]{:S(2)}, u32[]{:S(2)}) collective-permute-start(bf16[512,128]{1,0:T(8,128)(2,1)S(1)} %dynamic-slice_bitcast_fusion.refs_3_), channel_id=1, source_target_pairs={{0,24},{2,26},{4,28},{6,30},{8,16},{10,18},{12,20},{14,22},{16,8},... | collective-permute-start | bytes 393224 | tf_op jit(solution)/shard_map/ppermute | solution.py:56
  9.8 1.6 %collective-permute-start = (s32[1,128]{1,0:T(1,128)S(1)}, s32[1,128]{1,0:T(1,128)S(1)}, u32[]{:S(2)}, u32[]{:S(2)}) collective-permute-start(s32[1,128]{1,0:T(1,128)S(1)} %pad_add_fusion.2), channel_id=1, source_target_pairs={{0,2},{2,0},{4,6},{6,4},{8,10},{10,8},{12,14},{14,12},{16,18},{18,... | collective-permute-start | bytes 1544 | tf_op jit(solution)/shard_map/ppermute | solution.py:56
  11.4 1.9 %collective-permute-done = s32[1,128]{1,0:T(1,128)S(1)} collective-permute-done((s32[1,128]{1,0:T(1,128)S(1)}, s32[1,128]{1,0:T(1,128)S(1)}, u32[]{:S(2)}, u32[]{:S(2)}) %collective-permute-start) | collective-permute-done | bytes 544 | tf_op jit(solution)/shard_map/ppermute | solution.py:56
  13.4 1.7 %collective-permute-start.1 = (s32[2,128]{1,0:T(2,128)S(1)}, s32[2,128]{1,0:T(2,128)S(1)}, u32[]{:S(2)}, u32[]{:S(2)}) collective-permute-start(s32[2,128]{1,0:T(2,128)S(1)} %pad_add_fusion.1), channel_id=1, source_target_pairs={{0,4},{2,6},{4,0},{6,2},{8,12},{10,14},{12,8},{14,10},{16,20},{18,... | collective-permute-start | bytes 3080 | tf_op jit(solution)/shard_map/ppermute | solution.py:56
  19.1 3.1 %shard_map.111 = (bf16[256,128]{1,0:T(8,128)(2,1)S(1)}, bf16[256,128]{1,0:T(8,128)(2,1)S(1)}, bf16[256,128]{1,0:T(8,128)(2,1)S(1)}, bf16[256,128]{1,0:T(8,128)(2,1)S(1)}) custom-call(s32[4,128]{1,0:T(4,128)S(1)} %pad_add_fusion.refs_0_.scalar_ref, s32[4,8,1,128]{3,2,1,0:T(1,128)S(1)} %reshape.61.refs_1_, ...), custom_call_target="tpu_custom_call" | custom-call | bytes 10500000 | tf_op jit(solution)/shard_map/pallas_call | solution.py:477
  22.5 2.6 %collective-permute-start.10 = (bf16[256,128]{1,0:T(8,128)(2,1)S(1)}, bf16[256,128]{1,0:T(8,128)(2,1)S(1)}, u32[]{:S(2)}, u32[]{:S(2)}) collective-permute-start(bf16[256,128]{1,0:T(8,128)(2,1)S(1)} %get-tuple-element.40), channel_id=1, source_target_pairs={{0,6},{2,4},{4,2},{6,0},{8,14},{10,12},{12,10},{14,8},{16,22},{18,... | collective-permute-start | bytes 196616 | tf_op jit(solution)/shard_map/ppermute | solution.py:56
  26.0 1.7 %collective-permute-done.10.refs_0_.refs_10_ = bf16[256,128]{1,0:T(8,128)(2,1)S(1)} collective-permute-done((bf16[256,128]{1,0:T(8,128)(2,1)S(1)}, bf16[256,128]{1,0:T(8,128)(2,1)S(1)}, u32[]{:S(2)}, u32[]{:S(2)}) %collective-permute-start.10) | collective-permute-done | bytes 65568 | tf_op jit(solution)/shard_map/ppermute | solution.py:56
  27.7 1.7 %collective-permute-done.11.refs_1_.refs_9_ = bf16[256,128]{1,0:T(8,128)(2,1)S(1)} collective-permute-done((bf16[256,128]{1,0:T(8,128)(2,1)S(1)}, bf16[256,128]{1,0:T(8,128)(2,1)S(1)}, u32[]{:S(2)}, u32[]{:S(2)}) %collective-permute-start.11) | collective-permute-done | bytes 65568 | tf_op jit(solution)/shard_map/ppermute | solution.py:56
  29.9 5.0 %shard_map.112 = (bf16[256,2048]{1,0:T(8,128)(2,1)S(1)}, f32[256,512]{1,0:T(8,128)S(1)}, f32[256,128]{1,0:T(8,128)S(1)}, bf16[256,512]{1,0:T(8,128)(2,1)S(1)}, b...) custom-call(s32[4,128]{1,0:T(4,128)S(1)} %pad_add_fusion.refs_0_.scalar_ref, ...), custom_call_target="tpu_custom_call" | custom-call | bytes 24500000 | tf_op jit(solution)/shard_map/pallas_call | solution.py:491
  34.9 2.1 %shard_map.113 = (bf16[256,512]{1,0:T(8,128)(2,1)}, bf16[256,128]{1,0:T(8,128)(2,1)S(1)}, bf16[256,128]{1,0:T(8,128)(2,1)S(1)}, bf16[256,128]{1,0:T(8,128)(2,1)S(1)}, bf16[256,128]{1,0:T(8,128)(2,1)S(1)}) custom-call(s32[4,128]{1,0:T(4,128)S(1)} %pad_add_fusion.refs_0_.scalar_ref, bf16[256,2048]{1,0:T(8,128)(2,1)S(1)} %get-tuple-element.45.refs_0_, ...), custom_call_target="tpu_custom_call" | custom-call | bytes 7000000 | tf_op jit(solution)/shard_map/pallas_call | solution.py:518
  41.8 9.4 %collective-permute-done.15.refs_3_ = bf16[64,3072]{1,0:T(8,128)(2,1)S(1)} collective-permute-done((bf16[64,3072]{1,0:T(8,128)(2,1)S(1)}, bf16[64,3072]{1,0:T(8,128)(2,1)S(1)}, u32[]{:S(2)}, u32[]{:S(2)}) %collective-permute-start.15) | collective-permute-done | bytes 393248 | tf_op jit(solution)/shard_map/ppermute | solution.py:56
  51.2 7.6 %collective-permute-done.16.refs_4_ = bf16[64,3072]{1,0:T(8,128)(2,1)S(1)} collective-permute-done((bf16[64,3072]{1,0:T(8,128)(2,1)S(1)}, bf16[64,3072]{1,0:T(8,128)(2,1)S(1)}, u32[]{:S(2)}, u32[]{:S(2)}) %collective-permute-start.16) | collective-permute-done | bytes 393248 | tf_op jit(solution)/shard_map/ppermute | solution.py:56
  59.1 3.7 %collective-permute-start.19 = (bf16[16,2560]{1,0:T(8,128)(2,1)S(1)}, bf16[16,2560]{1,0:T(8,128)(2,1)S(1)}, u32[]{:S(2)}, u32[]{:S(2)}) collective-permute-start(bf16[16,2560]{1,0:T(8,128)(2,1)S(1)} %get-tuple-element.73), channel_id=1, source_target_pairs={{0,24},{2,26},{4,28},{6,30},{8,16},{10,18},{12,20},{14,22},{16,8},... | collective-permute-start | bytes 245768 | tf_op jit(solution)/shard_map/ppermute | solution.py:56
  63.6 2.9 %shard_map.115 = (bf16[4,512,128]{2,1,0:T(8,128)(2,1)S(1)}, bf16[4,512,128]{2,1,0:T(8,128)(2,1)S(1)}) custom-call(s32[4,128]{1,0:T(4,128)S(1)} %pad_add_fusion.refs_0_.scalar_ref, s32[4,8,1,128]{3,2,1,0:T(1,128)S(1)} %reshape.61.refs_1_, s32[4,8,1,128]{3,2,1,0:T(1,128)S(1)} %collective-permute-done.2.refs_2_, ...), custom_call_target="tpu_custom_call" | custom-call | bytes 10500000 | tf_op jit(solution)/shard_map/pallas_call | solution.py:540
  66.6 3.0 %collective-permute-done.21 = bf16[16,2560]{1,0:T(8,128)(2,1)S(1)} collective-permute-done((bf16[16,2560]{1,0:T(8,128)(2,1)S(1)}, bf16[16,2560]{1,0:T(8,128)(2,1)S(1)}, u32[]{:S(2)}, u32[]{:S(2)}) %collective-permute-start.21) | collective-permute-done | bytes 81952 | tf_op jit(solution)/shard_map/ppermute | solution.py:56
  69.6 2.4 %collective-permute-start.24 = (bf16[16,2560]{1,0:T(8,128)(2,1)S(1)}, bf16[16,2560]{1,0:T(8,128)(2,1)S(1)}, u32[]{:S(2)}, u32[]{:S(2)}) collective-permute-start(bf16[16,2560]{1,0:T(8,128)(2,1)S(1)} %add_convert_fusion.2), channel_id=1, source_target_pairs={{0,24},{2,26},{4,28},{6,30},{8,16},{10,18},{12,20},{14,22},{16,8},... | collective-permute-start | bytes 245768 | tf_op jit(solution)/shard_map/ppermute | solution.py:56
  72.2 1.9 %collective-permute-start.22 = (bf16[16,2560]{1,0:T(8,128)(2,1)S(1)}, bf16[16,2560]{1,0:T(8,128)(2,1)S(1)}, u32[]{:S(2)}, u32[]{:S(2)}) collective-permute-start(bf16[16,2560]{1,0:T(8,128)(2,1)S(1)} %add_convert_fusion.2), channel_id=1, source_target_pairs={{0,8},{2,10},{4,12},{6,14},{8,0},{10,2},{12,4},{14,6},{16,24},{18,... | collective-permute-start | bytes 245768 | tf_op jit(solution)/shard_map/ppermute | solution.py:56
  74.1 2.7 %collective-permute-done.24 = bf16[16,2560]{1,0:T(8,128)(2,1)S(1)} collective-permute-done((bf16[16,2560]{1,0:T(8,128)(2,1)S(1)}, bf16[16,2560]{1,0:T(8,128)(2,1)S(1)}, u32[]{:S(2)}, u32[]{:S(2)}) %collective-permute-start.24) | collective-permute-done | bytes 81952 | tf_op jit(solution)/shard_map/ppermute | solution.py:56
  76.8 2.9 %collective-permute-done.23 = bf16[16,2560]{1,0:T(8,128)(2,1)S(1)} collective-permute-done((bf16[16,2560]{1,0:T(8,128)(2,1)S(1)}, bf16[16,2560]{1,0:T(8,128)(2,1)S(1)}, u32[]{:S(2)}, u32[]{:S(2)}) %collective-permute-start.23) | collective-permute-done | bytes 81952 | tf_op jit(solution)/shard_map/ppermute | solution.py:56
  83.5 1.7 %collective-permute-start.25 = (bf16[512,128]{1,0:T(8,128)(2,1)S(1)}, bf16[512,128]{1,0:T(8,128)(2,1)S(1)}, u32[]{:S(2)}, u32[]{:S(2)}) collective-permute-start(bf16[512,128]{1,0:T(8,128)(2,1)S(1)} %get-tuple-element.70), channel_id=1, source_target_pairs={{0,24},{2,26},{4,28},{6,30},{8,16},{10,18},{12,20},{14,22},{16,8},... | collective-permute-start | bytes 393224 | tf_op jit(solution)/shard_map/ppermute | solution.py:56
  85.2 6.2 %collective-permute-done.28.refs_1_ = bf16[64,2560]{1,0:T(8,128)(2,1)S(1)} collective-permute-done((bf16[64,2560]{1,0:T(8,128)(2,1)S(1)}, bf16[64,2560]{1,0:T(8,128)(2,1)S(1)}, u32[]{:S(2)}, u32[]{:S(2)}) %collective-permute-start.28) | collective-permute-done | bytes 327712 | tf_op jit(solution)/shard_map/ppermute | solution.py:56
  91.4 1.7 %shard_map.116 = (f32[256,2048]{1,0:T(8,128)}, f32[256,512]{1,0:T(8,128)}) custom-call(s32[4,128]{1,0:T(4,128)S(1)} %pad_add_fusion.refs_0_.scalar_ref, bf16[64,2560]{1,0:T(8,128)(2,1)S(1)} %pad_maximum_fusion.1.refs_0_, bf16[64,2560]{1,0:T(8,128)(2,1)S(1)} %collective-permute-done.28.refs_1_), custom_call_target="tpu_custom_call" | custom-call | bytes 3500000 | tf_op jit(solution)/shard_map/pallas_call | solution.py:587
  93.1 3.5 %collective-permute-done.27.refs_1_ = bf16[64,2560]{1,0:T(8,128)(2,1)S(1)} collective-permute-done((bf16[64,2560]{1,0:T(8,128)(2,1)S(1)}, bf16[64,2560]{1,0:T(8,128)(2,1)S(1)}, u32[]{:S(2)}, u32[]{:S(2)}) %collective-permute-start.27) | collective-permute-done | bytes 327712 | tf_op jit(solution)/shard_map/ppermute | solution.py:56
  96.7 1.7 %shard_map.117 = (f32[256,2048]{1,0:T(8,128)}, f32[256,512]{1,0:T(8,128)}) custom-call(s32[4,128]{1,0:T(4,128)S(1)} %pad_add_fusion.refs_0_.scalar_ref, bf16[64,2560]{1,0:T(8,128)(2,1)S(1)} %collective-permute-done.26.refs_0_, bf16[64,2560]{1,0:T(8,128)(2,1)S(1)} %collective-permute-done.27.refs_1_, ...), custom_call_target="tpu_custom_call", output_to_operand_aliasing={{0}: (3, {}), {1}: (4, {})} | custom-call | bytes 3500000 | tf_op jit(solution)/shard_map/pallas_call | solution.py:587
  (65 shorter events, 20.5 us)
Async XLA Ops:
  1.6 15.9 %collective-permute-start.8 = (bf16[512,128]{1,0:T(8,128)(2,1)S(1)}, bf16[512,128]{1,0:T(8,128)(2,1)S(1)}, u32[]{:S(2)}, u32[]{:S(2)}) collective-permute-start(bf16[512,128]{1,0:T(8,128)(2,1)S(1)} %dynamic-slice_bitcast_fusion.refs_3_), channel_id=1, source_target_pairs={{0,24},{2,26},{4,28},{6,30},{8,16},{10,18},{12,20},{14,22},{16,8},... | collective-permute-start | bytes 393224 | tf_op jit(solution)/shard_map/ppermute | solution.py:56
  6.7 11.1 %collective-permute-start.6 = (bf16[512,128]{1,0:T(8,128)(2,1)S(1)}, bf16[512,128]{1,0:T(8,128)(2,1)S(1)}, u32[]{:S(2)}, u32[]{:S(2)}) collective-permute-start(bf16[512,128]{1,0:T(8,128)(2,1)S(1)} %dynamic-slice_bitcast_fusion.refs_3_), channel_id=1, source_target_pairs={{0,16},{2,18},{4,20},{6,22},{8,24},{10,26},{12,28},{14,30},{16,0},... | collective-permute-start | bytes 393224 | tf_op jit(solution)/shard_map/ppermute | solution.py:56
  6.7 10.2 %collective-permute-start.4 = (bf16[512,128]{1,0:T(8,128)(2,1)S(1)}, bf16[512,128]{1,0:T(8,128)(2,1)S(1)}, u32[]{:S(2)}, u32[]{:S(2)}) collective-permute-start(bf16[512,128]{1,0:T(8,128)(2,1)S(1)} %dynamic-slice_bitcast_fusion.refs_3_), channel_id=1, source_target_pairs={{0,8},{2,10},{4,12},{6,14},{8,0},{10,2},{12,4},{14,6},{16,24},{18,... | collective-permute-start | bytes 393224 | tf_op jit(solution)/shard_map/ppermute | solution.py:56
  11.4 7.7 %collective-permute-start.3 = (bf16[512,128]{1,0:T(8,128)(2,1)S(1)}, bf16[512,128]{1,0:T(8,128)(2,1)S(1)}, u32[]{:S(2)}, u32[]{:S(2)}) collective-permute-start(bf16[512,128]{1,0:T(8,128)(2,1)S(1)} %dynamic-slice_bitcast_fusion.refs_3_), channel_id=1, source_target_pairs={{0,1},{1,0},{2,3},{3,2},{4,5},{5,4},{6,7},{7,6},{8,9},{9,8},{10,11... | collective-permute-start | bytes 393224 | tf_op jit(solution)/shard_map/ppermute | solution.py:48
  22.2 7.7 %collective-permute-start.13 = (bf16[256,2560]{1,0:T(8,128)(2,1)S(1)}, bf16[256,2560]{1,0:T(8,128)(2,1)S(1)}, u32[]{:S(2)}, u32[]{:S(2)}) collective-permute-start(bf16[256,2560]{1,0:T(8,128)(2,1)S(1)} %pad_maximum_fusion.refs_4_.refs_5_), channel_id=1, source_target_pairs={{0,1},{1,0},{2,3},{3,2},{4,5},{5,4},{6,7},{7,6},{8,9},{9,8},{10,11... | collective-permute-start | bytes 3932168 | tf_op jit(solution)/shard_map/ppermute | solution.py:48
  22.5 5.2 %collective-permute-start.10 = (bf16[256,128]{1,0:T(8,128)(2,1)S(1)}, bf16[256,128]{1,0:T(8,128)(2,1)S(1)}, u32[]{:S(2)}, u32[]{:S(2)}) collective-permute-start(bf16[256,128]{1,0:T(8,128)(2,1)S(1)} %get-tuple-element.40), channel_id=1, source_target_pairs={{0,6},{2,4},{4,2},{6,0},{8,14},{10,12},{12,10},{14,8},{16,22},{18,... | collective-permute-start | bytes 196616 | tf_op jit(solution)/shard_map/ppermute | solution.py:56
  25.1 4.3 %collective-permute-start.11 = (bf16[256,128]{1,0:T(8,128)(2,1)S(1)}, bf16[256,128]{1,0:T(8,128)(2,1)S(1)}, u32[]{:S(2)}, u32[]{:S(2)}) collective-permute-start(bf16[256,128]{1,0:T(8,128)(2,1)S(1)} %get-tuple-element.41), channel_id=1, source_target_pairs={{0,4},{2,6},{4,0},{6,2},{8,12},{10,14},{12,8},{14,10},{16,20},{18,... | collective-permute-start | bytes 196616 | tf_op jit(solution)/shard_map/ppermute | solution.py:56
  25.6 4.3 %collective-permute-start.12 = (bf16[256,128]{1,0:T(8,128)(2,1)S(1)}, bf16[256,128]{1,0:T(8,128)(2,1)S(1)}, u32[]{:S(2)}, u32[]{:S(2)}) collective-permute-start(bf16[256,128]{1,0:T(8,128)(2,1)S(1)} %get-tuple-element.42), channel_id=1, source_target_pairs={{0,2},{2,0},{4,6},{6,4},{8,10},{10,8},{12,14},{14,12},{16,18},{18,... | collective-permute-start | bytes 196616 | tf_op jit(solution)/shard_map/ppermute | solution.py:56
  38.3 13.0 %collective-permute-start.15 = (bf16[64,3072]{1,0:T(8,128)(2,1)S(1)}, bf16[64,3072]{1,0:T(8,128)(2,1)S(1)}, u32[]{:S(2)}, u32[]{:S(2)}) collective-permute-start(bf16[64,3072]{1,0:T(8,128)(2,1)S(1)} %get-tuple-element.55), channel_id=1, source_target_pairs={{0,6},{2,4},{4,2},{6,0},{8,14},{10,12},{12,10},{14,8},{16,22},{18,... | collective-permute-start | bytes 1179656 | tf_op jit(solution)/shard_map/ppermute | solution.py:56
  39.8 19.0 %collective-permute-start.16 = (bf16[64,3072]{1,0:T(8,128)(2,1)S(1)}, bf16[64,3072]{1,0:T(8,128)(2,1)S(1)}, u32[]{:S(2)}, u32[]{:S(2)}) collective-permute-start(bf16[64,3072]{1,0:T(8,128)(2,1)S(1)} %get-tuple-element.56), channel_id=1, source_target_pairs={{0,4},{2,6},{4,0},{6,2},{8,12},{10,14},{12,8},{14,10},{16,20},{18,... | collective-permute-start | bytes 1179656 | tf_op jit(solution)/shard_map/ppermute | solution.py:56
  40.7 18.2 %collective-permute-start.17 = (bf16[64,3072]{1,0:T(8,128)(2,1)S(1)}, bf16[64,3072]{1,0:T(8,128)(2,1)S(1)}, u32[]{:S(2)}, u32[]{:S(2)}) collective-permute-start(bf16[64,3072]{1,0:T(8,128)(2,1)S(1)} %get-tuple-element.57), channel_id=1, source_target_pairs={{0,2},{2,0},{4,6},{6,4},{8,10},{10,8},{12,14},{14,12},{16,18},{18,... | collective-permute-start | bytes 1179656 | tf_op jit(solution)/shard_map/ppermute | solution.py:56
  59.1 7.5 %collective-permute-start.19 = (bf16[16,2560]{1,0:T(8,128)(2,1)S(1)}, bf16[16,2560]{1,0:T(8,128)(2,1)S(1)}, u32[]{:S(2)}, u32[]{:S(2)}) collective-permute-start(bf16[16,2560]{1,0:T(8,128)(2,1)S(1)} %get-tuple-element.73), channel_id=1, source_target_pairs={{0,24},{2,26},{4,28},{6,30},{8,16},{10,18},{12,20},{14,22},{16,8},... | collective-permute-start | bytes 245768 | tf_op jit(solution)/shard_map/ppermute | solution.py:56
  62.8 6.8 %collective-permute-start.21 = (bf16[16,2560]{1,0:T(8,128)(2,1)S(1)}, bf16[16,2560]{1,0:T(8,128)(2,1)S(1)}, u32[]{:S(2)}, u32[]{:S(2)}) collective-permute-start(bf16[16,2560]{1,0:T(8,128)(2,1)S(1)} %get-tuple-element.74), channel_id=1, source_target_pairs={{0,16},{2,18},{4,20},{6,22},{8,24},{10,26},{12,28},{14,30},{16,0},... | collective-permute-start | bytes 245768 | tf_op jit(solution)/shard_map/ppermute | solution.py:56
  62.8 6.8 %collective-permute-start.20 = (bf16[16,2560]{1,0:T(8,128)(2,1)S(1)}, bf16[16,2560]{1,0:T(8,128)(2,1)S(1)}, u32[]{:S(2)}, u32[]{:S(2)}) collective-permute-start(bf16[16,2560]{1,0:T(8,128)(2,1)S(1)} %get-tuple-element.75), channel_id=1, source_target_pairs={{0,8},{2,10},{4,12},{6,14},{8,0},{10,2},{12,4},{14,6},{16,24},{18,... | collective-permute-start | bytes 245768 | tf_op jit(solution)/shard_map/ppermute | solution.py:56
  66.5 16.8 %collective-permute-start.18 = (bf16[4,512,128]{2,1,0:T(8,128)(2,1)S(1)}, bf16[4,512,128]{2,1,0:T(8,128)(2,1)S(1)}, u32[]{:S(2)}, u32[]{:S(2)}) collective-permute-start(bf16[4,512,128]{2,1,0:T(8,128)(2,1)S(1)} %get-tuple-element.60), channel_id=1, source_target_pairs={{0,1},{1,0},{2,3},{3,2},{4,5},{5,4},{6,7},{7,6},{8,9},{9,8},{10,11... | collective-permute-start | bytes 1572872 | tf_op jit(solution)/shard_map/ppermute | solution.py:48
  69.6 7.1 %collective-permute-start.24 = (bf16[16,2560]{1,0:T(8,128)(2,1)S(1)}, bf16[16,2560]{1,0:T(8,128)(2,1)S(1)}, u32[]{:S(2)}, u32[]{:S(2)}) collective-permute-start(bf16[16,2560]{1,0:T(8,128)(2,1)S(1)} %add_convert_fusion.2), channel_id=1, source_target_pairs={{0,24},{2,26},{4,28},{6,30},{8,16},{10,18},{12,20},{14,22},{16,8},... | collective-permute-start | bytes 245768 | tf_op jit(solution)/shard_map/ppermute | solution.py:56
  72.1 7.6 %collective-permute-start.23 = (bf16[16,2560]{1,0:T(8,128)(2,1)S(1)}, bf16[16,2560]{1,0:T(8,128)(2,1)S(1)}, u32[]{:S(2)}, u32[]{:S(2)}) collective-permute-start(bf16[16,2560]{1,0:T(8,128)(2,1)S(1)} %add_convert_fusion.2), channel_id=1, source_target_pairs={{0,16},{2,18},{4,20},{6,22},{8,24},{10,26},{12,28},{14,30},{16,0},... | collective-permute-start | bytes 245768 | tf_op jit(solution)/shard_map/ppermute | solution.py:56
  72.2 7.5 %collective-permute-start.22 = (bf16[16,2560]{1,0:T(8,128)(2,1)S(1)}, bf16[16,2560]{1,0:T(8,128)(2,1)S(1)}, u32[]{:S(2)}, u32[]{:S(2)}) collective-permute-start(bf16[16,2560]{1,0:T(8,128)(2,1)S(1)} %add_convert_fusion.2), channel_id=1, source_target_pairs={{0,8},{2,10},{4,12},{6,14},{8,0},{10,2},{12,4},{14,6},{16,24},{18,... | collective-permute-start | bytes 245768 | tf_op jit(solution)/shard_map/ppermute | solution.py:56
  79.7 11.7 %collective-permute-start.28 = (bf16[64,2560]{1,0:T(8,128)(2,1)S(1)}, bf16[64,2560]{1,0:T(8,128)(2,1)S(1)}, u32[]{:S(2)}, u32[]{:S(2)}) collective-permute-start(bf16[64,2560]{1,0:T(8,128)(2,1)S(1)} %pad_maximum_fusion.1.refs_0_), channel_id=1, source_target_pairs={{0,6},{2,4},{4,2},{6,0},{8,14},{10,12},{12,10},{14,8},{16,22},{18,... | collective-permute-start | bytes 983048 | tf_op jit(solution)/shard_map/ppermute | solution.py:56
  81.3 15.4 %collective-permute-start.27 = (bf16[64,2560]{1,0:T(8,128)(2,1)S(1)}, bf16[64,2560]{1,0:T(8,128)(2,1)S(1)}, u32[]{:S(2)}, u32[]{:S(2)}) collective-permute-start(bf16[64,2560]{1,0:T(8,128)(2,1)S(1)} %pad_maximum_fusion.1.refs_0_), channel_id=1, source_target_pairs={{0,4},{2,6},{4,0},{6,2},{8,12},{10,14},{12,8},{14,10},{16,20},{18,... | collective-permute-start | bytes 983048 | tf_op jit(solution)/shard_map/ppermute | solution.py:56
  82.2 14.5 %collective-permute-start.26 = (bf16[64,2560]{1,0:T(8,128)(2,1)S(1)}, bf16[64,2560]{1,0:T(8,128)(2,1)S(1)}, u32[]{:S(2)}, u32[]{:S(2)}) collective-permute-start(bf16[64,2560]{1,0:T(8,128)(2,1)S(1)} %pad_maximum_fusion.1.refs_0_), channel_id=1, source_target_pairs={{0,2},{2,0},{4,6},{6,4},{8,10},{10,8},{12,14},{14,12},{16,18},{18,... | collective-permute-start | bytes 983048 | tf_op jit(solution)/shard_map/ppermute | solution.py:56
  83.5 14.9 %collective-permute-start.25 = (bf16[512,128]{1,0:T(8,128)(2,1)S(1)}, bf16[512,128]{1,0:T(8,128)(2,1)S(1)}, u32[]{:S(2)}, u32[]{:S(2)}) collective-permute-start(bf16[512,128]{1,0:T(8,128)(2,1)S(1)} %get-tuple-element.70), channel_id=1, source_target_pairs={{0,24},{2,26},{4,28},{6,30},{8,16},{10,18},{12,20},{14,22},{16,8},... | collective-permute-start | bytes 393224 | tf_op jit(solution)/shard_map/ppermute | solution.py:56
  85.2 13.2 %collective-permute-start.30 = (bf16[512,128]{1,0:T(8,128)(2,1)S(1)}, bf16[512,128]{1,0:T(8,128)(2,1)S(1)}, u32[]{:S(2)}, u32[]{:S(2)}) collective-permute-start(bf16[512,128]{1,0:T(8,128)(2,1)S(1)} %get-tuple-element.71), channel_id=1, source_target_pairs={{0,16},{2,18},{4,20},{6,22},{8,24},{10,26},{12,28},{14,30},{16,0},... | collective-permute-start | bytes 393224 | tf_op jit(solution)/shard_map/ppermute | solution.py:56
  91.4 7.0 %collective-permute-start.29 = (bf16[512,128]{1,0:T(8,128)(2,1)S(1)}, bf16[512,128]{1,0:T(8,128)(2,1)S(1)}, u32[]{:S(2)}, u32[]{:S(2)}) collective-permute-start(bf16[512,128]{1,0:T(8,128)(2,1)S(1)} %get-tuple-element.72), channel_id=1, source_target_pairs={{0,8},{2,10},{4,12},{6,14},{8,0},{10,2},{12,4},{14,6},{16,24},{18,... | collective-permute-start | bytes 393224 | tf_op jit(solution)/shard_map/ppermute | solution.py:56
  (9 other events, 35.8 us)

commit v15 on v14

--- a/solution.py
+++ b/solution.py
@@ -467,9 +467,10 @@
     )
     plane_ids = with_swapped(ids.reshape(tables, groups * slots, 1, slot_rows), bals)
     wide_cot = cotangent[0].astype(f32)
-    scalars = after(scalars, share, wide_cot)
+    scalars = after(scalars, share)
     for bit in range((groups - 1).bit_length()):
         scalars = jnp.concatenate([scalars, emb_swap(scalars, 1 << bit, embs)], axis=0)
+        scalars = after(scalars, wide_cot)
 
     fetched[0] = after(fetched[0], scalars)
     pieces = [piece for one in [share] + fetched for piece in with_swapped(one, bals)]

time: 99.4 us -> 99.1 us (level)
  waiting for transfers between devices: 43.5 us -> 42.5 us
    ppermute x23, waiting for transfers between devices: 42.5 us -> 41.3 us  [emb_swap(): return lax.ppermute(value, 'emb', [(i, i ^ step) for i in range(count)])]
  transfers between devices with their start and end apart: 31 -> 31, of which waited for: 15 -> 16; matrix products, arithmetic and copies ran while one was open for 5% -> 5% of each run, Pallas kernels for 9% -> 9%
where the time goes in v15:
time: 99.1 us; the launch traced here: 98.9 us
  waiting for transfers between devices  42.5 us (43%)
  starting transfers between devices  32.4 us (33%)
  Pallas kernels  16.8 us (17%)
  other arithmetic  3.95 us (4%)
  local copies, waits for them, and re-layouts  2.42 us (2%)
    ppermute x23, waiting for transfers between devices, emb_swap(): return lax.ppermute(value, 'emb', [(i, i ^ step) for i in range(count)])  41.3 us
    ppermute x23, starting transfers between devices, emb_swap(): return lax.ppermute(value, 'emb', [(i, i ^ step) for i in range(count)])  31.3 us
    pallas_call x1, Pallas kernels, on_device(): pl.pallas_call(functools.partial(layer_kernel, groups, slots, tables, bal...  4.98 us
    pallas_call x2, Pallas kernels, on_device(): pl.pallas_call(functools.partial(place_kernel, grad_scale, steps, slots,...  3.39 us
    pallas_call x1, Pallas kernels, on_device(): pl.pallas_call(functools.partial(lookup_kernel, groups, slots, tables, ba...  3.06 us
    pallas_call x1, Pallas kernels, table_sums(): pl.pallas_call(functools.partial(scatter_kernel, groups, slots, bals), ou...  2.9 us
    pallas_call x1, Pallas kernels, on_device(): pl.pallas_call(functools.partial(rows_kernel, groups, slots, bals), out_s...  2.15 us
  transfers between devices with their start and end apart: 31, of which 16 were waited for; matrix products, arithmetic and copies ran while one was open for 5% of the time, Pallas kernels for 9%

profile of v15, /device:TPU:0, one launch (start us, length us, event | category | flops | bytes accessed | tf_op | source)
XLA Modules:
  0.0 98.9 jit_solution(6362281375748566628)
XLA Ops:
  1.6 5.1 %collective-permute-start.8 = (bf16[512,128]{1,0:T(8,128)(2,1)S(1)}, bf16[512,128]{1,0:T(8,128)(2,1)S(1)}, u32[]{:S(2)}, u32[]{:S(2)}) collective-permute-start(bf16[512,128]{1,0:T(8,128)(2,1)S(1)} %dynamic-slice_bitcast_fusion.refs_3_), channel_id=1, source_target_pairs={{0,24},{2,26},{4,28},{6,30},{8,16},{10,18},{12,20},{14,22},{16,8},... | collective-permute-start | bytes 393224 | tf_op jit(solution)/shard_map/ppermute | solution.py:56
  8.8 1.6 %collective-permute-start = (s32[1,128]{1,0:T(1,128)S(1)}, s32[1,128]{1,0:T(1,128)S(1)}, u32[]{:S(2)}, u32[]{:S(2)}) collective-permute-start(s32[1,128]{1,0:T(1,128)S(1)} %pad_add_fusion.2), channel_id=1, source_target_pairs={{0,2},{2,0},{4,6},{6,4},{8,10},{10,8},{12,14},{14,12},{16,18},{18,... | collective-permute-start | bytes 1544 | tf_op jit(solution)/shard_map/ppermute | solution.py:56
  12.3 1.7 %collective-permute-start.1 = (s32[2,128]{1,0:T(2,128)S(1)}, s32[2,128]{1,0:T(2,128)S(1)}, u32[]{:S(2)}, u32[]{:S(2)}) collective-permute-start(s32[2,128]{1,0:T(2,128)S(1)} %pad_add_fusion.1), channel_id=1, source_target_pairs={{0,4},{2,6},{4,0},{6,2},{8,12},{10,14},{12,8},{14,10},{16,20},{18,... | collective-permute-start | bytes 3080 | tf_op jit(solution)/shard_map/ppermute | solution.py:56
  19.1 3.1 %shard_map.111 = (bf16[256,128]{1,0:T(8,128)(2,1)S(1)}, bf16[256,128]{1,0:T(8,128)(2,1)S(1)}, bf16[256,128]{1,0:T(8,128)(2,1)S(1)}, bf16[256,128]{1,0:T(8,128)(2,1)S(1)}) custom-call(s32[4,128]{1,0:T(4,128)S(1)} %pad_add_fusion.refs_0_.scalar_ref, s32[4,8,1,128]{3,2,1,0:T(1,128)S(1)} %reshape.61.refs_1_, ...), custom_call_target="tpu_custom_call" | custom-call | bytes 10500000 | tf_op jit(solution)/shard_map/pallas_call | solution.py:478
  22.5 2.4 %collective-permute-start.10 = (bf16[256,128]{1,0:T(8,128)(2,1)S(1)}, bf16[256,128]{1,0:T(8,128)(2,1)S(1)}, u32[]{:S(2)}, u32[]{:S(2)}) collective-permute-start(bf16[256,128]{1,0:T(8,128)(2,1)S(1)} %get-tuple-element.44), channel_id=1, source_target_pairs={{0,6},{2,4},{4,2},{6,0},{8,14},{10,12},{12,10},{14,8},{16,22},{18,... | collective-permute-start | bytes 196616 | tf_op jit(solution)/shard_map/ppermute | solution.py:56
  26.0 1.7 %collective-permute-done.10.refs_0_.refs_10_ = bf16[256,128]{1,0:T(8,128)(2,1)S(1)} collective-permute-done((bf16[256,128]{1,0:T(8,128)(2,1)S(1)}, bf16[256,128]{1,0:T(8,128)(2,1)S(1)}, u32[]{:S(2)}, u32[]{:S(2)}) %collective-permute-start.10) | collective-permute-done | bytes 65568 | tf_op jit(solution)/shard_map/ppermute | solution.py:56
  29.8 5.0 %shard_map.112 = (bf16[256,2048]{1,0:T(8,128)(2,1)S(1)}, f32[256,512]{1,0:T(8,128)S(1)}, f32[256,128]{1,0:T(8,128)S(1)}, bf16[256,512]{1,0:T(8,128)(2,1)S(1)}, b...) custom-call(s32[4,128]{1,0:T(4,128)S(1)} %pad_add_fusion.refs_0_.scalar_ref, ...), custom_call_target="tpu_custom_call" | custom-call | bytes 24500000 | tf_op jit(solution)/shard_map/pallas_call | solution.py:492
  34.8 2.1 %shard_map.113 = (bf16[256,512]{1,0:T(8,128)(2,1)}, bf16[256,128]{1,0:T(8,128)(2,1)S(1)}, bf16[256,128]{1,0:T(8,128)(2,1)S(1)}, bf16[256,128]{1,0:T(8,128)(2,1)S(1)}, bf16[256,128]{1,0:T(8,128)(2,1)S(1)}) custom-call(s32[4,128]{1,0:T(4,128)S(1)} %pad_add_fusion.refs_0_.scalar_ref, bf16[256,2048]{1,0:T(8,128)(2,1)S(1)} %get-tuple-element.49.refs_0_, ...), custom_call_target="tpu_custom_call" | custom-call | bytes 7000000 | tf_op jit(solution)/shard_map/pallas_call | solution.py:519
  38.2 1.6 %collective-permute-start.15 = (bf16[64,3072]{1,0:T(8,128)(2,1)S(1)}, bf16[64,3072]{1,0:T(8,128)(2,1)S(1)}, u32[]{:S(2)}, u32[]{:S(2)}) collective-permute-start(bf16[64,3072]{1,0:T(8,128)(2,1)S(1)} %get-tuple-element.59), channel_id=1, source_target_pairs={{0,6},{2,4},{4,2},{6,0},{8,14},{10,12},{12,10},{14,8},{16,22},{18,... | collective-permute-start | bytes 1179656 | tf_op jit(solution)/shard_map/ppermute | solution.py:56
  41.7 9.4 %collective-permute-done.15.refs_3_ = bf16[64,3072]{1,0:T(8,128)(2,1)S(1)} collective-permute-done((bf16[64,3072]{1,0:T(8,128)(2,1)S(1)}, bf16[64,3072]{1,0:T(8,128)(2,1)S(1)}, u32[]{:S(2)}, u32[]{:S(2)}) %collective-permute-start.15) | collective-permute-done | bytes 393248 | tf_op jit(solution)/shard_map/ppermute | solution.py:56
  51.1 7.6 %collective-permute-done.16.refs_4_ = bf16[64,3072]{1,0:T(8,128)(2,1)S(1)} collective-permute-done((bf16[64,3072]{1,0:T(8,128)(2,1)S(1)}, bf16[64,3072]{1,0:T(8,128)(2,1)S(1)}, u32[]{:S(2)}, u32[]{:S(2)}) %collective-permute-start.16) | collective-permute-done | bytes 393248 | tf_op jit(solution)/shard_map/ppermute | solution.py:56
  59.0 2.8 %collective-permute-start.19 = (bf16[16,2560]{1,0:T(8,128)(2,1)S(1)}, bf16[16,2560]{1,0:T(8,128)(2,1)S(1)}, u32[]{:S(2)}, u32[]{:S(2)}) collective-permute-start(bf16[16,2560]{1,0:T(8,128)(2,1)S(1)} %get-tuple-element.77), channel_id=1, source_target_pairs={{0,24},{2,26},{4,28},{6,30},{8,16},{10,18},{12,20},{14,22},{16,8},... | collective-permute-start | bytes 245768 | tf_op jit(solution)/shard_map/ppermute | solution.py:56
  61.8 1.7 %collective-permute-start.20 = (bf16[16,2560]{1,0:T(8,128)(2,1)S(1)}, bf16[16,2560]{1,0:T(8,128)(2,1)S(1)}, u32[]{:S(2)}, u32[]{:S(2)}) collective-permute-start(bf16[16,2560]{1,0:T(8,128)(2,1)S(1)} %get-tuple-element.79), channel_id=1, source_target_pairs={{0,8},{2,10},{4,12},{6,14},{8,0},{10,2},{12,4},{14,6},{16,24},{18,... | collective-permute-start | bytes 245768 | tf_op jit(solution)/shard_map/ppermute | solution.py:56
  63.5 2.9 %shard_map.115 = (bf16[4,512,128]{2,1,0:T(8,128)(2,1)S(1)}, bf16[4,512,128]{2,1,0:T(8,128)(2,1)S(1)}) custom-call(s32[4,128]{1,0:T(4,128)S(1)} %pad_add_fusion.refs_0_.scalar_ref, s32[4,8,1,128]{3,2,1,0:T(1,128)S(1)} %reshape.61.refs_1_, s32[4,8,1,128]{3,2,1,0:T(1,128)S(1)} %collective-permute-done.2.refs_2_, ...), custom_call_target="tpu_custom_call" | custom-call | bytes 10500000 | tf_op jit(solution)/shard_map/pallas_call | solution.py:541
  66.5 2.2 %collective-permute-done.21 = bf16[16,2560]{1,0:T(8,128)(2,1)S(1)} collective-permute-done((bf16[16,2560]{1,0:T(8,128)(2,1)S(1)}, bf16[16,2560]{1,0:T(8,128)(2,1)S(1)}, u32[]{:S(2)}, u32[]{:S(2)}) %collective-permute-start.21) | collective-permute-done | bytes 81952 | tf_op jit(solution)/shard_map/ppermute | solution.py:56
  68.7 2.7 %collective-permute-start.24 = (bf16[16,2560]{1,0:T(8,128)(2,1)S(1)}, bf16[16,2560]{1,0:T(8,128)(2,1)S(1)}, u32[]{:S(2)}, u32[]{:S(2)}) collective-permute-start(bf16[16,2560]{1,0:T(8,128)(2,1)S(1)} %add_convert_fusion.2), channel_id=1, source_target_pairs={{0,24},{2,26},{4,28},{6,30},{8,16},{10,18},{12,20},{14,22},{16,8},... | collective-permute-start | bytes 245768 | tf_op jit(solution)/shard_map/ppermute | solution.py:56
  71.4 1.7 %collective-permute-start.22 = (bf16[16,2560]{1,0:T(8,128)(2,1)S(1)}, bf16[16,2560]{1,0:T(8,128)(2,1)S(1)}, u32[]{:S(2)}, u32[]{:S(2)}) collective-permute-start(bf16[16,2560]{1,0:T(8,128)(2,1)S(1)} %add_convert_fusion.2), channel_id=1, source_target_pairs={{0,8},{2,10},{4,12},{6,14},{8,0},{10,2},{12,4},{14,6},{16,24},{18,... | collective-permute-start | bytes 245768 | tf_op jit(solution)/shard_map/ppermute | solution.py:56
  73.2 2.8 %collective-permute-done.24 = bf16[16,2560]{1,0:T(8,128)(2,1)S(1)} collective-permute-done((bf16[16,2560]{1,0:T(8,128)(2,1)S(1)}, bf16[16,2560]{1,0:T(8,128)(2,1)S(1)}, u32[]{:S(2)}, u32[]{:S(2)}) %collective-permute-start.24) | collective-permute-done | bytes 81952 | tf_op jit(solution)/shard_map/ppermute | solution.py:56
  75.9 2.9 %collective-permute-done.23 = bf16[16,2560]{1,0:T(8,128)(2,1)S(1)} collective-permute-done((bf16[16,2560]{1,0:T(8,128)(2,1)S(1)}, bf16[16,2560]{1,0:T(8,128)(2,1)S(1)}, u32[]{:S(2)}, u32[]{:S(2)}) %collective-permute-start.23) | collective-permute-done | bytes 81952 | tf_op jit(solution)/shard_map/ppermute | solution.py:56
  82.6 2.2 %collective-permute-start.25 = (bf16[512,128]{1,0:T(8,128)(2,1)S(1)}, bf16[512,128]{1,0:T(8,128)(2,1)S(1)}, u32[]{:S(2)}, u32[]{:S(2)}) collective-permute-start(bf16[512,128]{1,0:T(8,128)(2,1)S(1)} %get-tuple-element.74), channel_id=1, source_target_pairs={{0,24},{2,26},{4,28},{6,30},{8,16},{10,18},{12,20},{14,22},{16,8},... | collective-permute-start | bytes 393224 | tf_op jit(solution)/shard_map/ppermute | solution.py:56
  84.9 5.6 %collective-permute-done.28.refs_1_ = bf16[64,2560]{1,0:T(8,128)(2,1)S(1)} collective-permute-done((bf16[64,2560]{1,0:T(8,128)(2,1)S(1)}, bf16[64,2560]{1,0:T(8,128)(2,1)S(1)}, u32[]{:S(2)}, u32[]{:S(2)}) %collective-permute-start.28) | collective-permute-done | bytes 327712 | tf_op jit(solution)/shard_map/ppermute | solution.py:56
  90.9 1.7 %shard_map.116 = (f32[256,2048]{1,0:T(8,128)}, f32[256,512]{1,0:T(8,128)}) custom-call(s32[4,128]{1,0:T(4,128)S(1)} %pad_add_fusion.refs_0_.scalar_ref, bf16[64,2560]{1,0:T(8,128)(2,1)S(1)} %pad_maximum_fusion.1.refs_0_, bf16[64,2560]{1,0:T(8,128)(2,1)S(1)} %collective-permute-done.28.refs_1_), custom_call_target="tpu_custom_call" | custom-call | bytes 3500000 | tf_op jit(solution)/shard_map/pallas_call | solution.py:588
  92.7 3.7 %collective-permute-done.27.refs_1_ = bf16[64,2560]{1,0:T(8,128)(2,1)S(1)} collective-permute-done((bf16[64,2560]{1,0:T(8,128)(2,1)S(1)}, bf16[64,2560]{1,0:T(8,128)(2,1)S(1)}, u32[]{:S(2)}, u32[]{:S(2)}) %collective-permute-start.27) | collective-permute-done | bytes 327712 | tf_op jit(solution)/shard_map/ppermute | solution.py:56
  96.4 1.7 %shard_map.117 = (f32[256,2048]{1,0:T(8,128)}, f32[256,512]{1,0:T(8,128)}) custom-call(s32[4,128]{1,0:T(4,128)S(1)} %pad_add_fusion.refs_0_.scalar_ref, bf16[64,2560]{1,0:T(8,128)(2,1)S(1)} %collective-permute-done.26.refs_0_, bf16[64,2560]{1,0:T(8,128)(2,1)S(1)} %collective-permute-done.27.refs_1_, ...), custom_call_target="tpu_custom_call", output_to_operand_aliasing={{0}: (3, {}), {1}: (4, {})} | custom-call | bytes 3500000 | tf_op jit(solution)/shard_map/pallas_call | solution.py:588
  (65 shorter events, 22.1 us)
Async XLA Ops:
  1.6 14.9 %collective-permute-start.8 = (bf16[512,128]{1,0:T(8,128)(2,1)S(1)}, bf16[512,128]{1,0:T(8,128)(2,1)S(1)}, u32[]{:S(2)}, u32[]{:S(2)}) collective-permute-start(bf16[512,128]{1,0:T(8,128)(2,1)S(1)} %dynamic-slice_bitcast_fusion.refs_3_), channel_id=1, source_target_pairs={{0,24},{2,26},{4,28},{6,30},{8,16},{10,18},{12,20},{14,22},{16,8},... | collective-permute-start | bytes 393224 | tf_op jit(solution)/shard_map/ppermute | solution.py:56
  6.7 11.1 %collective-permute-start.6 = (bf16[512,128]{1,0:T(8,128)(2,1)S(1)}, bf16[512,128]{1,0:T(8,128)(2,1)S(1)}, u32[]{:S(2)}, u32[]{:S(2)}) collective-permute-start(bf16[512,128]{1,0:T(8,128)(2,1)S(1)} %dynamic-slice_bitcast_fusion.refs_3_), channel_id=1, source_target_pairs={{0,16},{2,18},{4,20},{6,22},{8,24},{10,26},{12,28},{14,30},{16,0},... | collective-permute-start | bytes 393224 | tf_op jit(solution)/shard_map/ppermute | solution.py:56
  6.7 9.2 %collective-permute-start.4 = (bf16[512,128]{1,0:T(8,128)(2,1)S(1)}, bf16[512,128]{1,0:T(8,128)(2,1)S(1)}, u32[]{:S(2)}, u32[]{:S(2)}) collective-permute-start(bf16[512,128]{1,0:T(8,128)(2,1)S(1)} %dynamic-slice_bitcast_fusion.refs_3_), channel_id=1, source_target_pairs={{0,8},{2,10},{4,12},{6,14},{8,0},{10,2},{12,4},{14,6},{16,24},{18,... | collective-permute-start | bytes 393224 | tf_op jit(solution)/shard_map/ppermute | solution.py:56
  7.4 11.5 %collective-permute-start.3 = (bf16[512,128]{1,0:T(8,128)(2,1)S(1)}, bf16[512,128]{1,0:T(8,128)(2,1)S(1)}, u32[]{:S(2)}, u32[]{:S(2)}) collective-permute-start(bf16[512,128]{1,0:T(8,128)(2,1)S(1)} %dynamic-slice_bitcast_fusion.refs_3_), channel_id=1, source_target_pairs={{0,1},{1,0},{2,3},{3,2},{4,5},{5,4},{6,7},{7,6},{8,9},{9,8},{10,11... | collective-permute-start | bytes 393224 | tf_op jit(solution)/shard_map/ppermute | solution.py:48
  22.2 7.6 %collective-permute-start.13 = (bf16[256,2560]{1,0:T(8,128)(2,1)S(1)}, bf16[256,2560]{1,0:T(8,128)(2,1)S(1)}, u32[]{:S(2)}, u32[]{:S(2)}) collective-permute-start(bf16[256,2560]{1,0:T(8,128)(2,1)S(1)} %pad_maximum_fusion.refs_4_.refs_5_), channel_id=1, source_target_pairs={{0,1},{1,0},{2,3},{3,2},{4,5},{5,4},{6,7},{7,6},{8,9},{9,8},{10,11... | collective-permute-start | bytes 3932168 | tf_op jit(solution)/shard_map/ppermute | solution.py:48
  22.5 5.2 %collective-permute-start.10 = (bf16[256,128]{1,0:T(8,128)(2,1)S(1)}, bf16[256,128]{1,0:T(8,128)(2,1)S(1)}, u32[]{:S(2)}, u32[]{:S(2)}) collective-permute-start(bf16[256,128]{1,0:T(8,128)(2,1)S(1)} %get-tuple-element.44), channel_id=1, source_target_pairs={{0,6},{2,4},{4,2},{6,0},{8,14},{10,12},{12,10},{14,8},{16,22},{18,... | collective-permute-start | bytes 196616 | tf_op jit(solution)/shard_map/ppermute | solution.py:56
  25.0 4.3 %collective-permute-start.11 = (bf16[256,128]{1,0:T(8,128)(2,1)S(1)}, bf16[256,128]{1,0:T(8,128)(2,1)S(1)}, u32[]{:S(2)}, u32[]{:S(2)}) collective-permute-start(bf16[256,128]{1,0:T(8,128)(2,1)S(1)} %get-tuple-element.45), channel_id=1, source_target_pairs={{0,4},{2,6},{4,0},{6,2},{8,12},{10,14},{12,8},{14,10},{16,20},{18,... | collective-permute-start | bytes 196616 | tf_op jit(solution)/shard_map/ppermute | solution.py:56
  25.5 4.3 %collective-permute-start.12 = (bf16[256,128]{1,0:T(8,128)(2,1)S(1)}, bf16[256,128]{1,0:T(8,128)(2,1)S(1)}, u32[]{:S(2)}, u32[]{:S(2)}) collective-permute-start(bf16[256,128]{1,0:T(8,128)(2,1)S(1)} %get-tuple-element.46), channel_id=1, source_target_pairs={{0,2},{2,0},{4,6},{6,4},{8,10},{10,8},{12,14},{14,12},{16,18},{18,... | collective-permute-start | bytes 196616 | tf_op jit(solution)/shard_map/ppermute | solution.py:56
  38.2 13.0 %collective-permute-start.15 = (bf16[64,3072]{1,0:T(8,128)(2,1)S(1)}, bf16[64,3072]{1,0:T(8,128)(2,1)S(1)}, u32[]{:S(2)}, u32[]{:S(2)}) collective-permute-start(bf16[64,3072]{1,0:T(8,128)(2,1)S(1)} %get-tuple-element.59), channel_id=1, source_target_pairs={{0,6},{2,4},{4,2},{6,0},{8,14},{10,12},{12,10},{14,8},{16,22},{18,... | collective-permute-start | bytes 1179656 | tf_op jit(solution)/shard_map/ppermute | solution.py:56
  39.7 19.0 %collective-permute-start.16 = (bf16[64,3072]{1,0:T(8,128)(2,1)S(1)}, bf16[64,3072]{1,0:T(8,128)(2,1)S(1)}, u32[]{:S(2)}, u32[]{:S(2)}) collective-permute-start(bf16[64,3072]{1,0:T(8,128)(2,1)S(1)} %get-tuple-element.60), channel_id=1, source_target_pairs={{0,4},{2,6},{4,0},{6,2},{8,12},{10,14},{12,8},{14,10},{16,20},{18,... | collective-permute-start | bytes 1179656 | tf_op jit(solution)/shard_map/ppermute | solution.py:56
  40.6 18.3 %collective-permute-start.17 = (bf16[64,3072]{1,0:T(8,128)(2,1)S(1)}, bf16[64,3072]{1,0:T(8,128)(2,1)S(1)}, u32[]{:S(2)}, u32[]{:S(2)}) collective-permute-start(bf16[64,3072]{1,0:T(8,128)(2,1)S(1)} %get-tuple-element.61), channel_id=1, source_target_pairs={{0,2},{2,0},{4,6},{6,4},{8,10},{10,8},{12,14},{14,12},{16,18},{18,... | collective-permute-start | bytes 1179656 | tf_op jit(solution)/shard_map/ppermute | solution.py:56
  59.0 7.4 %collective-permute-start.19 = (bf16[16,2560]{1,0:T(8,128)(2,1)S(1)}, bf16[16,2560]{1,0:T(8,128)(2,1)S(1)}, u32[]{:S(2)}, u32[]{:S(2)}) collective-permute-start(bf16[16,2560]{1,0:T(8,128)(2,1)S(1)} %get-tuple-element.77), channel_id=1, source_target_pairs={{0,24},{2,26},{4,28},{6,30},{8,16},{10,18},{12,20},{14,22},{16,8},... | collective-permute-start | bytes 245768 | tf_op jit(solution)/shard_map/ppermute | solution.py:56
  61.8 6.9 %collective-permute-start.21 = (bf16[16,2560]{1,0:T(8,128)(2,1)S(1)}, bf16[16,2560]{1,0:T(8,128)(2,1)S(1)}, u32[]{:S(2)}, u32[]{:S(2)}) collective-permute-start(bf16[16,2560]{1,0:T(8,128)(2,1)S(1)} %get-tuple-element.78), channel_id=1, source_target_pairs={{0,16},{2,18},{4,20},{6,22},{8,24},{10,26},{12,28},{14,30},{16,0},... | collective-permute-start | bytes 245768 | tf_op jit(solution)/shard_map/ppermute | solution.py:56
  61.8 6.9 %collective-permute-start.20 = (bf16[16,2560]{1,0:T(8,128)(2,1)S(1)}, bf16[16,2560]{1,0:T(8,128)(2,1)S(1)}, u32[]{:S(2)}, u32[]{:S(2)}) collective-permute-start(bf16[16,2560]{1,0:T(8,128)(2,1)S(1)} %get-tuple-element.79), channel_id=1, source_target_pairs={{0,8},{2,10},{4,12},{6,14},{8,0},{10,2},{12,4},{14,6},{16,24},{18,... | collective-permute-start | bytes 245768 | tf_op jit(solution)/shard_map/ppermute | solution.py:56
  66.4 16.1 %collective-permute-start.18 = (bf16[4,512,128]{2,1,0:T(8,128)(2,1)S(1)}, bf16[4,512,128]{2,1,0:T(8,128)(2,1)S(1)}, u32[]{:S(2)}, u32[]{:S(2)}) collective-permute-start(bf16[4,512,128]{2,1,0:T(8,128)(2,1)S(1)} %get-tuple-element.64), channel_id=1, source_target_pairs={{0,1},{1,0},{2,3},{3,2},{4,5},{5,4},{6,7},{7,6},{8,9},{9,8},{10,11... | collective-permute-start | bytes 1572872 | tf_op jit(solution)/shard_map/ppermute | solution.py:48
  68.7 7.2 %collective-permute-start.24 = (bf16[16,2560]{1,0:T(8,128)(2,1)S(1)}, bf16[16,2560]{1,0:T(8,128)(2,1)S(1)}, u32[]{:S(2)}, u32[]{:S(2)}) collective-permute-start(bf16[16,2560]{1,0:T(8,128)(2,1)S(1)} %add_convert_fusion.2), channel_id=1, source_target_pairs={{0,24},{2,26},{4,28},{6,30},{8,16},{10,18},{12,20},{14,22},{16,8},... | collective-permute-start | bytes 245768 | tf_op jit(solution)/shard_map/ppermute | solution.py:56
  71.4 7.4 %collective-permute-start.23 = (bf16[16,2560]{1,0:T(8,128)(2,1)S(1)}, bf16[16,2560]{1,0:T(8,128)(2,1)S(1)}, u32[]{:S(2)}, u32[]{:S(2)}) collective-permute-start(bf16[16,2560]{1,0:T(8,128)(2,1)S(1)} %add_convert_fusion.2), channel_id=1, source_target_pairs={{0,16},{2,18},{4,20},{6,22},{8,24},{10,26},{12,28},{14,30},{16,0},... | collective-permute-start | bytes 245768 | tf_op jit(solution)/shard_map/ppermute | solution.py:56
  71.4 7.4 %collective-permute-start.22 = (bf16[16,2560]{1,0:T(8,128)(2,1)S(1)}, bf16[16,2560]{1,0:T(8,128)(2,1)S(1)}, u32[]{:S(2)}, u32[]{:S(2)}) collective-permute-start(bf16[16,2560]{1,0:T(8,128)(2,1)S(1)} %add_convert_fusion.2), channel_id=1, source_target_pairs={{0,8},{2,10},{4,12},{6,14},{8,0},{10,2},{12,4},{14,6},{16,24},{18,... | collective-permute-start | bytes 245768 | tf_op jit(solution)/shard_map/ppermute | solution.py:56
  78.9 11.6 %collective-permute-start.28 = (bf16[64,2560]{1,0:T(8,128)(2,1)S(1)}, bf16[64,2560]{1,0:T(8,128)(2,1)S(1)}, u32[]{:S(2)}, u32[]{:S(2)}) collective-permute-start(bf16[64,2560]{1,0:T(8,128)(2,1)S(1)} %pad_maximum_fusion.1.refs_0_), channel_id=1, source_target_pairs={{0,6},{2,4},{4,2},{6,0},{8,14},{10,12},{12,10},{14,8},{16,22},{18,... | collective-permute-start | bytes 983048 | tf_op jit(solution)/shard_map/ppermute | solution.py:56
  80.4 15.9 %collective-permute-start.27 = (bf16[64,2560]{1,0:T(8,128)(2,1)S(1)}, bf16[64,2560]{1,0:T(8,128)(2,1)S(1)}, u32[]{:S(2)}, u32[]{:S(2)}) collective-permute-start(bf16[64,2560]{1,0:T(8,128)(2,1)S(1)} %pad_maximum_fusion.1.refs_0_), channel_id=1, source_target_pairs={{0,4},{2,6},{4,0},{6,2},{8,12},{10,14},{12,8},{14,10},{16,20},{18,... | collective-permute-start | bytes 983048 | tf_op jit(solution)/shard_map/ppermute | solution.py:56
  81.3 15.1 %collective-permute-start.26 = (bf16[64,2560]{1,0:T(8,128)(2,1)S(1)}, bf16[64,2560]{1,0:T(8,128)(2,1)S(1)}, u32[]{:S(2)}, u32[]{:S(2)}) collective-permute-start(bf16[64,2560]{1,0:T(8,128)(2,1)S(1)} %pad_maximum_fusion.1.refs_0_), channel_id=1, source_target_pairs={{0,2},{2,0},{4,6},{6,4},{8,10},{10,8},{12,14},{14,12},{16,18},{18,... | collective-permute-start | bytes 983048 | tf_op jit(solution)/shard_map/ppermute | solution.py:56
  82.6 15.4 %collective-permute-start.25 = (bf16[512,128]{1,0:T(8,128)(2,1)S(1)}, bf16[512,128]{1,0:T(8,128)(2,1)S(1)}, u32[]{:S(2)}, u32[]{:S(2)}) collective-permute-start(bf16[512,128]{1,0:T(8,128)(2,1)S(1)} %get-tuple-element.74), channel_id=1, source_target_pairs={{0,24},{2,26},{4,28},{6,30},{8,16},{10,18},{12,20},{14,22},{16,8},... | collective-permute-start | bytes 393224 | tf_op jit(solution)/shard_map/ppermute | solution.py:56
  84.9 13.2 %collective-permute-start.30 = (bf16[512,128]{1,0:T(8,128)(2,1)S(1)}, bf16[512,128]{1,0:T(8,128)(2,1)S(1)}, u32[]{:S(2)}, u32[]{:S(2)}) collective-permute-start(bf16[512,128]{1,0:T(8,128)(2,1)S(1)} %get-tuple-element.75), channel_id=1, source_target_pairs={{0,16},{2,18},{4,20},{6,22},{8,24},{10,26},{12,28},{14,30},{16,0},... | collective-permute-start | bytes 393224 | tf_op jit(solution)/shard_map/ppermute | solution.py:56
  90.5 7.6 %collective-permute-start.29 = (bf16[512,128]{1,0:T(8,128)(2,1)S(1)}, bf16[512,128]{1,0:T(8,128)(2,1)S(1)}, u32[]{:S(2)}, u32[]{:S(2)}) collective-permute-start(bf16[512,128]{1,0:T(8,128)(2,1)S(1)} %get-tuple-element.76), channel_id=1, source_target_pairs={{0,8},{2,10},{4,12},{6,14},{8,0},{10,2},{12,4},{14,6},{16,24},{18,... | collective-permute-start | bytes 393224 | tf_op jit(solution)/shard_map/ppermute | solution.py:56
  (9 other events, 38.2 us)

commit v16 on v15

--- a/solution.py
+++ b/solution.py
@@ -390,9 +390,13 @@
                 out[:, at : at + columns] = grad[index * height : (index + 1) * height, :]
 
 
-def place_kernel(scale, steps, slots, tables, bals, unit, scalar_ref, *refs):
+def place_kernel(scale, steps, slots, tables, bals, unit, table_scale, scalar_ref, *refs):
     pieces = refs[: len(steps)]
-    in_ref, out_ref, scaled_ref, sems = refs[-4:]
+    *refs, scaled_ref, sems = refs[len(steps) :]
+    if table_scale is None:
+        in_ref, out_ref = refs[-2:]
+    else:
+        in_ref, out_ref, sum_ref = refs[-3:]
     _, group_here, table_here = Scalars(scalar_ref, 0, bals, slots).place()
     features = in_ref.shape[1]
     copies = []
@@ -411,6 +415,11 @@
                 )
             )
             copies[-1].start()
+    if table_scale is not None:
+        total = refs[0][0].astype(f32)
+        for ref in refs[1:tables]:
+            total = total + ref[...].astype(f32)
+        sum_ref[...] = total * table_scale
     for copy in copies:
         copy.wait()
 
@@ -575,9 +584,6 @@
         sums = table_sums([grads[0]] + [emb_swap(grads[step], step, embs) for step in range(1, groups)])
         own_sums = over_cores(sums)
         swapped = [emb_swap(own_sums[step], step * groups, embs) for step in range(1, tables)]
-    table_sum = swapped[-1].astype(f32)
-    for value in swapped[:-1] + [own_sums[0]]:
-        table_sum = table_sum + value.astype(f32)
     table_scale = (distinct / (bals * item_ids.shape[1])) ** 0.5
 
     if owned:
@@ -585,28 +591,38 @@
         for steps in ([0] + list(range(groups - 1, 1, -1))[: groups // 2 - 1], None):
             steps = steps or [step for step in range(1, groups) if step not in done]
             done = steps
+            extra = [own_sums] + swapped if totals else []
+            sum_shape = [jax.ShapeDtypeStruct((part, columns), f32)] if totals else []
+            sum_scale = table_scale if totals else None
             totals = pl.pallas_call(
-                functools.partial(place_kernel, grad_scale, steps, slots, tables, bals, unit),
+                functools.partial(place_kernel, grad_scale, steps, slots, tables, bals, unit, sum_scale),
                 out_shape=[
                     jax.ShapeDtypeStruct((weight_part, features), f32),
                     jax.ShapeDtypeStruct((weight_part, width), f32),
-                ],
-                in_specs=[SMEM] + [VMEM] * len(steps) + [HBM] * len(totals),
-                out_specs=[HBM] * 2,
+                ]
+                + sum_shape,
+                in_specs=[SMEM] + [VMEM] * (len(steps) + len(extra)) + [HBM] * len(totals),
+                out_specs=[HBM] * 2 + [VMEM] * len(sum_shape),
                 scratch_shapes=[
                     pltpu.VMEM((len(steps) * tables * unit, features + width), f32),
                     pltpu.SemaphoreType.DMA((len(steps), 2)),
                 ],
-                input_output_aliases={1 + len(steps) + index: index for index in range(len(totals))},
+                input_output_aliases={
+                    1 + len(steps) + len(extra) + index: index for index in range(len(totals))
+                },
                 cost_estimate=estimate(1),
                 compiler_params=room(12),
-            )(scalars, *[back[step] for step in steps], *totals)
-        total_in, total_out = totals
+            )(scalars, *[back[step] for step in steps], *extra, *totals)
+        total_in, total_out, table_sum = totals
     else:
         total = lax.psum(over_cores(results).astype(f32), "emb") * grad_scale
         total_in, total_out = total[:, :features], total[:, features:]
-
-    return layer_out[None], (table_sum * table_scale)[None], total_in, total_out
+        table_sum = own_sums[0].astype(f32)
+        for value in swapped:
+            table_sum = table_sum + value.astype(f32)
+        table_sum = table_sum * table_scale
+
+    return layer_out[None], table_sum[None], total_in, total_out
 
 
 def solution(mesh):

time: 99.1 us -> 99.8 us (level)
  transfers between devices with their start and end apart: 31 -> 31, of which waited for: 16 -> 17; matrix products, arithmetic and copies ran while one was open for 5% -> 4% of each run, Pallas kernels for 9% -> 7%
where the time goes in v16:
time: 99.8 us; the launch traced here: 99.6 us
  waiting for transfers between devices  43.3 us (43%)
  starting transfers between devices  32.4 us (32%)
  Pallas kernels  17.5 us (18%)
  other arithmetic  3.17 us (3%)
  local copies, waits for them, and re-layouts  2.42 us (2%)
    ppermute x23, waiting for transfers between devices, emb_swap(): return lax.ppermute(value, 'emb', [(i, i ^ step) for i in range(count)])  42.1 us
    ppermute x23, starting transfers between devices, emb_swap(): return lax.ppermute(value, 'emb', [(i, i ^ step) for i in range(count)])  31.2 us
    pallas_call x1, Pallas kernels, on_device(): pl.pallas_call(functools.partial(layer_kernel, groups, slots, tables, bal...  4.98 us
    pallas_call x2, Pallas kernels, on_device(): pl.pallas_call(functools.partial(place_kernel, grad_scale, steps, slots,...  4.09 us
    pallas_call x1, Pallas kernels, on_device(): pl.pallas_call(functools.partial(lookup_kernel, groups, slots, tables, ba...  3.06 us
    pallas_call x1, Pallas kernels, table_sums(): pl.pallas_call(functools.partial(scatter_kernel, groups, slots, bals), ou...  2.9 us
    pallas_call x1, Pallas kernels, on_device(): pl.pallas_call(functools.partial(rows_kernel, groups, slots, bals), out_s...  2.15 us
  transfers between devices with their start and end apart: 31, of which 17 were waited for; matrix products, arithmetic and copies ran while one was open for 4% of the time, Pallas kernels for 7%

profile of v16, /device:TPU:0, one launch (start us, length us, event | category | flops | bytes accessed | tf_op | source)
XLA Modules:
  0.0 99.6 jit_solution(8983767119465673440)
XLA Ops:
  1.6 5.1 %collective-permute-start.8 = (bf16[512,128]{1,0:T(8,128)(2,1)S(1)}, bf16[512,128]{1,0:T(8,128)(2,1)S(1)}, u32[]{:S(2)}, u32[]{:S(2)}) collective-permute-start(bf16[512,128]{1,0:T(8,128)(2,1)S(1)} %dynamic-slice_bitcast_fusion.refs_3_), channel_id=1, source_target_pairs={{0,24},{2,26},{4,28},{6,30},{8,16},{10,18},{12,20},{14,22},{16,8},... | collective-permute-start | bytes 393224 | tf_op jit(solution)/shard_map/ppermute | solution.py:56
  8.8 1.6 %collective-permute-start = (s32[1,128]{1,0:T(1,128)S(1)}, s32[1,128]{1,0:T(1,128)S(1)}, u32[]{:S(2)}, u32[]{:S(2)}) collective-permute-start(s32[1,128]{1,0:T(1,128)S(1)} %pad_add_fusion.2), channel_id=1, source_target_pairs={{0,2},{2,0},{4,6},{6,4},{8,10},{10,8},{12,14},{14,12},{16,18},{18,... | collective-permute-start | bytes 1544 | tf_op jit(solution)/shard_map/ppermute | solution.py:56
  12.3 1.7 %collective-permute-start.1 = (s32[2,128]{1,0:T(2,128)S(1)}, s32[2,128]{1,0:T(2,128)S(1)}, u32[]{:S(2)}, u32[]{:S(2)}) collective-permute-start(s32[2,128]{1,0:T(2,128)S(1)} %pad_add_fusion.1), channel_id=1, source_target_pairs={{0,4},{2,6},{4,0},{6,2},{8,12},{10,14},{12,8},{14,10},{16,20},{18,... | collective-permute-start | bytes 3080 | tf_op jit(solution)/shard_map/ppermute | solution.py:56
  19.1 3.1 %shard_map.111 = (bf16[256,128]{1,0:T(8,128)(2,1)S(1)}, bf16[256,128]{1,0:T(8,128)(2,1)S(1)}, bf16[256,128]{1,0:T(8,128)(2,1)S(1)}, bf16[256,128]{1,0:T(8,128)(2,1)S(1)}) custom-call(s32[4,128]{1,0:T(4,128)S(1)} %pad_add_fusion.refs_0_.scalar_ref, s32[4,8,1,128]{3,2,1,0:T(1,128)S(1)} %reshape.59.refs_1_, ...), custom_call_target="tpu_custom_call" | custom-call | bytes 10500000 | tf_op jit(solution)/shard_map/pallas_call | solution.py:487
  22.5 2.4 %collective-permute-start.10 = (bf16[256,128]{1,0:T(8,128)(2,1)S(1)}, bf16[256,128]{1,0:T(8,128)(2,1)S(1)}, u32[]{:S(2)}, u32[]{:S(2)}) collective-permute-start(bf16[256,128]{1,0:T(8,128)(2,1)S(1)} %get-tuple-element.45), channel_id=1, source_target_pairs={{0,6},{2,4},{4,2},{6,0},{8,14},{10,12},{12,10},{14,8},{16,22},{18,... | collective-permute-start | bytes 196616 | tf_op jit(solution)/shard_map/ppermute | solution.py:56
  26.0 1.7 %collective-permute-done.10.refs_0_.refs_10_ = bf16[256,128]{1,0:T(8,128)(2,1)S(1)} collective-permute-done((bf16[256,128]{1,0:T(8,128)(2,1)S(1)}, bf16[256,128]{1,0:T(8,128)(2,1)S(1)}, u32[]{:S(2)}, u32[]{:S(2)}) %collective-permute-start.10) | collective-permute-done | bytes 65568 | tf_op jit(solution)/shard_map/ppermute | solution.py:56
  29.8 5.0 %shard_map.112 = (bf16[256,2048]{1,0:T(8,128)(2,1)S(1)}, f32[256,512]{1,0:T(8,128)S(1)}, f32[256,128]{1,0:T(8,128)S(1)}, bf16[256,512]{1,0:T(8,128)(2,1)S(1)}, b...) custom-call(s32[4,128]{1,0:T(4,128)S(1)} %pad_add_fusion.refs_0_.scalar_ref, ...), custom_call_target="tpu_custom_call" | custom-call | bytes 24500000 | tf_op jit(solution)/shard_map/pallas_call | solution.py:501
  34.8 2.1 %shard_map.113 = (bf16[256,512]{1,0:T(8,128)(2,1)}, bf16[256,128]{1,0:T(8,128)(2,1)S(1)}, bf16[256,128]{1,0:T(8,128)(2,1)S(1)}, bf16[256,128]{1,0:T(8,128)(2,1)S(1)}, bf16[256,128]{1,0:T(8,128)(2,1)S(1)}) custom-call(s32[4,128]{1,0:T(4,128)S(1)} %pad_add_fusion.refs_0_.scalar_ref, bf16[256,2048]{1,0:T(8,128)(2,1)S(1)} %get-tuple-element.50.refs_0_, ...), custom_call_target="tpu_custom_call" | custom-call | bytes 7000000 | tf_op jit(solution)/shard_map/pallas_call | solution.py:528
  38.2 1.6 %collective-permute-start.15 = (bf16[64,3072]{1,0:T(8,128)(2,1)S(1)}, bf16[64,3072]{1,0:T(8,128)(2,1)S(1)}, u32[]{:S(2)}, u32[]{:S(2)}) collective-permute-start(bf16[64,3072]{1,0:T(8,128)(2,1)S(1)} %get-tuple-element.60), channel_id=1, source_target_pairs={{0,6},{2,4},{4,2},{6,0},{8,14},{10,12},{12,10},{14,8},{16,22},{18,... | collective-permute-start | bytes 1179656 | tf_op jit(solution)/shard_map/ppermute | solution.py:56
  41.7 9.4 %collective-permute-done.15.refs_3_ = bf16[64,3072]{1,0:T(8,128)(2,1)S(1)} collective-permute-done((bf16[64,3072]{1,0:T(8,128)(2,1)S(1)}, bf16[64,3072]{1,0:T(8,128)(2,1)S(1)}, u32[]{:S(2)}, u32[]{:S(2)}) %collective-permute-start.15) | collective-permute-done | bytes 393248 | tf_op jit(solution)/shard_map/ppermute | solution.py:56
  51.1 7.6 %collective-permute-done.16.refs_4_ = bf16[64,3072]{1,0:T(8,128)(2,1)S(1)} collective-permute-done((bf16[64,3072]{1,0:T(8,128)(2,1)S(1)}, bf16[64,3072]{1,0:T(8,128)(2,1)S(1)}, u32[]{:S(2)}, u32[]{:S(2)}) %collective-permute-start.16) | collective-permute-done | bytes 393248 | tf_op jit(solution)/shard_map/ppermute | solution.py:56
  59.0 2.8 %collective-permute-start.18 = (bf16[16,2560]{1,0:T(8,128)(2,1)S(1)}, bf16[16,2560]{1,0:T(8,128)(2,1)S(1)}, u32[]{:S(2)}, u32[]{:S(2)}) collective-permute-start(bf16[16,2560]{1,0:T(8,128)(2,1)S(1)} %get-tuple-element.79), channel_id=1, source_target_pairs={{0,24},{2,26},{4,28},{6,30},{8,16},{10,18},{12,20},{14,22},{16,8},... | collective-permute-start | bytes 245768 | tf_op jit(solution)/shard_map/ppermute | solution.py:56
  61.8 1.7 %collective-permute-start.19 = (bf16[16,2560]{1,0:T(8,128)(2,1)S(1)}, bf16[16,2560]{1,0:T(8,128)(2,1)S(1)}, u32[]{:S(2)}, u32[]{:S(2)}) collective-permute-start(bf16[16,2560]{1,0:T(8,128)(2,1)S(1)} %get-tuple-element.81), channel_id=1, source_target_pairs={{0,8},{2,10},{4,12},{6,14},{8,0},{10,2},{12,4},{14,6},{16,24},{18,... | collective-permute-start | bytes 245768 | tf_op jit(solution)/shard_map/ppermute | solution.py:56
  63.5 2.9 %shard_map.115 = (bf16[4,512,128]{2,1,0:T(8,128)(2,1)S(1)}, bf16[4,512,128]{2,1,0:T(8,128)(2,1)S(1)}) custom-call(s32[4,128]{1,0:T(4,128)S(1)} %pad_add_fusion.refs_0_.scalar_ref, s32[4,8,1,128]{3,2,1,0:T(1,128)S(1)} %reshape.59.refs_1_, s32[4,8,1,128]{3,2,1,0:T(1,128)S(1)} %collective-permute-done.2.refs_2_, ...), custom_call_target="tpu_custom_call" | custom-call | bytes 10500000 | tf_op jit(solution)/shard_map/pallas_call | solution.py:550
  66.5 2.2 %collective-permute-done.20 = bf16[16,2560]{1,0:T(8,128)(2,1)S(1)} collective-permute-done((bf16[16,2560]{1,0:T(8,128)(2,1)S(1)}, bf16[16,2560]{1,0:T(8,128)(2,1)S(1)}, u32[]{:S(2)}, u32[]{:S(2)}) %collective-permute-start.20) | collective-permute-done | bytes 81952 | tf_op jit(solution)/shard_map/ppermute | solution.py:56
  68.7 2.7 %collective-permute-start.23 = (bf16[16,2560]{1,0:T(8,128)(2,1)S(1)}, bf16[16,2560]{1,0:T(8,128)(2,1)S(1)}, u32[]{:S(2)}, u32[]{:S(2)}) collective-permute-start(bf16[16,2560]{1,0:T(8,128)(2,1)S(1)} %add_convert_fusion.2), channel_id=1, source_target_pairs={{0,24},{2,26},{4,28},{6,30},{8,16},{10,18},{12,20},{14,22},{16,8},... | collective-permute-start | bytes 245768 | tf_op jit(solution)/shard_map/ppermute | solution.py:56
  71.4 1.7 %collective-permute-start.21 = (bf16[16,2560]{1,0:T(8,128)(2,1)S(1)}, bf16[16,2560]{1,0:T(8,128)(2,1)S(1)}, u32[]{:S(2)}, u32[]{:S(2)}) collective-permute-start(bf16[16,2560]{1,0:T(8,128)(2,1)S(1)} %add_convert_fusion.2), channel_id=1, source_target_pairs={{0,8},{2,10},{4,12},{6,14},{8,0},{10,2},{12,4},{14,6},{16,24},{18,... | collective-permute-start | bytes 245768 | tf_op jit(solution)/shard_map/ppermute | solution.py:56
  73.2 2.8 %collective-permute-done.23 = bf16[16,2560]{1,0:T(8,128)(2,1)S(1)} collective-permute-done((bf16[16,2560]{1,0:T(8,128)(2,1)S(1)}, bf16[16,2560]{1,0:T(8,128)(2,1)S(1)}, u32[]{:S(2)}, u32[]{:S(2)}) %collective-permute-start.23) | collective-permute-done | bytes 81952 | tf_op jit(solution)/shard_map/ppermute | solution.py:56
  75.9 2.9 %collective-permute-done.22 = bf16[16,2560]{1,0:T(8,128)(2,1)S(1)} collective-permute-done((bf16[16,2560]{1,0:T(8,128)(2,1)S(1)}, bf16[16,2560]{1,0:T(8,128)(2,1)S(1)}, u32[]{:S(2)}, u32[]{:S(2)}) %collective-permute-start.22) | collective-permute-done | bytes 81952 | tf_op jit(solution)/shard_map/ppermute | solution.py:56
  82.6 2.2 %collective-permute-start.30 = (bf16[512,128]{1,0:T(8,128)(2,1)S(1)}, bf16[512,128]{1,0:T(8,128)(2,1)S(1)}, u32[]{:S(2)}, u32[]{:S(2)}) collective-permute-start(bf16[512,128]{1,0:T(8,128)(2,1)S(1)} %get-tuple-element.76), channel_id=1, source_target_pairs={{0,24},{2,26},{4,28},{6,30},{8,16},{10,18},{12,20},{14,22},{16,8},... | collective-permute-start | bytes 393224 | tf_op jit(solution)/shard_map/ppermute | solution.py:56
  84.9 5.6 %collective-permute-done.28.refs_1_ = bf16[64,2560]{1,0:T(8,128)(2,1)S(1)} collective-permute-done((bf16[64,2560]{1,0:T(8,128)(2,1)S(1)}, bf16[64,2560]{1,0:T(8,128)(2,1)S(1)}, u32[]{:S(2)}, u32[]{:S(2)}) %collective-permute-start.28) | collective-permute-done | bytes 327712 | tf_op jit(solution)/shard_map/ppermute | solution.py:56
  90.9 1.7 %shard_map.116 = (f32[256,2048]{1,0:T(8,128)}, f32[256,512]{1,0:T(8,128)}) custom-call(s32[4,128]{1,0:T(4,128)S(1)} %pad_add_fusion.refs_0_.scalar_ref, bf16[64,2560]{1,0:T(8,128)(2,1)S(1)} %pad_maximum_fusion.1.refs_0_, bf16[64,2560]{1,0:T(8,128)(2,1)S(1)} %collective-permute-done.28.refs_1_), custom_call_target="tpu_custom_call" | custom-call | bytes 3500000 | tf_op jit(solution)/shard_map/pallas_call | solution.py:597
  92.6 3.7 %collective-permute-done.25.refs_1_ = bf16[64,2560]{1,0:T(8,128)(2,1)S(1)} collective-permute-done((bf16[64,2560]{1,0:T(8,128)(2,1)S(1)}, bf16[64,2560]{1,0:T(8,128)(2,1)S(1)}, u32[]{:S(2)}, u32[]{:S(2)}) %collective-permute-start.25) | collective-permute-done | bytes 327712 | tf_op jit(solution)/shard_map/ppermute | solution.py:56
  97.2 2.4 %shard_map.117 = (f32[256,2048]{1,0:T(8,128)}, f32[256,512]{1,0:T(8,128)}, f32[512,128]{1,0:T(8,128)}) custom-call(s32[4,128]{1,0:T(4,128)S(1)} %pad_add_fusion.refs_0_.scalar_ref, bf16[64,2560]{1,0:T(8,128)(2,1)S(1)} %collective-permute-done.24.refs_0_, ...), custom_call_target="tpu_custom_call", output_to_operand_aliasing={{0}: (7, {}), {1}: (8, {})} | custom-call | bytes 3500000 | tf_op jit(solution)/shard_map/pallas_call | solution.py:597
  (64 shorter events, 22.1 us)
Async XLA Ops:
  1.6 14.9 %collective-permute-start.8 = (bf16[512,128]{1,0:T(8,128)(2,1)S(1)}, bf16[512,128]{1,0:T(8,128)(2,1)S(1)}, u32[]{:S(2)}, u32[]{:S(2)}) collective-permute-start(bf16[512,128]{1,0:T(8,128)(2,1)S(1)} %dynamic-slice_bitcast_fusion.refs_3_), channel_id=1, source_target_pairs={{0,24},{2,26},{4,28},{6,30},{8,16},{10,18},{12,20},{14,22},{16,8},... | collective-permute-start | bytes 393224 | tf_op jit(solution)/shard_map/ppermute | solution.py:56
  6.7 11.1 %collective-permute-start.6 = (bf16[512,128]{1,0:T(8,128)(2,1)S(1)}, bf16[512,128]{1,0:T(8,128)(2,1)S(1)}, u32[]{:S(2)}, u32[]{:S(2)}) collective-permute-start(bf16[512,128]{1,0:T(8,128)(2,1)S(1)} %dynamic-slice_bitcast_fusion.refs_3_), channel_id=1, source_target_pairs={{0,16},{2,18},{4,20},{6,22},{8,24},{10,26},{12,28},{14,30},{16,0},... | collective-permute-start | bytes 393224 | tf_op jit(solution)/shard_map/ppermute | solution.py:56
  6.7 9.2 %collective-permute-start.4 = (bf16[512,128]{1,0:T(8,128)(2,1)S(1)}, bf16[512,128]{1,0:T(8,128)(2,1)S(1)}, u32[]{:S(2)}, u32[]{:S(2)}) collective-permute-start(bf16[512,128]{1,0:T(8,128)(2,1)S(1)} %dynamic-slice_bitcast_fusion.refs_3_), channel_id=1, source_target_pairs={{0,8},{2,10},{4,12},{6,14},{8,0},{10,2},{12,4},{14,6},{16,24},{18,... | collective-permute-start | bytes 393224 | tf_op jit(solution)/shard_map/ppermute | solution.py:56
  7.4 11.5 %collective-permute-start.3 = (bf16[512,128]{1,0:T(8,128)(2,1)S(1)}, bf16[512,128]{1,0:T(8,128)(2,1)S(1)}, u32[]{:S(2)}, u32[]{:S(2)}) collective-permute-start(bf16[512,128]{1,0:T(8,128)(2,1)S(1)} %dynamic-slice_bitcast_fusion.refs_3_), channel_id=1, source_target_pairs={{0,1},{1,0},{2,3},{3,2},{4,5},{5,4},{6,7},{7,6},{8,9},{9,8},{10,11... | collective-permute-start | bytes 393224 | tf_op jit(solution)/shard_map/ppermute | solution.py:48
  22.2 7.6 %collective-permute-start.13 = (bf16[256,2560]{1,0:T(8,128)(2,1)S(1)}, bf16[256,2560]{1,0:T(8,128)(2,1)S(1)}, u32[]{:S(2)}, u32[]{:S(2)}) collective-permute-start(bf16[256,2560]{1,0:T(8,128)(2,1)S(1)} %pad_maximum_fusion.refs_4_.refs_5_), channel_id=1, source_target_pairs={{0,1},{1,0},{2,3},{3,2},{4,5},{5,4},{6,7},{7,6},{8,9},{9,8},{10,11... | collective-permute-start | bytes 3932168 | tf_op jit(solution)/shard_map/ppermute | solution.py:48
  22.5 5.2 %collective-permute-start.10 = (bf16[256,128]{1,0:T(8,128)(2,1)S(1)}, bf16[256,128]{1,0:T(8,128)(2,1)S(1)}, u32[]{:S(2)}, u32[]{:S(2)}) collective-permute-start(bf16[256,128]{1,0:T(8,128)(2,1)S(1)} %get-tuple-element.45), channel_id=1, source_target_pairs={{0,6},{2,4},{4,2},{6,0},{8,14},{10,12},{12,10},{14,8},{16,22},{18,... | collective-permute-start | bytes 196616 | tf_op jit(solution)/shard_map/ppermute | solution.py:56
  25.0 4.3 %collective-permute-start.11 = (bf16[256,128]{1,0:T(8,128)(2,1)S(1)}, bf16[256,128]{1,0:T(8,128)(2,1)S(1)}, u32[]{:S(2)}, u32[]{:S(2)}) collective-permute-start(bf16[256,128]{1,0:T(8,128)(2,1)S(1)} %get-tuple-element.46), channel_id=1, source_target_pairs={{0,4},{2,6},{4,0},{6,2},{8,12},{10,14},{12,8},{14,10},{16,20},{18,... | collective-permute-start | bytes 196616 | tf_op jit(solution)/shard_map/ppermute | solution.py:56
  25.5 4.3 %collective-permute-start.12 = (bf16[256,128]{1,0:T(8,128)(2,1)S(1)}, bf16[256,128]{1,0:T(8,128)(2,1)S(1)}, u32[]{:S(2)}, u32[]{:S(2)}) collective-permute-start(bf16[256,128]{1,0:T(8,128)(2,1)S(1)} %get-tuple-element.47), channel_id=1, source_target_pairs={{0,2},{2,0},{4,6},{6,4},{8,10},{10,8},{12,14},{14,12},{16,18},{18,... | collective-permute-start | bytes 196616 | tf_op jit(solution)/shard_map/ppermute | solution.py:56
  38.2 13.0 %collective-permute-start.15 = (bf16[64,3072]{1,0:T(8,128)(2,1)S(1)}, bf16[64,3072]{1,0:T(8,128)(2,1)S(1)}, u32[]{:S(2)}, u32[]{:S(2)}) collective-permute-start(bf16[64,3072]{1,0:T(8,128)(2,1)S(1)} %get-tuple-element.60), channel_id=1, source_target_pairs={{0,6},{2,4},{4,2},{6,0},{8,14},{10,12},{12,10},{14,8},{16,22},{18,... | collective-permute-start | bytes 1179656 | tf_op jit(solution)/shard_map/ppermute | solution.py:56
  39.7 19.0 %collective-permute-start.16 = (bf16[64,3072]{1,0:T(8,128)(2,1)S(1)}, bf16[64,3072]{1,0:T(8,128)(2,1)S(1)}, u32[]{:S(2)}, u32[]{:S(2)}) collective-permute-start(bf16[64,3072]{1,0:T(8,128)(2,1)S(1)} %get-tuple-element.61), channel_id=1, source_target_pairs={{0,4},{2,6},{4,0},{6,2},{8,12},{10,14},{12,8},{14,10},{16,20},{18,... | collective-permute-start | bytes 1179656 | tf_op jit(solution)/shard_map/ppermute | solution.py:56
  40.6 18.3 %collective-permute-start.17 = (bf16[64,3072]{1,0:T(8,128)(2,1)S(1)}, bf16[64,3072]{1,0:T(8,128)(2,1)S(1)}, u32[]{:S(2)}, u32[]{:S(2)}) collective-permute-start(bf16[64,3072]{1,0:T(8,128)(2,1)S(1)} %get-tuple-element.62), channel_id=1, source_target_pairs={{0,2},{2,0},{4,6},{6,4},{8,10},{10,8},{12,14},{14,12},{16,18},{18,... | collective-permute-start | bytes 1179656 | tf_op jit(solution)/shard_map/ppermute | solution.py:56
  59.0 7.4 %collective-permute-start.18 = (bf16[16,2560]{1,0:T(8,128)(2,1)S(1)}, bf16[16,2560]{1,0:T(8,128)(2,1)S(1)}, u32[]{:S(2)}, u32[]{:S(2)}) collective-permute-start(bf16[16,2560]{1,0:T(8,128)(2,1)S(1)} %get-tuple-element.79), channel_id=1, source_target_pairs={{0,24},{2,26},{4,28},{6,30},{8,16},{10,18},{12,20},{14,22},{16,8},... | collective-permute-start | bytes 245768 | tf_op jit(solution)/shard_map/ppermute | solution.py:56
  61.8 6.9 %collective-permute-start.20 = (bf16[16,2560]{1,0:T(8,128)(2,1)S(1)}, bf16[16,2560]{1,0:T(8,128)(2,1)S(1)}, u32[]{:S(2)}, u32[]{:S(2)}) collective-permute-start(bf16[16,2560]{1,0:T(8,128)(2,1)S(1)} %get-tuple-element.80), channel_id=1, source_target_pairs={{0,16},{2,18},{4,20},{6,22},{8,24},{10,26},{12,28},{14,30},{16,0},... | collective-permute-start | bytes 245768 | tf_op jit(solution)/shard_map/ppermute | solution.py:56
  61.8 6.9 %collective-permute-start.19 = (bf16[16,2560]{1,0:T(8,128)(2,1)S(1)}, bf16[16,2560]{1,0:T(8,128)(2,1)S(1)}, u32[]{:S(2)}, u32[]{:S(2)}) collective-permute-start(bf16[16,2560]{1,0:T(8,128)(2,1)S(1)} %get-tuple-element.81), channel_id=1, source_target_pairs={{0,8},{2,10},{4,12},{6,14},{8,0},{10,2},{12,4},{14,6},{16,24},{18,... | collective-permute-start | bytes 245768 | tf_op jit(solution)/shard_map/ppermute | solution.py:56
  66.4 16.1 %collective-permute-start.26 = (bf16[4,512,128]{2,1,0:T(8,128)(2,1)S(1)}, bf16[4,512,128]{2,1,0:T(8,128)(2,1)S(1)}, u32[]{:S(2)}, u32[]{:S(2)}) collective-permute-start(bf16[4,512,128]{2,1,0:T(8,128)(2,1)S(1)} %get-tuple-element.66), channel_id=1, source_target_pairs={{0,1},{1,0},{2,3},{3,2},{4,5},{5,4},{6,7},{7,6},{8,9},{9,8},{10,11... | collective-permute-start | bytes 1572872 | tf_op jit(solution)/shard_map/ppermute | solution.py:48
  68.7 7.2 %collective-permute-start.23 = (bf16[16,2560]{1,0:T(8,128)(2,1)S(1)}, bf16[16,2560]{1,0:T(8,128)(2,1)S(1)}, u32[]{:S(2)}, u32[]{:S(2)}) collective-permute-start(bf16[16,2560]{1,0:T(8,128)(2,1)S(1)} %add_convert_fusion.2), channel_id=1, source_target_pairs={{0,24},{2,26},{4,28},{6,30},{8,16},{10,18},{12,20},{14,22},{16,8},... | collective-permute-start | bytes 245768 | tf_op jit(solution)/shard_map/ppermute | solution.py:56
  71.4 7.4 %collective-permute-start.22 = (bf16[16,2560]{1,0:T(8,128)(2,1)S(1)}, bf16[16,2560]{1,0:T(8,128)(2,1)S(1)}, u32[]{:S(2)}, u32[]{:S(2)}) collective-permute-start(bf16[16,2560]{1,0:T(8,128)(2,1)S(1)} %add_convert_fusion.2), channel_id=1, source_target_pairs={{0,16},{2,18},{4,20},{6,22},{8,24},{10,26},{12,28},{14,30},{16,0},... | collective-permute-start | bytes 245768 | tf_op jit(solution)/shard_map/ppermute | solution.py:56
  71.4 7.4 %collective-permute-start.21 = (bf16[16,2560]{1,0:T(8,128)(2,1)S(1)}, bf16[16,2560]{1,0:T(8,128)(2,1)S(1)}, u32[]{:S(2)}, u32[]{:S(2)}) collective-permute-start(bf16[16,2560]{1,0:T(8,128)(2,1)S(1)} %add_convert_fusion.2), channel_id=1, source_target_pairs={{0,8},{2,10},{4,12},{6,14},{8,0},{10,2},{12,4},{14,6},{16,24},{18,... | collective-permute-start | bytes 245768 | tf_op jit(solution)/shard_map/ppermute | solution.py:56
  78.9 11.6 %collective-permute-start.28 = (bf16[64,2560]{1,0:T(8,128)(2,1)S(1)}, bf16[64,2560]{1,0:T(8,128)(2,1)S(1)}, u32[]{:S(2)}, u32[]{:S(2)}) collective-permute-start(bf16[64,2560]{1,0:T(8,128)(2,1)S(1)} %pad_maximum_fusion.1.refs_0_), channel_id=1, source_target_pairs={{0,6},{2,4},{4,2},{6,0},{8,14},{10,12},{12,10},{14,8},{16,22},{18,... | collective-permute-start | bytes 983048 | tf_op jit(solution)/shard_map/ppermute | solution.py:56
  80.4 15.9 %collective-permute-start.25 = (bf16[64,2560]{1,0:T(8,128)(2,1)S(1)}, bf16[64,2560]{1,0:T(8,128)(2,1)S(1)}, u32[]{:S(2)}, u32[]{:S(2)}) collective-permute-start(bf16[64,2560]{1,0:T(8,128)(2,1)S(1)} %pad_maximum_fusion.1.refs_0_), channel_id=1, source_target_pairs={{0,4},{2,6},{4,0},{6,2},{8,12},{10,14},{12,8},{14,10},{16,20},{18,... | collective-permute-start | bytes 983048 | tf_op jit(solution)/shard_map/ppermute | solution.py:56
  81.3 15.1 %collective-permute-start.24 = (bf16[64,2560]{1,0:T(8,128)(2,1)S(1)}, bf16[64,2560]{1,0:T(8,128)(2,1)S(1)}, u32[]{:S(2)}, u32[]{:S(2)}) collective-permute-start(bf16[64,2560]{1,0:T(8,128)(2,1)S(1)} %pad_maximum_fusion.1.refs_0_), channel_id=1, source_target_pairs={{0,2},{2,0},{4,6},{6,4},{8,10},{10,8},{12,14},{14,12},{16,18},{18,... | collective-permute-start | bytes 983048 | tf_op jit(solution)/shard_map/ppermute | solution.py:56
  82.6 13.7 %collective-permute-start.30 = (bf16[512,128]{1,0:T(8,128)(2,1)S(1)}, bf16[512,128]{1,0:T(8,128)(2,1)S(1)}, u32[]{:S(2)}, u32[]{:S(2)}) collective-permute-start(bf16[512,128]{1,0:T(8,128)(2,1)S(1)} %get-tuple-element.76), channel_id=1, source_target_pairs={{0,24},{2,26},{4,28},{6,30},{8,16},{10,18},{12,20},{14,22},{16,8},... | collective-permute-start | bytes 393224 | tf_op jit(solution)/shard_map/ppermute | solution.py:56
  84.9 11.5 %collective-permute-start.29 = (bf16[512,128]{1,0:T(8,128)(2,1)S(1)}, bf16[512,128]{1,0:T(8,128)(2,1)S(1)}, u32[]{:S(2)}, u32[]{:S(2)}) collective-permute-start(bf16[512,128]{1,0:T(8,128)(2,1)S(1)} %get-tuple-element.77), channel_id=1, source_target_pairs={{0,16},{2,18},{4,20},{6,22},{8,24},{10,26},{12,28},{14,30},{16,0},... | collective-permute-start | bytes 393224 | tf_op jit(solution)/shard_map/ppermute | solution.py:56
  90.5 6.7 %collective-permute-start.27 = (bf16[512,128]{1,0:T(8,128)(2,1)S(1)}, bf16[512,128]{1,0:T(8,128)(2,1)S(1)}, u32[]{:S(2)}, u32[]{:S(2)}) collective-permute-start(bf16[512,128]{1,0:T(8,128)(2,1)S(1)} %get-tuple-element.78), channel_id=1, source_target_pairs={{0,8},{2,10},{4,12},{6,14},{8,0},{10,2},{12,4},{14,6},{16,24},{18,... | collective-permute-start | bytes 393224 | tf_op jit(solution)/shard_map/ppermute | solution.py:56
  (9 other events, 38.2 us)
